TPU v7x, 32 devices: a whole 2x2x4 slice. The times are simulated.
32 devices in a mesh: slab: 16 (over z, x, core), cell: 2 (over y).
Axes of the slice: x: 2, y: 2, z: 4, core: 2. Of those that a mesh axis runs over, the one named last changes fastest.
Arguments:
- charges: float32 [8, 128, 2048], P(None, 'slab', 'cell'), may hold values from -6 to 6
- counts: int32 [128, 2048], P('slab', 'cell'), may hold values from 1 to 8
- projection: float32 [8, 64, 128, 2048], P(None, None, 'slab', 'cell'), may hold values from -1.2 to 1.2
- near_blocks: float32 [6, 8, 8, 128, 2048], P(None, None, None, 'slab', 'cell'), may hold values from -0.9 to 0.9
- neighbours: int32 [6, 128, 2048], P(None, 'slab', 'cell'), may hold values from 0 to 26, as said below
- spectrum: float32 [512, 64, 512], P(None, None, 'slab'), may hold values from 0.25 to 4, as said below
Outputs:
- potentials: float32 [8, 128, 2048], P(None, 'slab', 'cell')
Inputs may be any that keep to these rules, and one draw needn't show every extreme that they name: `counts`: 8 is reached. neighbours[k, x, c] codes an offset in the 3 x 3 x 3 block of cells around c as in the near_field step; entry k = 0 is 13, the cell itself, and the 6 entries of a cell are distinct. spectrum[kx, kz, ky] = spectrum[(-kx) mod 512, (-kz) mod 64, (-ky) mod 512].
All inputs are finite; a program needn't handle non-finite values.
Results may differ from a plain program's by a relative error of at most 0.00005.
Values sent between devices are 32-bit elements; how exact they have to be, the bound alone decides.
No kernel may reach another device: no remote copies, remote signals or barrier semaphores. Data moves between devices by JAX's collectives and lax.ppermute only.
A program may use at most 192 MiB of HBM per device.

v0:
```python
import math

import jax
import jax.numpy as jnp
from jax import lax
from jax.sharding import PartitionSpec as P

NX = 512
NY = 512
NZ = 64
TX = 4
TY = 4
TZ = 4
NZC = 16


def padded(value, sides, width):
    for axis, dim in sides:
        count, length = (lax.axis_size(axis), value.shape[dim])
        up = [(i, (i + 1) % count) for i in range(count)]
        down = [(j, i) for i, j in up]
        last = lax.slice_in_dim(value, length - width, length, axis=dim)
        first = lax.slice_in_dim(value, 0, width, axis=dim)
        before = lax.ppermute(last, axis, up)
        after = lax.ppermute(first, axis, down)
        value = jnp.concatenate([before, value, after], axis=dim)
    return value


def wave_tables(row_count, col_count, length):
    products = (
        lax.broadcasted_iota(jnp.int32, (row_count, col_count), 0)
        * lax.broadcasted_iota(jnp.int32, (row_count, col_count), 1)
        % length
    )
    angle_rad = products.astype(jnp.float32) * (2.0 * math.pi / length)
    return (jnp.cos(angle_rad), jnp.sin(angle_rad))


def depth_rows(freq_ids, valid, weights):
    depth_ids = lax.broadcasted_iota(jnp.int32, (freq_ids.shape[0], NZ), 1)
    products = freq_ids[:, None] * depth_ids % NZ
    angle_rad = products.astype(jnp.float32) * (2.0 * math.pi / NZ)
    basis = jnp.stack([jnp.cos(angle_rad), -jnp.sin(angle_rad)])
    return (basis * valid[None, :, None], basis * weights[None, :, None])


def half_depth_tables(cell_count):
    lower = NZ // (2 * cell_count)
    row_ids = lax.broadcasted_iota(jnp.int32, (cell_count * (lower + 1),), 0)
    block_ids = row_ids // (lower + 1)
    slot_ids = row_ids % (lower + 1)
    freq_ids = jnp.where(slot_ids < lower, block_ids * lower + slot_ids, NZ // 2)
    valid = jnp.where((slot_ids < lower) | (block_ids == 0), 1.0, 0.0).astype(jnp.float32)
    doubled = jnp.where((slot_ids < lower) & (freq_ids > 0), 2.0, 1.0).astype(jnp.float32)
    forward_table, backward_table = depth_rows(freq_ids, valid, valid * doubled)
    return (forward_table, backward_table, freq_ids)


def combine_halves(first_part, second, orient):
    half_width = first_part.shape[-1] // 2
    real_part = first_part[..., :half_width] + orient * second[..., half_width:]
    imag_part = first_part[..., half_width:] - orient * second[..., :half_width]
    return jnp.concatenate([real_part, imag_part], axis=-1)


def transform_axis(pattern, cosine, sine_tab, values, orient):
    first_part = jnp.einsum(pattern, cosine, values, precision=lax.Precision.HIGHEST)
    second = jnp.einsum(pattern, sine_tab, values, precision=lax.Precision.HIGHEST)
    return combine_halves(first_part, second, orient)


def twiddle(values, twist_cos, twist_sin, orient):
    half_width = values.shape[-1] // 2
    real_part = values[..., :half_width]
    imag_part = values[..., half_width:]
    new_real = real_part * twist_cos + orient * imag_part * twist_sin
    new_imag = imag_part * twist_cos - orient * real_part * twist_sin
    return jnp.concatenate([new_real, new_imag], axis=-1)


def transform_rows(planes_block, cosine, sine_tab, orient):
    flat_rows = planes_block.reshape(-1, planes_block.shape[-1])
    first_part = jnp.dot(flat_rows, cosine, precision=lax.Precision.HIGHEST).reshape(
        planes_block.shape
    )
    second = jnp.dot(flat_rows, sine_tab, precision=lax.Precision.HIGHEST).reshape(
        planes_block.shape
    )
    real_part = first_part[:, 0] + orient * second[:, 1]
    imag_part = first_part[:, 1] - orient * second[:, 0]
    return jnp.stack([real_part, imag_part], axis=1)


def per_device(charges, counts, projection, near_blocks, neighbours, spectrum):
    panels, cell_planes, cell_cols = charges.shape
    planes = cell_planes * TX
    rows_cell = cell_cols // NZC
    slot_ids = lax.broadcasted_iota(jnp.int32, charges.shape, 0)
    panel_mask = (slot_ids < counts[None]).astype(jnp.float32)
    masked = charges * panel_mask
    tile_values = jnp.einsum("ptxc,pxc->txc", projection, masked, precision=lax.Precision.HIGHEST)
    grid_field = (
        tile_values.reshape(TX, TY, TZ, cell_planes, rows_cell, NZC)
        .transpose(3, 0, 5, 2, 4, 1)
        .reshape(planes, NZ, rows_cell * TY)
    )
    cell_count = lax.axis_size("cell")
    forward_table, backward_table, freq_ids = half_depth_tables(cell_count)
    depth_count = forward_table.shape[1] // cell_count
    spectra_z = jnp.einsum(
        "wkz,xzy->xwky", forward_table, grid_field, precision=lax.Precision.HIGHEST
    )
    cosine_y, sine_y = wave_tables(NY, NY, NY)
    pencils = transform_rows(
        lax.all_to_all(spectra_z, "cell", split_axis=2, concat_axis=3, tiled=True),
        cosine_y,
        sine_y,
        1.0,
    )
    columns = lax.all_to_all(pencils, "slab", split_axis=3, concat_axis=0, tiled=True)
    col_width = columns.shape[2] * columns.shape[3]
    flat_rows = columns.reshape(NX, 2 * col_width)
    first_row = lax.axis_index("cell") * depth_count
    kernel_ids = lax.dynamic_slice_in_dim(freq_ids, first_row, depth_count, 0)
    kernel = jnp.take(spectrum, kernel_ids, axis=1).reshape(NX, col_width) * (1.0 / (NX * NY * NZ))
    kernel_both = jnp.concatenate([kernel, kernel], axis=1)
    slab_count = lax.axis_size("slab")
    local_rows = NX // slab_count
    cosine_s, sine_s = wave_tables(slab_count, slab_count, slab_count)
    cosine_r, sine_r = wave_tables(local_rows, local_rows, local_rows)
    twist_cos, twist_sin = wave_tables(slab_count, local_rows, NX)
    twist_cos = twist_cos[:, :, None]
    twist_sin = twist_sin[:, :, None]
    section_one = transform_axis(
        "ks,src->krc",
        cosine_s,
        sine_s,
        flat_rows.reshape(slab_count, local_rows, 2 * col_width),
        1.0,
    )
    section_one = twiddle(section_one, twist_cos, twist_sin, 1.0)
    section_two = transform_axis("jr,krc->jkc", cosine_r, sine_r, section_one, 1.0)
    weighted = section_two.reshape(NX, 2 * col_width) * kernel_both
    section_one = transform_axis(
        "rj,jkc->krc",
        cosine_r,
        sine_r,
        weighted.reshape(local_rows, slab_count, 2 * col_width),
        -1.0,
    )
    section_one = twiddle(section_one, twist_cos, twist_sin, -1.0)
    section_two = transform_axis("sk,krc->src", cosine_s, sine_s, section_one, -1.0)
    returned_x = section_two.reshape(NX, 2 * col_width)
    returned = lax.all_to_all(
        returned_x.reshape(columns.shape), "slab", split_axis=0, concat_axis=3, tiled=True
    )
    inverse_rows = transform_rows(returned, cosine_y, sine_y, -1.0)
    grid_potential = jnp.einsum(
        "wkz,xwky->xzy",
        backward_table,
        lax.all_to_all(inverse_rows, "cell", split_axis=3, concat_axis=2, tiled=True),
        precision=lax.Precision.HIGHEST,
    )
    tile_potential = (
        grid_potential.reshape(cell_planes, TX, NZC, TZ, rows_cell, TY)
        .transpose(1, 5, 3, 0, 4, 2)
        .reshape(TX * TY * TZ, cell_planes, cell_cols)
    )
    far_field = jnp.einsum(
        "ptxc,txc->pxc", projection, tile_potential, precision=lax.Precision.HIGHEST
    )
    block = masked.reshape(panels, cell_planes, rows_cell, NZC)
    extended = padded(block, (("slab", 1), ("cell", 2)), 1)
    flat_ext = extended.reshape(panels, -1)
    step_x = neighbours // 9 - 1
    step_y = neighbours // 3 % 3 - 1
    step_z = neighbours % 3 - 1
    plane_ids = lax.broadcasted_iota(jnp.int32, neighbours.shape, 1)
    col_ids = lax.broadcasted_iota(jnp.int32, neighbours.shape, 2)
    row_ids = col_ids // NZC
    depth_ids = col_ids % NZC
    near_ids = ((plane_ids + step_x + 1) * (rows_cell + 2) + row_ids + step_y + 1) * NZC + (
        depth_ids + step_z
    ) % NZC
    near_count = neighbours.shape[0]
    picked = jnp.take(flat_ext, near_ids.reshape(-1), axis=1).reshape(
        panels, near_count, cell_planes, cell_cols
    )
    near_field = jnp.einsum("kpqxc,qkxc->pxc", near_blocks, picked, precision=lax.Precision.HIGHEST)
    return (far_field + near_field) * panel_mask


def solution(mesh):
    in_specs = (
        P(None, "slab", "cell"),
        P("slab", "cell"),
        P(None, None, "slab", "cell"),
        P(None, None, None, "slab", "cell"),
        P(None, "slab", "cell"),
        P(None, None, "slab"),
    )
    out_specs = P(None, "slab", "cell")
    return jax.shard_map(
        per_device, mesh=mesh, in_specs=in_specs, out_specs=out_specs, check_vma=False
    )
```

profile of v0, /device:TPU:0, one launch (start us, length us, event | category | flops | bytes accessed | tf_op | source)
XLA Modules:
  0.0 881.7 jit_solution(17038607616216216445)
XLA Ops:
  0.2 1.0 fusion.187
  1.2 8.3 multiply_reduce_fusion.1
  9.5 9.0 %reshape.268 = f32[4,4,4,8,64,16]{5,4,3,2,1,0:T(8,128)} reshape(f32[64,8,1024]{2,1,0:T(8,128)S(1)} %bitcast.133) | data formatting | bytes 4194304 | tf_op jit(solution)/shard_map/reshape | solution.py:104
  18.5 59.1 %copy.118 = f32[8,4,16,4,64,4]{5,4,3,2,1,0:T(8,128)} copy(f32[8,4,16,4,64,4]{2,4,0,3,5,1:T(8,128)} %bitcast.117) | data formatting | bytes 4194304 | tf_op jit(solution)/shard_map/transpose | solution.py:105
  77.6 55.5 %reshape.294 = f32[32,64,256,1]{2,1,0,3:T(8,128)S(1)} reshape(f32[8,4,16,4,64,4]{5,4,3,2,1,0:T(8,128)} %copy.118) | data formatting | bytes 4194304 | tf_op jit(solution)/shard_map/reshape | solution.py:106
  133.1 2.4 fusion.14
  135.4 1.3 copy.119
  136.7 30.8 %all_to_all.63 = f32[32,2,34,256]{3,0,1,2:T(8,128)S(1)} all-to-all(f32[32,2,34,256]{3,0,1,2:T(8,128)S(1)} %copy.119), channel_id=1, replica_groups=mesh['slab'=16,'cell'=2] {'cell'}, dimensions={2} | all-to-all | bytes 4456448 | tf_op jit(solution)/shard_map/all_to_all | solution.py:116
  167.5 1.8 copy.121
  169.4 2.8 dot_general.57
  172.2 10.6 %fusion.32 = f32[32,2,17,512]{3,0,2,1:T(8,128)S(1)} fusion(f32[32,2,17,512]{3,0,2,1:T(8,128)} %dot_general.57), kind=kOutput, calls=%fused_computation.65 | convolution fusion | flops 3426222080 | bytes 4456448 | tf_op jit(solution)/shard_map/dot_general | solution.py:84
  182.7 8.8 fusion.36
  192.5 9.8 %copy.122 = f32[32,2,17,512]{0,1,2,3:T(2,128)} copy(f32[32,2,17,512]{3,0,2,1:T(8,128)S(1)} %pad_maximum_fusion.4) | data formatting | bytes 4456448 | tf_op jit(solution)/shard_map/stack | solution.py:92
  202.2 11.8 %reshape.309 = f32[16,1,34816]{2,1,0:T(1,128)} reshape(f32[512,17,2,32]{3,2,1,0:T(2,128)} %bitcast.121) | data formatting | bytes 4456448
  214.0 6.3 all-to-all-start.1
  222.4 4.1 collective-permute-start.1
  226.6 2.8 gather_fusion
  229.4 4.4 copy.128
  233.8 4.0 gather.13
  239.0 1.6 fusion.24
  240.6 26.1 %all-to-all-done.1 = f32[16,1,34816]{2,1,0:T(1,128)} async-done(((f32[16,1,34816]{2,1,0:T(1,128)}), f32[16,1,34816]{2,1,0:T(1,128)}, u32[]{:S(2)}, u32[]{:S(2)}) %all-to-all-start.1) | async-done | bytes 2228256 | tf_op jit(solution)/shard_map/all_to_all | solution.py:121
  267.2 7.6 reduce.6
  274.8 11.5 %reshape.310 = f32[512,17,2,32]{3,2,1,0:T(2,128)} reshape(f32[16,34816]{1,0:T(8,128)S(1)} %reduce.6) | data formatting | bytes 4456448
  286.4 15.0 %copy.123 = f32[32,2,17,16,32]{4,2,1,0,3:T(8,128)} copy(f32[32,2,17,16,32]{0,1,2,4,3:T(2,128)} %bitcast.122) | data formatting | bytes 4456448 | tf_op jit(solution)/shard_map/all_to_all | solution.py:121
  301.3 8.4 reshape_reshape.6
  309.8 3.2 fusion.6
  313.0 3.2 fusion.8
  317.5 2.7 fusion.2
  320.2 2.9 fusion.4
  324.4 2.7 fusion.42
  327.2 2.8 fusion.41
  329.9 1.4 copy.200
  331.3 1.4 copy.199
  333.6 2.3 fusion.13
  335.9 2.1 fusion.12
  339.2 7.4 copy.132
  346.6 6.5 reshape_reshape.7
  353.1 9.8 %copy.133 = f32[512,2,17,32]{3,1,2,0:T(2,128)} copy(f32[512,2,17,32]{0,3,2,1:T(8,128)S(1)} %reshape_reshape.7) | data formatting | bytes 4456448 | tf_op jit(solution)/shard_map/reshape;reshape | solution.py:156
  362.9 11.8 %reshape.311 = f32[16,1,34816]{2,1,0:T(1,128)} reshape(f32[512,17,2,32]{3,2,1,0:T(2,128)} %bitcast.123) | data formatting | bytes 4456448
  374.7 12.3 %all-to-all-start.2 = ((f32[16,1,34816]{2,1,0:T(1,128)}), f32[16,1,34816]{2,1,0:T(1,128)}, u32[]{:S(2)}, u32[]{:S(2)}) async-start(f32[16,1,34816]{2,1,0:T(1,128)} %reshape.311), calls=%async_computation.2 | async-start | bytes 4456448 | tf_op jit(solution)/shard_map/all_to_all | solution.py:155
  388.0 1.7 collective-permute-start.3
  389.7 2.3 collective-permute-done.2
  393.1 3.8 copy.145
  396.9 164.5 %gather_fusion.1 = f32[49152,8]{1,0:T(8,128)} fusion(f32[8,10560]{0,1:T(8,128)} %bitcast.118, s32[49152]{0:T(1024)S(1)} %broadcast_clamp_fusion), kind=kCustom, calls=%fused_computation.1 | custom fusion | bytes 3342336 | tf_op jit(solution)/shard_map/jit(_take)/gather | solution.py:187
  561.4 7.6 reduce.7
  569.0 11.8 %reshape.312 = f32[512,17,2,32]{3,2,1,0:T(2,128)} reshape(f32[16,34816]{1,0:T(8,128)S(1)} %reduce.7) | data formatting | bytes 4456448
  580.8 12.1 %copy.198 = f32[16,32,2,17,32]{4,0,1,3,2:T(8,128)} copy(f32[16,32,2,17,32]{4,2,3,1,0:T(2,128)} %bitcast.124) | data formatting | bytes 4456448 | tf_op jit(solution)/shard_map/all_to_all | solution.py:155
  592.9 6.5 dot_general.68
  599.4 8.8 fusion.30
  608.2 9.0 %fusion.34 = f32[32,2,17,512]{3,0,2,1:T(8,128)S(1)} fusion(f32[32,2,17,512]{3,0,2,1:T(8,128)S(1)} %dot_general.68), kind=kOutput, calls=%fused_computation.67 | convolution fusion | flops 3426222080 | bytes 4456448 | tf_op jit(solution)/shard_map/dot_general | solution.py:87
  618.2 9.7 %copy.136 = f32[32,2,17,512]{0,1,2,3:T(2,128)} copy(f32[32,2,17,512]{3,0,2,1:T(8,128)S(1)} %pad_maximum_fusion.5) | data formatting | bytes 4456448 | tf_op jit(solution)/shard_map/stack | solution.py:92
  627.9 15.1 %reshape.313 = f32[2,1,278528]{2,1,0:T(1,128)} reshape(f32[512,17,2,32]{3,2,1,0:T(2,128)} %bitcast.126) | data formatting | bytes 4456448
  643.0 3.8 all-to-all-start.3
  646.8 17.6 %select_bitcast_fusion = f32[8,1024,6,8]{3,1,0,2:T(8,128)} fusion(f32[8,6,8,1024]{0,3,2,1:T(8,128)} %bitcast.128, pred[6,8,1024]{2,1,0:T(8,128)(4,1)S(1)} %get-tuple-element.5), kind=kLoop, calls=%fused_computation.2 | loop fusion | flops 393216 | bytes 3194880
  664.4 15.4 %copy.178 = f32[8,1024,6,8]{1,0,3,2:T(8,128)} copy(f32[8,1024,6,8]{3,1,0,2:T(8,128)} %select_bitcast_fusion) | data formatting | bytes 3145728
  679.8 6.8 multiply_reduce_fusion.2
  686.5 8.6 reduce.8
  695.1 13.4 %reshape.314 = f32[512,17,2,32]{3,2,1,0:T(2,128)} reshape(f32[2,278528]{1,0:T(2,128)} %reduce.8) | data formatting | bytes 4456448
  708.6 11.3 %copy.138 = f32[32,2,2,17,256]{4,0,3,2,1:T(8,128)S(1)} copy(f32[32,2,2,17,256]{0,1,3,4,2:T(2,128)} %bitcast.127) | data formatting | bytes 4456448 | tf_op jit(solution)/shard_map/all_to_all | solution.py:162
  719.9 4.9 fusion.17
  724.8 71.4 %reshape.270 = f32[8,4,16,4,64,4]{5,4,3,2,1,0:T(8,128)} reshape(f32[32,64,256]{2,1,0:T(8,128)} %fusion.17) | data formatting | bytes 4194304 | tf_op jit(solution)/shard_map/reshape | solution.py:166
  796.2 62.2 %copy.140 = f32[4,4,4,8,64,16]{5,4,3,2,1,0:T(8,128)} copy(f32[4,4,4,8,64,16]{1,4,2,5,0,3:T(8,128)} %bitcast.39) | data formatting | bytes 4194304 | tf_op jit(solution)/shard_map/transpose | solution.py:167
  858.4 14.2 %reshape.271 = f32[64,8,1024]{2,1,0:T(8,128)S(1)} reshape(f32[4,4,4,8,64,16]{5,4,3,2,1,0:T(8,128)} %copy.140) | data formatting | bytes 4194304 | tf_op jit(solution)/shard_map/reshape | solution.py:168
  872.6 8.2 multiply_reduce_fusion
  (72 shorter events, 13.2 us)
Async XLA Ops:
  0.2 132.9 %copy-start.8 = (f32[1,34,64]{2,1,0:T(8,128)}, f32[1,34,64]{2,1,0:T(8,128)S(1)}, u32[]{:S(2)}) copy-start(f32[1,34,64]{2,1,0:T(8,128)S(1)} %get-tuple-element.25) | copy-start | bytes 26116
  0.2 132.9 %copy-start.10 = (f32[1,34,64]{2,1,0:T(8,128)}, f32[1,34,64]{2,1,0:T(8,128)S(1)}, u32[]{:S(2)}) copy-start(f32[1,34,64]{2,1,0:T(8,128)S(1)} %get-tuple-element.26) | copy-start | bytes 26116
  172.2 10.6 %copy-start.3 = (f32[32,2,17,512]{3,0,2,1:T(8,128)S(1)}, f32[32,2,17,512]{3,0,2,1:T(8,128)}, u32[]{:S(2)}) copy-start(f32[32,2,17,512]{3,0,2,1:T(8,128)} %dot_general.57) | copy-start | bytes 6684676
  214.0 6.3 copy-start.4
  214.0 6.3 copy-start.5
  214.0 52.6 %all-to-all-start.1 = ((f32[16,1,34816]{2,1,0:T(1,128)}), f32[16,1,34816]{2,1,0:T(1,128)}, u32[]{:S(2)}, u32[]{:S(2)}) async-start(f32[16,1,34816]{2,1,0:T(1,128)} %reshape.309), calls=%async_computation.1 | async-start | bytes 4456448 | tf_op jit(solution)/shard_map/all_to_all | solution.py:121
  221.1 5.4 copy-start.1
  222.0 165.3 %collective-permute-start = (f32[8,1,64,16]{3,2,1,0:T(8,128)}, f32[8,1,64,16]{3,2,1,0:T(8,128)S(1)}, u32[]{:S(2)}, u32[]{:S(2)}) collective-permute-start(f32[8,1,64,16]{3,2,1,0:T(8,128)} %get-tuple-element.24), channel_id=1, source_target_pairs={{0,2},{2,4},{4,6},{6,8},{8,10},{10,12},{12,14},{14,16},{16,18},{18... | collective-permute-start | bytes 98312 | tf_op jit(solution)/shard_map/ppermute | solution.py:24
  222.4 165.1 %collective-permute-start.1 = (f32[8,1,64,16]{3,2,1,0:T(8,128)}, f32[8,1,64,16]{3,2,1,0:T(8,128)S(1)}, u32[]{:S(2)}, u32[]{:S(2)}) collective-permute-start(f32[8,1,64,16]{3,2,1,0:T(8,128)} %get-tuple-element.23), channel_id=1, source_target_pairs={{2,0},{4,2},{6,4},{8,6},{10,8},{12,10},{14,12},{16,14},{18,16},{20... | collective-permute-start | bytes 98312 | tf_op jit(solution)/shard_map/ppermute | solution.py:25
  233.8 4.2 copy-start.7
  323.1 1.3 copy-start
  374.7 12.6 %copy-start.2 = (f32[8,8,64,16]{3,2,1,0:T(8,128)S(1)}, f32[8,8,64,16]{3,2,1,0:T(8,128)}, u32[]{:S(2)}) copy-start(f32[8,8,64,16]{3,2,1,0:T(8,128)} %copy-done.1) | copy-start | bytes 786436
  374.7 186.7 %all-to-all-start.2 = ((f32[16,1,34816]{2,1,0:T(1,128)}), f32[16,1,34816]{2,1,0:T(1,128)}, u32[]{:S(2)}, u32[]{:S(2)}) async-start(f32[16,1,34816]{2,1,0:T(1,128)} %reshape.311), calls=%async_computation.2 | async-start | bytes 4456448 | tf_op jit(solution)/shard_map/all_to_all | solution.py:155
  387.6 4.4 collective-permute-start.2
  388.0 4.5 collective-permute-start.3
  643.0 43.6 %all-to-all-start.3 = ((f32[2,1,278528]{2,1,0:T(1,128)}), f32[2,1,278528]{2,1,0:T(1,128)S(1)}, u32[]{:S(2)}, u32[]{:S(2)}) async-start(f32[2,1,278528]{2,1,0:T(1,128)} %reshape.313), calls=%async_computation.3 | async-start | bytes 4456448 | tf_op jit(solution)/shard_map/all_to_all | solution.py:162
  708.6 11.3 %copy-start.9 = (f32[1,34,64]{2,1,0:T(8,128)S(1)}, f32[1,34,64]{2,1,0:T(8,128)}, u32[]{:S(2)}) copy-start(f32[1,34,64]{2,1,0:T(8,128)} %copy-done.8) | copy-start | bytes 26116
  708.6 11.3 %copy-start.11 = (f32[1,34,64]{2,1,0:T(8,128)S(1)}, f32[1,34,64]{2,1,0:T(8,128)}, u32[]{:S(2)}) copy-start(f32[1,34,64]{2,1,0:T(8,128)} %copy-done.10) | copy-start | bytes 26116
  872.5 8.2 copy-start.6
where the time goes:
time: 892 us; the launch traced here: 882 us
  local copies, waits for them, and re-layouts  650 us (73%)
  other arithmetic  75.7 us (8%)
  matrix products  66.3 us (7%)
  blocking collectives  30.8 us (3%)
  starting transfers between devices  28.9 us (3%)
  waiting for transfers between devices  28.8 us (3%)
    gather x1, local copies, waits for them, and re-layouts, per_device(): jnp.take(flat_ext, near_ids.reshape(-1), axis=1)  164 us
    unnamed x33, local copies, waits for them, and re-layouts  91.5 us
    reshape x1, local copies, waits for them, and re-layouts, per_device(): grid_potential.reshape(cell_planes, TX, NZC, TZ, rows_cell, TY)  71.4 us
    transpose x1, local copies, waits for them, and re-layouts, per_device(): tile_potential = grid_potential.reshape(cell_planes, TX, NZC, TZ, rows_ce...  62.2 us
    transpose x1, local copies, waits for them, and re-layouts, per_device(): grid_field = tile_values.reshape(TX, TY, TZ, cell_planes, rows_cell, NZC)...  59.1 us
    reshape x1, local copies, waits for them, and re-layouts, per_device(): grid_field = tile_values.reshape(TX, TY, TZ, cell_planes, rows_cell, NZC)...  55.5 us
    all_to_all x1, blocking collectives, per_device(): lax.all_to_all(spectra_z, 'cell', split_axis=2, concat_axis=3, tiled=True)  30.8 us
    all_to_all x1, waiting for transfers between devices, per_device(): lax.all_to_all(pencils, 'slab', split_axis=3, concat_axis=0, tiled=True)  26.1 us
  transfers between devices with their start and end apart: 7, of which 3 were waited for; matrix products, arithmetic and copies ran while one was open for 38% of the time, Pallas kernels for 0%

commit v1 on v0

--- a/solution.py
+++ b/solution.py
@@ -1,17 +1,607 @@
+import functools
 import math
 
 import jax
 import jax.numpy as jnp
+import ml_dtypes
+import numpy as np
 from jax import lax
+from jax.experimental import pallas as pl
+from jax.experimental.pallas import tpu as pltpu
 from jax.sharding import PartitionSpec as P
 
-NX = 512
-NY = 512
-NZ = 64
 TX = 4
 TY = 4
 TZ = 4
 NZC = 16
+LANES = 128
+CHUNKS = 4
+VMEM_LIMIT = 56 * 1024 * 1024
+
+
+def halves(table):
+    high = table.astype(np.float32).astype(ml_dtypes.bfloat16)
+    low = (table - high.astype(np.float64)).astype(np.float32).astype(ml_dtypes.bfloat16)
+    return (high, low)
+
+
+def wave(rows, cols, length):
+    angle = (rows[:, None] * cols[None, :] % length) * (2.0 * math.pi / length)
+    return (np.cos(angle), np.sin(angle))
+
+
+def local_order(planes, cell):
+    return (np.arange(planes)[None, :] * cell + np.arange(cell)[:, None]).reshape(-1)
+
+
+class Plan:
+    def __init__(self, slabs, cells, panels, cell_planes, cell_cols, near, nx, nz, ny):
+        self.slabs, self.cells = (slabs, cells)
+        self.panels, self.cell_planes, self.cell_cols, self.near = (panels, cell_planes, cell_cols, near)
+        self.nx, self.ny, self.nz = (nx, ny, nz)
+        self.planes = cell_planes * TX
+        self.kz_group = LANES // self.planes
+        self.slots = nz // (2 * cells)
+        self.groups = self.slots // self.kz_group if self.kz_group else 0
+        self.row_block = LANES // NZC
+        self.lane_blocks = cell_cols // LANES
+        self.y_local = ny // cells
+        self.ky_local = ny // slabs
+
+    def fits(self):
+        return (
+            self.cells == 2
+            and self.cell_planes == 8
+            and self.kz_group == TY
+            and self.groups % CHUNKS == 0
+            and self.slabs % self.kz_group == 0
+            and self.ky_local % 16 == 0
+            and self.lane_blocks % 2 == 0
+            and self.nx % LANES == 0
+            and self.nx == self.ny
+        )
+
+    def depth_tables(self):
+        slots = np.arange(self.slots).reshape(self.groups, self.kz_group)
+        depth = np.arange(NZC)[None, :] * TZ + np.arange(TZ)[:, None]
+        forward = np.zeros(
+            (self.cells, self.kz_group, self.groups, 2, self.row_block, TZ, self.row_block, NZC)
+        )
+        backward = np.zeros_like(forward)
+        for cell in range(self.cells):
+            for group in range(self.groups):
+                for member in range(self.kz_group):
+                    freq = cell * self.slots + slots[group, member]
+                    angle = (freq * depth % self.nz) * (2.0 * math.pi / self.nz)
+                    real, imag = (np.cos(angle), -np.sin(angle))
+                    factor = 2.0
+                    if freq == 0:
+                        imag = np.cos(depth * math.pi)
+                        factor = 1.0
+                    for row in range(self.row_block):
+                        forward[cell, member, group, 0, row, :, row, :] = real
+                        forward[cell, member, group, 1, row, :, row, :] = imag
+                        backward[cell, member, group, 0, row, :, row, :] = factor * real
+                        backward[cell, member, group, 1, row, :, row, :] = factor * imag
+        shape = (self.cells, self.slots * 2 * self.row_block, TZ * LANES)
+        return (forward.reshape(shape), backward.reshape(shape))
+
+    def y_order(self):
+        rows = np.arange(self.ny // TY).reshape(-1, self.row_block)
+        return (rows[:, None, :] * TY + np.arange(TY)[None, :, None]).reshape(-1)
+
+    def x_order(self):
+        inner = local_order(self.cell_planes, TX)
+        return (np.arange(self.slabs)[:, None] * self.planes + inner[None, :]).reshape(-1)
+
+
+def split(value):
+    high = value.astype(jnp.bfloat16)
+    low = (value - high.astype(jnp.float32)).astype(jnp.bfloat16)
+    return (high, low)
+
+
+def product(left, right, dims=((1,), (0,))):
+    def dot(a, b):
+        return lax.dot_general(a, b, (dims, ((), ())), preferred_element_type=jnp.float32)
+
+    return dot(left[0], right[0]) + (dot(left[0], right[1]) + dot(left[1], right[0]))
+
+
+def swap_groups(parts, width):
+    count = len(parts)
+    lane = lax.broadcasted_iota(jnp.int32, parts[0].shape, 1)
+    parts = list(parts)
+    step = count // 2
+    while step >= 1:
+        shift = step * width
+        upper = (lane // shift) % 2 == 1
+        for i in range(count):
+            if i & step:
+                continue
+            first, second = (parts[i], parts[i + step])
+            parts[i] = jnp.where(upper, pltpu.roll(second, shift, 1), first)
+            parts[i + step] = jnp.where(upper, second, pltpu.roll(first, LANES - shift, 1))
+        step //= 2
+    return parts
+
+
+def project_kernel(plan, me_ref, charges, counts, projection, high, low, *refs):
+    outs, scratch = (refs[:-1], refs[-1])
+    me = me_ref[0]
+    blocks = charges.shape[2] // LANES
+    slot = lax.broadcasted_iota(jnp.int32, charges.shape, 0)
+    masked = jnp.where(slot < counts[...][None], charges[...], 0.0)
+    for block in range(blocks):
+        lanes = pl.ds(block * LANES, LANES)
+        own = masked[:, :, block * LANES : (block + 1) * LANES]
+        for tx in range(TX):
+            for ty in range(TY):
+                for tz in range(TZ):
+                    t = (tx * TY + ty) * TZ + tz
+                    total = projection[0, t, :, lanes] * own[0]
+                    for p in range(1, plan.panels):
+                        total = total + projection[p, t, :, lanes] * own[p]
+                    row = block * LANES + (ty * TX + tx) * plan.cell_planes
+                    scratch[row : row + plan.cell_planes, tz * LANES : (tz + 1) * LANES] = total
+    data = split(scratch[...])
+    rows = plan.groups * 2 * plan.row_block
+    for place in range(plan.cells):
+        cell = lax.rem(me + place, plan.cells)
+        spectra = product((high[cell], low[cell]), data, ((1,), (1,)))
+        for block in range(blocks):
+            parts = [
+                spectra[k * rows : (k + 1) * rows, block * LANES : (block + 1) * LANES]
+                for k in range(plan.kz_group)
+            ]
+            parts = swap_groups(parts, plan.planes)
+            for ty in range(TY):
+                value = parts[ty].reshape(plan.groups, 2, plan.row_block, LANES)
+                first = (block * TY + ty) * plan.row_block
+                per_chunk = plan.groups // CHUNKS
+                for chunk in range(CHUNKS):
+                    outs[place * CHUNKS + chunk][:, :, first : first + plan.row_block, :] = value[
+                        chunk * per_chunk : (chunk + 1) * per_chunk
+                    ]
+
+
+def project(plan, me, charges, counts, projection, high, low):
+    blocks = 2
+    width = blocks * LANES
+    rows = blocks * TY * plan.row_block
+    per_chunk = plan.groups // CHUNKS
+    out = jax.ShapeDtypeStruct((per_chunk, 2, plan.y_local, LANES), jnp.float32)
+    return pl.pallas_call(
+        functools.partial(project_kernel, plan),
+        grid=(plan.cell_cols // width,),
+        in_specs=[
+            pl.BlockSpec(memory_space=pltpu.SMEM),
+            pl.BlockSpec((plan.panels, plan.cell_planes, width), lambda i: (0, 0, i)),
+            pl.BlockSpec((plan.cell_planes, width), lambda i: (0, i)),
+            pl.BlockSpec((plan.panels, TX * TY * TZ, plan.cell_planes, width), lambda i: (0, 0, 0, i)),
+            pl.BlockSpec(high.shape, lambda i: (0, 0, 0)),
+            pl.BlockSpec(low.shape, lambda i: (0, 0, 0)),
+        ],
+        out_specs=[pl.BlockSpec((per_chunk, 2, rows, LANES), lambda i: (0, 0, i, 0))] * (plan.cells * CHUNKS),
+        out_shape=[out] * (plan.cells * CHUNKS),
+        scratch_shapes=[pltpu.VMEM((width, TZ * LANES), jnp.float32)],
+        compiler_params=pltpu.CompilerParams(vmem_limit_bytes=VMEM_LIMIT),
+        cost_estimate=pl.CostEstimate(
+            flops=2 * projection.size, bytes_accessed=4 * projection.size, transcendentals=0
+        ),
+        name="project_depth",
+    )(me, charges, counts, projection, high, low)
+
+
+def forward_y_kernel(plan, special, me_ref, own, received, high, low, out, scratch):
+    me = me_ref[0]
+    half = plan.y_local
+    for place, source in enumerate((own, received)):
+        first = pl.multiple_of(lax.rem(me + place, plan.cells) * half, half)
+        scratch[pl.ds(first, half), 0:LANES] = source[0, 0]
+        scratch[pl.ds(first, half), LANES : 2 * LANES] = source[0, 1]
+    sums = product((high[...], low[...]), split(scratch[...]))
+    cosine, sine = (sums[: plan.ny], sums[plan.ny :])
+    real = cosine[:, :LANES] + sine[:, LANES:]
+    imag = cosine[:, LANES:] - sine[:, :LANES]
+    shape = (plan.slabs, plan.ky_local, LANES)
+    out[:, 0, 0] = real.reshape(shape)
+    out[:, 0, 1] = imag.reshape(shape)
+    if special:
+        @pl.when((me == 0) & (pl.program_id(0) == 0))
+        def _():
+            low_rows = plan.ky_local // 2
+            middle = plan.ny // 2
+            small = (plan.slabs, low_rows, LANES)
+            lane = lax.broadcasted_iota(jnp.int32, small, 2)
+            row = lax.broadcasted_iota(jnp.int32, (middle, LANES), 0)
+            for part in range(2):
+                cols = slice(part * LANES, (part + 1) * LANES)
+                above = jnp.where(row == 0, cosine[middle : middle + 1, cols], -sine[:middle, cols])
+                rows = slice(part * low_rows, (part + 1) * low_rows)
+                packed = cosine[:middle, cols].reshape(small)
+                out[:, 0, 0, rows] = jnp.where(lane < plan.planes, packed, out[:, 0, 0, rows])
+                out[:, 0, 1, rows] = jnp.where(lane < plan.planes, above.reshape(small), out[:, 0, 1, rows])
+
+
+def forward_y(plan, special, me, own, received, high, low):
+    count = own.shape[0]
+    block = (1, 2, plan.y_local, LANES)
+    return pl.pallas_call(
+        functools.partial(forward_y_kernel, plan, special),
+        grid=(count,),
+        in_specs=[
+            pl.BlockSpec(memory_space=pltpu.SMEM),
+            pl.BlockSpec(block, lambda i: (i, 0, 0, 0)),
+            pl.BlockSpec(block, lambda i: (i, 0, 0, 0)),
+            pl.BlockSpec(high.shape, lambda i: (0, 0)),
+            pl.BlockSpec(low.shape, lambda i: (0, 0)),
+        ],
+        out_specs=pl.BlockSpec((plan.slabs, 1, 2, plan.ky_local, LANES), lambda i: (0, i, 0, 0, 0)),
+        out_shape=jax.ShapeDtypeStruct((plan.slabs, count, 2, plan.ky_local, LANES), jnp.float32),
+        scratch_shapes=[pltpu.VMEM((plan.ny, 2 * LANES), jnp.float32)],
+        compiler_params=pltpu.CompilerParams(vmem_limit_bytes=VMEM_LIMIT),
+        cost_estimate=pl.CostEstimate(
+            flops=12 * plan.ny * plan.ny * 2 * LANES * count,
+            bytes_accessed=8 * own.size * 2 + 4 * high.size,
+            transcendentals=0,
+        ),
+        name="forward_second",
+    )(me, own, received, high, low)
+
+
+def along_x_kernel(plan, special, values, weights, edge, fwd_high, fwd_low, bwd_high, bwd_low, out, data):
+    group = plan.kz_group
+    rows = 2 * plan.ky_local
+    for block in range(plan.slabs // group):
+        parts = [values[block * group + i, 0].reshape(rows, LANES) for i in range(group)]
+        parts = swap_groups(parts, plan.planes)
+        for k in range(group):
+            data[k * rows : (k + 1) * rows, block * LANES : (block + 1) * LANES] = parts[k]
+    sums = product(split(data[...]), (fwd_high[...], fwd_low[...]))
+    count = plan.ky_local
+    for k in range(group):
+        re_rows = slice(k * rows, k * rows + count)
+        im_rows = slice(k * rows + count, (k + 1) * rows)
+        weight = weights[0, k]
+        second = weight
+        if special and k == 0:
+            second = jnp.where(pl.program_id(0) == 0, edge[...], weight)
+        data[re_rows] = weight * sums[re_rows, : plan.nx] + second * sums[im_rows, plan.nx :]
+        data[im_rows] = second * sums[im_rows, : plan.nx] - weight * sums[re_rows, plan.nx :]
+    sums = product(split(data[...]), (bwd_high[...], bwd_low[...]))
+    for k in range(group):
+        re_rows = slice(k * rows, k * rows + count)
+        im_rows = slice(k * rows + count, (k + 1) * rows)
+        data[re_rows] = sums[re_rows, : plan.nx] - sums[im_rows, plan.nx :]
+        data[im_rows] = sums[im_rows, : plan.nx] + sums[re_rows, plan.nx :]
+    for block in range(plan.slabs // group):
+        parts = [
+            data[k * rows : (k + 1) * rows, block * LANES : (block + 1) * LANES] for k in range(group)
+        ]
+        parts = swap_groups(parts, plan.planes)
+        for i in range(group):
+            out[block * group + i, 0] = parts[i].reshape(2, plan.ky_local, LANES)
+
+
+def along_x(plan, special, first_group, values, weights, edge, tables):
+    count = values.shape[1]
+    block = (plan.slabs, 1, 2, plan.ky_local, LANES)
+    return pl.pallas_call(
+        functools.partial(along_x_kernel, plan, special),
+        grid=(count,),
+        in_specs=[
+            pl.BlockSpec(block, lambda i: (0, i, 0, 0, 0)),
+            pl.BlockSpec(
+                (1, plan.kz_group, plan.ky_local, plan.nx), lambda i: (first_group + i, 0, 0, 0)
+            ),
+            pl.BlockSpec(edge.shape, lambda i: (0, 0)),
+        ]
+        + [pl.BlockSpec(table.shape, lambda i: (0, 0)) for table in tables],
+        out_specs=pl.BlockSpec(block, lambda i: (0, i, 0, 0, 0)),
+        out_shape=jax.ShapeDtypeStruct(values.shape, jnp.float32),
+        scratch_shapes=[pltpu.VMEM((plan.kz_group * 2 * plan.ky_local, plan.nx), jnp.float32)],
+        compiler_params=pltpu.CompilerParams(vmem_limit_bytes=VMEM_LIMIT),
+        cost_estimate=pl.CostEstimate(
+            flops=24 * plan.nx * plan.nx * 2 * LANES * count,
+            bytes_accessed=8 * values.size + 8 * tables[0].size,
+            transcendentals=0,
+        ),
+        name="along_first",
+    )(values, weights, edge, *tables)
+
+
+def backward_y_kernel(plan, special, me_ref, values, high, low, own, send, scratch):
+    me = me_ref[0]
+    shape = (plan.ny, LANES)
+    real = values[:, 0, 0].reshape(shape)
+    imag = values[:, 0, 1].reshape(shape)
+    both = split(jnp.concatenate([real, imag], axis=1))
+    sums = product((high[...], low[...]), both)
+    cosine, sine = (sums[: plan.ny], sums[plan.ny :])
+    half = (plan.cells, plan.y_local, LANES)
+    scratch[0] = (cosine[:, :LANES] - sine[:, LANES:]).reshape(half)
+    scratch[1] = (cosine[:, LANES:] + sine[:, :LANES]).reshape(half)
+    if special:
+        @pl.when((me == 0) & (pl.program_id(0) == 0))
+        def _():
+            width = plan.planes
+            low_rows = plan.ky_local // 2
+            middle = plan.ny // 2
+            flat = (middle, LANES)
+            lane = lax.broadcasted_iota(jnp.int32, flat, 1)
+            row = lax.broadcasted_iota(jnp.int32, flat, 0)
+            packed = values[:, 0, 0, 0:low_rows].reshape(flat)
+            packed = jnp.where(
+                lane // width == 1, pltpu.roll(values[:, 0, 1, 0:low_rows].reshape(flat), width, 1), packed
+            )
+            packed = jnp.where(
+                lane // width == 2, pltpu.roll(values[:, 0, 0, low_rows:].reshape(flat), 2 * width, 1), packed
+            )
+            packed = jnp.where(
+                lane // width == 3, pltpu.roll(values[:, 0, 1, low_rows:].reshape(flat), 3 * width, 1), packed
+            )
+            ends = packed[0:1]
+            packed = jnp.where(row == 0, packed, 2.0 * packed)
+            pair = split(packed)
+            table = (high[:, 0:middle], low[:, 0:middle])
+            small = product(table, pair)
+            cos_part = small[: plan.ny]
+            other = pltpu.roll(small[plan.ny :], LANES - width, 1)
+            far_row = lax.broadcasted_iota(jnp.int32, shape, 0)
+            sign = jnp.where(far_row % (TY * plan.row_block) // plan.row_block % 2 == 0, 1.0, -1.0)
+            total = cos_part - other + sign * pltpu.roll(
+                jnp.broadcast_to(ends, (plan.row_block, LANES)), LANES - width, 1
+            )[0:1]
+            far_lane = lax.broadcasted_iota(jnp.int32, shape, 1)
+            keep = (far_lane < width).reshape(half)
+            scratch[0] = jnp.where(keep, total.reshape(half), scratch[0])
+            scratch[1] = jnp.where(keep, pltpu.roll(total, LANES - 2 * width, 1).reshape(half), scratch[1])
+    for part in range(2):
+        own[0, part] = scratch[part, me]
+        send[0, part] = scratch[part, lax.rem(me + 1, plan.cells)]
+
+
+def backward_y(plan, special, me, values, high, low):
+    count = values.shape[1]
+    block = pl.BlockSpec((1, 2, plan.y_local, LANES), lambda i: (i, 0, 0, 0))
+    out = jax.ShapeDtypeStruct((count, 2, plan.y_local, LANES), jnp.float32)
+    return pl.pallas_call(
+        functools.partial(backward_y_kernel, plan, special),
+        grid=(count,),
+        in_specs=[
+            pl.BlockSpec(memory_space=pltpu.SMEM),
+            pl.BlockSpec((plan.slabs, 1, 2, plan.ky_local, LANES), lambda i: (0, i, 0, 0, 0)),
+            pl.BlockSpec(high.shape, lambda i: (0, 0)),
+            pl.BlockSpec(low.shape, lambda i: (0, 0)),
+        ],
+        out_specs=[block, block],
+        out_shape=[out, out],
+        scratch_shapes=[pltpu.VMEM((2, plan.cells, plan.y_local, LANES), jnp.float32)],
+        compiler_params=pltpu.CompilerParams(vmem_limit_bytes=VMEM_LIMIT),
+        cost_estimate=pl.CostEstimate(
+            flops=12 * plan.ny * plan.ny * 2 * LANES * count,
+            bytes_accessed=8 * values.size + 4 * high.size,
+            transcendentals=0,
+        ),
+        name="backward_second",
+    )(me, values, high, low)
+
+
+def gather_kernel(plan, me_ref, counts, near, projection, high, low, *refs):
+    parts_in, out, data = (refs[: 2 * CHUNKS], refs[2 * CHUNKS], refs[2 * CHUNKS + 1])
+    me = me_ref[0]
+    blocks = counts.shape[1] // LANES
+    rows = plan.groups * 2 * plan.row_block
+    total = None
+    for place in range(plan.cells):
+        sources = parts_in[place * CHUNKS : (place + 1) * CHUNKS]
+        for block in range(blocks):
+            parts = []
+            for ty in range(TY):
+                first = (block * TY + ty) * plan.row_block
+                pieces = [source[:, :, first : first + plan.row_block, :] for source in sources]
+                parts.append(jnp.concatenate(pieces, axis=0).reshape(rows, LANES))
+            parts = swap_groups(parts, plan.planes)
+            data[:, block * LANES : (block + 1) * LANES] = jnp.concatenate(parts, axis=0)
+        cell = lax.rem(me + place, plan.cells)
+        term = product(split(data[...].T), (high[cell], low[cell]))
+        total = term if total is None else total + term
+    data_out = refs[2 * CHUNKS + 2]
+    data_out[...] = total
+    slot = lax.broadcasted_iota(jnp.int32, near.shape, 0)
+    for block in range(blocks):
+        lanes = pl.ds(block * LANES, LANES)
+        far = [None] * plan.panels
+        for tx in range(TX):
+            for ty in range(TY):
+                row = block * LANES + (ty * TX + tx) * plan.cell_planes
+                for tz in range(TZ):
+                    t = (tx * TY + ty) * TZ + tz
+                    potential = data_out[row : row + plan.cell_planes, tz * LANES : (tz + 1) * LANES]
+                    for p in range(plan.panels):
+                        term = projection[p, t, :, lanes] * potential
+                        far[p] = term if far[p] is None else far[p] + term
+        for p in range(plan.panels):
+            value = far[p] + near[p, :, lanes]
+            out[p, :, lanes] = jnp.where(counts[:, lanes] > p, value, 0.0)
+
+
+def gather(plan, me, counts, near, projection, high, low, parts):
+    blocks = 2
+    width = blocks * LANES
+    rows = blocks * TY * plan.row_block
+    per_chunk = plan.groups // CHUNKS
+    panel_spec = pl.BlockSpec((plan.panels, plan.cell_planes, width), lambda i: (0, 0, i))
+    return pl.pallas_call(
+        functools.partial(gather_kernel, plan),
+        grid=(plan.cell_cols // width,),
+        in_specs=[
+            pl.BlockSpec(memory_space=pltpu.SMEM),
+            pl.BlockSpec((plan.cell_planes, width), lambda i: (0, i)),
+            panel_spec,
+            pl.BlockSpec((plan.panels, TX * TY * TZ, plan.cell_planes, width), lambda i: (0, 0, 0, i)),
+            pl.BlockSpec(high.shape, lambda i: (0, 0, 0)),
+            pl.BlockSpec(low.shape, lambda i: (0, 0, 0)),
+        ]
+        + [pl.BlockSpec((per_chunk, 2, rows, LANES), lambda i: (0, 0, i, 0))] * len(parts),
+        out_specs=panel_spec,
+        out_shape=jax.ShapeDtypeStruct(near.shape, jnp.float32),
+        scratch_shapes=[
+            pltpu.VMEM((plan.slots * 2 * plan.row_block, width), jnp.float32),
+            pltpu.VMEM((width, TZ * LANES), jnp.float32),
+        ],
+        compiler_params=pltpu.CompilerParams(vmem_limit_bytes=VMEM_LIMIT),
+        cost_estimate=pl.CostEstimate(
+            flops=2 * projection.size, bytes_accessed=4 * projection.size, transcendentals=0
+        ),
+        name="depth_gather",
+    )(me, counts, near, projection, high, low, *parts)
+
+
+def near_kernel(plan, extended, codes, blocks_ref, out):
+    step = pl.program_id(0)
+    lane = lax.broadcasted_iota(jnp.int32, (plan.cell_planes, LANES), 1)
+    depth = lane % NZC
+    digits = []
+    for k in range(plan.near):
+        code = codes[k]
+        digits.append((code // 9, code // 3 % 3, code % 3))
+    total = [None] * plan.panels
+    for q in range(plan.panels):
+        shifted = []
+        for dx in range(3):
+            before, here, after = (
+                extended[q, dx, :, pl.ds(pl.multiple_of((step + i) * LANES, LANES), LANES)] for i in range(3)
+            )
+            up = jnp.where(lane < NZC, pltpu.roll(before, NZC, 1), pltpu.roll(here, NZC, 1))
+            down = jnp.where(
+                lane >= LANES - NZC, pltpu.roll(after, LANES - NZC, 1), pltpu.roll(here, LANES - NZC, 1)
+            )
+            for value in (up, here, down):
+                under = jnp.where(
+                    depth == 0, pltpu.roll(value, LANES - NZC + 1, 1), pltpu.roll(value, 1, 1)
+                )
+                over = jnp.where(
+                    depth == NZC - 1, pltpu.roll(value, NZC - 1, 1), pltpu.roll(value, LANES - 1, 1)
+                )
+                shifted.append((under, value, over))
+        for k in range(plan.near):
+            digit_x, digit_y, digit_z = digits[k]
+
+            def choose(digit, options):
+                return jnp.where(digit == 0, options[0], jnp.where(digit == 1, options[1], options[2]))
+
+            by_z = [choose(digit_z, options) for options in shifted]
+            by_y = [choose(digit_y, by_z[3 * i : 3 * i + 3]) for i in range(3)]
+            picked = choose(digit_x, by_y)
+            for p in range(plan.panels):
+                term = blocks_ref[k, p, q] * picked
+                total[p] = term if total[p] is None else total[p] + term
+    for p in range(plan.panels):
+        out[p] = total[p]
+
+
+def near_field(plan, extended, neighbours, near_blocks):
+    return pl.pallas_call(
+        functools.partial(near_kernel, plan),
+        grid=(plan.lane_blocks,),
+        in_specs=[
+            pl.BlockSpec(extended.shape, lambda i: (0, 0, 0, 0)),
+            pl.BlockSpec((plan.near, plan.cell_planes, LANES), lambda i: (0, 0, i)),
+            pl.BlockSpec(
+                (plan.near, plan.panels, plan.panels, plan.cell_planes, LANES), lambda i: (0, 0, 0, 0, i)
+            ),
+        ],
+        out_specs=pl.BlockSpec((plan.panels, plan.cell_planes, LANES), lambda i: (0, 0, i)),
+        out_shape=jax.ShapeDtypeStruct((plan.panels, plan.cell_planes, plan.cell_cols), jnp.float32),
+        compiler_params=pltpu.CompilerParams(vmem_limit_bytes=VMEM_LIMIT),
+        cost_estimate=pl.CostEstimate(
+            flops=2 * near_blocks.size, bytes_accessed=4 * near_blocks.size, transcendentals=0
+        ),
+        name="near_blocks",
+    )(extended, neighbours, near_blocks)
+
+
+def ring_pairs(axis):
+    count = lax.axis_size(axis)
+    up = [(i, (i + 1) % count) for i in range(count)]
+    return (up, [(j, i) for i, j in up])
+
+
+def extended_charges(plan, masked):
+    up, down = ring_pairs("cell")
+    left = lax.ppermute(masked[:, :, -NZC:], "cell", up)
+    right = lax.ppermute(masked[:, :, :NZC], "cell", down)
+    rest = jnp.zeros((plan.panels, plan.cell_planes, LANES - NZC), jnp.float32)
+    wide = jnp.concatenate([rest, left, masked, right, rest], axis=2)
+    up, down = ring_pairs("slab")
+    before = lax.ppermute(wide[:, -1:], "slab", up)
+    after = lax.ppermute(wide[:, :1], "slab", down)
+    whole = jnp.concatenate([before, wide, after], axis=1)
+    planes = plan.cell_planes
+    return jnp.stack([whole[:, i : i + planes] for i in range(3)], axis=1)
+
+
+def spectrum_weights(plan, spectrum):
+    me = lax.axis_index("cell")
+    scale = 1.0 / (plan.nx * plan.ny * plan.nz)
+    by_depth = jnp.transpose(spectrum, (1, 2, 0))
+    own = lax.dynamic_slice_in_dim(by_depth, me * plan.slots, plan.slots, 0)
+    pair = jnp.stack([by_depth[0], by_depth[plan.nz // 2]])
+    half = plan.ky_local // 2
+    lower = lax.ppermute(pair[:, :half], "slab", [(j, 2 * j) for j in range(plan.slabs // 2)])
+    upper = lax.ppermute(pair[:, half:], "slab", [(j, 2 * j + 1) for j in range(plan.slabs // 2)])
+    edge = lax.ppermute(pair[:, :1], "slab", [(plan.slabs // 2, 0)])
+    packed = lower + upper
+    first = lax.axis_index("slab") == 0
+    row = lax.broadcasted_iota(jnp.int32, packed.shape, 1)
+    packed_edge = jnp.where(first & (row == 0), edge, packed)
+    shape = own[0].shape
+    slot = lax.broadcasted_iota(jnp.int32, own.shape, 0)
+    weights = jnp.where((me == 0) & (slot == 0), packed.reshape(shape)[None], own)
+    second = jnp.where(me == 0, packed_edge.reshape(shape), own[0])
+    grouped = (plan.groups, plan.kz_group) + shape
+    return ((weights * scale).reshape(grouped), second * scale)
+
+
+def per_device(charges, counts, projection, near_blocks, neighbours, spectrum):
+    panels, cell_planes, cell_cols = charges.shape
+    cells, slabs = (lax.axis_size("cell"), lax.axis_size("slab"))
+    nx, nz, local = spectrum.shape
+    plan = Plan(slabs, cells, panels, cell_planes, cell_cols, neighbours.shape[0], nx, nz, local * slabs)
+    if not plan.fits():
+        return plain_device(charges, counts, projection, near_blocks, neighbours, spectrum)
+    me = lax.axis_index("cell").astype(jnp.int32).reshape(1)
+    depth_forward, depth_backward = plan.depth_tables()
+    freqs = np.arange(plan.ny)
+    cos_y, sin_y = wave(freqs, plan.y_order(), plan.ny)
+    y_forward = halves(np.concatenate([cos_y, sin_y], axis=0))
+    y_backward = halves(np.concatenate([cos_y.T, sin_y.T], axis=0))
+    cos_x, sin_x = wave(plan.x_order(), np.arange(plan.nx), plan.nx)
+    x_tables = halves(np.concatenate([cos_x, sin_x], axis=1)) + halves(
+        np.concatenate([cos_x.T, sin_x.T], axis=1)
+    )
+    weights, edge = spectrum_weights(plan, spectrum)
+    spectra = project(plan, me, charges, counts, projection, *halves(depth_forward))
+    own, send = (spectra[:CHUNKS], spectra[CHUNKS:])
+    exchange = [(i, (i + 1) % cells) for i in range(cells)]
+    per_chunk = plan.groups // CHUNKS
+    back_own, back_received = ([], [])
+    for chunk in range(CHUNKS):
+        special = chunk == 0
+        received = lax.ppermute(send[chunk], "cell", exchange)
+        pencils = forward_y(plan, special, me, own[chunk], received, *y_forward)
+        columns = lax.all_to_all(pencils, "slab", split_axis=0, concat_axis=0, tiled=True)
+        columns = along_x(plan, special, chunk * per_chunk, columns, weights, edge, x_tables)
+        pencils = lax.all_to_all(columns, "slab", split_axis=0, concat_axis=0, tiled=True)
+        kept, sent = backward_y(plan, special, me, pencils, *y_backward)
+        back_own.append(kept)
+        back_received.append(lax.ppermute(sent, "cell", exchange))
+    slot = lax.broadcasted_iota(jnp.int32, charges.shape, 0)
+    masked = jnp.where(slot < counts[None], charges, 0.0)
+    near = near_field(plan, extended_charges(plan, masked), neighbours, near_blocks)
+    return gather(plan, me, counts, near, projection, *halves(depth_backward), back_own + back_received)
 
 
 def padded(value, sides, width):
@@ -37,23 +627,23 @@
     return (jnp.cos(angle_rad), jnp.sin(angle_rad))
 
 
-def depth_rows(freq_ids, valid, weights):
-    depth_ids = lax.broadcasted_iota(jnp.int32, (freq_ids.shape[0], NZ), 1)
-    products = freq_ids[:, None] * depth_ids % NZ
-    angle_rad = products.astype(jnp.float32) * (2.0 * math.pi / NZ)
+def depth_rows(nz, freq_ids, valid, weights):
+    depth_ids = lax.broadcasted_iota(jnp.int32, (freq_ids.shape[0], nz), 1)
+    products = freq_ids[:, None] * depth_ids % nz
+    angle_rad = products.astype(jnp.float32) * (2.0 * math.pi / nz)
     basis = jnp.stack([jnp.cos(angle_rad), -jnp.sin(angle_rad)])
     return (basis * valid[None, :, None], basis * weights[None, :, None])
 
 
-def half_depth_tables(cell_count):
-    lower = NZ // (2 * cell_count)
+def half_depth_tables(nz, cell_count):
+    lower = nz // (2 * cell_count)
     row_ids = lax.broadcasted_iota(jnp.int32, (cell_count * (lower + 1),), 0)
     block_ids = row_ids // (lower + 1)
     slot_ids = row_ids % (lower + 1)
-    freq_ids = jnp.where(slot_ids < lower, block_ids * lower + slot_ids, NZ // 2)
+    freq_ids = jnp.where(slot_ids < lower, block_ids * lower + slot_ids, nz // 2)
     valid = jnp.where((slot_ids < lower) | (block_ids == 0), 1.0, 0.0).astype(jnp.float32)
     doubled = jnp.where((slot_ids < lower) & (freq_ids > 0), 2.0, 1.0).astype(jnp.float32)
-    forward_table, backward_table = depth_rows(freq_ids, valid, valid * doubled)
+    forward_table, backward_table = depth_rows(nz, freq_ids, valid, valid * doubled)
     return (forward_table, backward_table, freq_ids)
 
 
@@ -92,8 +682,9 @@
     return jnp.stack([real_part, imag_part], axis=1)
 
 
-def per_device(charges, counts, projection, near_blocks, neighbours, spectrum):
+def plain_device(charges, counts, projection, near_blocks, neighbours, spectrum):
     panels, cell_planes, cell_cols = charges.shape
+    nx, nz, ny = (spectrum.shape[0], spectrum.shape[1], spectrum.shape[2] * lax.axis_size("slab"))
     planes = cell_planes * TX
     rows_cell = cell_cols // NZC
     slot_ids = lax.broadcasted_iota(jnp.int32, charges.shape, 0)
@@ -103,15 +694,15 @@
     grid_field = (
         tile_values.reshape(TX, TY, TZ, cell_planes, rows_cell, NZC)
         .transpose(3, 0, 5, 2, 4, 1)
-        .reshape(planes, NZ, rows_cell * TY)
+        .reshape(planes, nz, rows_cell * TY)
     )
     cell_count = lax.axis_size("cell")
-    forward_table, backward_table, freq_ids = half_depth_tables(cell_count)
+    forward_table, backward_table, freq_ids = half_depth_tables(nz, cell_count)
     depth_count = forward_table.shape[1] // cell_count
     spectra_z = jnp.einsum(
         "wkz,xzy->xwky", forward_table, grid_field, precision=lax.Precision.HIGHEST
     )
-    cosine_y, sine_y = wave_tables(NY, NY, NY)
+    cosine_y, sine_y = wave_tables(ny, ny, ny)
     pencils = transform_rows(
         lax.all_to_all(spectra_z, "cell", split_axis=2, concat_axis=3, tiled=True),
         cosine_y,
@@ -120,16 +711,16 @@
     )
     columns = lax.all_to_all(pencils, "slab", split_axis=3, concat_axis=0, tiled=True)
     col_width = columns.shape[2] * columns.shape[3]
-    flat_rows = columns.reshape(NX, 2 * col_width)
+    flat_rows = columns.reshape(nx, 2 * col_width)
     first_row = lax.axis_index("cell") * depth_count
     kernel_ids = lax.dynamic_slice_in_dim(freq_ids, first_row, depth_count, 0)
-    kernel = jnp.take(spectrum, kernel_ids, axis=1).reshape(NX, col_width) * (1.0 / (NX * NY * NZ))
+    kernel = jnp.take(spectrum, kernel_ids, axis=1).reshape(nx, col_width) * (1.0 / (nx * ny * nz))
     kernel_both = jnp.concatenate([kernel, kernel], axis=1)
     slab_count = lax.axis_size("slab")
-    local_rows = NX // slab_count
+    local_rows = nx // slab_count
     cosine_s, sine_s = wave_tables(slab_count, slab_count, slab_count)
     cosine_r, sine_r = wave_tables(local_rows, local_rows, local_rows)
-    twist_cos, twist_sin = wave_tables(slab_count, local_rows, NX)
+    twist_cos, twist_sin = wave_tables(slab_count, local_rows, nx)
     twist_cos = twist_cos[:, :, None]
     twist_sin = twist_sin[:, :, None]
     section_one = transform_axis(
@@ -141,7 +732,7 @@
     )
     section_one = twiddle(section_one, twist_cos, twist_sin, 1.0)
     section_two = transform_axis("jr,krc->jkc", cosine_r, sine_r, section_one, 1.0)
-    weighted = section_two.reshape(NX, 2 * col_width) * kernel_both
+    weighted = section_two.reshape(nx, 2 * col_width) * kernel_both
     section_one = transform_axis(
         "rj,jkc->krc",
         cosine_r,
@@ -151,7 +742,7 @@
     )
     section_one = twiddle(section_one, twist_cos, twist_sin, -1.0)
     section_two = transform_axis("sk,krc->src", cosine_s, sine_s, section_one, -1.0)
-    returned_x = section_two.reshape(NX, 2 * col_width)
+    returned_x = section_two.reshape(nx, 2 * col_width)
     returned = lax.all_to_all(
         returned_x.reshape(columns.shape), "slab", split_axis=0, concat_axis=3, tiled=True
     )

time: 892 us -> 224 us (0.25); the launches traced: 882 us -> 223 us
  local copies, waits for them, and re-layouts: 650 us -> 5.77 us
  Pallas kernels: 0 us -> 87 us
  other arithmetic: 75.7 us -> 4.36 us
  matrix products: 66.3 us -> 0 us
  waiting for transfers between devices: 28.8 us -> 68.1 us
  blocking collectives: 30.8 us -> 0 us
  starting transfers between devices: 28.9 us -> 57.2 us
    gather x4 -> x0, local copies, waits for them, and re-layouts: 176 us -> none  [the longest x1 164 us: per_device(): jnp.take(flat_ext, near_ids.reshape(-1), axis=1)]
    reshape x6 -> x0, local copies, waits for them, and re-layouts: 151 us -> none  [the longest x1 71.4 us: per_device(): grid_potential.reshape(cell_planes, TX, NZC, TZ, rows_cell, TY)]
    transpose x3 -> x0, local copies, waits for them, and re-layouts: 123 us -> none  [the longest x1 62.2 us: per_device(): tile_potential = grid_potential.reshape(cell_planes, TX, NZC, TZ, rows_ce...]
    pallas_call x0 -> x15, Pallas kernels: none -> 87 us  [the longest x4 22.6 us: along_x(): pl.pallas_call(functools.partial(along_x_kernel, plan, special), grid=(co...]
    unnamed x33 -> x43, local copies, waits for them, and re-layouts: 91.5 us -> 4.67 us
    dot_general x14 -> x0, matrix products: 66.3 us -> none  [the longest x2 19.3 us: transform_rows(): jnp.dot(flat_rows, cosine, precision=lax.Precision.HIGHEST)]
    another operation x5 -> x0, local copies, waits for them, and re-layouts: 44.2 us -> none  [the longest x2 19.4 us: transform_rows(): return jnp.stack([real_part, imag_part], axis=1)]
    all_to_all x5 -> x0, local copies, waits for them, and re-layouts: 40.8 us -> none  [the longest x2 15.5 us: per_device(): lax.all_to_all(pencils, 'slab', split_axis=3, concat_axis=0, tiled=True)]
  transfers between devices with their start and end apart: 7 -> 23, of which waited for: 3 -> 14; matrix products, arithmetic and copies ran while one was open for 38% -> 2% of each run, Pallas kernels for 0% -> 29%
where the time goes in v1:
time: 224 us; the launch traced here: 223 us
  Pallas kernels  87 us (39%)
  waiting for transfers between devices  68.1 us (30%)
  starting transfers between devices  57.2 us (26%)
  local copies, waits for them, and re-layouts  5.77 us (3%)
  other arithmetic  4.36 us (2%)
    ppermute x4, waiting for transfers between devices, per_device(): received = lax.ppermute(send[chunk], 'cell', exchange)  23.7 us
    pallas_call x4, Pallas kernels, along_x(): pl.pallas_call(functools.partial(along_x_kernel, plan, special), grid=(co...  22.6 us
    all_to_all x4, waiting for transfers between devices, per_device(): lax.all_to_all(columns, 'slab', split_axis=0, concat_axis=0, tiled=True)  20.9 us
    all_to_all x4, starting transfers between devices, per_device(): lax.all_to_all(pencils, 'slab', split_axis=0, concat_axis=0, tiled=True)  19.2 us
    all_to_all x4, starting transfers between devices, per_device(): lax.all_to_all(columns, 'slab', split_axis=0, concat_axis=0, tiled=True)  16.4 us
    pallas_call x1, Pallas kernels, near_field(): pl.pallas_call(functools.partial(near_kernel, plan), grid=(plan.lane_bloc...  15.5 us
    pallas_call x4, Pallas kernels, backward_y(): pl.pallas_call(functools.partial(backward_y_kernel, plan, special), grid=...  15 us
    pallas_call x4, Pallas kernels, forward_y(): pl.pallas_call(functools.partial(forward_y_kernel, plan, special), grid=(...  14.6 us
  transfers between devices with their start and end apart: 23, of which 14 were waited for; matrix products, arithmetic and copies ran while one was open for 2% of the time, Pallas kernels for 29%

profile of v1, /device:TPU:0, one launch (start us, length us, event | category | flops | bytes accessed | tf_op | source)
XLA Modules:
  0.0 222.8 jit_solution(2708641003513710910)
XLA Ops:
  0.0 9.6 %project_depth.1 = (f32[1,2,256,128]{3,2,1,0:T(8,128)}, f32[1,2,256,128]{3,2,1,0:T(8,128)}, f32[1,2,256,128]{3,2,1,0:T(8,128)}, f32[1,2,256,128]{3,2,1,0:T(8,128...) custom-call(s32[1]{0:T(128)} %bitcast.me_ref, ...), custom_call_target="tpu_custom_call" | custom-call | flops 8388608 | bytes 16777216 | tf_op jit(solution)/shard_map/project_depth/pallas_call | solution.py:174
  9.6 3.0 %collective-permute-start.4 = (f32[1,2,256,128]{3,2,1,0:T(8,128)}, f32[1,2,256,128]{3,2,1,0:T(8,128)S(1)}, u32[]{:S(2)}, u32[]{:S(2)}) collective-permute-start(f32[1,2,256,128]{3,2,1,0:T(8,128)} %get-tuple-element.22), channel_id=1, source_target_pairs={{0,1},{1,0},{2,3},{3,2},{4,5},{5,4},{6,7},{7,6},{8,9},{9,8},{10,11... | collective-permute-start | bytes 786440 | tf_op jit(solution)/shard_map/ppermute | solution.py:593
  12.6 6.5 %collective-permute-done.4.received = f32[1,2,256,128]{3,2,1,0:T(8,128)S(1)} collective-permute-done((f32[1,2,256,128]{3,2,1,0:T(8,128)}, f32[1,2,256,128]{3,2,1,0:T(8,128)S(1)}, u32[]{:S(2)}, u32[]{:S(2)}) %collective-permute-start.4) | collective-permute-done | bytes 262176 | tf_op jit(solution)/shard_map/ppermute | solution.py:593
  19.1 0.7 copy-done.15
  19.8 3.7 %forward_second.4 = f32[16,1,2,32,128]{4,3,2,1,0:T(8,128)} custom-call(s32[1]{0:T(128)} %bitcast.me_ref, f32[1,2,256,128]{3,2,1,0:T(8,128)} %get-tuple-element.21.own, f32[1,2,256,128]{3,2,1,0:T(8,128)} %copy-done.15, bf16[1024,512]{1,0:T(8,128)(2,1)} %constant.48.clone.high, bf16[1024,512]{1,0:T(8,128)(2,1)} %constant.49.clone.low), custom_call_target="tpu_custom_call" | custom-call | flops 805306368 | bytes 3145728 | tf_op jit(solution)/shard_map/forward_second/pallas_call | solution.py:230
  23.5 6.1 %all-to-all-start = ((f32[16,1,2,32,128]{4,3,2,1,0:T(8,128)}), f32[16,1,2,32,128]{4,3,2,1,0:T(8,128)S(1)}, u32[]{:S(2)}, u32[]{:S(2)}) async-start(f32[16,1,2,32,128]{4,3,2,1,0:T(8,128)} %forward_second.4), calls=%async_computation | async-start | bytes 1048576 | tf_op jit(solution)/shard_map/all_to_all | solution.py:595
  29.7 1.5 collective-permute-start.8
  31.2 7.2 %collective-permute-done.8.received = f32[1,2,256,128]{3,2,1,0:T(8,128)S(1)} collective-permute-done((f32[1,2,256,128]{3,2,1,0:T(8,128)S(1)}, f32[1,2,256,128]{3,2,1,0:T(8,128)S(1)}, u32[]{:S(2)}, u32[]{:S(2)}) %collective-permute-start.8) | collective-permute-done | bytes 262176 | tf_op jit(solution)/shard_map/ppermute | solution.py:593
  38.4 0.7 copy-done.16
  39.1 3.7 %forward_second.5 = f32[16,1,2,32,128]{4,3,2,1,0:T(8,128)} custom-call(s32[1]{0:T(128)} %bitcast.me_ref, f32[1,2,256,128]{3,2,1,0:T(8,128)} %get-tuple-element.24.own, f32[1,2,256,128]{3,2,1,0:T(8,128)} %copy-done.16, bf16[1024,512]{1,0:T(8,128)(2,1)} %constant.48.clone.high, bf16[1024,512]{1,0:T(8,128)(2,1)} %constant.49.clone.low), custom_call_target="tpu_custom_call" | custom-call | flops 805306368 | bytes 3145728 | tf_op jit(solution)/shard_map/forward_second/pallas_call | solution.py:230
  42.8 1.4 all-to-all-done.values
  44.2 4.3 %all-to-all-start.2 = ((f32[16,1,2,32,128]{4,3,2,1,0:T(8,128)}), f32[16,1,2,32,128]{4,3,2,1,0:T(8,128)S(1)}, u32[]{:S(2)}, u32[]{:S(2)}) async-start(f32[16,1,2,32,128]{4,3,2,1,0:T(8,128)} %forward_second.5), calls=%async_computation.2 | async-start | bytes 1048576 | tf_op jit(solution)/shard_map/all_to_all | solution.py:595
  48.5 1.5 collective-permute-start.9
  50.0 7.2 %collective-permute-done.9.received = f32[1,2,256,128]{3,2,1,0:T(8,128)S(1)} collective-permute-done((f32[1,2,256,128]{3,2,1,0:T(8,128)S(1)}, f32[1,2,256,128]{3,2,1,0:T(8,128)S(1)}, u32[]{:S(2)}, u32[]{:S(2)}) %collective-permute-start.9) | collective-permute-done | bytes 262176 | tf_op jit(solution)/shard_map/ppermute | solution.py:593
  57.2 0.7 copy-done.17
  57.9 3.6 %forward_second.6 = f32[16,1,2,32,128]{4,3,2,1,0:T(8,128)} custom-call(s32[1]{0:T(128)} %bitcast.me_ref, f32[1,2,256,128]{3,2,1,0:T(8,128)} %get-tuple-element.27.own, f32[1,2,256,128]{3,2,1,0:T(8,128)} %copy-done.17, bf16[1024,512]{1,0:T(8,128)(2,1)} %constant.48.clone.high, bf16[1024,512]{1,0:T(8,128)(2,1)} %constant.49.clone.low), custom_call_target="tpu_custom_call" | custom-call | flops 805306368 | bytes 3145728 | tf_op jit(solution)/shard_map/forward_second/pallas_call | solution.py:230
  61.5 1.4 all-to-all-done.2.values
  63.0 4.3 %all-to-all-start.4 = ((f32[16,1,2,32,128]{4,3,2,1,0:T(8,128)}), f32[16,1,2,32,128]{4,3,2,1,0:T(8,128)S(1)}, u32[]{:S(2)}, u32[]{:S(2)}) async-start(f32[16,1,2,32,128]{4,3,2,1,0:T(8,128)} %forward_second.6), calls=%async_computation.4 | async-start | bytes 1048576 | tf_op jit(solution)/shard_map/all_to_all | solution.py:595
  67.3 1.5 collective-permute-start.10
  68.8 0.9 fusion.7
  69.7 1.3 collective-permute-start.7
  71.0 1.4 collective-permute-start.6
  72.5 0.7 collective-permute-start.5
  73.2 2.8 %collective-permute-done.10.received = f32[1,2,256,128]{3,2,1,0:T(8,128)S(1)} collective-permute-done((f32[1,2,256,128]{3,2,1,0:T(8,128)S(1)}, f32[1,2,256,128]{3,2,1,0:T(8,128)S(1)}, u32[]{:S(2)}, u32[]{:S(2)}) %collective-permute-start.10) | collective-permute-done | bytes 262176 | tf_op jit(solution)/shard_map/ppermute | solution.py:593
  76.0 0.7 copy-done.14
  76.7 3.6 %forward_second.7 = f32[16,1,2,32,128]{4,3,2,1,0:T(8,128)} custom-call(s32[1]{0:T(128)} %bitcast.me_ref, f32[1,2,256,128]{3,2,1,0:T(8,128)} %get-tuple-element.30.own, f32[1,2,256,128]{3,2,1,0:T(8,128)} %copy-done.14, bf16[1024,512]{1,0:T(8,128)(2,1)} %constant.48.clone.high, bf16[1024,512]{1,0:T(8,128)(2,1)} %constant.49.clone.low), custom_call_target="tpu_custom_call" | custom-call | flops 805306368 | bytes 3145728 | tf_op jit(solution)/shard_map/forward_second/pallas_call | solution.py:230
  80.3 1.4 all-to-all-done.4.values
  81.7 4.5 %all-to-all-start.6 = ((f32[16,1,2,32,128]{4,3,2,1,0:T(8,128)}), f32[16,1,2,32,128]{4,3,2,1,0:T(8,128)S(1)}, u32[]{:S(2)}, u32[]{:S(2)}) async-start(f32[16,1,2,32,128]{4,3,2,1,0:T(8,128)} %forward_second.7), calls=%async_computation.6 | async-start | bytes 1048576 | tf_op jit(solution)/shard_map/all_to_all | solution.py:595
  86.3 2.4 %select_multiply_fusion = (f32[16,32,512]{2,1,0:T(8,128)}, f32[16,32,512]{2,1,0:T(8,128)S(1)}) fusion(f32[32,512]{1,0:T(8,128)S(1)} %bitcast.33, pred[16]{0:T(512)(128)(4,1)S(1)} %compare_and_fusion.1, f32[512,64,32]{0,2,1:T(8,128)} %param.23, s32[]{:T(128)S(6)} %select_n.24), kind=kLoop, calls=%fused_computation | loop fusion | flops 524288 | bytes 3211284 | tf_op jit(solution)/shard_map/mul | solution.py:565
  88.8 0.6 fusion.6.edge
  89.4 5.6 %along_first.4 = f32[16,1,2,32,128]{4,3,2,1,0:T(8,128)} custom-call(f32[16,1,2,32,128]{4,3,2,1,0:T(8,128)} %copy-done, f32[4,4,32,512]{3,2,1,0:T(8,128)} %bitcast.27, f32[32,512]{1,0:T(8,128)} %fusion.6.edge, bf16[512,1024]{1,0:T(8,128)(2,1)} %constant.50.clone.fwd_high, bf16[512,1024]{1,0:T(8,128)(2,1)} %constant.51.clone.fwd_low, ...), custom_call_target="tpu_custom_call" | custom-call | flops 1610612736 | bytes 5242880 | tf_op jit(solution)/shard_map/along_first/pallas_call | solution.py:290
  95.0 5.6 %all-to-all-done.6.values = f32[16,1,2,32,128]{4,3,2,1,0:T(8,128)S(1)} async-done(((f32[16,1,2,32,128]{4,3,2,1,0:T(8,128)}), f32[16,1,2,32,128]{4,3,2,1,0:T(8,128)S(1)}, u32[]{:S(2)}, u32[]{:S(2)}) %all-to-all-start.6) | async-done | bytes 524320 | tf_op jit(solution)/shard_map/all_to_all | solution.py:595
  100.7 4.1 %all-to-all-start.1 = ((f32[16,1,2,32,128]{4,3,2,1,0:T(8,128)}), f32[16,1,2,32,128]{4,3,2,1,0:T(8,128)S(1)}, u32[]{:S(2)}, u32[]{:S(2)}) async-start(f32[16,1,2,32,128]{4,3,2,1,0:T(8,128)} %along_first.4), calls=%async_computation.1 | async-start | bytes 1048576 | tf_op jit(solution)/shard_map/all_to_all | solution.py:597
  104.8 5.6 %along_first.5 = f32[16,1,2,32,128]{4,3,2,1,0:T(8,128)} custom-call(f32[16,1,2,32,128]{4,3,2,1,0:T(8,128)} %copy-done.1, f32[4,4,32,512]{3,2,1,0:T(8,128)} %bitcast.28, f32[32,512]{1,0:T(8,128)} %fusion.6.edge, bf16[512,1024]{1,0:T(8,128)(2,1)} %constant.50.clone.fwd_high, bf16[512,1024]{1,0:T(8,128)(2,1)} %constant.51.clone.fwd_low, ...), custom_call_target="tpu_custom_call" | custom-call | flops 1610612736 | bytes 5242880 | tf_op jit(solution)/shard_map/along_first/pallas_call | solution.py:290
  110.4 8.8 %all-to-all-done.1.values = f32[16,1,2,32,128]{4,3,2,1,0:T(8,128)S(1)} async-done(((f32[16,1,2,32,128]{4,3,2,1,0:T(8,128)}), f32[16,1,2,32,128]{4,3,2,1,0:T(8,128)S(1)}, u32[]{:S(2)}, u32[]{:S(2)}) %all-to-all-start.1) | async-done | bytes 524320 | tf_op jit(solution)/shard_map/all_to_all | solution.py:597
  119.3 4.1 %all-to-all-start.3 = ((f32[16,1,2,32,128]{4,3,2,1,0:T(8,128)}), f32[16,1,2,32,128]{4,3,2,1,0:T(8,128)S(1)}, u32[]{:S(2)}, u32[]{:S(2)}) async-start(f32[16,1,2,32,128]{4,3,2,1,0:T(8,128)} %along_first.5), calls=%async_computation.3 | async-start | bytes 1048576 | tf_op jit(solution)/shard_map/all_to_all | solution.py:597
  123.4 5.6 %along_first.6 = f32[16,1,2,32,128]{4,3,2,1,0:T(8,128)} custom-call(f32[16,1,2,32,128]{4,3,2,1,0:T(8,128)} %copy-done.2, f32[4,4,32,512]{3,2,1,0:T(8,128)} %bitcast.29, f32[32,512]{1,0:T(8,128)} %fusion.6.edge, bf16[512,1024]{1,0:T(8,128)(2,1)} %constant.50.clone.fwd_high, bf16[512,1024]{1,0:T(8,128)(2,1)} %constant.51.clone.fwd_low, ...), custom_call_target="tpu_custom_call" | custom-call | flops 1610612736 | bytes 5242880 | tf_op jit(solution)/shard_map/along_first/pallas_call | solution.py:290
  129.0 8.8 %all-to-all-done.3.values = f32[16,1,2,32,128]{4,3,2,1,0:T(8,128)S(1)} async-done(((f32[16,1,2,32,128]{4,3,2,1,0:T(8,128)}), f32[16,1,2,32,128]{4,3,2,1,0:T(8,128)S(1)}, u32[]{:S(2)}, u32[]{:S(2)}) %all-to-all-start.3) | async-done | bytes 524320 | tf_op jit(solution)/shard_map/all_to_all | solution.py:597
  137.8 4.1 %all-to-all-start.5 = ((f32[16,1,2,32,128]{4,3,2,1,0:T(8,128)}), f32[16,1,2,32,128]{4,3,2,1,0:T(8,128)S(1)}, u32[]{:S(2)}, u32[]{:S(2)}) async-start(f32[16,1,2,32,128]{4,3,2,1,0:T(8,128)} %along_first.6), calls=%async_computation.5 | async-start | bytes 1048576 | tf_op jit(solution)/shard_map/all_to_all | solution.py:597
  142.1 1.5 collective-permute-start.1
  143.6 0.6 collective-permute-start
  144.1 1.9 collective-permute-done.1
  146.0 1.5 collective-permute-done
  147.6 5.6 %along_first.7 = f32[16,1,2,32,128]{4,3,2,1,0:T(8,128)} custom-call(f32[16,1,2,32,128]{4,3,2,1,0:T(8,128)} %copy-done.3, f32[4,4,32,512]{3,2,1,0:T(8,128)} %bitcast.30, f32[32,512]{1,0:T(8,128)} %fusion.6.edge, bf16[512,1024]{1,0:T(8,128)(2,1)} %constant.50.clone.fwd_high, bf16[512,1024]{1,0:T(8,128)(2,1)} %constant.51.clone.fwd_low, ...), custom_call_target="tpu_custom_call" | custom-call | flops 1610612736 | bytes 5242880 | tf_op jit(solution)/shard_map/along_first/pallas_call | solution.py:290
  153.2 3.2 %all-to-all-done.5.values = f32[16,1,2,32,128]{4,3,2,1,0:T(8,128)S(1)} async-done(((f32[16,1,2,32,128]{4,3,2,1,0:T(8,128)}), f32[16,1,2,32,128]{4,3,2,1,0:T(8,128)S(1)}, u32[]{:S(2)}, u32[]{:S(2)}) %all-to-all-start.5) | async-done | bytes 524320 | tf_op jit(solution)/shard_map/all_to_all | solution.py:597
  156.4 4.1 %all-to-all-start.7 = ((f32[16,1,2,32,128]{4,3,2,1,0:T(8,128)}), f32[16,1,2,32,128]{4,3,2,1,0:T(8,128)S(1)}, u32[]{:S(2)}, u32[]{:S(2)}) async-start(f32[16,1,2,32,128]{4,3,2,1,0:T(8,128)} %along_first.7), calls=%async_computation.7 | async-start | bytes 1048576 | tf_op jit(solution)/shard_map/all_to_all | solution.py:597
  160.6 0.5 collective-permute-start.2
  161.0 4.0 %collective-permute-start.3 = (f32[8,1,1280]{2,1,0:T(1,128)S(1)}, f32[8,1,1280]{2,1,0:T(1,128)S(1)}, u32[]{:S(2)}, u32[]{:S(2)}) collective-permute-start(f32[8,1,1280]{2,1,0:T(1,128)S(1)} %get-tuple-element.46), channel_id=1, source_target_pairs={{2,0},{4,2},{6,4},{8,6},{10,8},{12,10},{14,12},{16,14},{18,16},{20... | collective-permute-start | bytes 122888 | tf_op jit(solution)/shard_map/ppermute | solution.py:540
  165.1 10.3 %collective-permute-done.2 = f32[8,1,1280]{2,1,0:T(1,128)S(1)} collective-permute-done((f32[8,1,1280]{2,1,0:T(1,128)S(1)}, f32[8,1,1280]{2,1,0:T(1,128)S(1)}, u32[]{:S(2)}, u32[]{:S(2)}) %collective-permute-start.2) | collective-permute-done | bytes 40992 | tf_op jit(solution)/shard_map/ppermute | solution.py:539
  175.4 0.1 fusion.1
  175.5 4.4 %backward_second.4 = (f32[1,2,256,128]{3,2,1,0:T(8,128)}, f32[1,2,256,128]{3,2,1,0:T(8,128)}) custom-call(s32[1]{0:T(128)} %bitcast.me_ref, f32[16,1,2,32,128]{4,3,2,1,0:T(8,128)} %copy-done.5, bf16[1024,512]{1,0:T(8,128)(2,1)} %constant.54.clone.high, bf16[1024,512]{1,0:T(8,128)(2,1)} %constant.55.clone.low), custom_call_target="tpu_custom_call" | custom-call | flops 805306368 | bytes 3145728 | tf_op jit(solution)/shard_map/backward_second/pallas_call | solution.py:369
  179.9 0.6 collective-permute-start.11
  180.5 3.6 %backward_second.5 = (f32[1,2,256,128]{3,2,1,0:T(8,128)}, f32[1,2,256,128]{3,2,1,0:T(8,128)}) custom-call(s32[1]{0:T(128)} %bitcast.me_ref, f32[16,1,2,32,128]{4,3,2,1,0:T(8,128)} %copy-done.6, bf16[1024,512]{1,0:T(8,128)(2,1)} %constant.54.clone.high, bf16[1024,512]{1,0:T(8,128)(2,1)} %constant.55.clone.low), custom_call_target="tpu_custom_call" | custom-call | flops 805306368 | bytes 3145728 | tf_op jit(solution)/shard_map/backward_second/pallas_call | solution.py:369
  184.1 1.4 collective-permute-start.12
  185.5 3.6 %backward_second.6 = (f32[1,2,256,128]{3,2,1,0:T(8,128)}, f32[1,2,256,128]{3,2,1,0:T(8,128)}) custom-call(s32[1]{0:T(128)} %bitcast.me_ref, f32[16,1,2,32,128]{4,3,2,1,0:T(8,128)} %copy-done.7, bf16[1024,512]{1,0:T(8,128)(2,1)} %constant.54.clone.high, bf16[1024,512]{1,0:T(8,128)(2,1)} %constant.55.clone.low), custom_call_target="tpu_custom_call" | custom-call | flops 805306368 | bytes 3145728 | tf_op jit(solution)/shard_map/backward_second/pallas_call | solution.py:369
  189.0 0.6 collective-permute-start.13
  189.7 0.8 copy-done.8
  190.5 3.6 %backward_second.7 = (f32[1,2,256,128]{3,2,1,0:T(8,128)}, f32[1,2,256,128]{3,2,1,0:T(8,128)}) custom-call(s32[1]{0:T(128)} %bitcast.me_ref, f32[16,1,2,32,128]{4,3,2,1,0:T(8,128)} %copy-done.8, bf16[1024,512]{1,0:T(8,128)(2,1)} %constant.54.clone.high, bf16[1024,512]{1,0:T(8,128)(2,1)} %constant.55.clone.low), custom_call_target="tpu_custom_call" | custom-call | flops 805306368 | bytes 3145728 | tf_op jit(solution)/shard_map/backward_second/pallas_call | solution.py:369
  194.0 1.4 collective-permute-start.14
  195.4 1.1 pad_maximum_fusion.extended
  196.5 15.5 %near_blocks.1.near = f32[8,8,1024]{2,1,0:T(8,128)} custom-call(f32[8,3,8,1280]{3,2,1,0:T(8,128)} %pad_maximum_fusion.extended, s32[6,8,1024]{2,1,0:T(8,128)} %codes.1, f32[6,8,8,8,1024]{4,3,2,1,0:T(8,128)} %blocks_ref.1), custom_call_target="tpu_custom_call" | custom-call | flops 6291456 | bytes 12582912 | tf_op jit(solution)/shard_map/near_blocks/pallas_call | solution.py:506
  212.1 0.7 copy-done.10
  212.9 0.1 copy-done.13
  213.0 9.8 %depth_gather.1 = f32[8,8,1024]{2,1,0:T(8,128)} custom-call(s32[1]{0:T(128)} %bitcast.me_ref, s32[8,1024]{1,0:T(8,128)} %counts.3, f32[8,8,1024]{2,1,0:T(8,128)} %near_blocks.1.near, f32[8,64,8,1024]{3,2,1,0:T(8,128)} %projection.3, bf16[2,256,512]{2,1,0:T(8,128)(2,1)} %constant.56.clone.high, bf16[2,256,512]{2,1,0:T(8,128)(2,1)} %constant.57.clone.low, ...), custom_call_target="tpu_custom_call" | custom-call | flops 8388608 | bytes 16777216 | tf_op jit(solution)/shard_map/depth_gather/pallas_call | solution.py:436
  (55 shorter events, 0.6 us)
Async XLA Ops:
  9.6 20.1 %copy-start.20 = (f32[1,2,256,128]{3,2,1,0:T(8,128)S(1)}, f32[1,2,256,128]{3,2,1,0:T(8,128)}, u32[]{:S(2)}) copy-start(f32[1,2,256,128]{3,2,1,0:T(8,128)} %get-tuple-element.25) | copy-start | bytes 786436
  9.6 9.5 %collective-permute-start.4 = (f32[1,2,256,128]{3,2,1,0:T(8,128)}, f32[1,2,256,128]{3,2,1,0:T(8,128)S(1)}, u32[]{:S(2)}, u32[]{:S(2)}) collective-permute-start(f32[1,2,256,128]{3,2,1,0:T(8,128)} %get-tuple-element.22), channel_id=1, source_target_pairs={{0,1},{1,0},{2,3},{3,2},{4,5},{5,4},{6,7},{7,6},{8,9},{9,8},{10,11... | collective-permute-start | bytes 786440 | tf_op jit(solution)/shard_map/ppermute | solution.py:593
  19.1 0.7 copy-start.15
  19.8 28.7 %copy-start.19 = (f32[1,2,256,128]{3,2,1,0:T(8,128)S(1)}, f32[1,2,256,128]{3,2,1,0:T(8,128)}, u32[]{:S(2)}) copy-start(f32[1,2,256,128]{3,2,1,0:T(8,128)} %get-tuple-element.28) | copy-start | bytes 786436
  23.5 20.6 %all-to-all-start = ((f32[16,1,2,32,128]{4,3,2,1,0:T(8,128)}), f32[16,1,2,32,128]{4,3,2,1,0:T(8,128)S(1)}, u32[]{:S(2)}, u32[]{:S(2)}) async-start(f32[16,1,2,32,128]{4,3,2,1,0:T(8,128)} %forward_second.4), calls=%async_computation | async-start | bytes 1048576 | tf_op jit(solution)/shard_map/all_to_all | solution.py:595
  29.7 8.7 %collective-permute-start.8 = (f32[1,2,256,128]{3,2,1,0:T(8,128)S(1)}, f32[1,2,256,128]{3,2,1,0:T(8,128)S(1)}, u32[]{:S(2)}, u32[]{:S(2)}) collective-permute-start(f32[1,2,256,128]{3,2,1,0:T(8,128)S(1)} %copy-done.20), channel_id=1, source_target_pairs={{0,1},{1,0},{2,3},{3,2},{4,5},{5,4},{6,7},{7,6},{8,9},{9,8},{10,11... | collective-permute-start | bytes 786440 | tf_op jit(solution)/shard_map/ppermute | solution.py:593
  38.4 0.7 copy-start.16
  39.1 28.2 %copy-start.18 = (f32[1,2,256,128]{3,2,1,0:T(8,128)S(1)}, f32[1,2,256,128]{3,2,1,0:T(8,128)}, u32[]{:S(2)}) copy-start(f32[1,2,256,128]{3,2,1,0:T(8,128)} %get-tuple-element.31) | copy-start | bytes 786436
  44.2 36.1 %copy-start = (f32[16,1,2,32,128]{4,3,2,1,0:T(8,128)}, f32[16,1,2,32,128]{4,3,2,1,0:T(8,128)S(1)}, u32[]{:S(2)}) copy-start(f32[16,1,2,32,128]{4,3,2,1,0:T(8,128)S(1)} %all-to-all-done.values) | copy-start | bytes 1572868
  44.2 18.8 %all-to-all-start.2 = ((f32[16,1,2,32,128]{4,3,2,1,0:T(8,128)}), f32[16,1,2,32,128]{4,3,2,1,0:T(8,128)S(1)}, u32[]{:S(2)}, u32[]{:S(2)}) async-start(f32[16,1,2,32,128]{4,3,2,1,0:T(8,128)} %forward_second.5), calls=%async_computation.2 | async-start | bytes 1048576 | tf_op jit(solution)/shard_map/all_to_all | solution.py:595
  48.5 8.7 %collective-permute-start.9 = (f32[1,2,256,128]{3,2,1,0:T(8,128)S(1)}, f32[1,2,256,128]{3,2,1,0:T(8,128)S(1)}, u32[]{:S(2)}, u32[]{:S(2)}) collective-permute-start(f32[1,2,256,128]{3,2,1,0:T(8,128)S(1)} %copy-done.19), channel_id=1, source_target_pairs={{0,1},{1,0},{2,3},{3,2},{4,5},{5,4},{6,7},{7,6},{8,9},{9,8},{10,11... | collective-permute-start | bytes 786440 | tf_op jit(solution)/shard_map/ppermute | solution.py:593
  57.2 0.7 copy-start.17
  63.0 25.8 %copy-start.1 = (f32[16,1,2,32,128]{4,3,2,1,0:T(8,128)}, f32[16,1,2,32,128]{4,3,2,1,0:T(8,128)S(1)}, u32[]{:S(2)}) copy-start(f32[16,1,2,32,128]{4,3,2,1,0:T(8,128)S(1)} %all-to-all-done.2.values) | copy-start | bytes 1572868
  63.0 18.8 %all-to-all-start.4 = ((f32[16,1,2,32,128]{4,3,2,1,0:T(8,128)}), f32[16,1,2,32,128]{4,3,2,1,0:T(8,128)S(1)}, u32[]{:S(2)}, u32[]{:S(2)}) async-start(f32[16,1,2,32,128]{4,3,2,1,0:T(8,128)} %forward_second.6), calls=%async_computation.4 | async-start | bytes 1048576 | tf_op jit(solution)/shard_map/all_to_all | solution.py:595
  67.3 8.7 %collective-permute-start.10 = (f32[1,2,256,128]{3,2,1,0:T(8,128)S(1)}, f32[1,2,256,128]{3,2,1,0:T(8,128)S(1)}, u32[]{:S(2)}, u32[]{:S(2)}) collective-permute-start(f32[1,2,256,128]{3,2,1,0:T(8,128)S(1)} %copy-done.18), channel_id=1, source_target_pairs={{0,1},{1,0},{2,3},{3,2},{4,5},{5,4},{6,7},{7,6},{8,9},{9,8},{10,11... | collective-permute-start | bytes 786440 | tf_op jit(solution)/shard_map/ppermute | solution.py:593
  69.7 16.5 %collective-permute-start.7 = (f32[2,1,512]{2,1,0:T(1,128)S(1)}, f32[2,1,512]{2,1,0:T(1,128)S(1)}, u32[]{:S(2)}, u32[]{:S(2)}) collective-permute-start(f32[2,1,512]{2,1,0:T(1,128)S(1)} %pad_maximum_fusion.3), channel_id=1, source_target_pairs={{16,0},{17,1}} | collective-permute-start | bytes 12296 | tf_op jit(solution)/shard_map/ppermute | solution.py:555
  71.0 15.2 %collective-permute-start.6 = (f32[2,16,512]{2,1,0:T(8,128)S(1)}, f32[2,16,512]{2,1,0:T(8,128)S(1)}, u32[]{:S(2)}, u32[]{:S(2)}) collective-permute-start(f32[2,16,512]{2,1,0:T(8,128)S(1)} %get-tuple-element.49), channel_id=1, source_target_pairs={{0,2},{2,6},{4,10},{6,14},{8,18},{10,22},{12,26},{14,30},{1,3},{3,... | collective-permute-start | bytes 196616 | tf_op jit(solution)/shard_map/ppermute | solution.py:554
  72.5 13.8 %collective-permute-start.5 = (f32[2,16,512]{2,1,0:T(8,128)S(1)}, f32[2,16,512]{2,1,0:T(8,128)S(1)}, u32[]{:S(2)}, u32[]{:S(2)}) collective-permute-start(f32[2,16,512]{2,1,0:T(8,128)S(1)} %get-tuple-element.50), channel_id=1, source_target_pairs={{0,0},{2,4},{4,8},{6,12},{8,16},{10,20},{12,24},{14,28},{1,1},{3,5... | collective-permute-start | bytes 196616 | tf_op jit(solution)/shard_map/ppermute | solution.py:553
  76.0 0.7 copy-start.14
  81.7 13.3 %copy-start.2 = (f32[16,1,2,32,128]{4,3,2,1,0:T(8,128)}, f32[16,1,2,32,128]{4,3,2,1,0:T(8,128)S(1)}, u32[]{:S(2)}) copy-start(f32[16,1,2,32,128]{4,3,2,1,0:T(8,128)S(1)} %all-to-all-done.4.values) | copy-start | bytes 1572868
  81.7 18.9 %all-to-all-start.6 = ((f32[16,1,2,32,128]{4,3,2,1,0:T(8,128)}), f32[16,1,2,32,128]{4,3,2,1,0:T(8,128)S(1)}, u32[]{:S(2)}, u32[]{:S(2)}) async-start(f32[16,1,2,32,128]{4,3,2,1,0:T(8,128)} %forward_second.7), calls=%async_computation.6 | async-start | bytes 1048576 | tf_op jit(solution)/shard_map/all_to_all | solution.py:595
  100.7 18.6 %copy-start.3 = (f32[16,1,2,32,128]{4,3,2,1,0:T(8,128)}, f32[16,1,2,32,128]{4,3,2,1,0:T(8,128)S(1)}, u32[]{:S(2)}) copy-start(f32[16,1,2,32,128]{4,3,2,1,0:T(8,128)S(1)} %all-to-all-done.6.values) | copy-start | bytes 1572868
  100.7 18.6 %all-to-all-start.1 = ((f32[16,1,2,32,128]{4,3,2,1,0:T(8,128)}), f32[16,1,2,32,128]{4,3,2,1,0:T(8,128)S(1)}, u32[]{:S(2)}, u32[]{:S(2)}) async-start(f32[16,1,2,32,128]{4,3,2,1,0:T(8,128)} %along_first.4), calls=%async_computation.1 | async-start | bytes 1048576 | tf_op jit(solution)/shard_map/all_to_all | solution.py:597
  110.4 31.5 %copy-start.4 = (f32[8,8,1024]{2,1,0:T(8,128)S(1)}, f32[8,8,1024]{2,1,0:T(8,128)}, u32[]{:S(2)}) copy-start(f32[8,8,1024]{2,1,0:T(8,128)} %charges.1) | copy-start | bytes 786436
  110.4 31.5 %copy-start.9 = (s32[8,1024]{1,0:T(8,128)S(1)}, s32[8,1024]{1,0:T(8,128)}, u32[]{:S(2)}) copy-start(s32[8,1024]{1,0:T(8,128)} %counts.3) | copy-start | bytes 98308
  119.3 18.6 %copy-start.5 = (f32[16,1,2,32,128]{4,3,2,1,0:T(8,128)}, f32[16,1,2,32,128]{4,3,2,1,0:T(8,128)S(1)}, u32[]{:S(2)}) copy-start(f32[16,1,2,32,128]{4,3,2,1,0:T(8,128)S(1)} %all-to-all-done.1.values) | copy-start | bytes 1572868
  119.3 18.6 %all-to-all-start.3 = ((f32[16,1,2,32,128]{4,3,2,1,0:T(8,128)}), f32[16,1,2,32,128]{4,3,2,1,0:T(8,128)S(1)}, u32[]{:S(2)}, u32[]{:S(2)}) async-start(f32[16,1,2,32,128]{4,3,2,1,0:T(8,128)} %along_first.5), calls=%async_computation.3 | async-start | bytes 1048576 | tf_op jit(solution)/shard_map/all_to_all | solution.py:597
  137.8 15.4 %copy-start.6 = (f32[16,1,2,32,128]{4,3,2,1,0:T(8,128)}, f32[16,1,2,32,128]{4,3,2,1,0:T(8,128)S(1)}, u32[]{:S(2)}) copy-start(f32[16,1,2,32,128]{4,3,2,1,0:T(8,128)S(1)} %all-to-all-done.3.values) | copy-start | bytes 1572868
  137.8 18.6 %all-to-all-start.5 = ((f32[16,1,2,32,128]{4,3,2,1,0:T(8,128)}), f32[16,1,2,32,128]{4,3,2,1,0:T(8,128)S(1)}, u32[]{:S(2)}, u32[]{:S(2)}) async-start(f32[16,1,2,32,128]{4,3,2,1,0:T(8,128)} %along_first.6), calls=%async_computation.5 | async-start | bytes 1048576 | tf_op jit(solution)/shard_map/all_to_all | solution.py:597
  142.1 3.9 %collective-permute-start.1 = (f32[8,8,16]{2,1,0:T(8,128)S(1)}, f32[8,8,16]{2,1,0:T(8,128)S(1)}, u32[]{:S(2)}, u32[]{:S(2)}) collective-permute-start(f32[8,8,16]{2,1,0:T(8,128)S(1)} %get-tuple-element.47), channel_id=1, source_target_pairs={{1,0},{0,1},{3,2},{2,3},{5,4},{4,5},{7,6},{6,7},{9,8},{8,9},{11,10... | collective-permute-start | bytes 12296 | tf_op jit(solution)/shard_map/ppermute | solution.py:535
  143.6 3.9 %collective-permute-start = (f32[8,8,16]{2,1,0:T(8,128)S(1)}, f32[8,8,16]{2,1,0:T(8,128)S(1)}, u32[]{:S(2)}, u32[]{:S(2)}) collective-permute-start(f32[8,8,16]{2,1,0:T(8,128)S(1)} %get-tuple-element.48), channel_id=1, source_target_pairs={{0,1},{1,0},{2,3},{3,2},{4,5},{5,4},{6,7},{7,6},{8,9},{9,8},{10,11... | collective-permute-start | bytes 12296 | tf_op jit(solution)/shard_map/ppermute | solution.py:534
  156.4 29.0 %copy-start.7 = (f32[16,1,2,32,128]{4,3,2,1,0:T(8,128)}, f32[16,1,2,32,128]{4,3,2,1,0:T(8,128)S(1)}, u32[]{:S(2)}) copy-start(f32[16,1,2,32,128]{4,3,2,1,0:T(8,128)S(1)} %all-to-all-done.5.values) | copy-start | bytes 1572868
  156.4 33.2 %all-to-all-start.7 = ((f32[16,1,2,32,128]{4,3,2,1,0:T(8,128)}), f32[16,1,2,32,128]{4,3,2,1,0:T(8,128)S(1)}, u32[]{:S(2)}, u32[]{:S(2)}) async-start(f32[16,1,2,32,128]{4,3,2,1,0:T(8,128)} %along_first.7), calls=%async_computation.7 | async-start | bytes 1048576 | tf_op jit(solution)/shard_map/all_to_all | solution.py:597
  160.6 14.8 %collective-permute-start.2 = (f32[8,1,1280]{2,1,0:T(1,128)S(1)}, f32[8,1,1280]{2,1,0:T(1,128)S(1)}, u32[]{:S(2)}, u32[]{:S(2)}) collective-permute-start(f32[8,1,1280]{2,1,0:T(1,128)S(1)} %get-tuple-element.45), channel_id=1, source_target_pairs={{0,2},{2,4},{4,6},{6,8},{8,10},{10,12},{12,14},{14,16},{16,18},{18... | collective-permute-start | bytes 122888 | tf_op jit(solution)/shard_map/ppermute | solution.py:539
  161.0 14.4 %collective-permute-start.3 = (f32[8,1,1280]{2,1,0:T(1,128)S(1)}, f32[8,1,1280]{2,1,0:T(1,128)S(1)}, u32[]{:S(2)}, u32[]{:S(2)}) collective-permute-start(f32[8,1,1280]{2,1,0:T(1,128)S(1)} %get-tuple-element.46), channel_id=1, source_target_pairs={{2,0},{4,2},{6,4},{8,6},{10,8},{12,10},{14,12},{16,14},{18,16},{20... | collective-permute-start | bytes 122888 | tf_op jit(solution)/shard_map/ppermute | solution.py:540
  179.9 32.1 %collective-permute-start.11 = (f32[1,2,256,128]{3,2,1,0:T(8,128)}, f32[1,2,256,128]{3,2,1,0:T(8,128)S(1)}, u32[]{:S(2)}, u32[]{:S(2)}) collective-permute-start(f32[1,2,256,128]{3,2,1,0:T(8,128)} %get-tuple-element.33), channel_id=1, source_target_pairs={{0,1},{1,0},{2,3},{3,2},{4,5},{5,4},{6,7},{7,6},{8,9},{9,8},{10,11... | collective-permute-start | bytes 786440 | tf_op jit(solution)/shard_map/ppermute | solution.py:600
  184.1 27.9 %collective-permute-start.12 = (f32[1,2,256,128]{3,2,1,0:T(8,128)}, f32[1,2,256,128]{3,2,1,0:T(8,128)S(1)}, u32[]{:S(2)}, u32[]{:S(2)}) collective-permute-start(f32[1,2,256,128]{3,2,1,0:T(8,128)} %get-tuple-element.34), channel_id=1, source_target_pairs={{0,1},{1,0},{2,3},{3,2},{4,5},{5,4},{6,7},{7,6},{8,9},{9,8},{10,11... | collective-permute-start | bytes 786440 | tf_op jit(solution)/shard_map/ppermute | solution.py:600
  189.0 23.0 %collective-permute-start.13 = (f32[1,2,256,128]{3,2,1,0:T(8,128)}, f32[1,2,256,128]{3,2,1,0:T(8,128)S(1)}, u32[]{:S(2)}, u32[]{:S(2)}) collective-permute-start(f32[1,2,256,128]{3,2,1,0:T(8,128)} %get-tuple-element.35), channel_id=1, source_target_pairs={{0,1},{1,0},{2,3},{3,2},{4,5},{5,4},{6,7},{7,6},{8,9},{9,8},{10,11... | collective-permute-start | bytes 786440 | tf_op jit(solution)/shard_map/ppermute | solution.py:600
  189.7 0.8 copy-start.8
  194.0 18.0 %collective-permute-start.14 = (f32[1,2,256,128]{3,2,1,0:T(8,128)}, f32[1,2,256,128]{3,2,1,0:T(8,128)S(1)}, u32[]{:S(2)}, u32[]{:S(2)}) collective-permute-start(f32[1,2,256,128]{3,2,1,0:T(8,128)} %get-tuple-element.36), channel_id=1, source_target_pairs={{0,1},{1,0},{2,3},{3,2},{4,5},{5,4},{6,7},{7,6},{8,9},{9,8},{10,11... | collective-permute-start | bytes 786440 | tf_op jit(solution)/shard_map/ppermute | solution.py:600
  212.0 0.7 copy-start.10
  212.0 0.8 copy-start.11
  212.0 0.9 copy-start.12
  212.1 1.0 copy-start.13

commit v2 on v0

--- a/solution.py
+++ b/solution.py
@@ -1,17 +1,571 @@
+import functools
 import math
 
 import jax
 import jax.numpy as jnp
+import ml_dtypes
+import numpy as np
 from jax import lax
+from jax.experimental import pallas as pl
+from jax.experimental.pallas import tpu as pltpu
 from jax.sharding import PartitionSpec as P
 
-NX = 512
-NY = 512
-NZ = 64
 TX = 4
 TY = 4
 TZ = 4
 NZC = 16
+LANES = 128
+CHUNKS = 2
+VMEM_LIMIT = 56 * 1024 * 1024
+
+
+def halves(table):
+    high = table.astype(np.float32).astype(ml_dtypes.bfloat16)
+    low = (table - high.astype(np.float64)).astype(np.float32).astype(ml_dtypes.bfloat16)
+    return (high, low)
+
+
+def wave(rows, cols, length):
+    angle = (rows[:, None] * cols[None, :] % length) * (2.0 * math.pi / length)
+    return (np.cos(angle), np.sin(angle))
+
+
+class Plan:
+    def __init__(self, slabs, cells, panels, cell_planes, cell_cols, near, nx, nz, ny):
+        self.slabs, self.cells = (slabs, cells)
+        self.panels, self.cell_planes, self.cell_cols, self.near = (panels, cell_planes, cell_cols, near)
+        self.nx, self.ny, self.nz = (nx, ny, nz)
+        self.slots = slabs * cells
+        self.tx_chunk = TX // CHUNKS
+        self.width = cell_planes * self.tx_chunk
+        self.y_lanes = LANES // self.width if self.width else 1
+        self.row_block = LANES // NZC
+        self.step_blocks = self.y_lanes // TY
+        self.steps = cell_cols // (LANES * self.step_blocks) if self.step_blocks else 0
+        self.x_chunk = nx // CHUNKS
+        self.ky_local = ny // slabs
+
+    def fits(self):
+        return (
+            self.slots * 2 == self.nz
+            and self.cell_planes == 8
+            and self.step_blocks * TY * self.width == LANES
+            and self.slabs % self.y_lanes == 0
+            and self.ky_local % 8 == 0
+            and self.steps * self.step_blocks * LANES == self.cell_cols
+            and self.x_chunk % LANES == 0
+            and self.ny % 1024 == self.nx % 1024 == 512
+        )
+
+    def depth_tables(self):
+        depth = np.arange(NZC)[None, :] * TZ + np.arange(TZ)[:, None]
+        forward = np.zeros((self.slots, 2, self.row_block, TZ, self.row_block, NZC))
+        backward = np.zeros_like(forward)
+        for freq in range(self.slots):
+            angle = (freq * depth % self.nz) * (2.0 * math.pi / self.nz)
+            real, imag = (np.cos(angle), -np.sin(angle))
+            factor = 2.0
+            if freq == 0:
+                imag = np.cos(depth * math.pi)
+                factor = 1.0
+            for row in range(self.row_block):
+                forward[freq, 0, row, :, row, :] = real
+                forward[freq, 1, row, :, row, :] = imag
+                backward[freq, 0, row, :, row, :] = factor * real
+                backward[freq, 1, row, :, row, :] = factor * imag
+        shape = (self.slots * 2 * self.row_block, TZ * LANES)
+        return (forward.reshape(shape), backward.reshape(shape))
+
+    def y_order(self):
+        rows = np.arange(self.ny // TY).reshape(-1, self.row_block)
+        return (rows[:, None, :] * TY + np.arange(TY)[None, :, None]).reshape(-1)
+
+    def x_order(self):
+        chunk, slab, tile, plane = np.meshgrid(
+            np.arange(CHUNKS),
+            np.arange(self.slabs),
+            np.arange(self.tx_chunk),
+            np.arange(self.cell_planes),
+            indexing="ij",
+        )
+        return ((slab * self.cell_planes + plane) * TX + chunk * self.tx_chunk + tile).reshape(-1)
+
+
+def split(value):
+    high = value.astype(jnp.bfloat16)
+    low = (value - high.astype(jnp.float32)).astype(jnp.bfloat16)
+    return (high, low)
+
+
+def product(left, right, dims=((1,), (0,))):
+    def dot(a, b):
+        return lax.dot_general(a, b, (dims, ((), ())), preferred_element_type=jnp.float32)
+
+    return dot(left[0], right[0]) + (dot(left[0], right[1]) + dot(left[1], right[0]))
+
+
+def swap_groups(parts, width):
+    count = len(parts)
+    lane = lax.broadcasted_iota(jnp.int32, parts[0].shape, 1)
+    parts = list(parts)
+    step = count // 2
+    while step >= 1:
+        shift = step * width
+        upper = (lane // shift) % 2 == 1
+        for i in range(count):
+            if i & step:
+                continue
+            first, second = (parts[i], parts[i + step])
+            parts[i] = jnp.where(upper, pltpu.roll(second, shift, 1), first)
+            parts[i + step] = jnp.where(upper, second, pltpu.roll(first, LANES - shift, 1))
+        step //= 2
+    return parts
+
+
+def project_kernel(plan, charges, counts, projection, high, low, out, scratch):
+    planes = plan.cell_planes
+    slot = lax.broadcasted_iota(jnp.int32, charges.shape, 0)
+    masked = jnp.where(slot < counts[...][None], charges[...], 0.0)
+    for block in range(plan.step_blocks):
+        lanes = pl.ds(block * LANES, LANES)
+        own = masked[:, :, block * LANES : (block + 1) * LANES]
+        for tx in range(plan.tx_chunk):
+            for ty in range(TY):
+                for tz in range(TZ):
+                    t = (tx * TY + ty) * TZ + tz
+                    total = projection[0, t, :, lanes] * own[0]
+                    for p in range(1, plan.panels):
+                        total = total + projection[p, t, :, lanes] * own[p]
+                    row = ((block * TY + ty) * plan.tx_chunk + tx) * planes
+                    scratch[row : row + planes, tz * LANES : (tz + 1) * LANES] = total
+    spectra = product((high[...], low[...]), split(scratch[...]), ((1,), (1,)))
+    out[:, :, 0] = spectra.reshape(plan.slots, 2, plan.row_block, LANES)
+
+
+def projection_spec(plan, chunk):
+    shape = (plan.panels, TX * TY * TZ // CHUNKS, plan.cell_planes, plan.step_blocks * LANES)
+    return pl.BlockSpec(shape, lambda i: (0, chunk, 0, i))
+
+
+def panel_spec(plan):
+    return pl.BlockSpec((plan.panels, plan.cell_planes, plan.step_blocks * LANES), lambda i: (0, 0, i))
+
+
+def count_spec(plan):
+    return pl.BlockSpec((plan.cell_planes, plan.step_blocks * LANES), lambda i: (0, i))
+
+
+def piece_shape(plan):
+    return (plan.slots, 2, plan.steps, plan.row_block, LANES)
+
+
+def piece_spec(plan):
+    return pl.BlockSpec((plan.slots, 2, 1, plan.row_block, LANES), lambda i: (0, 0, i, 0, 0))
+
+
+def whole_spec(array):
+    return pl.BlockSpec(array.shape, lambda i: (0,) * array.ndim)
+
+
+def project(plan, chunk, charges, counts, projection, high, low):
+    return pl.pallas_call(
+        functools.partial(project_kernel, plan),
+        grid=(plan.steps,),
+        in_specs=[
+            panel_spec(plan),
+            count_spec(plan),
+            projection_spec(plan, chunk),
+            whole_spec(high),
+            whole_spec(low),
+        ],
+        out_specs=piece_spec(plan),
+        out_shape=jax.ShapeDtypeStruct(piece_shape(plan), jnp.float32),
+        scratch_shapes=[pltpu.VMEM((LANES, TZ * LANES), jnp.float32)],
+        compiler_params=pltpu.CompilerParams(vmem_limit_bytes=VMEM_LIMIT),
+        cost_estimate=pl.CostEstimate(
+            flops=2 * projection.size // CHUNKS,
+            bytes_accessed=4 * projection.size // CHUNKS,
+            transcendentals=0,
+        ),
+        name="project_depth",
+    )(charges, counts, projection, high, low)
+
+
+def forward_y_kernel(plan, me_ref, pieces, high, low, out, scratch):
+    rows = 2 * plan.steps * plan.row_block
+    width = plan.x_chunk
+    for cell in range(plan.cells):
+        for group in range(plan.slabs // plan.y_lanes):
+            parts = [
+                pieces[(group * plan.y_lanes + i) * plan.cells + cell].reshape(rows, LANES)
+                for i in range(plan.y_lanes)
+            ]
+            parts = swap_groups(parts, plan.width)
+            for place, value in enumerate(parts):
+                for part in range(2):
+                    for step in range(plan.steps):
+                        source = (part * plan.steps + step) * plan.row_block
+                        row = ((cell * plan.steps + step) * plan.y_lanes + place) * plan.row_block
+                        col = part * width + group * LANES
+                        scratch[row : row + plan.row_block, col : col + LANES] = value[
+                            source : source + plan.row_block
+                        ]
+    sums = product((high[...], low[...]), split(scratch[...]))
+    cosine, sine = (sums[: plan.ny], sums[plan.ny :])
+    special = me_ref[0] == 0
+
+    @pl.when(jnp.logical_not(special))
+    def _():
+        out[:, :width] = cosine[:, :width] + sine[:, width:]
+        out[:, width:] = cosine[:, width:] - sine[:, :width]
+
+    @pl.when(special)
+    def _():
+        middle = plan.ny // 2
+        row = lax.broadcasted_iota(jnp.int32, (middle, width), 0)
+        for part in range(2):
+            rows = slice(part * middle, (part + 1) * middle)
+            cols = slice(part * width, (part + 1) * width)
+            other = (1 - part) * middle
+            out[rows, :width] = cosine[rows, cols]
+            out[rows, width:] = jnp.where(row == 0, cosine[other : other + 1, cols], -sine[rows, cols])
+
+
+def forward_y(plan, me, pieces, high, low):
+    return pl.pallas_call(
+        functools.partial(forward_y_kernel, plan),
+        grid=(1,),
+        in_specs=[
+            pl.BlockSpec(memory_space=pltpu.SMEM),
+            whole_spec(pieces),
+            whole_spec(high),
+            whole_spec(low),
+        ],
+        out_specs=pl.BlockSpec((plan.ny, 2 * plan.x_chunk), lambda i: (0, 0)),
+        out_shape=jax.ShapeDtypeStruct((plan.ny, 2 * plan.x_chunk), jnp.float32),
+        scratch_shapes=[pltpu.VMEM((plan.ny, 2 * plan.x_chunk), jnp.float32)],
+        compiler_params=pltpu.CompilerParams(vmem_limit_bytes=VMEM_LIMIT),
+        cost_estimate=pl.CostEstimate(
+            flops=12 * plan.ny * plan.ny * 2 * plan.x_chunk,
+            bytes_accessed=8 * pieces.size + 4 * high.size,
+            transcendentals=0,
+        ),
+        name="forward_second",
+    )(me, pieces, high, low)
+
+
+def forward_x_kernel(plan, weights, edge, high, low, *refs):
+    rows_in, (out_high, out_low) = (refs[:CHUNKS], refs[CHUNKS:])
+    width = plan.x_chunk
+    rows = weights.shape[0]
+    real = jnp.concatenate([value[:, :width] for value in rows_in], axis=1)
+    imag = jnp.concatenate([value[:, width:] for value in rows_in], axis=1)
+    sums = product(split(jnp.concatenate([real, imag], axis=0)), (high[...], low[...]))
+    weight = weights[...]
+    row = lax.broadcasted_iota(jnp.int32, weight.shape, 0)
+    second = jnp.where(row == 0, edge[0], weight)
+    new_real = weight * sums[:rows, : plan.nx] + second * sums[rows:, plan.nx :]
+    new_imag = second * sums[rows:, : plan.nx] - weight * sums[:rows, plan.nx :]
+    out_high[0], out_low[0] = split(new_real)
+    out_high[1], out_low[1] = split(new_imag)
+
+
+def forward_x(plan, weights, edge, high, low, pencils):
+    rows = plan.ny // edge.shape[0]
+    out = jax.ShapeDtypeStruct((2, plan.ny, plan.nx), jnp.bfloat16)
+    out_spec = pl.BlockSpec((2, rows, plan.nx), lambda i: (0, i, 0))
+    return pl.pallas_call(
+        functools.partial(forward_x_kernel, plan),
+        grid=(edge.shape[0],),
+        in_specs=[
+            pl.BlockSpec((rows, plan.nx), lambda i: (i, 0)),
+            pl.BlockSpec((1, 1, plan.nx), lambda i: (i, 0, 0)),
+            whole_spec(high),
+            whole_spec(low),
+        ]
+        + [pl.BlockSpec((rows, 2 * plan.x_chunk), lambda i: (i, 0))] * CHUNKS,
+        out_specs=[out_spec, out_spec],
+        out_shape=[out, out],
+        compiler_params=pltpu.CompilerParams(vmem_limit_bytes=VMEM_LIMIT),
+        cost_estimate=pl.CostEstimate(
+            flops=24 * plan.nx * plan.nx * plan.ny,
+            bytes_accessed=20 * plan.nx * plan.ny + 4 * high.size,
+            transcendentals=0,
+        ),
+        name="forward_first",
+    )(weights, edge, high, low, *pencils)
+
+
+def backward_kernel(plan, me_ref, in_high, in_low, x_high, x_low, y_high, y_low, out, scratch):
+    width = plan.x_chunk
+    shape = (2 * plan.ny, plan.nx)
+    sums = product(
+        (in_high[...].reshape(shape), in_low[...].reshape(shape)), (x_high[0], x_low[0])
+    )
+    real = sums[: plan.ny, :width] - sums[plan.ny :, width:]
+    imag = sums[plan.ny :, :width] + sums[: plan.ny, width:]
+    scratch[:, :width] = real
+    scratch[:, width:] = imag
+    special = me_ref[0] == 0
+    middle = plan.ny // 2
+    ends = (scratch[0:1, width:], scratch[middle : middle + 1, width:])
+
+    @pl.when(special)
+    def _():
+        row = lax.broadcasted_iota(jnp.int32, scratch.shape, 0)
+        scratch[...] = jnp.where(row % middle == 0, scratch[...], 2.0 * scratch[...])
+
+    pair = split(scratch[...])
+    halves_sum = []
+    for part in range(2):
+        rows = slice(part * middle, (part + 1) * middle)
+        halves_sum.append(
+            product((y_high[:, rows], y_low[:, rows]), (pair[0][rows], pair[1][rows]))
+        )
+    first, second = halves_sum
+
+    @pl.when(jnp.logical_not(special))
+    def _():
+        both = first + second
+        scratch[:, :width] = both[: plan.ny, :width] - both[plan.ny :, width:]
+        scratch[:, width:] = both[: plan.ny, width:] + both[plan.ny :, :width]
+
+    @pl.when(special)
+    def _():
+        row = lax.broadcasted_iota(jnp.int32, (plan.ny, width), 0)
+        sign = jnp.where(row // plan.row_block % 2 == 0, 1.0, -1.0)
+        scratch[:, :width] = first[: plan.ny, :width] - first[plan.ny :, width:] + sign * ends[0]
+        scratch[:, width:] = second[: plan.ny, :width] - second[plan.ny :, width:] + ends[1]
+
+    for cell in range(plan.cells):
+        for group in range(plan.slabs // plan.y_lanes):
+            parts = []
+            for place in range(plan.y_lanes):
+                pieces = []
+                for part in range(2):
+                    for step in range(plan.steps):
+                        row = ((cell * plan.steps + step) * plan.y_lanes + place) * plan.row_block
+                        col = part * width + group * LANES
+                        pieces.append(scratch[row : row + plan.row_block, col : col + LANES])
+                parts.append(jnp.concatenate(pieces, axis=0))
+            parts = swap_groups(parts, plan.width)
+            for i in range(plan.y_lanes):
+                out[(group * plan.y_lanes + i) * plan.cells + cell] = parts[i].reshape(
+                    2, plan.steps, plan.row_block, LANES
+                )
+
+
+def backward(plan, chunk, me, high, low, x_tables, y_tables):
+    x_spec = pl.BlockSpec((1, plan.nx, 2 * plan.x_chunk), lambda i: (chunk, 0, 0))
+    return pl.pallas_call(
+        functools.partial(backward_kernel, plan),
+        grid=(1,),
+        in_specs=[
+            pl.BlockSpec(memory_space=pltpu.SMEM),
+            whole_spec(high),
+            whole_spec(low),
+            x_spec,
+            x_spec,
+            whole_spec(y_tables[0]),
+            whole_spec(y_tables[1]),
+        ],
+        out_specs=pl.BlockSpec(piece_shape(plan), lambda i: (0, 0, 0, 0, 0)),
+        out_shape=jax.ShapeDtypeStruct(piece_shape(plan), jnp.float32),
+        scratch_shapes=[pltpu.VMEM((plan.ny, 2 * plan.x_chunk), jnp.float32)],
+        compiler_params=pltpu.CompilerParams(vmem_limit_bytes=VMEM_LIMIT),
+        cost_estimate=pl.CostEstimate(
+            flops=24 * plan.nx * plan.ny * 2 * plan.x_chunk,
+            bytes_accessed=4 * high.size + 8 * plan.nx * plan.x_chunk * 2 + 4 * y_tables[0].size,
+            transcendentals=0,
+        ),
+        name="backward_plane",
+    )(me, high, low, *x_tables, *y_tables)
+
+
+def gather_kernel(plan, last, counts, before, projection, high, low, pieces, out, scratch):
+    planes = plan.cell_planes
+    rows = plan.slots * 2 * plan.row_block
+    scratch[...] = product(split(pieces[...].reshape(rows, LANES).T), (high[...], low[...]))
+    for block in range(plan.step_blocks):
+        lanes = pl.ds(block * LANES, LANES)
+        far = [before[p, :, lanes] for p in range(plan.panels)]
+        for tx in range(plan.tx_chunk):
+            for ty in range(TY):
+                row = ((block * TY + ty) * plan.tx_chunk + tx) * planes
+                for tz in range(TZ):
+                    t = (tx * TY + ty) * TZ + tz
+                    potential = scratch[row : row + planes, tz * LANES : (tz + 1) * LANES]
+                    for p in range(plan.panels):
+                        far[p] = far[p] + projection[p, t, :, lanes] * potential
+        for p in range(plan.panels):
+            out[p, :, lanes] = jnp.where(counts[:, lanes] > p, far[p], 0.0) if last else far[p]
+
+
+def gather(plan, chunk, counts, before, projection, high, low, pieces):
+    return pl.pallas_call(
+        functools.partial(gather_kernel, plan, chunk == CHUNKS - 1),
+        grid=(plan.steps,),
+        in_specs=[
+            count_spec(plan),
+            panel_spec(plan),
+            projection_spec(plan, chunk),
+            whole_spec(high),
+            whole_spec(low),
+            piece_spec(plan),
+        ],
+        out_specs=panel_spec(plan),
+        out_shape=jax.ShapeDtypeStruct(before.shape, jnp.float32),
+        scratch_shapes=[pltpu.VMEM((LANES, TZ * LANES), jnp.float32)],
+        compiler_params=pltpu.CompilerParams(vmem_limit_bytes=VMEM_LIMIT),
+        cost_estimate=pl.CostEstimate(
+            flops=2 * projection.size // CHUNKS,
+            bytes_accessed=4 * projection.size // CHUNKS,
+            transcendentals=0,
+        ),
+        name="depth_gather",
+    )(counts, before, projection, high, low, pieces)
+
+
+def near_kernel(plan, extended, codes, blocks_ref, out):
+    step = pl.program_id(0)
+    lane = lax.broadcasted_iota(jnp.int32, (plan.cell_planes, LANES), 1)
+    depth = lane % NZC
+    digits = []
+    for k in range(plan.near):
+        code = codes[k]
+        digits.append((code // 9, code // 3 % 3, code % 3))
+    total = [None] * plan.panels
+    for q in range(plan.panels):
+        shifted = []
+        for dx in range(3):
+            before, here, after = (
+                extended[q, dx, :, pl.ds(pl.multiple_of((step + i) * LANES, LANES), LANES)] for i in range(3)
+            )
+            up = jnp.where(lane < NZC, pltpu.roll(before, NZC, 1), pltpu.roll(here, NZC, 1))
+            down = jnp.where(
+                lane >= LANES - NZC, pltpu.roll(after, LANES - NZC, 1), pltpu.roll(here, LANES - NZC, 1)
+            )
+            for value in (up, here, down):
+                under = jnp.where(
+                    depth == 0, pltpu.roll(value, LANES - NZC + 1, 1), pltpu.roll(value, 1, 1)
+                )
+                over = jnp.where(
+                    depth == NZC - 1, pltpu.roll(value, NZC - 1, 1), pltpu.roll(value, LANES - 1, 1)
+                )
+                shifted.append((under, value, over))
+        for k in range(plan.near):
+            digit_x, digit_y, digit_z = digits[k]
+
+            def choose(digit, options):
+                return jnp.where(digit == 0, options[0], jnp.where(digit == 1, options[1], options[2]))
+
+            by_z = [choose(digit_z, options) for options in shifted]
+            by_y = [choose(digit_y, by_z[3 * i : 3 * i + 3]) for i in range(3)]
+            picked = choose(digit_x, by_y)
+            for p in range(plan.panels):
+                term = blocks_ref[k, p, q] * picked
+                total[p] = term if total[p] is None else total[p] + term
+    for p in range(plan.panels):
+        out[p] = total[p]
+
+
+def near_field(plan, extended, neighbours, near_blocks):
+    return pl.pallas_call(
+        functools.partial(near_kernel, plan),
+        grid=(plan.cell_cols // LANES,),
+        in_specs=[
+            pl.BlockSpec(extended.shape, lambda i: (0, 0, 0, 0)),
+            pl.BlockSpec((plan.near, plan.cell_planes, LANES), lambda i: (0, 0, i)),
+            pl.BlockSpec(
+                (plan.near, plan.panels, plan.panels, plan.cell_planes, LANES), lambda i: (0, 0, 0, 0, i)
+            ),
+        ],
+        out_specs=pl.BlockSpec((plan.panels, plan.cell_planes, LANES), lambda i: (0, 0, i)),
+        out_shape=jax.ShapeDtypeStruct((plan.panels, plan.cell_planes, plan.cell_cols), jnp.float32),
+        compiler_params=pltpu.CompilerParams(vmem_limit_bytes=VMEM_LIMIT),
+        cost_estimate=pl.CostEstimate(
+            flops=2 * near_blocks.size, bytes_accessed=4 * near_blocks.size, transcendentals=0
+        ),
+        name="near_blocks",
+    )(extended, neighbours, near_blocks)
+
+
+def ring_pairs(axis):
+    count = lax.axis_size(axis)
+    up = [(i, (i + 1) % count) for i in range(count)]
+    return (up, [(j, i) for i, j in up])
+
+
+def extended_charges(plan, masked):
+    up, down = ring_pairs("cell")
+    left = lax.ppermute(masked[:, :, -NZC:], "cell", up)
+    right = lax.ppermute(masked[:, :, :NZC], "cell", down)
+    rest = jnp.zeros((plan.panels, plan.cell_planes, LANES - NZC), jnp.float32)
+    wide = jnp.concatenate([rest, left, masked, right, rest], axis=2)
+    up, down = ring_pairs("slab")
+    before = lax.ppermute(wide[:, -1:], "slab", up)
+    after = lax.ppermute(wide[:, :1], "slab", down)
+    whole = jnp.concatenate([before, wide, after], axis=1)
+    planes = plan.cell_planes
+    return jnp.stack([whole[:, i : i + planes] for i in range(3)], axis=1)
+
+
+def spectrum_weights(plan, spectrum):
+    slab, cell = (lax.axis_index("slab"), lax.axis_index("cell"))
+    scale = 1.0 / (plan.nx * plan.ny * plan.nz)
+    by_depth = jnp.transpose(spectrum, (1, 2, 0))
+    shape = (plan.slabs, plan.cells) + by_depth.shape[1:]
+    own = lax.dynamic_index_in_dim(by_depth[: plan.slots].reshape(shape), cell, 1, keepdims=False)
+    dest = lax.broadcasted_iota(jnp.int32, own.shape, 0)
+    swapped = (cell == 0) & (slab >= plan.slabs // 2) & (dest == 0)
+    own = jnp.where(swapped, by_depth[plan.slots][None], own) * scale
+    weights = lax.all_to_all(own, "slab", split_axis=0, concat_axis=0, tiled=True)
+    weights = weights.reshape(plan.ny, plan.nx)
+    far = lax.ppermute(by_depth[0, :1], "slab", [(plan.slabs // 2, 0)]) * scale
+    near = by_depth[plan.slots, :1] * scale
+    steps = 4
+    edge = weights.reshape(steps, -1, plan.nx)[:, 0]
+    step = lax.broadcasted_iota(jnp.int32, edge.shape, 0)
+    first = (slab == 0) & (cell == 0)
+    edge = jnp.where(first & (step == 0), far, edge)
+    edge = jnp.where(first & (step == steps // 2), near, edge)
+    return (weights, edge[:, None])
+
+
+def per_device(charges, counts, projection, near_blocks, neighbours, spectrum):
+    panels, cell_planes, cell_cols = charges.shape
+    cells, slabs = (lax.axis_size("cell"), lax.axis_size("slab"))
+    nx, nz, local = spectrum.shape
+    plan = Plan(slabs, cells, panels, cell_planes, cell_cols, neighbours.shape[0], nx, nz, local * slabs)
+    if not plan.fits():
+        return plain_device(charges, counts, projection, near_blocks, neighbours, spectrum)
+    me = (lax.axis_index("slab") * cells + lax.axis_index("cell")).astype(jnp.int32).reshape(1)
+    depth_forward, depth_backward = plan.depth_tables()
+    freqs = np.arange(plan.ny)
+    cos_y, sin_y = wave(freqs, plan.y_order(), plan.ny)
+    y_forward = halves(np.concatenate([cos_y, sin_y], axis=0))
+    y_backward = halves(np.concatenate([cos_y.T, sin_y.T], axis=0))
+    cos_x, sin_x = wave(plan.x_order(), np.arange(plan.nx), plan.nx)
+    x_forward = halves(np.concatenate([cos_x, sin_x], axis=1))
+    chunked = (CHUNKS, plan.x_chunk, plan.nx)
+    both_x = np.concatenate([cos_x.reshape(chunked), sin_x.reshape(chunked)], axis=1)
+    x_backward = halves(both_x.transpose(0, 2, 1))
+    axes = ("slab", "cell")
+    weights, edge = spectrum_weights(plan, spectrum)
+    pencils = []
+    for chunk in range(CHUNKS):
+        pieces = project(plan, chunk, charges, counts, projection, *halves(depth_forward))
+        pieces = lax.all_to_all(pieces, axes, split_axis=0, concat_axis=0, tiled=True)
+        pencils.append(forward_y(plan, me, pieces, *y_forward))
+    high, low = forward_x(plan, weights, edge, *x_forward, pencils)
+    slot = lax.broadcasted_iota(jnp.int32, charges.shape, 0)
+    masked = jnp.where(slot < counts[None], charges, 0.0)
+    total = near_field(plan, extended_charges(plan, masked), neighbours, near_blocks)
+    for chunk in range(CHUNKS):
+        pieces = backward(plan, chunk, me, high, low, x_backward, y_backward)
+        pieces = lax.all_to_all(pieces, axes, split_axis=0, concat_axis=0, tiled=True)
+        total = gather(plan, chunk, counts, total, projection, *halves(depth_backward), pieces)
+    return total
 
 
 def padded(value, sides, width):
@@ -37,23 +591,23 @@
     return (jnp.cos(angle_rad), jnp.sin(angle_rad))
 
 
-def depth_rows(freq_ids, valid, weights):
-    depth_ids = lax.broadcasted_iota(jnp.int32, (freq_ids.shape[0], NZ), 1)
-    products = freq_ids[:, None] * depth_ids % NZ
-    angle_rad = products.astype(jnp.float32) * (2.0 * math.pi / NZ)
+def depth_rows(nz, freq_ids, valid, weights):
+    depth_ids = lax.broadcasted_iota(jnp.int32, (freq_ids.shape[0], nz), 1)
+    products = freq_ids[:, None] * depth_ids % nz
+    angle_rad = products.astype(jnp.float32) * (2.0 * math.pi / nz)
     basis = jnp.stack([jnp.cos(angle_rad), -jnp.sin(angle_rad)])
     return (basis * valid[None, :, None], basis * weights[None, :, None])
 
 
-def half_depth_tables(cell_count):
-    lower = NZ // (2 * cell_count)
+def half_depth_tables(nz, cell_count):
+    lower = nz // (2 * cell_count)
     row_ids = lax.broadcasted_iota(jnp.int32, (cell_count * (lower + 1),), 0)
     block_ids = row_ids // (lower + 1)
     slot_ids = row_ids % (lower + 1)
-    freq_ids = jnp.where(slot_ids < lower, block_ids * lower + slot_ids, NZ // 2)
+    freq_ids = jnp.where(slot_ids < lower, block_ids * lower + slot_ids, nz // 2)
     valid = jnp.where((slot_ids < lower) | (block_ids == 0), 1.0, 0.0).astype(jnp.float32)
     doubled = jnp.where((slot_ids < lower) & (freq_ids > 0), 2.0, 1.0).astype(jnp.float32)
-    forward_table, backward_table = depth_rows(freq_ids, valid, valid * doubled)
+    forward_table, backward_table = depth_rows(nz, freq_ids, valid, valid * doubled)
     return (forward_table, backward_table, freq_ids)
 
 
@@ -92,8 +646,9 @@
     return jnp.stack([real_part, imag_part], axis=1)
 
 
-def per_device(charges, counts, projection, near_blocks, neighbours, spectrum):
+def plain_device(charges, counts, projection, near_blocks, neighbours, spectrum):
     panels, cell_planes, cell_cols = charges.shape
+    nx, nz, ny = (spectrum.shape[0], spectrum.shape[1], spectrum.shape[2] * lax.axis_size("slab"))
     planes = cell_planes * TX
     rows_cell = cell_cols // NZC
     slot_ids = lax.broadcasted_iota(jnp.int32, charges.shape, 0)
@@ -103,15 +658,15 @@
     grid_field = (
         tile_values.reshape(TX, TY, TZ, cell_planes, rows_cell, NZC)
         .transpose(3, 0, 5, 2, 4, 1)
-        .reshape(planes, NZ, rows_cell * TY)
+        .reshape(planes, nz, rows_cell * TY)
     )
     cell_count = lax.axis_size("cell")
-    forward_table, backward_table, freq_ids = half_depth_tables(cell_count)
+    forward_table, backward_table, freq_ids = half_depth_tables(nz, cell_count)
     depth_count = forward_table.shape[1] // cell_count
     spectra_z = jnp.einsum(
         "wkz,xzy->xwky", forward_table, grid_field, precision=lax.Precision.HIGHEST
     )
-    cosine_y, sine_y = wave_tables(NY, NY, NY)
+    cosine_y, sine_y = wave_tables(ny, ny, ny)
     pencils = transform_rows(
         lax.all_to_all(spectra_z, "cell", split_axis=2, concat_axis=3, tiled=True),
         cosine_y,
@@ -120,16 +675,16 @@
     )
     columns = lax.all_to_all(pencils, "slab", split_axis=3, concat_axis=0, tiled=True)
     col_width = columns.shape[2] * columns.shape[3]
-    flat_rows = columns.reshape(NX, 2 * col_width)
+    flat_rows = columns.reshape(nx, 2 * col_width)
     first_row = lax.axis_index("cell") * depth_count
     kernel_ids = lax.dynamic_slice_in_dim(freq_ids, first_row, depth_count, 0)
-    kernel = jnp.take(spectrum, kernel_ids, axis=1).reshape(NX, col_width) * (1.0 / (NX * NY * NZ))
+    kernel = jnp.take(spectrum, kernel_ids, axis=1).reshape(nx, col_width) * (1.0 / (nx * ny * nz))
     kernel_both = jnp.concatenate([kernel, kernel], axis=1)
     slab_count = lax.axis_size("slab")
-    local_rows = NX // slab_count
+    local_rows = nx // slab_count
     cosine_s, sine_s = wave_tables(slab_count, slab_count, slab_count)
     cosine_r, sine_r = wave_tables(local_rows, local_rows, local_rows)
-    twist_cos, twist_sin = wave_tables(slab_count, local_rows, NX)
+    twist_cos, twist_sin = wave_tables(slab_count, local_rows, nx)
     twist_cos = twist_cos[:, :, None]
     twist_sin = twist_sin[:, :, None]
     section_one = transform_axis(
@@ -141,7 +696,7 @@
     )
     section_one = twiddle(section_one, twist_cos, twist_sin, 1.0)
     section_two = transform_axis("jr,krc->jkc", cosine_r, sine_r, section_one, 1.0)
-    weighted = section_two.reshape(NX, 2 * col_width) * kernel_both
+    weighted = section_two.reshape(nx, 2 * col_width) * kernel_both
     section_one = transform_axis(
         "rj,jkc->krc",
         cosine_r,
@@ -151,7 +706,7 @@
     )
     section_one = twiddle(section_one, twist_cos, twist_sin, -1.0)
     section_two = transform_axis("sk,krc->src", cosine_s, sine_s, section_one, -1.0)
-    returned_x = section_two.reshape(NX, 2 * col_width)
+    returned_x = section_two.reshape(nx, 2 * col_width)
     returned = lax.all_to_all(
         returned_x.reshape(columns.shape), "slab", split_axis=0, concat_axis=3, tiled=True
     )

time: 892 us -> 216 us (0.24)
  local copies, waits for them, and re-layouts: 650 us -> 4.91 us
  Pallas kernels: 0 us -> 82.9 us
  other arithmetic: 75.7 us -> 3.77 us
  matrix products: 66.3 us -> 0 us
  waiting for transfers between devices: 28.8 us -> 87.7 us
  blocking collectives: 30.8 us -> 0 us
    gather x4 -> x0, local copies, waits for them, and re-layouts: 176 us -> none  [the longest x1 164 us: per_device(): jnp.take(flat_ext, near_ids.reshape(-1), axis=1)]
    reshape x6 -> x0, local copies, waits for them, and re-layouts: 151 us -> none  [the longest x1 71.4 us: per_device(): grid_potential.reshape(cell_planes, TX, NZC, TZ, rows_cell, TY)]
    transpose x3 -> x0, local copies, waits for them, and re-layouts: 123 us -> none  [the longest x1 62.2 us: per_device(): tile_potential = grid_potential.reshape(cell_planes, TX, NZC, TZ, rows_ce...]
    unnamed x33 -> x14, local copies, waits for them, and re-layouts: 91.5 us -> 2.03 us
    pallas_call x0 -> x10, Pallas kernels: none -> 82.9 us  [the longest x2 23.3 us: backward(): pl.pallas_call(functools.partial(backward_kernel, plan), grid=(1,), in_sp...]
    dot_general x14 -> x0, matrix products: 66.3 us -> none  [the longest x2 19.3 us: transform_rows(): jnp.dot(flat_rows, cosine, precision=lax.Precision.HIGHEST)]
    another operation x5 -> x0, local copies, waits for them, and re-layouts: 44.2 us -> none  [the longest x2 19.4 us: transform_rows(): return jnp.stack([real_part, imag_part], axis=1)]
    all_to_all x5 -> x0, local copies, waits for them, and re-layouts: 40.8 us -> none  [the longest x2 15.5 us: per_device(): lax.all_to_all(pencils, 'slab', split_axis=3, concat_axis=0, tiled=True)]
  transfers between devices with their start and end apart: 7 -> 10, of which waited for: 3 -> 7; matrix products, arithmetic and copies ran while one was open for 38% -> 1% of each run, Pallas kernels for 0% -> 24%
where the time goes in v2:
time: 216 us; the launch traced here: 214 us
  waiting for transfers between devices  87.7 us (41%)
  Pallas kernels  82.9 us (38%)
  starting transfers between devices  34.6 us (16%)
  local copies, waits for them, and re-layouts  4.91 us (2%)
  other arithmetic  3.77 us (2%)
    all_to_all x4, waiting for transfers between devices, per_device(): lax.all_to_all(pieces, axes, split_axis=0, concat_axis=0, tiled=True)  34.1 us
    ppermute x1, waiting for transfers between devices, spectrum_weights(): far = lax.ppermute(by_depth[0, :1], 'slab', [(plan.slabs // 2, 0)]) * scale  24.2 us
    pallas_call x2, Pallas kernels, backward(): pl.pallas_call(functools.partial(backward_kernel, plan), grid=(1,), in_sp...  23.3 us
    all_to_all x4, starting transfers between devices, per_device(): lax.all_to_all(pieces, axes, split_axis=0, concat_axis=0, tiled=True)  16.6 us
    all_to_all x1, waiting for transfers between devices, spectrum_weights(): lax.all_to_all(own, 'slab', split_axis=0, concat_axis=0, tiled=True)  16.2 us
    pallas_call x1, Pallas kernels, near_field(): pl.pallas_call(functools.partial(near_kernel, plan), grid=(plan.cell_cols...  15.5 us
    pallas_call x2, Pallas kernels, project(): pl.pallas_call(functools.partial(project_kernel, plan), grid=(plan.steps,...  13.5 us
    pallas_call x2, Pallas kernels, gather(): pl.pallas_call(functools.partial(gather_kernel, plan, chunk == CHUNKS - 1...  12.9 us
  transfers between devices with their start and end apart: 10, of which 7 were waited for; matrix products, arithmetic and copies ran while one was open for 1% of the time, Pallas kernels for 24%

profile of v2, /device:TPU:0, one launch (start us, length us, event | category | flops | bytes accessed | tf_op | source)
XLA Modules:
  0.0 214.0 jit_solution(10222317985377784044)
XLA Ops:
  0.0 1.8 slice.51
  1.8 0.8 slice_bitcast_fusion
  2.7 1.2 fusion
  3.8 7.4 %all-to-all-start = ((f32[16,32,512]{2,1,0:T(8,128)}), f32[16,32,512]{2,1,0:T(8,128)S(1)}, u32[]{:S(2)}, u32[]{:S(2)}) async-start(f32[16,32,512]{2,1,0:T(8,128)} %fusion), calls=%async_computation | async-start | bytes 2097152 | tf_op jit(solution)/shard_map/all_to_all | solution.py:522
  11.2 6.8 %project_depth.2 = f32[32,2,4,8,128]{4,3,2,1,0:T(8,128)} custom-call(f32[8,8,1024]{2,1,0:T(8,128)} %charges.3, s32[8,1024]{1,0:T(8,128)} %counts.7, f32[8,64,8,1024]{3,2,1,0:T(8,128)} %projection.7, bf16[512,512]{1,0:T(8,128)(2,1)} %constant.26.clone.high, bf16[512,512]{1,0:T(8,128)(2,1)} %constant.17.clone.low), custom_call_target="tpu_custom_call" | custom-call | flops 4194304 | bytes 8388608 | tf_op jit(solution)/shard_map/project_depth/pallas_call | solution.py:171
  18.0 16.2 %all-to-all-done = f32[16,32,512]{2,1,0:T(8,128)S(1)} async-done(((f32[16,32,512]{2,1,0:T(8,128)}), f32[16,32,512]{2,1,0:T(8,128)S(1)}, u32[]{:S(2)}, u32[]{:S(2)}) %all-to-all-start) | async-done | bytes 1048608 | tf_op jit(solution)/shard_map/all_to_all | solution.py:522
  34.1 0.0 copy-start.3
  34.1 6.8 %all-to-all-start.1 = ((f32[32,2,4,8,128]{4,3,2,1,0:T(8,128)}), f32[32,2,4,8,128]{4,3,2,1,0:T(8,128)S(1)}, u32[]{:S(2)}, u32[]{:S(2)}) async-start(f32[32,2,4,8,128]{4,3,2,1,0:T(8,128)} %project_depth.2), calls=%async_computation.1 | async-start | bytes 2097152 | tf_op jit(solution)/shard_map/all_to_all | solution.py:558
  41.0 6.8 %project_depth.3 = f32[32,2,4,8,128]{4,3,2,1,0:T(8,128)} custom-call(f32[8,8,1024]{2,1,0:T(8,128)} %charges.3, s32[8,1024]{1,0:T(8,128)} %counts.7, f32[8,64,8,1024]{3,2,1,0:T(8,128)} %projection.7, bf16[512,512]{1,0:T(8,128)(2,1)} %constant.26.clone.high, bf16[512,512]{1,0:T(8,128)(2,1)} %constant.17.clone.low), custom_call_target="tpu_custom_call" | custom-call | flops 4194304 | bytes 8388608 | tf_op jit(solution)/shard_map/project_depth/pallas_call | solution.py:171
  47.7 19.5 %all-to-all-done.1.pieces = f32[32,2,4,8,128]{4,3,2,1,0:T(8,128)S(1)} async-done(((f32[32,2,4,8,128]{4,3,2,1,0:T(8,128)}), f32[32,2,4,8,128]{4,3,2,1,0:T(8,128)S(1)}, u32[]{:S(2)}, u32[]{:S(2)}) %all-to-all-start.1) | async-done | bytes 1048608 | tf_op jit(solution)/shard_map/all_to_all | solution.py:558
  67.2 0.0 copy-start.4
  67.2 3.6 %all-to-all-start.2 = ((f32[32,2,4,8,128]{4,3,2,1,0:T(8,128)}), f32[32,2,4,8,128]{4,3,2,1,0:T(8,128)S(1)}, u32[]{:S(2)}, u32[]{:S(2)}) async-start(f32[32,2,4,8,128]{4,3,2,1,0:T(8,128)} %project_depth.3), calls=%async_computation.2 | async-start | bytes 2097152 | tf_op jit(solution)/shard_map/all_to_all | solution.py:558
  70.8 0.7 slice_multiply_fusion
  71.6 1.3 collective-permute-start.4
  72.9 24.2 %collective-permute-done.4 = f32[1,512]{1,0:T(1,128)S(1)} collective-permute-done((f32[1,512]{1,0:T(1,128)S(1)}, f32[1,512]{1,0:T(1,128)S(1)}, u32[]{:S(2)}, u32[]{:S(2)}) %collective-permute-start.4) | collective-permute-done | bytes 2080 | tf_op jit(solution)/shard_map/ppermute | solution.py:524
  97.1 0.0 copy-done.3
  97.1 0.7 broadcast_select_fusion.1.edge
  97.8 0.0 copy-done.4
  97.8 5.3 %forward_second.2.refs_0_ = f32[512,512]{1,0:T(8,128)} custom-call(s32[1]{0:T(128)} %bitcast.5.me_ref, f32[32,2,4,8,128]{4,3,2,1,0:T(8,128)} %copy-done.4, bf16[1024,512]{1,0:T(8,128)(2,1)} %constant.18.clone.high, bf16[1024,512]{1,0:T(8,128)(2,1)} %constant.54.clone.low), custom_call_target="tpu_custom_call" | custom-call | flops 1610612736 | bytes 4194304 | tf_op jit(solution)/shard_map/forward_second/pallas_call | solution.py:235
  103.1 0.0 all-to-all-done.2.pieces
  103.1 0.0 copy-start.5
  103.1 1.0 copy-done.5
  104.1 5.3 %forward_second.3.refs_1_ = f32[512,512]{1,0:T(8,128)} custom-call(s32[1]{0:T(128)} %bitcast.5.me_ref, f32[32,2,4,8,128]{4,3,2,1,0:T(8,128)} %copy-done.5, bf16[1024,512]{1,0:T(8,128)(2,1)} %constant.18.clone.high, bf16[1024,512]{1,0:T(8,128)(2,1)} %constant.54.clone.low), custom_call_target="tpu_custom_call" | custom-call | flops 1610612736 | bytes 4194304 | tf_op jit(solution)/shard_map/forward_second/pallas_call | solution.py:235
  109.4 7.1 %forward_first.1 = (bf16[2,512,512]{2,1,0:T(8,128)(2,1)}, bf16[2,512,512]{2,1,0:T(8,128)(2,1)}) custom-call(f32[512,512]{1,0:T(8,128)} %bitcast.30, f32[4,1,512]{2,1,0:T(1,128)} %broadcast_select_fusion.1.edge, bf16[512,1024]{1,0:T(8,128)(2,1)} %constant.55.clone.high, bf16[512,1024]{1,0:T(8,128)(2,1)} %constant.56.clone.low, ...), custom_call_target="tpu_custom_call" | custom-call | flops 3221225472 | bytes 7340032 | tf_op jit(solution)/shard_map/forward_first/pallas_call | solution.py:277
  116.5 11.7 %backward_plane.2 = f32[32,2,4,8,128]{4,3,2,1,0:T(8,128)} custom-call(s32[1]{0:T(128)} %bitcast.5.me_ref, bf16[2,512,512]{2,1,0:T(8,128)(2,1)} %get-tuple-element.7.in_high, bf16[2,512,512]{2,1,0:T(8,128)(2,1)} %get-tuple-element.8.in_low, bf16[2,512,512]{2,1,0:T(8,128)(2,1)} %constant.57.clone.x_high, bf16[2,512,512]{2,1,0:T(8,128)(2,1)} %constant.58.clone.x_low, ...), custom_call_target="tpu_custom_call" | custom-call | flops 3221225472 | bytes 6291456 | tf_op jit(solution)/shard_map/backward_plane/pallas_call | solution.py:360
  128.2 2.6 %all-to-all-start.3 = ((f32[32,2,4,8,128]{4,3,2,1,0:T(8,128)}), f32[32,2,4,8,128]{4,3,2,1,0:T(8,128)S(1)}, u32[]{:S(2)}, u32[]{:S(2)}) async-start(f32[32,2,4,8,128]{4,3,2,1,0:T(8,128)} %backward_plane.2), calls=%async_computation.3 | async-start | bytes 2097152 | tf_op jit(solution)/shard_map/all_to_all | solution.py:566
  130.8 0.0 copy-start.2
  130.8 0.0 copy-start.6
  130.8 11.6 %backward_plane.3 = f32[32,2,4,8,128]{4,3,2,1,0:T(8,128)} custom-call(s32[1]{0:T(128)} %bitcast.5.me_ref, bf16[2,512,512]{2,1,0:T(8,128)(2,1)} %get-tuple-element.7.in_high, bf16[2,512,512]{2,1,0:T(8,128)(2,1)} %get-tuple-element.8.in_low, bf16[2,512,512]{2,1,0:T(8,128)(2,1)} %constant.57.clone.x_high, bf16[2,512,512]{2,1,0:T(8,128)(2,1)} %constant.58.clone.x_low, ...), custom_call_target="tpu_custom_call" | custom-call | flops 3221225472 | bytes 6291456 | tf_op jit(solution)/shard_map/backward_plane/pallas_call | solution.py:360
  142.4 14.6 %all-to-all-done.3.pieces = f32[32,2,4,8,128]{4,3,2,1,0:T(8,128)S(1)} async-done(((f32[32,2,4,8,128]{4,3,2,1,0:T(8,128)}), f32[32,2,4,8,128]{4,3,2,1,0:T(8,128)S(1)}, u32[]{:S(2)}, u32[]{:S(2)}) %all-to-all-start.3) | async-done | bytes 1048608 | tf_op jit(solution)/shard_map/all_to_all | solution.py:566
  157.0 0.0 copy-start
  157.0 3.5 %all-to-all-start.4 = ((f32[32,2,4,8,128]{4,3,2,1,0:T(8,128)}), f32[32,2,4,8,128]{4,3,2,1,0:T(8,128)S(1)}, u32[]{:S(2)}, u32[]{:S(2)}) async-start(f32[32,2,4,8,128]{4,3,2,1,0:T(8,128)} %backward_plane.3), calls=%async_computation.4 | async-start | bytes 2097152 | tf_op jit(solution)/shard_map/all_to_all | solution.py:566
  160.6 0.0 copy-done.2
  160.6 0.0 copy-done.6
  160.6 0.1 fusion.5
  160.7 1.8 collective-permute-start
  162.5 0.3 collective-permute-start.1
  162.8 6.3 %collective-permute-done = f32[8,8,16]{2,1,0:T(8,128)S(1)} collective-permute-done((f32[8,8,16]{2,1,0:T(8,128)S(1)}, f32[8,8,16]{2,1,0:T(8,128)S(1)}, u32[]{:S(2)}, u32[]{:S(2)}) %collective-permute-start) | collective-permute-done | bytes 4128 | tf_op jit(solution)/shard_map/ppermute | solution.py:501
  169.1 0.5 collective-permute-done.1
  169.5 0.1 concatenate.10
  169.6 0.1 fusion.4
  169.7 0.1 collective-permute-start.2
  169.8 7.2 %collective-permute-start.3 = (f32[8,1,1280]{2,1,0:T(1,128)S(1)}, f32[8,1,1280]{2,1,0:T(1,128)S(1)}, u32[]{:S(2)}, u32[]{:S(2)}) collective-permute-start(f32[8,1,1280]{2,1,0:T(1,128)S(1)} %get-tuple-element.14), channel_id=1, source_target_pairs={{2,0},{4,2},{6,4},{8,6},{10,8},{12,10},{14,12},{16,14},{18,16},{20... | collective-permute-start | bytes 122888 | tf_op jit(solution)/shard_map/ppermute | solution.py:507
  177.0 6.5 %collective-permute-done.2 = f32[8,1,1280]{2,1,0:T(1,128)S(1)} collective-permute-done((f32[8,1,1280]{2,1,0:T(1,128)S(1)}, f32[8,1,1280]{2,1,0:T(1,128)S(1)}, u32[]{:S(2)}, u32[]{:S(2)}) %collective-permute-start.2) | collective-permute-done | bytes 40992 | tf_op jit(solution)/shard_map/ppermute | solution.py:506
  183.5 0.0 collective-permute-done.3
  183.5 0.1 fusion.2
  183.6 1.0 pad_maximum_fusion.extended
  184.6 15.5 %near_blocks.1.before = f32[8,8,1024]{2,1,0:T(8,128)} custom-call(f32[8,3,8,1280]{3,2,1,0:T(8,128)} %pad_maximum_fusion.extended, s32[6,8,1024]{2,1,0:T(8,128)} %codes.1, f32[6,8,8,8,1024]{4,3,2,1,0:T(8,128)} %blocks_ref.1), custom_call_target="tpu_custom_call" | custom-call | flops 6291456 | bytes 12582912 | tf_op jit(solution)/shard_map/near_blocks/pallas_call | solution.py:473
  200.1 0.0 copy-done
  200.1 6.5 %depth_gather.2.before = f32[8,8,1024]{2,1,0:T(8,128)} custom-call(s32[8,1024]{1,0:T(8,128)} %counts.7, f32[8,8,1024]{2,1,0:T(8,128)} %near_blocks.1.before, f32[8,64,8,1024]{3,2,1,0:T(8,128)} %projection.7, bf16[512,512]{1,0:T(8,128)(2,1)} %constant.61.clone.high, bf16[512,512]{1,0:T(8,128)(2,1)} %constant.62.clone.low, f32[32,2,4,8,128]{4,3,2,1,0:T(8,128)} %copy-done), custom_call_target="tpu_custom_call" | custom-call | flops 4194304 | bytes 8388608 | tf_op jit(solution)/shard_map/depth_gather/pallas_call | solution.py:405
  206.6 0.0 all-to-all-done.4.pieces
  206.6 0.0 copy-start.1
  206.6 1.0 copy-done.1
  207.6 6.4 %depth_gather.3 = f32[8,8,1024]{2,1,0:T(8,128)} custom-call(s32[8,1024]{1,0:T(8,128)} %counts.7, f32[8,8,1024]{2,1,0:T(8,128)} %depth_gather.2.before, f32[8,64,8,1024]{3,2,1,0:T(8,128)} %projection.7, bf16[512,512]{1,0:T(8,128)(2,1)} %constant.61.clone.high, bf16[512,512]{1,0:T(8,128)(2,1)} %constant.62.clone.low, f32[32,2,4,8,128]{4,3,2,1,0:T(8,128)} %copy-done.1), custom_call_target="tpu_custom_call" | custom-call | flops 4194304 | bytes 8388608 | tf_op jit(solution)/shard_map/depth_gather/pallas_call | solution.py:405
  (5 shorter events, 0.0 us)
Async XLA Ops:
  3.8 30.3 %all-to-all-start = ((f32[16,32,512]{2,1,0:T(8,128)}), f32[16,32,512]{2,1,0:T(8,128)S(1)}, u32[]{:S(2)}, u32[]{:S(2)}) async-start(f32[16,32,512]{2,1,0:T(8,128)} %fusion), calls=%async_computation | async-start | bytes 2097152 | tf_op jit(solution)/shard_map/all_to_all | solution.py:522
  34.1 62.9 %copy-start.3 = (f32[16,32,512]{2,1,0:T(8,128)}, f32[16,32,512]{2,1,0:T(8,128)S(1)}, u32[]{:S(2)}) copy-start(f32[16,32,512]{2,1,0:T(8,128)S(1)} %all-to-all-done) | copy-start | bytes 3145732
  34.1 33.0 %all-to-all-start.1 = ((f32[32,2,4,8,128]{4,3,2,1,0:T(8,128)}), f32[32,2,4,8,128]{4,3,2,1,0:T(8,128)S(1)}, u32[]{:S(2)}, u32[]{:S(2)}) async-start(f32[32,2,4,8,128]{4,3,2,1,0:T(8,128)} %project_depth.2), calls=%async_computation.1 | async-start | bytes 2097152 | tf_op jit(solution)/shard_map/all_to_all | solution.py:558
  67.2 30.6 %copy-start.4 = (f32[32,2,4,8,128]{4,3,2,1,0:T(8,128)}, f32[32,2,4,8,128]{4,3,2,1,0:T(8,128)S(1)}, u32[]{:S(2)}) copy-start(f32[32,2,4,8,128]{4,3,2,1,0:T(8,128)S(1)} %all-to-all-done.1.pieces) | copy-start | bytes 3145732
  67.2 35.9 %all-to-all-start.2 = ((f32[32,2,4,8,128]{4,3,2,1,0:T(8,128)}), f32[32,2,4,8,128]{4,3,2,1,0:T(8,128)S(1)}, u32[]{:S(2)}, u32[]{:S(2)}) async-start(f32[32,2,4,8,128]{4,3,2,1,0:T(8,128)} %project_depth.3), calls=%async_computation.2 | async-start | bytes 2097152 | tf_op jit(solution)/shard_map/all_to_all | solution.py:558
  71.6 25.5 %collective-permute-start.4 = (f32[1,512]{1,0:T(1,128)S(1)}, f32[1,512]{1,0:T(1,128)S(1)}, u32[]{:S(2)}, u32[]{:S(2)}) collective-permute-start(f32[1,512]{1,0:T(1,128)S(1)} %get-tuple-element.10), channel_id=1, source_target_pairs={{16,0},{17,1}} | collective-permute-start | bytes 6152 | tf_op jit(solution)/shard_map/ppermute | solution.py:524
  103.1 1.0 copy-start.5
  128.2 28.9 %all-to-all-start.3 = ((f32[32,2,4,8,128]{4,3,2,1,0:T(8,128)}), f32[32,2,4,8,128]{4,3,2,1,0:T(8,128)S(1)}, u32[]{:S(2)}, u32[]{:S(2)}) async-start(f32[32,2,4,8,128]{4,3,2,1,0:T(8,128)} %backward_plane.2), calls=%async_computation.3 | async-start | bytes 2097152 | tf_op jit(solution)/shard_map/all_to_all | solution.py:566
  130.8 29.8 %copy-start.2 = (f32[8,8,1024]{2,1,0:T(8,128)S(1)}, f32[8,8,1024]{2,1,0:T(8,128)}, u32[]{:S(2)}) copy-start(f32[8,8,1024]{2,1,0:T(8,128)} %charges.3) | copy-start | bytes 786436
  130.8 29.8 %copy-start.6 = (s32[8,1024]{1,0:T(8,128)S(1)}, s32[8,1024]{1,0:T(8,128)}, u32[]{:S(2)}) copy-start(s32[8,1024]{1,0:T(8,128)} %counts.7) | copy-start | bytes 98308
  157.0 43.1 %copy-start = (f32[32,2,4,8,128]{4,3,2,1,0:T(8,128)}, f32[32,2,4,8,128]{4,3,2,1,0:T(8,128)S(1)}, u32[]{:S(2)}) copy-start(f32[32,2,4,8,128]{4,3,2,1,0:T(8,128)S(1)} %all-to-all-done.3.pieces) | copy-start | bytes 3145732
  157.0 49.5 %all-to-all-start.4 = ((f32[32,2,4,8,128]{4,3,2,1,0:T(8,128)}), f32[32,2,4,8,128]{4,3,2,1,0:T(8,128)S(1)}, u32[]{:S(2)}, u32[]{:S(2)}) async-start(f32[32,2,4,8,128]{4,3,2,1,0:T(8,128)} %backward_plane.3), calls=%async_computation.4 | async-start | bytes 2097152 | tf_op jit(solution)/shard_map/all_to_all | solution.py:566
  160.7 8.3 %collective-permute-start = (f32[8,8,16]{2,1,0:T(8,128)S(1)}, f32[8,8,16]{2,1,0:T(8,128)S(1)}, u32[]{:S(2)}, u32[]{:S(2)}) collective-permute-start(f32[8,8,16]{2,1,0:T(8,128)S(1)} %get-tuple-element.16), channel_id=1, source_target_pairs={{0,1},{1,0},{2,3},{3,2},{4,5},{5,4},{6,7},{7,6},{8,9},{9,8},{10,11... | collective-permute-start | bytes 12296 | tf_op jit(solution)/shard_map/ppermute | solution.py:501
  162.5 7.0 %collective-permute-start.1 = (f32[8,8,16]{2,1,0:T(8,128)S(1)}, f32[8,8,16]{2,1,0:T(8,128)S(1)}, u32[]{:S(2)}, u32[]{:S(2)}) collective-permute-start(f32[8,8,16]{2,1,0:T(8,128)S(1)} %get-tuple-element.15), channel_id=1, source_target_pairs={{1,0},{0,1},{3,2},{2,3},{5,4},{4,5},{7,6},{6,7},{9,8},{8,9},{11,10... | collective-permute-start | bytes 12296 | tf_op jit(solution)/shard_map/ppermute | solution.py:502
  169.7 13.8 %collective-permute-start.2 = (f32[8,1,1280]{2,1,0:T(1,128)S(1)}, f32[8,1,1280]{2,1,0:T(1,128)S(1)}, u32[]{:S(2)}, u32[]{:S(2)}) collective-permute-start(f32[8,1,1280]{2,1,0:T(1,128)S(1)} %get-tuple-element.13), channel_id=1, source_target_pairs={{0,2},{2,4},{4,6},{6,8},{8,10},{10,12},{12,14},{14,16},{16,18},{18... | collective-permute-start | bytes 122888 | tf_op jit(solution)/shard_map/ppermute | solution.py:506
  169.8 13.7 %collective-permute-start.3 = (f32[8,1,1280]{2,1,0:T(1,128)S(1)}, f32[8,1,1280]{2,1,0:T(1,128)S(1)}, u32[]{:S(2)}, u32[]{:S(2)}) collective-permute-start(f32[8,1,1280]{2,1,0:T(1,128)S(1)} %get-tuple-element.14), channel_id=1, source_target_pairs={{2,0},{4,2},{6,4},{8,6},{10,8},{12,10},{14,12},{16,14},{18,16},{20... | collective-permute-start | bytes 122888 | tf_op jit(solution)/shard_map/ppermute | solution.py:507
  206.6 1.0 copy-start.1

commit v3 on v2

--- a/solution.py
+++ b/solution.py
@@ -16,7 +16,7 @@
 NZC = 16
 LANES = 128
 CHUNKS = 2
-VMEM_LIMIT = 56 * 1024 * 1024
+VMEM_LIMIT = 40 * 1024 * 1024
 
 
 def halves(table):
@@ -59,15 +59,16 @@
 
     def depth_tables(self):
         depth = np.arange(NZC)[None, :] * TZ + np.arange(TZ)[:, None]
+        scale = 1.0 / (self.nx * self.ny * self.nz)
         forward = np.zeros((self.slots, 2, self.row_block, TZ, self.row_block, NZC))
         backward = np.zeros_like(forward)
         for freq in range(self.slots):
             angle = (freq * depth % self.nz) * (2.0 * math.pi / self.nz)
             real, imag = (np.cos(angle), -np.sin(angle))
-            factor = 2.0
+            factor = 2.0 * scale
             if freq == 0:
                 imag = np.cos(depth * math.pi)
-                factor = 1.0
+                factor = scale
             for row in range(self.row_block):
                 forward[freq, 0, row, :, row, :] = real
                 forward[freq, 1, row, :, row, :] = imag
@@ -76,19 +77,24 @@
         shape = (self.slots * 2 * self.row_block, TZ * LANES)
         return (forward.reshape(shape), backward.reshape(shape))
 
-    def y_order(self):
-        rows = np.arange(self.ny // TY).reshape(-1, self.row_block)
-        return (rows[:, None, :] * TY + np.arange(TY)[None, :, None]).reshape(-1)
-
-    def x_order(self):
-        chunk, slab, tile, plane = np.meshgrid(
-            np.arange(CHUNKS),
-            np.arange(self.slabs),
-            np.arange(self.tx_chunk),
-            np.arange(self.cell_planes),
+    def y_rows(self):
+        parity, cell, step, block, tile, row = np.meshgrid(
+            *[np.arange(n) for n in (2, self.cells, self.steps, self.step_blocks, TY // 2, self.row_block)],
             indexing="ij",
         )
-        return ((slab * self.cell_planes + plane) * TX + chunk * self.tx_chunk + tile).reshape(-1)
+        cell_row = ((cell * self.steps + step) * self.step_blocks + block) * self.row_block + row
+        return (cell_row * TY + 2 * tile + parity).reshape(2, -1)
+
+    def x_columns(self):
+        parity, slab, tile, plane = np.meshgrid(
+            *[np.arange(n) for n in (2, self.slabs, TX // 2, self.cell_planes)], indexing="ij"
+        )
+        return ((slab * self.cell_planes + plane) * TX + 2 * tile + parity).reshape(2, -1)
+
+    def row_of(self, cell, step, place):
+        block, tile = (place // TY, place % TY)
+        inner = (cell * self.steps + step) * self.step_blocks + block
+        return (tile % 2) * (self.ny // 2) + (inner * (TY // 2) + tile // 2) * self.row_block
 
 
 def split(value):
@@ -98,10 +104,9 @@
 
 
 def product(left, right, dims=((1,), (0,))):
-    def dot(a, b):
-        return lax.dot_general(a, b, (dims, ((), ())), preferred_element_type=jnp.float32)
-
-    return dot(left[0], right[0]) + (dot(left[0], right[1]) + dot(left[1], right[0]))
+    first = jnp.concatenate([left[0], left[0], left[1]], axis=dims[0][0])
+    second = jnp.concatenate([right[0], right[1], right[0]], axis=dims[1][0])
+    return lax.dot_general(first, second, (dims, ((), ())), preferred_element_type=jnp.float32)
 
 
 def swap_groups(parts, width):
@@ -124,6 +129,7 @@
 
 def project_kernel(plan, charges, counts, projection, high, low, out, scratch):
     planes = plan.cell_planes
+    first = pl.program_id(0) * LANES
     slot = lax.broadcasted_iota(jnp.int32, charges.shape, 0)
     masked = jnp.where(slot < counts[...][None], charges[...], 0.0)
     for block in range(plan.step_blocks):
@@ -131,20 +137,26 @@
         own = masked[:, :, block * LANES : (block + 1) * LANES]
         for tx in range(plan.tx_chunk):
             for ty in range(TY):
+                row = ((block * TY + ty) * plan.tx_chunk + tx) * planes
+                rows = pl.ds(pl.multiple_of(first + row, planes), planes)
                 for tz in range(TZ):
-                    t = (tx * TY + ty) * TZ + tz
-                    total = projection[0, t, :, lanes] * own[0]
+                    t = ty * TZ + tz
+                    total = projection[0, tx, 0, t, :, lanes] * own[0]
                     for p in range(1, plan.panels):
-                        total = total + projection[p, t, :, lanes] * own[p]
-                    row = ((block * TY + ty) * plan.tx_chunk + tx) * planes
-                    scratch[row : row + planes, tz * LANES : (tz + 1) * LANES] = total
-    spectra = product((high[...], low[...]), split(scratch[...]), ((1,), (1,)))
-    out[:, :, 0] = spectra.reshape(plan.slots, 2, plan.row_block, LANES)
+                        total = total + projection[p, tx, 0, t, :, lanes] * own[p]
+                    scratch[rows, tz * LANES : (tz + 1) * LANES] = total
+
+    @pl.when(pl.program_id(0) == plan.steps - 1)
+    def _():
+        spectra = product((high[...], low[...]), split(scratch[...]), ((1,), (1,)))
+        shape = (plan.slots, 2, plan.row_block, LANES)
+        for step in range(plan.steps):
+            out[:, :, step] = spectra[:, step * LANES : (step + 1) * LANES].reshape(shape)
 
 
 def projection_spec(plan, chunk):
-    shape = (plan.panels, TX * TY * TZ // CHUNKS, plan.cell_planes, plan.step_blocks * LANES)
-    return pl.BlockSpec(shape, lambda i: (0, chunk, 0, i))
+    shape = (plan.panels, TX // CHUNKS, 1, TY * TZ, plan.cell_planes, plan.step_blocks * LANES)
+    return pl.BlockSpec(shape, lambda i: (0, 0, chunk, 0, 0, i))
 
 
 def panel_spec(plan):
@@ -159,12 +171,16 @@
     return (plan.slots, 2, plan.steps, plan.row_block, LANES)
 
 
-def piece_spec(plan):
-    return pl.BlockSpec((plan.slots, 2, 1, plan.row_block, LANES), lambda i: (0, 0, i, 0, 0))
-
-
-def whole_spec(array):
-    return pl.BlockSpec(array.shape, lambda i: (0,) * array.ndim)
+def whole_spec(shape):
+    return pl.BlockSpec(shape, lambda i: (0,) * len(shape))
+
+
+def projection_cost(projection):
+    return pl.CostEstimate(
+        flops=2 * projection.size // CHUNKS,
+        bytes_accessed=4 * projection.size // CHUNKS,
+        transcendentals=0,
+    )
 
 
 def project(plan, chunk, charges, counts, projection, high, low):
@@ -175,228 +191,207 @@
             panel_spec(plan),
             count_spec(plan),
             projection_spec(plan, chunk),
-            whole_spec(high),
-            whole_spec(low),
+            whole_spec(high.shape),
+            whole_spec(low.shape),
         ],
-        out_specs=piece_spec(plan),
+        out_specs=whole_spec(piece_shape(plan)),
         out_shape=jax.ShapeDtypeStruct(piece_shape(plan), jnp.float32),
-        scratch_shapes=[pltpu.VMEM((LANES, TZ * LANES), jnp.float32)],
+        scratch_shapes=[pltpu.VMEM((plan.steps * LANES, TZ * LANES), jnp.float32)],
         compiler_params=pltpu.CompilerParams(vmem_limit_bytes=VMEM_LIMIT),
-        cost_estimate=pl.CostEstimate(
-            flops=2 * projection.size // CHUNKS,
-            bytes_accessed=4 * projection.size // CHUNKS,
-            transcendentals=0,
-        ),
+        cost_estimate=projection_cost(projection),
         name="project_depth",
     )(charges, counts, projection, high, low)
 
 
-def forward_y_kernel(plan, me_ref, pieces, high, low, out, scratch):
+def forward_plane(plan, special, pieces, y_table, x_table, rows_ref, freq_ref):
     rows = 2 * plan.steps * plan.row_block
     width = plan.x_chunk
+    middle = plan.ny // 2
     for cell in range(plan.cells):
         for group in range(plan.slabs // plan.y_lanes):
-            parts = [
-                pieces[(group * plan.y_lanes + i) * plan.cells + cell].reshape(rows, LANES)
-                for i in range(plan.y_lanes)
-            ]
+            first = cell * plan.slabs + group * plan.y_lanes
+            parts = [pieces[first + i].reshape(rows, LANES) for i in range(plan.y_lanes)]
             parts = swap_groups(parts, plan.width)
             for place, value in enumerate(parts):
                 for part in range(2):
                     for step in range(plan.steps):
                         source = (part * plan.steps + step) * plan.row_block
-                        row = ((cell * plan.steps + step) * plan.y_lanes + place) * plan.row_block
+                        row = plan.row_of(cell, step, place)
                         col = part * width + group * LANES
-                        scratch[row : row + plan.row_block, col : col + LANES] = value[
+                        rows_ref[row : row + plan.row_block, col : col + LANES] = value[
                             source : source + plan.row_block
                         ]
-    sums = product((high[...], low[...]), split(scratch[...]))
-    cosine, sine = (sums[: plan.ny], sums[plan.ny :])
-    special = me_ref[0] == 0
+    high, low = y_table
+    even = product((high[0], low[0]), split(rows_ref[:middle]))
+    odd = product((high[1], low[1]), split(rows_ref[middle:]))
+    for upper, sums in ((0, even + odd), (1, even - odd)):
+        cosine, sine = (sums[:middle], sums[middle:])
+        start = upper * middle
+        freq_ref[start : start + middle] = cosine[:, :width] + sine[:, width:]
+        start += plan.ny
+        freq_ref[start : start + middle] = cosine[:, width:] - sine[:, :width]
+
+    @pl.when(special)
+    def _():
+        row = lax.broadcasted_iota(jnp.int32, (middle, width), 0)
+        below, above = (even + odd, even - odd)
+        for upper, sums, other in ((0, below, above), (1, above, below)):
+            cols = slice(upper * width, (upper + 1) * width)
+            start = upper * middle
+            freq_ref[start : start + middle] = sums[:middle, cols]
+            start += plan.ny
+            freq_ref[start : start + middle] = jnp.where(row == 0, other[0:1, cols], -sums[middle:, cols])
+
+    high, low = x_table
+    return product(split(freq_ref[...]), (high[0], low[0]))
+
+
+def backward_plane(plan, special, freqs, x_table, y_table, out, rows_ref):
+    width = plan.x_chunk
+    middle = plan.ny // 2
+    high, low = x_table
+    sums = product(split(freqs), (high[0], low[0]))
+    real = sums[: plan.ny, :width] - sums[plan.ny :, width:]
+    imag = sums[plan.ny :, :width] + sums[: plan.ny, width:]
+    high, low = y_table
 
     @pl.when(jnp.logical_not(special))
     def _():
-        out[:, :width] = cosine[:, :width] + sine[:, width:]
-        out[:, width:] = cosine[:, width:] - sine[:, :width]
+        for parity in range(2):
+            joined = []
+            for value in (real, imag):
+                below, above = (value[:middle], value[middle:])
+                joined.append(below + above if parity == 0 else below - above)
+            pair = split(jnp.concatenate(joined, axis=1))
+            rows = product((high[parity], low[parity]), pair)
+            cosine, sine = (rows[:middle], rows[middle:])
+            start = parity * middle
+            rows_ref[start : start + middle, :width] = cosine[:, :width] - sine[:, width:]
+            rows_ref[start : start + middle, width:] = cosine[:, width:] + sine[:, :width]
 
     @pl.when(special)
     def _():
-        middle = plan.ny // 2
         row = lax.broadcasted_iota(jnp.int32, (middle, width), 0)
-        for part in range(2):
-            rows = slice(part * middle, (part + 1) * middle)
-            cols = slice(part * width, (part + 1) * width)
-            other = (1 - part) * middle
-            out[rows, :width] = cosine[rows, cols]
-            out[rows, width:] = jnp.where(row == 0, cosine[other : other + 1, cols], -sine[rows, cols])
-
-
-def forward_y(plan, me, pieces, high, low):
-    return pl.pallas_call(
-        functools.partial(forward_y_kernel, plan),
-        grid=(1,),
-        in_specs=[
-            pl.BlockSpec(memory_space=pltpu.SMEM),
-            whole_spec(pieces),
-            whole_spec(high),
-            whole_spec(low),
-        ],
-        out_specs=pl.BlockSpec((plan.ny, 2 * plan.x_chunk), lambda i: (0, 0)),
-        out_shape=jax.ShapeDtypeStruct((plan.ny, 2 * plan.x_chunk), jnp.float32),
-        scratch_shapes=[pltpu.VMEM((plan.ny, 2 * plan.x_chunk), jnp.float32)],
-        compiler_params=pltpu.CompilerParams(vmem_limit_bytes=VMEM_LIMIT),
-        cost_estimate=pl.CostEstimate(
-            flops=12 * plan.ny * plan.ny * 2 * plan.x_chunk,
-            bytes_accessed=8 * pieces.size + 4 * high.size,
-            transcendentals=0,
-        ),
-        name="forward_second",
-    )(me, pieces, high, low)
-
-
-def forward_x_kernel(plan, weights, edge, high, low, *refs):
-    rows_in, (out_high, out_low) = (refs[:CHUNKS], refs[CHUNKS:])
-    width = plan.x_chunk
-    rows = weights.shape[0]
-    real = jnp.concatenate([value[:, :width] for value in rows_in], axis=1)
-    imag = jnp.concatenate([value[:, width:] for value in rows_in], axis=1)
-    sums = product(split(jnp.concatenate([real, imag], axis=0)), (high[...], low[...]))
-    weight = weights[...]
-    row = lax.broadcasted_iota(jnp.int32, weight.shape, 0)
-    second = jnp.where(row == 0, edge[0], weight)
-    new_real = weight * sums[:rows, : plan.nx] + second * sums[rows:, plan.nx :]
-    new_imag = second * sums[rows:, : plan.nx] - weight * sums[:rows, plan.nx :]
-    out_high[0], out_low[0] = split(new_real)
-    out_high[1], out_low[1] = split(new_imag)
-
-
-def forward_x(plan, weights, edge, high, low, pencils):
-    rows = plan.ny // edge.shape[0]
-    out = jax.ShapeDtypeStruct((2, plan.ny, plan.nx), jnp.bfloat16)
-    out_spec = pl.BlockSpec((2, rows, plan.nx), lambda i: (0, i, 0))
-    return pl.pallas_call(
-        functools.partial(forward_x_kernel, plan),
-        grid=(edge.shape[0],),
-        in_specs=[
-            pl.BlockSpec((rows, plan.nx), lambda i: (i, 0)),
-            pl.BlockSpec((1, 1, plan.nx), lambda i: (i, 0, 0)),
-            whole_spec(high),
-            whole_spec(low),
-        ]
-        + [pl.BlockSpec((rows, 2 * plan.x_chunk), lambda i: (i, 0))] * CHUNKS,
-        out_specs=[out_spec, out_spec],
-        out_shape=[out, out],
-        compiler_params=pltpu.CompilerParams(vmem_limit_bytes=VMEM_LIMIT),
-        cost_estimate=pl.CostEstimate(
-            flops=24 * plan.nx * plan.nx * plan.ny,
-            bytes_accessed=20 * plan.nx * plan.ny + 4 * high.size,
-            transcendentals=0,
-        ),
-        name="forward_first",
-    )(weights, edge, high, low, *pencils)
-
-
-def backward_kernel(plan, me_ref, in_high, in_low, x_high, x_low, y_high, y_low, out, scratch):
-    width = plan.x_chunk
-    shape = (2 * plan.ny, plan.nx)
-    sums = product(
-        (in_high[...].reshape(shape), in_low[...].reshape(shape)), (x_high[0], x_low[0])
-    )
-    real = sums[: plan.ny, :width] - sums[plan.ny :, width:]
-    imag = sums[plan.ny :, :width] + sums[: plan.ny, width:]
-    scratch[:, :width] = real
-    scratch[:, width:] = imag
-    special = me_ref[0] == 0
-    middle = plan.ny // 2
-    ends = (scratch[0:1, width:], scratch[middle : middle + 1, width:])
-
-    @pl.when(special)
-    def _():
-        row = lax.broadcasted_iota(jnp.int32, scratch.shape, 0)
-        scratch[...] = jnp.where(row % middle == 0, scratch[...], 2.0 * scratch[...])
-
-    pair = split(scratch[...])
-    halves_sum = []
-    for part in range(2):
-        rows = slice(part * middle, (part + 1) * middle)
-        halves_sum.append(
-            product((y_high[:, rows], y_low[:, rows]), (pair[0][rows], pair[1][rows]))
-        )
-    first, second = halves_sum
-
-    @pl.when(jnp.logical_not(special))
-    def _():
-        both = first + second
-        scratch[:, :width] = both[: plan.ny, :width] - both[plan.ny :, width:]
-        scratch[:, width:] = both[: plan.ny, width:] + both[plan.ny :, :width]
-
-    @pl.when(special)
-    def _():
-        row = lax.broadcasted_iota(jnp.int32, (plan.ny, width), 0)
-        sign = jnp.where(row // plan.row_block % 2 == 0, 1.0, -1.0)
-        scratch[:, :width] = first[: plan.ny, :width] - first[plan.ny :, width:] + sign * ends[0]
-        scratch[:, width:] = second[: plan.ny, :width] - second[plan.ny :, width:] + ends[1]
+        columns, ends = ([], [])
+        for upper in range(2):
+            part = slice(upper * middle, (upper + 1) * middle)
+            stacked = [jnp.where(row == 0, value[part], 2.0 * value[part]) for value in (real, imag)]
+            columns.append(jnp.concatenate(stacked, axis=0))
+            ends.append(imag[upper * middle : upper * middle + 1])
+        pair = split(jnp.concatenate(columns, axis=1))
+        for parity in range(2):
+            table = tuple(
+                jnp.concatenate([t[parity, :middle], -t[parity, middle:]], axis=1) for t in (high, low)
+            )
+            rows = product(table, pair)
+            sign = 1.0 - 2.0 * parity
+            start = parity * middle
+            rows_ref[start : start + middle, :width] = rows[:, :width] + sign * ends[0]
+            rows_ref[start : start + middle, width:] = sign * rows[:, width:] + ends[1]
 
     for cell in range(plan.cells):
         for group in range(plan.slabs // plan.y_lanes):
             parts = []
             for place in range(plan.y_lanes):
-                pieces = []
+                tiles = []
                 for part in range(2):
                     for step in range(plan.steps):
-                        row = ((cell * plan.steps + step) * plan.y_lanes + place) * plan.row_block
+                        row = plan.row_of(cell, step, place)
                         col = part * width + group * LANES
-                        pieces.append(scratch[row : row + plan.row_block, col : col + LANES])
-                parts.append(jnp.concatenate(pieces, axis=0))
+                        tiles.append(rows_ref[row : row + plan.row_block, col : col + LANES])
+                parts.append(jnp.concatenate(tiles, axis=0))
             parts = swap_groups(parts, plan.width)
+            first = cell * plan.slabs + group * plan.y_lanes
             for i in range(plan.y_lanes):
-                out[(group * plan.y_lanes + i) * plan.cells + cell] = parts[i].reshape(
-                    2, plan.steps, plan.row_block, LANES
-                )
-
-
-def backward(plan, chunk, me, high, low, x_tables, y_tables):
-    x_spec = pl.BlockSpec((1, plan.nx, 2 * plan.x_chunk), lambda i: (chunk, 0, 0))
+                out[first + i] = parts[i].reshape(2, plan.steps, plan.row_block, LANES)
+
+
+def first_plane_kernel(plan, me_ref, pieces, y_high, y_low, x_high, x_low, out, rows_ref, freq_ref):
+    special = me_ref[0] == 0
+    out[...] = forward_plane(plan, special, pieces, (y_high, y_low), (x_high, x_low), rows_ref, freq_ref)
+
+
+def middle_plane_kernel(
+    plan, me_ref, pieces, even, weights, edge, yf_high, yf_low, xf_high, xf_low, xb_high, xb_low,
+    yb_high, yb_low, out, rest, rows_ref, freq_ref, sum_ref
+):
+    special = me_ref[0] == 0
+    width = plan.x_chunk
+    odd = forward_plane(plan, special, pieces, (yf_high, yf_low), (xf_high, xf_low), rows_ref, freq_ref)
+    row = lax.broadcasted_iota(jnp.int32, (plan.ny, width), 0)
+    results = []
+    for upper in range(2):
+        sums = even[...] - odd if upper else even[...] + odd
+        cols = slice(upper * width, (upper + 1) * width)
+        weight = weights[:, cols]
+        second = jnp.where(special & (row == 0), edge[0:1, cols], weight)
+        second = jnp.where(special & (row == plan.ny // 2), edge[1:2, cols], second)
+        real = weight * sums[: plan.ny, :width] + second * sums[plan.ny :, width:]
+        imag = second * sums[plan.ny :, :width] - weight * sums[: plan.ny, width:]
+        results.append((real, imag))
+    for part in range(2):
+        rows = slice(part * plan.ny, (part + 1) * plan.ny)
+        below, above = (results[0][part], results[1][part])
+        sum_ref[rows] = below + above
+        rest[rows] = below - above
+    backward_plane(plan, special, sum_ref[...], (xb_high, xb_low), (yb_high, yb_low), out, rows_ref)
+
+
+def last_plane_kernel(plan, me_ref, freqs, x_high, x_low, y_high, y_low, out, rows_ref):
+    special = me_ref[0] == 0
+    backward_plane(plan, special, freqs[...], (x_high, x_low), (y_high, y_low), out, rows_ref)
+
+
+def plane_call(plan, kernel, name, chunks, me, arrays, tables, out_shapes, scratch, work):
+    def table_spec(table, chunk):
+        if chunk is None:
+            return whole_spec(table.shape)
+        return pl.BlockSpec((1,) + table.shape[1:], lambda i: (chunk, 0, 0))
+
+    specs = [whole_spec(array.shape) for array in arrays]
+    flat = []
+    for pair, chunk in zip(tables, chunks):
+        for table in pair:
+            specs.append(table_spec(table, chunk))
+            flat.append(table)
+    size = sum(4 * array.size for array in arrays) + sum(2 * table.size for table in flat)
     return pl.pallas_call(
-        functools.partial(backward_kernel, plan),
+        functools.partial(kernel, plan),
         grid=(1,),
-        in_specs=[
-            pl.BlockSpec(memory_space=pltpu.SMEM),
-            whole_spec(high),
-            whole_spec(low),
-            x_spec,
-            x_spec,
-            whole_spec(y_tables[0]),
-            whole_spec(y_tables[1]),
-        ],
-        out_specs=pl.BlockSpec(piece_shape(plan), lambda i: (0, 0, 0, 0, 0)),
-        out_shape=jax.ShapeDtypeStruct(piece_shape(plan), jnp.float32),
-        scratch_shapes=[pltpu.VMEM((plan.ny, 2 * plan.x_chunk), jnp.float32)],
+        in_specs=[pl.BlockSpec(memory_space=pltpu.SMEM)] + specs,
+        out_specs=[whole_spec(shape) for shape in out_shapes],
+        out_shape=[jax.ShapeDtypeStruct(shape, jnp.float32) for shape in out_shapes],
+        scratch_shapes=[pltpu.VMEM(shape, jnp.float32) for shape in scratch],
         compiler_params=pltpu.CompilerParams(vmem_limit_bytes=VMEM_LIMIT),
         cost_estimate=pl.CostEstimate(
-            flops=24 * plan.nx * plan.ny * 2 * plan.x_chunk,
-            bytes_accessed=4 * high.size + 8 * plan.nx * plan.x_chunk * 2 + 4 * y_tables[0].size,
-            transcendentals=0,
+            flops=work * 12 * plan.nx * plan.ny * plan.x_chunk, bytes_accessed=size, transcendentals=0
         ),
-        name="backward_plane",
-    )(me, high, low, *x_tables, *y_tables)
+        name=name,
+    )(me, *arrays, *flat)
 
 
 def gather_kernel(plan, last, counts, before, projection, high, low, pieces, out, scratch):
     planes = plan.cell_planes
     rows = plan.slots * 2 * plan.row_block
-    scratch[...] = product(split(pieces[...].reshape(rows, LANES).T), (high[...], low[...]))
+    first = pl.program_id(0) * LANES
+
+    @pl.when(pl.program_id(0) == 0)
+    def _():
+        columns = [pieces[:, :, step].reshape(rows, LANES) for step in range(plan.steps)]
+        scratch[...] = product(split(jnp.concatenate(columns, axis=1).T), (high[...], low[...]))
+
     for block in range(plan.step_blocks):
         lanes = pl.ds(block * LANES, LANES)
         far = [before[p, :, lanes] for p in range(plan.panels)]
         for tx in range(plan.tx_chunk):
             for ty in range(TY):
                 row = ((block * TY + ty) * plan.tx_chunk + tx) * planes
+                rows_at = pl.ds(pl.multiple_of(first + row, planes), planes)
                 for tz in range(TZ):
-                    t = (tx * TY + ty) * TZ + tz
-                    potential = scratch[row : row + planes, tz * LANES : (tz + 1) * LANES]
+                    t = ty * TZ + tz
+                    potential = scratch[rows_at, tz * LANES : (tz + 1) * LANES]
                     for p in range(plan.panels):
-                        far[p] = far[p] + projection[p, t, :, lanes] * potential
+                        far[p] = far[p] + projection[p, tx, 0, t, :, lanes] * potential
         for p in range(plan.panels):
             out[p, :, lanes] = jnp.where(counts[:, lanes] > p, far[p], 0.0) if last else far[p]
 
@@ -409,19 +404,15 @@
             count_spec(plan),
             panel_spec(plan),
             projection_spec(plan, chunk),
-            whole_spec(high),
-            whole_spec(low),
-            piece_spec(plan),
+            whole_spec(high.shape),
+            whole_spec(low.shape),
+            whole_spec(pieces.shape),
         ],
         out_specs=panel_spec(plan),
         out_shape=jax.ShapeDtypeStruct(before.shape, jnp.float32),
-        scratch_shapes=[pltpu.VMEM((LANES, TZ * LANES), jnp.float32)],
+        scratch_shapes=[pltpu.VMEM((plan.steps * LANES, TZ * LANES), jnp.float32)],
         compiler_params=pltpu.CompilerParams(vmem_limit_bytes=VMEM_LIMIT),
-        cost_estimate=pl.CostEstimate(
-            flops=2 * projection.size // CHUNKS,
-            bytes_accessed=4 * projection.size // CHUNKS,
-            transcendentals=0,
-        ),
+        cost_estimate=projection_cost(projection),
         name="depth_gather",
     )(counts, before, projection, high, low, pieces)
 
@@ -474,7 +465,7 @@
         functools.partial(near_kernel, plan),
         grid=(plan.cell_cols // LANES,),
         in_specs=[
-            pl.BlockSpec(extended.shape, lambda i: (0, 0, 0, 0)),
+            whole_spec(extended.shape),
             pl.BlockSpec((plan.near, plan.cell_planes, LANES), lambda i: (0, 0, i)),
             pl.BlockSpec(
                 (plan.near, plan.panels, plan.panels, plan.cell_planes, LANES), lambda i: (0, 0, 0, 0, i)
@@ -496,10 +487,14 @@
     return (up, [(j, i) for i, j in up])
 
 
-def extended_charges(plan, masked):
+def extend_rows(plan, masked):
     up, down = ring_pairs("cell")
     left = lax.ppermute(masked[:, :, -NZC:], "cell", up)
     right = lax.ppermute(masked[:, :, :NZC], "cell", down)
+    return (left, right)
+
+
+def extend_planes(plan, masked, left, right):
     rest = jnp.zeros((plan.panels, plan.cell_planes, LANES - NZC), jnp.float32)
     wide = jnp.concatenate([rest, left, masked, right, rest], axis=2)
     up, down = ring_pairs("slab")
@@ -512,24 +507,14 @@
 
 def spectrum_weights(plan, spectrum):
     slab, cell = (lax.axis_index("slab"), lax.axis_index("cell"))
-    scale = 1.0 / (plan.nx * plan.ny * plan.nz)
     by_depth = jnp.transpose(spectrum, (1, 2, 0))
-    shape = (plan.slabs, plan.cells) + by_depth.shape[1:]
-    own = lax.dynamic_index_in_dim(by_depth[: plan.slots].reshape(shape), cell, 1, keepdims=False)
+    own = lax.dynamic_slice_in_dim(by_depth, cell * plan.slabs, plan.slabs, 0)
     dest = lax.broadcasted_iota(jnp.int32, own.shape, 0)
     swapped = (cell == 0) & (slab >= plan.slabs // 2) & (dest == 0)
-    own = jnp.where(swapped, by_depth[plan.slots][None], own) * scale
+    own = jnp.where(swapped, by_depth[plan.slots][None], own)
     weights = lax.all_to_all(own, "slab", split_axis=0, concat_axis=0, tiled=True)
-    weights = weights.reshape(plan.ny, plan.nx)
-    far = lax.ppermute(by_depth[0, :1], "slab", [(plan.slabs // 2, 0)]) * scale
-    near = by_depth[plan.slots, :1] * scale
-    steps = 4
-    edge = weights.reshape(steps, -1, plan.nx)[:, 0]
-    step = lax.broadcasted_iota(jnp.int32, edge.shape, 0)
-    first = (slab == 0) & (cell == 0)
-    edge = jnp.where(first & (step == 0), far, edge)
-    edge = jnp.where(first & (step == steps // 2), near, edge)
-    return (weights, edge[:, None])
+    far = lax.ppermute(by_depth[0, :1], "slab", [(plan.slabs // 2, 0)])
+    return (weights.reshape(plan.ny, plan.nx), far, by_depth[plan.slots, :1])
 
 
 def per_device(charges, counts, projection, near_blocks, neighbours, spectrum):
@@ -539,33 +524,56 @@
     plan = Plan(slabs, cells, panels, cell_planes, cell_cols, neighbours.shape[0], nx, nz, local * slabs)
     if not plan.fits():
         return plain_device(charges, counts, projection, near_blocks, neighbours, spectrum)
-    me = (lax.axis_index("slab") * cells + lax.axis_index("cell")).astype(jnp.int32).reshape(1)
-    depth_forward, depth_backward = plan.depth_tables()
-    freqs = np.arange(plan.ny)
-    cos_y, sin_y = wave(freqs, plan.y_order(), plan.ny)
-    y_forward = halves(np.concatenate([cos_y, sin_y], axis=0))
-    y_backward = halves(np.concatenate([cos_y.T, sin_y.T], axis=0))
-    cos_x, sin_x = wave(plan.x_order(), np.arange(plan.nx), plan.nx)
-    x_forward = halves(np.concatenate([cos_x, sin_x], axis=1))
-    chunked = (CHUNKS, plan.x_chunk, plan.nx)
-    both_x = np.concatenate([cos_x.reshape(chunked), sin_x.reshape(chunked)], axis=1)
-    x_backward = halves(both_x.transpose(0, 2, 1))
-    axes = ("slab", "cell")
-    weights, edge = spectrum_weights(plan, spectrum)
-    pencils = []
-    for chunk in range(CHUNKS):
-        pieces = project(plan, chunk, charges, counts, projection, *halves(depth_forward))
-        pieces = lax.all_to_all(pieces, axes, split_axis=0, concat_axis=0, tiled=True)
-        pencils.append(forward_y(plan, me, pieces, *y_forward))
-    high, low = forward_x(plan, weights, edge, *x_forward, pencils)
+    me = (lax.axis_index("cell") * slabs + lax.axis_index("slab")).astype(jnp.int32).reshape(1)
+    depth_forward, depth_backward = [halves(table) for table in plan.depth_tables()]
+    y_rows, x_cols, low_ids = (plan.y_rows(), plan.x_columns(), np.arange(plan.ny // 2))
+    y_waves = [wave(low_ids, rows, plan.ny) for rows in y_rows]
+    x_waves = [wave(cols, low_ids, plan.nx) for cols in x_cols]
+    y_forward = halves(np.stack([np.concatenate(pair, axis=0) for pair in y_waves]))
+    y_backward = halves(np.stack([np.concatenate([t.T for t in pair], axis=0) for pair in y_waves]))
+    x_forward = halves(np.stack([np.concatenate(pair, axis=1) for pair in x_waves]))
+    x_backward = halves(np.stack([np.concatenate([t.T for t in pair], axis=1) for pair in x_waves]))
+    split_projection = projection.reshape(
+        (panels, TX // CHUNKS, CHUNKS, TY * TZ, cell_planes, cell_cols)
+    )
+    axes = ("cell", "slab")
+
+    def exchange(pieces):
+        return lax.all_to_all(pieces, axes, split_axis=0, concat_axis=0, tiled=True)
+
+    rows_shape = (plan.ny, 2 * plan.x_chunk)
+    freq_shape = (2 * plan.ny, plan.x_chunk)
+    both_shape = (2 * plan.ny, plan.nx)
+    weights, far, near = spectrum_weights(plan, spectrum)
     slot = lax.broadcasted_iota(jnp.int32, charges.shape, 0)
     masked = jnp.where(slot < counts[None], charges, 0.0)
-    total = near_field(plan, extended_charges(plan, masked), neighbours, near_blocks)
-    for chunk in range(CHUNKS):
-        pieces = backward(plan, chunk, me, high, low, x_backward, y_backward)
-        pieces = lax.all_to_all(pieces, axes, split_axis=0, concat_axis=0, tiled=True)
-        total = gather(plan, chunk, counts, total, projection, *halves(depth_backward), pieces)
-    return total
+    left, right = extend_rows(plan, masked)
+    pieces = [project(plan, i, charges, counts, split_projection, *depth_forward) for i in range(CHUNKS)]
+    pieces[0], far, left, right = lax.optimization_barrier((pieces[0], far, left, right))
+    edge = jnp.concatenate([far, near], axis=0)
+    extended = extend_planes(plan, masked, left, right)
+    even_pieces = exchange(pieces[0])
+    pieces[1], extended = lax.optimization_barrier((pieces[1], extended))
+    odd_pieces = exchange(pieces[1])
+    (even,) = plane_call(
+        plan, first_plane_kernel, "even_planes", (None, 0), me, [even_pieces], [y_forward, x_forward],
+        [both_shape], [rows_shape, freq_shape], 2,
+    )
+    total = near_field(plan, extended, neighbours, near_blocks)
+    even, total = lax.optimization_barrier((even, total))
+    back, rest = plane_call(
+        plan, middle_plane_kernel, "middle_planes", (None, 1, 0, None), me,
+        [odd_pieces, even, weights, edge], [y_forward, x_forward, x_backward, y_backward],
+        [piece_shape(plan), freq_shape], [rows_shape, freq_shape, freq_shape], 4,
+    )
+    even_back = exchange(back)
+    (back,) = plane_call(
+        plan, last_plane_kernel, "odd_planes", (1, None), me, [rest], [x_backward, y_backward],
+        [piece_shape(plan)], [rows_shape], 2,
+    )
+    odd_back = exchange(back)
+    total = gather(plan, 0, counts, total, split_projection, *depth_backward, even_back)
+    return gather(plan, 1, counts, total, split_projection, *depth_backward, odd_back)
 
 
 def padded(value, sides, width):

time: 216 us -> 185 us (0.86)
  Pallas kernels: 82.9 us -> 54.9 us
  local copies, waits for them, and re-layouts: 4.91 us -> 26.4 us
  waiting for transfers between devices: 87.7 us -> 71.6 us
  starting transfers between devices: 34.6 us -> 28.2 us
    pallas_call x5 -> x3, Pallas kernels: 41 us -> 15.8 us  [plane_call(): pl.pallas_call(functools.partial(kernel, plan), grid=(1,), in_specs=[pl.B...]
    unnamed x14 -> x66, local copies, waits for them, and re-layouts: 2.03 us -> 21.7 us
    all_to_all x1, waiting for transfers between devices: 16.2 us -> 0.01 us  [spectrum_weights(): lax.all_to_all(own, 'slab', split_axis=0, concat_axis=0, tiled=True)]
    all_to_all x4, waiting for transfers between devices: 34.1 us -> 46.2 us  [exchange(): return lax.all_to_all(pieces, axes, split_axis=0, concat_axis=0, tiled=True)]
    ppermute x5, waiting for transfers between devices: 37.4 us -> 25.4 us  [the longest x1 16 us: spectrum_weights(): far = lax.ppermute(by_depth[0, :1], 'slab', [(plan.slabs // 2, 0)])]
    all_to_all x4, starting transfers between devices: 16.6 us -> 13 us  [exchange(): return lax.all_to_all(pieces, axes, split_axis=0, concat_axis=0, tiled=True)]
    ppermute x5, starting transfers between devices: 10.6 us -> 7.81 us  [the longest x1 4.19 us: extend_planes(): after = lax.ppermute(wide[:, :1], 'slab', down)]
  transfers between devices with their start and end apart: 10 -> 10, of which waited for: 7 -> 6; matrix products, arithmetic and copies ran while one was open for 1% -> 2% of each run, Pallas kernels for 24% -> 21%
where the time goes in v3:
time: 185 us; the launch traced here: 184 us
  waiting for transfers between devices  71.6 us (39%)
  Pallas kernels  54.9 us (30%)
  starting transfers between devices  28.2 us (15%)
  local copies, waits for them, and re-layouts  26.4 us (14%)
  other arithmetic  2.57 us (1%)
    all_to_all x4, waiting for transfers between devices, exchange(): return lax.all_to_all(pieces, axes, split_axis=0, concat_axis=0, tiled=True)  46.2 us
    unnamed x66, local copies, waits for them, and re-layouts  21.7 us
    ppermute x1, waiting for transfers between devices, spectrum_weights(): far = lax.ppermute(by_depth[0, :1], 'slab', [(plan.slabs // 2, 0)])  16 us
    pallas_call x3, Pallas kernels, plane_call(): pl.pallas_call(functools.partial(kernel, plan), grid=(1,), in_specs=[pl.B...  15.8 us
    pallas_call x1, Pallas kernels, near_field(): pl.pallas_call(functools.partial(near_kernel, plan), grid=(plan.cell_cols...  14.9 us
    all_to_all x4, starting transfers between devices, exchange(): return lax.all_to_all(pieces, axes, split_axis=0, concat_axis=0, tiled=True)  13 us
    pallas_call x2, Pallas kernels, project(): pl.pallas_call(functools.partial(project_kernel, plan), grid=(plan.steps,...  12.7 us
    pallas_call x2, Pallas kernels, gather(): pl.pallas_call(functools.partial(gather_kernel, plan, chunk == CHUNKS - 1...  11.4 us
  transfers between devices with their start and end apart: 10, of which 6 were waited for; matrix products, arithmetic and copies ran while one was open for 2% of the time, Pallas kernels for 21%

profile of v3, /device:TPU:0, one launch (start us, length us, event | category | flops | bytes accessed | tf_op | source)
XLA Modules:
  0.0 184.0 jit_solution(10935999024725616426)
XLA Ops:
  0.0 0.9 slice_bitcast_fusion
  1.0 2.4 %bitcast_select_fusion = f32[16,32,512]{2,1,0:T(8,128)} fusion(f32[512,64,32]{0,2,1:T(8,128)} %param.23, s32[]{:T(128)S(6)} %select_n.12, f32[32,512]{1,0:T(8,128)S(1)} %slice_bitcast_fusion, pred[16]{0:T(512)(128)(4,1)S(1)} %compare_and_fusion), kind=kLoop, calls=%fused_computation | loop fusion | flops 262144 | bytes 2162708 | tf_op jit(solution)/shard_map/jit(_where)/select_n | solution.py:514
  3.3 7.4 %all-to-all-start.2 = ((f32[16,32,512]{2,1,0:T(8,128)}), f32[16,32,512]{2,1,0:T(8,128)S(1)}, u32[]{:S(2)}, u32[]{:S(2)}) async-start(f32[16,32,512]{2,1,0:T(8,128)} %bitcast_select_fusion), calls=%async_computation.2 | async-start | bytes 2097152 | tf_op jit(solution)/shard_map/all_to_all | solution.py:515
  10.8 0.0 copy-start.32
  10.8 0.1 fusion.4
  10.8 1.5 collective-permute-start.1
  12.4 0.5 collective-permute-start.2
  12.9 0.7 slice_bitcast_fusion.1
  13.6 1.3 collective-permute-start
  14.9 6.4 %project_depth.2 = f32[32,2,4,8,128]{4,3,2,1,0:T(8,128)} custom-call(f32[8,8,1024]{2,1,0:T(8,128)S(1)} %copy-done.1, s32[8,1024]{1,0:T(8,128)S(1)} %copy-done.9, f32[8,2,2,16,8,1024]{5,4,3,2,1,0:T(8,128)} %bitcast.22, bf16[512,512]{1,0:T(8,128)(2,1)S(1)} %copy-done.4, bf16[512,512]{1,0:T(8,128)(2,1)S(1)} %copy-done.5), custom_call_target="tpu_custom_call" | custom-call | flops 4194304 | bytes 8388608 | tf_op jit(solution)/shard_map/project_depth/pallas_call | solution.py:187
  21.3 16.0 %collective-permute-done = f32[1,512]{1,0:T(1,128)S(1)} collective-permute-done((f32[1,512]{1,0:T(1,128)S(1)}, f32[1,512]{1,0:T(1,128)S(1)}, u32[]{:S(2)}, u32[]{:S(2)}) %collective-permute-start) | collective-permute-done | bytes 2080 | tf_op jit(solution)/shard_map/ppermute | solution.py:516
  37.3 0.0 collective-permute-done.1
  37.3 0.0 collective-permute-done.2
  37.3 0.0 all-to-all-done.2
  37.3 0.0 copy-done.32
  37.3 3.2 %all-to-all-start = ((f32[32,2,4,8,128]{4,3,2,1,0:T(8,128)}), f32[32,2,4,8,128]{4,3,2,1,0:T(8,128)S(1)}, u32[]{:S(2)}, u32[]{:S(2)}) async-start(f32[32,2,4,8,128]{4,3,2,1,0:T(8,128)} %project_depth.2), calls=%async_computation | async-start | bytes 2097152 | tf_op jit(solution)/shard_map/all_to_all | solution.py:542
  40.5 1.8 concatenate.13
  42.2 1.1 fusion.3
  43.4 0.3 collective-permute-start.3
  43.7 4.2 %collective-permute-start.4 = (f32[8,1,1280]{2,1,0:T(1,128)S(1)}, f32[8,1,1280]{2,1,0:T(1,128)S(1)}, u32[]{:S(2)}, u32[]{:S(2)}) collective-permute-start(f32[8,1,1280]{2,1,0:T(1,128)S(1)} %get-tuple-element.30), channel_id=1, source_target_pairs={{2,0},{4,2},{6,4},{8,6},{10,8},{12,10},{14,12},{16,14},{18,16},{20... | collective-permute-start | bytes 122888 | tf_op jit(solution)/shard_map/ppermute | solution.py:502
  47.9 6.3 %project_depth.3 = f32[32,2,4,8,128]{4,3,2,1,0:T(8,128)} custom-call(f32[8,8,1024]{2,1,0:T(8,128)S(1)} %copy-done.1, s32[8,1024]{1,0:T(8,128)S(1)} %copy-done.9, f32[8,2,2,16,8,1024]{5,4,3,2,1,0:T(8,128)} %bitcast.23, bf16[512,512]{1,0:T(8,128)(2,1)S(1)} %copy-done.4, bf16[512,512]{1,0:T(8,128)(2,1)S(1)} %copy-done.5), custom_call_target="tpu_custom_call" | custom-call | flops 4194304 | bytes 8388608 | tf_op jit(solution)/shard_map/project_depth/pallas_call | solution.py:187
  54.2 9.4 %collective-permute-done.3 = f32[8,1,1280]{2,1,0:T(1,128)S(1)} collective-permute-done((f32[8,1,1280]{2,1,0:T(1,128)S(1)}, f32[8,1,1280]{2,1,0:T(1,128)S(1)}, u32[]{:S(2)}, u32[]{:S(2)}) %collective-permute-start.3) | collective-permute-done | bytes 40992 | tf_op jit(solution)/shard_map/ppermute | solution.py:501
  63.6 0.0 collective-permute-done.4
  63.6 0.0 copy-done.31
  63.6 0.1 fusion.1
  63.7 0.1 pad_maximum_fusion.extended
  63.8 3.9 %all-to-all-done.pieces = f32[32,2,4,8,128]{4,3,2,1,0:T(8,128)S(1)} async-done(((f32[32,2,4,8,128]{4,3,2,1,0:T(8,128)}), f32[32,2,4,8,128]{4,3,2,1,0:T(8,128)S(1)}, u32[]{:S(2)}, u32[]{:S(2)}) %all-to-all-start) | async-done | bytes 1048608 | tf_op jit(solution)/shard_map/all_to_all | solution.py:542
  67.6 3.4 %all-to-all-start.1 = ((f32[32,2,4,8,128]{4,3,2,1,0:T(8,128)}), f32[32,2,4,8,128]{4,3,2,1,0:T(8,128)}, u32[]{:S(2)}, u32[]{:S(2)}) async-start(f32[32,2,4,8,128]{4,3,2,1,0:T(8,128)} %project_depth.3), calls=%async_computation.1 | async-start | bytes 2097152 | tf_op jit(solution)/shard_map/all_to_all | solution.py:542
  71.1 0.0 copy-start
  71.1 4.6 %copy-done = f32[6,8,8,8,1024]{4,3,2,1,0:T(8,128)S(1)} copy-done((f32[6,8,8,8,1024]{4,3,2,1,0:T(8,128)S(1)}, f32[6,8,8,8,1024]{4,3,2,1,0:T(8,128)}, u32[]{:S(2)}) %copy-start) | copy-done | bytes 12582936
  75.6 0.9 copy-done.10
  76.6 14.9 %near_blocks.1.before = f32[8,8,1024]{2,1,0:T(8,128)S(1)} custom-call(f32[8,3,8,1280]{3,2,1,0:T(8,128)S(1)} %pad_maximum_fusion.extended, s32[6,8,1024]{2,1,0:T(8,128)S(1)} %copy-done.10, f32[6,8,8,8,1024]{4,3,2,1,0:T(8,128)S(1)} %copy-done), custom_call_target="tpu_custom_call" | custom-call | flops 6291456 | bytes 12582912 | tf_op jit(solution)/shard_map/near_blocks/pallas_call | solution.py:464
  91.5 0.0 copy-start.6
  91.5 0.7 copy-done.6
  92.3 2.8 %even_planes.1.even = f32[1024,512]{1,0:T(8,128)S(1)} custom-call(s32[1]{0:T(128)} %bitcast.me_ref, f32[32,2,4,8,128]{4,3,2,1,0:T(8,128)S(1)} %all-to-all-done.pieces, bf16[2,512,256]{2,1,0:T(8,128)(2,1)S(1)} %copy-done.19, bf16[2,512,256]{2,1,0:T(8,128)(2,1)S(1)} %copy-done.21, bf16[2,256,512]{2,1,0:T(8,128)(2,1)S(1)} %copy-done.23, ...), custom_call_target="tpu_custom_call" | custom-call | flops 1610612736 | bytes 3145728 | tf_op jit(solution)/shard_map/even_planes/pallas_call | solution.py:358
  95.1 0.0 copy-start.27
  95.1 1.3 copy-done.27
  96.4 1.8 all-to-all-done.1.pieces
  98.2 0.0 copy-done.13
  98.2 1.0 copy-done.15
  99.3 1.0 copy-done.17
  100.3 1.0 copy-done.20
  101.3 1.0 copy-done.22
  102.4 1.0 copy-done.24
  103.4 1.0 copy-done.26
  104.5 1.6 copy-done.28
  106.1 10.0 %middle_planes.1 = (f32[32,2,4,8,128]{4,3,2,1,0:T(8,128)}, f32[1024,256]{1,0:T(8,128)S(1)}) custom-call(s32[1]{0:T(128)} %bitcast.me_ref, f32[32,2,4,8,128]{4,3,2,1,0:T(8,128)} %all-to-all-done.1.pieces, f32[1024,512]{1,0:T(8,128)S(1)} %copy-done.28, f32[512,512]{1,0:T(8,128)S(1)} %bitcast.21, f32[2,512]{1,0:T(2,128)S(1)} %pad_maximum_fusion.3.edge, ...), custom_call_target="tpu_custom_call" | custom-call | flops 3221225472 | bytes 8392704 | tf_op jit(solution)/shard_map/middle_planes/pallas_call | solution.py:358
  116.0 1.0 copy-done.29
  117.0 3.8 %all-to-all-start.3 = ((f32[32,2,4,8,128]{4,3,2,1,0:T(8,128)}), f32[32,2,4,8,128]{4,3,2,1,0:T(8,128)S(1)}, u32[]{:S(2)}, u32[]{:S(2)}) async-start(f32[32,2,4,8,128]{4,3,2,1,0:T(8,128)} %get-tuple-element.23), calls=%async_computation.3 | async-start | bytes 2097152 | tf_op jit(solution)/shard_map/all_to_all | solution.py:542
  120.8 0.0 copy-start.2
  120.8 0.0 copy-start.3
  120.9 0.0 copy-start.16
  120.9 1.1 copy-done.16
  122.0 1.0 copy-done.18
  123.0 1.2 copy-done.30
  124.3 3.1 %odd_planes.1 = f32[32,2,4,8,128]{4,3,2,1,0:T(8,128)S(1)} custom-call(s32[1]{0:T(128)} %bitcast.me_ref, f32[1024,256]{1,0:T(8,128)S(1)} %copy-done.30, bf16[2,256,512]{2,1,0:T(8,128)(2,1)S(1)} %copy-done.12, bf16[2,256,512]{2,1,0:T(8,128)(2,1)S(1)} %copy-done.14, bf16[2,512,256]{2,1,0:T(8,128)(2,1)S(1)} %copy-done.16, bf16[2,512,256]{2,1,0:T(8,128)(2,1)S(1)} %copy-done.18), custom_call_target="tpu_custom_call" | custom-call | flops 1610612736 | bytes 3145728 | tf_op jit(solution)/shard_map/odd_planes/pallas_call | solution.py:358
  127.4 1.0 copy-done.8
  128.3 19.7 %all-to-all-done.3.pieces = f32[32,2,4,8,128]{4,3,2,1,0:T(8,128)S(1)} async-done(((f32[32,2,4,8,128]{4,3,2,1,0:T(8,128)}), f32[32,2,4,8,128]{4,3,2,1,0:T(8,128)S(1)}, u32[]{:S(2)}, u32[]{:S(2)}) %all-to-all-start.3) | async-done | bytes 1048608 | tf_op jit(solution)/shard_map/all_to_all | solution.py:542
  148.0 2.6 %all-to-all-start.4 = ((f32[32,2,4,8,128]{4,3,2,1,0:T(8,128)}), f32[32,2,4,8,128]{4,3,2,1,0:T(8,128)S(1)}, u32[]{:S(2)}, u32[]{:S(2)}) async-start(f32[32,2,4,8,128]{4,3,2,1,0:T(8,128)} %copy-done.8), calls=%async_computation.4 | async-start | bytes 2097152 | tf_op jit(solution)/shard_map/all_to_all | solution.py:542
  150.7 0.0 copy-start.7
  150.7 0.9 copy-done.7
  151.6 5.3 %depth_gather.2.before = f32[8,8,1024]{2,1,0:T(8,128)S(1)} custom-call(s32[8,1024]{1,0:T(8,128)S(1)} %copy-done.9, f32[8,8,1024]{2,1,0:T(8,128)S(1)} %copy-done.7, f32[8,2,2,16,8,1024]{5,4,3,2,1,0:T(8,128)} %bitcast.24, bf16[512,512]{1,0:T(8,128)(2,1)S(1)} %copy-done.2, bf16[512,512]{1,0:T(8,128)(2,1)S(1)} %copy-done.3, ...), custom_call_target="tpu_custom_call" | custom-call | flops 4194304 | bytes 8388608 | tf_op jit(solution)/shard_map/depth_gather/pallas_call | solution.py:400
  157.0 20.9 %all-to-all-done.4.pieces = f32[32,2,4,8,128]{4,3,2,1,0:T(8,128)S(1)} async-done(((f32[32,2,4,8,128]{4,3,2,1,0:T(8,128)}), f32[32,2,4,8,128]{4,3,2,1,0:T(8,128)S(1)}, u32[]{:S(2)}, u32[]{:S(2)}) %all-to-all-start.4) | async-done | bytes 1048608 | tf_op jit(solution)/shard_map/all_to_all | solution.py:542
  177.9 6.1 %depth_gather.3 = f32[8,8,1024]{2,1,0:T(8,128)} custom-call(s32[8,1024]{1,0:T(8,128)S(1)} %copy-done.9, f32[8,8,1024]{2,1,0:T(8,128)S(1)} %depth_gather.2.before, f32[8,2,2,16,8,1024]{5,4,3,2,1,0:T(8,128)} %bitcast.25, bf16[512,512]{1,0:T(8,128)(2,1)S(1)} %copy-done.2, bf16[512,512]{1,0:T(8,128)(2,1)S(1)} %copy-done.3, ...), custom_call_target="tpu_custom_call" | custom-call | flops 4194304 | bytes 8388608 | tf_op jit(solution)/shard_map/depth_gather/pallas_call | solution.py:400
  (42 shorter events, 0.1 us)
Async XLA Ops:
  0.0 14.9 %copy-start.4 = (bf16[512,512]{1,0:T(8,128)(2,1)S(1)}, bf16[512,512]{1,0:T(8,128)(2,1)}, u32[]{:S(2)}) copy-start(bf16[512,512]{1,0:T(8,128)(2,1)} %constant.44.clone.high) | copy-start | bytes 1572868
  0.0 14.9 %copy-start.5 = (bf16[512,512]{1,0:T(8,128)(2,1)S(1)}, bf16[512,512]{1,0:T(8,128)(2,1)}, u32[]{:S(2)}) copy-start(bf16[512,512]{1,0:T(8,128)(2,1)} %constant.45.clone.low) | copy-start | bytes 1572868
  0.0 10.7 %copy-start.9 = (s32[8,1024]{1,0:T(8,128)S(1)}, s32[8,1024]{1,0:T(8,128)}, u32[]{:S(2)}) copy-start(s32[8,1024]{1,0:T(8,128)} %counts.7) | copy-start | bytes 98308
  0.0 10.7 %copy-start.1 = (f32[8,8,1024]{2,1,0:T(8,128)S(1)}, f32[8,8,1024]{2,1,0:T(8,128)}, u32[]{:S(2)}) copy-start(f32[8,8,1024]{2,1,0:T(8,128)} %charges.3) | copy-start | bytes 786436
  3.3 34.0 %all-to-all-start.2 = ((f32[16,32,512]{2,1,0:T(8,128)}), f32[16,32,512]{2,1,0:T(8,128)S(1)}, u32[]{:S(2)}, u32[]{:S(2)}) async-start(f32[16,32,512]{2,1,0:T(8,128)} %bitcast_select_fusion), calls=%async_computation.2 | async-start | bytes 2097152 | tf_op jit(solution)/shard_map/all_to_all | solution.py:515
  10.8 26.5 %copy-start.32 = (f32[8,8,1024]{2,1,0:T(8,128)}, f32[8,8,1024]{2,1,0:T(8,128)S(1)}, u32[]{:S(2)}) copy-start(f32[8,8,1024]{2,1,0:T(8,128)S(1)} %fusion.2) | copy-start | bytes 786436
  10.8 26.4 %collective-permute-start.1 = (f32[8,8,16]{2,1,0:T(8,128)S(1)}, f32[8,8,16]{2,1,0:T(8,128)S(1)}, u32[]{:S(2)}, u32[]{:S(2)}) collective-permute-start(f32[8,8,16]{2,1,0:T(8,128)S(1)} %get-tuple-element.32), channel_id=1, source_target_pairs={{0,1},{1,0},{2,3},{3,2},{4,5},{5,4},{6,7},{7,6},{8,9},{9,8},{10,11... | collective-permute-start | bytes 12296 | tf_op jit(solution)/shard_map/ppermute | solution.py:492
  12.4 24.9 %collective-permute-start.2 = (f32[8,8,16]{2,1,0:T(8,128)S(1)}, f32[8,8,16]{2,1,0:T(8,128)S(1)}, u32[]{:S(2)}, u32[]{:S(2)}) collective-permute-start(f32[8,8,16]{2,1,0:T(8,128)S(1)} %get-tuple-element.31), channel_id=1, source_target_pairs={{1,0},{0,1},{3,2},{2,3},{5,4},{4,5},{7,6},{6,7},{9,8},{8,9},{11,10... | collective-permute-start | bytes 12296 | tf_op jit(solution)/shard_map/ppermute | solution.py:493
  13.6 23.7 %collective-permute-start = (f32[1,512]{1,0:T(1,128)S(1)}, f32[1,512]{1,0:T(1,128)S(1)}, u32[]{:S(2)}, u32[]{:S(2)}) collective-permute-start(f32[1,512]{1,0:T(1,128)S(1)} %get-tuple-element.26), channel_id=1, source_target_pairs={{16,0},{17,1}} | collective-permute-start | bytes 6152 | tf_op jit(solution)/shard_map/ppermute | solution.py:516
  37.3 30.4 %all-to-all-start = ((f32[32,2,4,8,128]{4,3,2,1,0:T(8,128)}), f32[32,2,4,8,128]{4,3,2,1,0:T(8,128)S(1)}, u32[]{:S(2)}, u32[]{:S(2)}) async-start(f32[32,2,4,8,128]{4,3,2,1,0:T(8,128)} %project_depth.2), calls=%async_computation | async-start | bytes 2097152 | tf_op jit(solution)/shard_map/all_to_all | solution.py:542
  43.4 20.2 %collective-permute-start.3 = (f32[8,1,1280]{2,1,0:T(1,128)S(1)}, f32[8,1,1280]{2,1,0:T(1,128)S(1)}, u32[]{:S(2)}, u32[]{:S(2)}) collective-permute-start(f32[8,1,1280]{2,1,0:T(1,128)S(1)} %get-tuple-element.29), channel_id=1, source_target_pairs={{0,2},{2,4},{4,6},{6,8},{8,10},{10,12},{12,14},{14,16},{16,18},{18... | collective-permute-start | bytes 122888 | tf_op jit(solution)/shard_map/ppermute | solution.py:501
  43.7 19.9 %copy-start.31 = (f32[8,8,1280]{2,1,0:T(8,128)S(1)}, f32[8,8,1280]{2,1,0:T(8,128)}, u32[]{:S(2)}) copy-start(f32[8,8,1280]{2,1,0:T(8,128)} %concatenate.13) | copy-start | bytes 983044
  43.7 19.9 %collective-permute-start.4 = (f32[8,1,1280]{2,1,0:T(1,128)S(1)}, f32[8,1,1280]{2,1,0:T(1,128)S(1)}, u32[]{:S(2)}, u32[]{:S(2)}) collective-permute-start(f32[8,1,1280]{2,1,0:T(1,128)S(1)} %get-tuple-element.30), channel_id=1, source_target_pairs={{2,0},{4,2},{6,4},{8,6},{10,8},{12,10},{14,12},{16,14},{18,16},{20... | collective-permute-start | bytes 122888 | tf_op jit(solution)/shard_map/ppermute | solution.py:502
  67.6 30.6 %all-to-all-start.1 = ((f32[32,2,4,8,128]{4,3,2,1,0:T(8,128)}), f32[32,2,4,8,128]{4,3,2,1,0:T(8,128)}, u32[]{:S(2)}, u32[]{:S(2)}) async-start(f32[32,2,4,8,128]{4,3,2,1,0:T(8,128)} %project_depth.3), calls=%async_computation.1 | async-start | bytes 2097152 | tf_op jit(solution)/shard_map/all_to_all | solution.py:542
  71.1 4.6 %copy-start = (f32[6,8,8,8,1024]{4,3,2,1,0:T(8,128)S(1)}, f32[6,8,8,8,1024]{4,3,2,1,0:T(8,128)}, u32[]{:S(2)}) copy-start(f32[6,8,8,8,1024]{4,3,2,1,0:T(8,128)} %blocks_ref.1) | copy-start | bytes 37748740
  75.6 0.9 copy-start.10
  76.6 15.7 %copy-start.19 = (bf16[2,512,256]{2,1,0:T(8,128)(2,1)S(1)}, bf16[2,512,256]{2,1,0:T(8,128)(2,1)}, u32[]{:S(2)}) copy-start(bf16[2,512,256]{2,1,0:T(8,128)(2,1)} %constant.46.clone.y_high.yf_high) | copy-start | bytes 1572868
  76.6 15.7 %copy-start.21 = (bf16[2,512,256]{2,1,0:T(8,128)(2,1)S(1)}, bf16[2,512,256]{2,1,0:T(8,128)(2,1)}, u32[]{:S(2)}) copy-start(bf16[2,512,256]{2,1,0:T(8,128)(2,1)} %constant.47.clone.y_low.yf_low) | copy-start | bytes 1572868
  76.6 15.7 %copy-start.23 = (bf16[2,256,512]{2,1,0:T(8,128)(2,1)S(1)}, bf16[2,256,512]{2,1,0:T(8,128)(2,1)}, u32[]{:S(2)}) copy-start(bf16[2,256,512]{2,1,0:T(8,128)(2,1)} %constant.48.clone.x_high.xf_high) | copy-start | bytes 1572868
  76.6 15.7 %copy-start.25 = (bf16[2,256,512]{2,1,0:T(8,128)(2,1)S(1)}, bf16[2,256,512]{2,1,0:T(8,128)(2,1)}, u32[]{:S(2)}) copy-start(bf16[2,256,512]{2,1,0:T(8,128)(2,1)} %constant.49.clone.x_low.xf_low) | copy-start | bytes 1572868
  91.5 0.7 copy-start.6
  92.2 6.0 %copy-start.11 = (bf16[2,256,512]{2,1,0:T(8,128)(2,1)S(1)}, bf16[2,256,512]{2,1,0:T(8,128)(2,1)}, u32[]{:S(2)}) copy-start(bf16[2,256,512]{2,1,0:T(8,128)(2,1)} %constant.50.clone.xb_high.x_high) | copy-start | bytes 1572868
  92.2 6.0 %copy-start.13 = (bf16[2,256,512]{2,1,0:T(8,128)(2,1)S(1)}, bf16[2,256,512]{2,1,0:T(8,128)(2,1)}, u32[]{:S(2)}) copy-start(bf16[2,256,512]{2,1,0:T(8,128)(2,1)} %constant.51.clone.xb_low.x_low) | copy-start | bytes 1572868
  95.1 1.3 copy-start.27
  98.2 1.0 copy-start.15
  99.3 1.0 copy-start.17
  100.3 1.0 copy-start.20
  101.3 1.0 copy-start.22
  102.4 1.0 copy-start.24
  103.4 1.0 copy-start.26
  104.5 1.6 copy-start.28
  106.1 14.8 %copy-start.12 = (bf16[2,256,512]{2,1,0:T(8,128)(2,1)S(1)}, bf16[2,256,512]{2,1,0:T(8,128)(2,1)}, u32[]{:S(2)}) copy-start(bf16[2,256,512]{2,1,0:T(8,128)(2,1)} %constant.50.clone.xb_high.x_high) | copy-start | bytes 1572868
  106.1 14.8 %copy-start.14 = (bf16[2,256,512]{2,1,0:T(8,128)(2,1)S(1)}, bf16[2,256,512]{2,1,0:T(8,128)(2,1)}, u32[]{:S(2)}) copy-start(bf16[2,256,512]{2,1,0:T(8,128)(2,1)} %constant.51.clone.xb_low.x_low) | copy-start | bytes 1572868
  116.0 1.0 copy-start.29
  117.0 31.0 %all-to-all-start.3 = ((f32[32,2,4,8,128]{4,3,2,1,0:T(8,128)}), f32[32,2,4,8,128]{4,3,2,1,0:T(8,128)S(1)}, u32[]{:S(2)}, u32[]{:S(2)}) async-start(f32[32,2,4,8,128]{4,3,2,1,0:T(8,128)} %get-tuple-element.23), calls=%async_computation.3 | async-start | bytes 2097152 | tf_op jit(solution)/shard_map/all_to_all | solution.py:542
  120.8 29.8 %copy-start.2 = (bf16[512,512]{1,0:T(8,128)(2,1)S(1)}, bf16[512,512]{1,0:T(8,128)(2,1)}, u32[]{:S(2)}) copy-start(bf16[512,512]{1,0:T(8,128)(2,1)} %constant.54.clone.high) | copy-start | bytes 1572868
  120.8 29.8 %copy-start.3 = (bf16[512,512]{1,0:T(8,128)(2,1)S(1)}, bf16[512,512]{1,0:T(8,128)(2,1)}, u32[]{:S(2)}) copy-start(bf16[512,512]{1,0:T(8,128)(2,1)} %constant.55.clone.low) | copy-start | bytes 1572868
  120.9 1.1 copy-start.16
  122.0 1.0 copy-start.18
  123.0 1.2 copy-start.30
  127.4 1.0 copy-start.8
  148.0 29.8 %all-to-all-start.4 = ((f32[32,2,4,8,128]{4,3,2,1,0:T(8,128)}), f32[32,2,4,8,128]{4,3,2,1,0:T(8,128)S(1)}, u32[]{:S(2)}, u32[]{:S(2)}) async-start(f32[32,2,4,8,128]{4,3,2,1,0:T(8,128)} %copy-done.8), calls=%async_computation.4 | async-start | bytes 2097152 | tf_op jit(solution)/shard_map/all_to_all | solution.py:542
  150.7 1.0 copy-start.7

commit v4 on v3

--- a/solution.py
+++ b/solution.py
@@ -16,7 +16,7 @@
 NZC = 16
 LANES = 128
 CHUNKS = 2
-VMEM_LIMIT = 40 * 1024 * 1024
+VMEM_LIMIT = 60 * 1024 * 1024
 
 
 def halves(table):
@@ -44,6 +44,8 @@
         self.steps = cell_cols // (LANES * self.step_blocks) if self.step_blocks else 0
         self.x_chunk = nx // CHUNKS
         self.ky_local = ny // slabs
+        self.outer = math.gcd(slabs, 4)
+        self.inner = slabs // self.outer
 
     def fits(self):
         return (
@@ -127,44 +129,53 @@
     return parts
 
 
-def project_kernel(plan, charges, counts, projection, high, low, out, scratch):
+def lane_copies(plan, chunk, projection, held, sems):
+    width = plan.step_blocks * LANES
+    return [
+        pltpu.make_async_copy(
+            projection.at[:, :, chunk, :, :, pl.ds(step * width, width)], held.at[step], sems.at[step]
+        )
+        for step in range(plan.steps)
+    ]
+
+
+def wait_lanes(held, sems, step):
+    pltpu.make_async_copy(held.at[step], held.at[step], sems.at[step]).wait()
+
+
+def project_kernel(plan, chunk, charges, counts, high, low, projection, out, scratch, held, sems):
     planes = plan.cell_planes
-    first = pl.program_id(0) * LANES
-    slot = lax.broadcasted_iota(jnp.int32, charges.shape, 0)
-    masked = jnp.where(slot < counts[...][None], charges[...], 0.0)
-    for block in range(plan.step_blocks):
-        lanes = pl.ds(block * LANES, LANES)
-        own = masked[:, :, block * LANES : (block + 1) * LANES]
-        for tx in range(plan.tx_chunk):
-            for ty in range(TY):
-                row = ((block * TY + ty) * plan.tx_chunk + tx) * planes
-                rows = pl.ds(pl.multiple_of(first + row, planes), planes)
-                for tz in range(TZ):
-                    t = ty * TZ + tz
-                    total = projection[0, tx, 0, t, :, lanes] * own[0]
-                    for p in range(1, plan.panels):
-                        total = total + projection[p, tx, 0, t, :, lanes] * own[p]
-                    scratch[rows, tz * LANES : (tz + 1) * LANES] = total
-
-    @pl.when(pl.program_id(0) == plan.steps - 1)
-    def _():
-        spectra = product((high[...], low[...]), split(scratch[...]), ((1,), (1,)))
-        shape = (plan.slots, 2, plan.row_block, LANES)
-        for step in range(plan.steps):
-            out[:, :, step] = spectra[:, step * LANES : (step + 1) * LANES].reshape(shape)
-
-
-def projection_spec(plan, chunk):
-    shape = (plan.panels, TX // CHUNKS, 1, TY * TZ, plan.cell_planes, plan.step_blocks * LANES)
-    return pl.BlockSpec(shape, lambda i: (0, 0, chunk, 0, 0, i))
-
-
-def panel_spec(plan):
-    return pl.BlockSpec((plan.panels, plan.cell_planes, plan.step_blocks * LANES), lambda i: (0, 0, i))
-
-
-def count_spec(plan):
-    return pl.BlockSpec((plan.cell_planes, plan.step_blocks * LANES), lambda i: (0, i))
+    for copy in lane_copies(plan, chunk, projection, held, sems):
+        copy.start()
+
+    def body(step, carry):
+        wait_lanes(held, sems, step)
+        for block in range(plan.step_blocks):
+            start = pl.multiple_of((step * plan.step_blocks + block) * LANES, LANES)
+            count = counts[:, pl.ds(start, LANES)]
+            own = [jnp.where(count > p, charges[p, :, pl.ds(start, LANES)], 0.0) for p in range(plan.panels)]
+            lanes = slice(block * LANES, (block + 1) * LANES)
+            for tx in range(plan.tx_chunk):
+                for ty in range(TY):
+                    row = step * LANES + ((block * TY + ty) * plan.tx_chunk + tx) * planes
+                    rows = pl.ds(pl.multiple_of(row, planes), planes)
+                    for tz in range(TZ):
+                        t = ty * TZ + tz
+                        total = held[step, 0, tx, t, :, lanes] * own[0]
+                        for p in range(1, plan.panels):
+                            total = total + held[step, p, tx, t, :, lanes] * own[p]
+                        scratch[rows, tz * LANES : (tz + 1) * LANES] = total
+        return carry
+
+    lax.fori_loop(0, plan.steps, body, 0)
+    spectra = product((high[...], low[...]), split(scratch[...]), ((1,), (1,)))
+    shape = (plan.slots, 2, plan.row_block, LANES)
+    for step in range(plan.steps):
+        out[:, :, step] = spectra[:, step * LANES : (step + 1) * LANES].reshape(shape)
+
+
+def held_shape(plan):
+    return (plan.steps, plan.panels, plan.tx_chunk, TY * TZ, plan.cell_planes, plan.step_blocks * LANES)
 
 
 def piece_shape(plan):
@@ -175,32 +186,32 @@
     return pl.BlockSpec(shape, lambda i: (0,) * len(shape))
 
 
-def projection_cost(projection):
-    return pl.CostEstimate(
-        flops=2 * projection.size // CHUNKS,
-        bytes_accessed=4 * projection.size // CHUNKS,
-        transcendentals=0,
-    )
+def projection_call(plan, kernel, name, arrays, projection, out_shape):
+    return pl.pallas_call(
+        kernel,
+        grid=(1,),
+        in_specs=[whole_spec(array.shape) for array in arrays] + [pl.BlockSpec(memory_space=pl.ANY)],
+        out_specs=whole_spec(out_shape),
+        out_shape=jax.ShapeDtypeStruct(out_shape, jnp.float32),
+        scratch_shapes=[
+            pltpu.VMEM((plan.steps * LANES, TZ * LANES), jnp.float32),
+            pltpu.VMEM(held_shape(plan), jnp.float32),
+            pltpu.SemaphoreType.DMA((plan.steps,)),
+        ],
+        compiler_params=pltpu.CompilerParams(vmem_limit_bytes=VMEM_LIMIT),
+        cost_estimate=pl.CostEstimate(
+            flops=2 * projection.size // CHUNKS,
+            bytes_accessed=4 * projection.size // CHUNKS,
+            transcendentals=0,
+        ),
+        name=name,
+    )(*arrays, projection)
 
 
 def project(plan, chunk, charges, counts, projection, high, low):
-    return pl.pallas_call(
-        functools.partial(project_kernel, plan),
-        grid=(plan.steps,),
-        in_specs=[
-            panel_spec(plan),
-            count_spec(plan),
-            projection_spec(plan, chunk),
-            whole_spec(high.shape),
-            whole_spec(low.shape),
-        ],
-        out_specs=whole_spec(piece_shape(plan)),
-        out_shape=jax.ShapeDtypeStruct(piece_shape(plan), jnp.float32),
-        scratch_shapes=[pltpu.VMEM((plan.steps * LANES, TZ * LANES), jnp.float32)],
-        compiler_params=pltpu.CompilerParams(vmem_limit_bytes=VMEM_LIMIT),
-        cost_estimate=projection_cost(projection),
-        name="project_depth",
-    )(charges, counts, projection, high, low)
+    kernel = functools.partial(project_kernel, plan, chunk)
+    arrays = [charges, counts, high, low]
+    return projection_call(plan, kernel, "project_depth", arrays, projection, piece_shape(plan))
 
 
 def forward_plane(plan, special, pieces, y_table, x_table, rows_ref, freq_ref):
@@ -311,13 +322,35 @@
     out[...] = forward_plane(plan, special, pieces, (y_high, y_low), (x_high, x_low), rows_ref, freq_ref)
 
 
-def middle_plane_kernel(
-    plan, me_ref, pieces, even, weights, edge, yf_high, yf_low, xf_high, xf_low, xb_high, xb_low,
-    yb_high, yb_low, out, rest, rows_ref, freq_ref, sum_ref
-):
+def middle_plane_kernel(plan, me_ref, edge, pieces, yf_high, yf_low, xf_high, xf_low, *refs):
+    late, refs = (refs[:5], refs[5:])
+    strips, refs = (refs[: plan.inner], refs[plan.inner :])
+    out, rest, rows_ref, freq_ref, sum_ref, weights = refs[:6]
+    even, xb_high, xb_low, yb_high, yb_low, sems = refs[6:]
+    slab = lax.rem(me_ref[0], plan.slabs)
+    outer_id, inner_id = (slab // plan.inner, lax.rem(slab, plan.inner))
+    held = (even, xb_high, xb_low, yb_high, yb_low)
+    copies = [pltpu.make_async_copy(late[0], even, sems.at[0])]
+    for i in range(plan.inner):
+        for j in range(plan.outer):
+            owner = lax.rem(outer_id - j + plan.outer, plan.outer) * plan.inner
+            owner = owner + lax.rem(inner_id - i + plan.inner, plan.inner)
+            rows = pl.ds(pl.multiple_of(owner * plan.ky_local, plan.ky_local), plan.ky_local)
+            copies.append(
+                pltpu.make_async_copy(
+                    strips[i].at[j], weights.at[rows], sems.at[len(held) + i * plan.outer + j]
+                )
+            )
+    early = len(copies)
+    for n in range(1, len(held)):
+        copies.append(pltpu.make_async_copy(late[n], held[n], sems.at[n]))
+    for copy in copies:
+        copy.start()
     special = me_ref[0] == 0
     width = plan.x_chunk
     odd = forward_plane(plan, special, pieces, (yf_high, yf_low), (xf_high, xf_low), rows_ref, freq_ref)
+    for copy in copies[:early]:
+        copy.wait()
     row = lax.broadcasted_iota(jnp.int32, (plan.ny, width), 0)
     results = []
     for upper in range(2):
@@ -334,7 +367,10 @@
         below, above = (results[0][part], results[1][part])
         sum_ref[rows] = below + above
         rest[rows] = below - above
-    backward_plane(plan, special, sum_ref[...], (xb_high, xb_low), (yb_high, yb_low), out, rows_ref)
+    for copy in copies[early:]:
+        copy.wait()
+    x_table = (xb_high.at[pl.ds(0, 1)], xb_low.at[pl.ds(0, 1)])
+    backward_plane(plan, special, sum_ref[...], x_table, (yb_high, yb_low), out, rows_ref)
 
 
 def last_plane_kernel(plan, me_ref, freqs, x_high, x_low, y_high, y_low, out, rows_ref):
@@ -342,79 +378,67 @@
     backward_plane(plan, special, freqs[...], (x_high, x_low), (y_high, y_low), out, rows_ref)
 
 
-def plane_call(plan, kernel, name, chunks, me, arrays, tables, out_shapes, scratch, work):
-    def table_spec(table, chunk):
-        if chunk is None:
-            return whole_spec(table.shape)
-        return pl.BlockSpec((1,) + table.shape[1:], lambda i: (chunk, 0, 0))
-
+def plane_call(plan, kernel, name, me, arrays, tables, late, out_shapes, scratch, work):
     specs = [whole_spec(array.shape) for array in arrays]
     flat = []
-    for pair, chunk in zip(tables, chunks):
+    for pair, chunk in tables:
         for table in pair:
-            specs.append(table_spec(table, chunk))
+            shape = table.shape if chunk is None else (1,) + table.shape[1:]
+            first = 0 if chunk is None else chunk
+            specs.append(pl.BlockSpec(shape, lambda i, first=first: (first, 0, 0)))
             flat.append(table)
-    size = sum(4 * array.size for array in arrays) + sum(2 * table.size for table in flat)
+    specs += [pl.BlockSpec(memory_space=pl.ANY)] * len(late)
+    size = sum(4 * array.size for array in list(arrays) + list(late)) + sum(2 * t.size for t in flat)
     return pl.pallas_call(
         functools.partial(kernel, plan),
         grid=(1,),
         in_specs=[pl.BlockSpec(memory_space=pltpu.SMEM)] + specs,
         out_specs=[whole_spec(shape) for shape in out_shapes],
         out_shape=[jax.ShapeDtypeStruct(shape, jnp.float32) for shape in out_shapes],
-        scratch_shapes=[pltpu.VMEM(shape, jnp.float32) for shape in scratch],
+        scratch_shapes=scratch,
         compiler_params=pltpu.CompilerParams(vmem_limit_bytes=VMEM_LIMIT),
         cost_estimate=pl.CostEstimate(
             flops=work * 12 * plan.nx * plan.ny * plan.x_chunk, bytes_accessed=size, transcendentals=0
         ),
         name=name,
-    )(me, *arrays, *flat)
-
-
-def gather_kernel(plan, last, counts, before, projection, high, low, pieces, out, scratch):
+    )(me, *arrays, *flat, *late)
+
+
+def gather_kernel(plan, chunk, counts, before, pieces, high, low, projection, out, scratch, held, sems):
     planes = plan.cell_planes
     rows = plan.slots * 2 * plan.row_block
-    first = pl.program_id(0) * LANES
-
-    @pl.when(pl.program_id(0) == 0)
-    def _():
-        columns = [pieces[:, :, step].reshape(rows, LANES) for step in range(plan.steps)]
-        scratch[...] = product(split(jnp.concatenate(columns, axis=1).T), (high[...], low[...]))
-
-    for block in range(plan.step_blocks):
-        lanes = pl.ds(block * LANES, LANES)
-        far = [before[p, :, lanes] for p in range(plan.panels)]
-        for tx in range(plan.tx_chunk):
-            for ty in range(TY):
-                row = ((block * TY + ty) * plan.tx_chunk + tx) * planes
-                rows_at = pl.ds(pl.multiple_of(first + row, planes), planes)
-                for tz in range(TZ):
-                    t = ty * TZ + tz
-                    potential = scratch[rows_at, tz * LANES : (tz + 1) * LANES]
-                    for p in range(plan.panels):
-                        far[p] = far[p] + projection[p, tx, 0, t, :, lanes] * potential
-        for p in range(plan.panels):
-            out[p, :, lanes] = jnp.where(counts[:, lanes] > p, far[p], 0.0) if last else far[p]
+    for copy in lane_copies(plan, chunk, projection, held, sems):
+        copy.start()
+    columns = [pieces[:, :, step].reshape(rows, LANES) for step in range(plan.steps)]
+    scratch[...] = product(split(jnp.concatenate(columns, axis=1).T), (high[...], low[...]))
+
+    def body(step, carry):
+        wait_lanes(held, sems, step)
+        for block in range(plan.step_blocks):
+            cells = pl.ds(pl.multiple_of((step * plan.step_blocks + block) * LANES, LANES), LANES)
+            lanes = slice(block * LANES, (block + 1) * LANES)
+            far = [before[p, :, cells] for p in range(plan.panels)]
+            for tx in range(plan.tx_chunk):
+                for ty in range(TY):
+                    row = step * LANES + ((block * TY + ty) * plan.tx_chunk + tx) * planes
+                    rows_at = pl.ds(pl.multiple_of(row, planes), planes)
+                    for tz in range(TZ):
+                        t = ty * TZ + tz
+                        potential = scratch[rows_at, tz * LANES : (tz + 1) * LANES]
+                        for p in range(plan.panels):
+                            far[p] = far[p] + held[step, p, tx, t, :, lanes] * potential
+            for p in range(plan.panels):
+                value = jnp.where(counts[:, cells] > p, far[p], 0.0) if chunk == CHUNKS - 1 else far[p]
+                out[p, :, cells] = value
+        return carry
+
+    lax.fori_loop(0, plan.steps, body, 0)
 
 
 def gather(plan, chunk, counts, before, projection, high, low, pieces):
-    return pl.pallas_call(
-        functools.partial(gather_kernel, plan, chunk == CHUNKS - 1),
-        grid=(plan.steps,),
-        in_specs=[
-            count_spec(plan),
-            panel_spec(plan),
-            projection_spec(plan, chunk),
-            whole_spec(high.shape),
-            whole_spec(low.shape),
-            whole_spec(pieces.shape),
-        ],
-        out_specs=panel_spec(plan),
-        out_shape=jax.ShapeDtypeStruct(before.shape, jnp.float32),
-        scratch_shapes=[pltpu.VMEM((plan.steps * LANES, TZ * LANES), jnp.float32)],
-        compiler_params=pltpu.CompilerParams(vmem_limit_bytes=VMEM_LIMIT),
-        cost_estimate=projection_cost(projection),
-        name="depth_gather",
-    )(counts, before, projection, high, low, pieces)
+    kernel = functools.partial(gather_kernel, plan, chunk)
+    arrays = [counts, before, pieces, high, low]
+    return projection_call(plan, kernel, "depth_gather", arrays, projection, before.shape)
 
 
 def near_kernel(plan, extended, codes, blocks_ref, out):
@@ -505,16 +529,38 @@
     return jnp.stack([whole[:, i : i + planes] for i in range(3)], axis=1)
 
 
-def spectrum_weights(plan, spectrum):
+def first_weights(plan, spectrum):
     slab, cell = (lax.axis_index("slab"), lax.axis_index("cell"))
     by_depth = jnp.transpose(spectrum, (1, 2, 0))
-    own = lax.dynamic_slice_in_dim(by_depth, cell * plan.slabs, plan.slabs, 0)
-    dest = lax.broadcasted_iota(jnp.int32, own.shape, 0)
-    swapped = (cell == 0) & (slab >= plan.slabs // 2) & (dest == 0)
-    own = jnp.where(swapped, by_depth[plan.slots][None], own)
-    weights = lax.all_to_all(own, "slab", split_axis=0, concat_axis=0, tiled=True)
     far = lax.ppermute(by_depth[0, :1], "slab", [(plan.slabs // 2, 0)])
-    return (weights.reshape(plan.ny, plan.nx), far, by_depth[plan.slots, :1])
+    blocks = []
+    for j in range(plan.outer):
+        group = lax.rem(slab // plan.inner + j, plan.outer)
+        own = lax.dynamic_slice_in_dim(by_depth, cell * plan.slabs + group * plan.inner, plan.inner, 0)
+        dest = lax.broadcasted_iota(jnp.int32, own.shape, 0)
+        swapped = (cell == 0) & (slab >= plan.slabs // 2) & (group == 0) & (dest == 0)
+        own = jnp.where(swapped, by_depth[plan.slots][None], own)
+        if j > 0:
+            shift = j * plan.inner
+            own = lax.ppermute(own, "slab", [(i, (i + shift) % plan.slabs) for i in range(plan.slabs)])
+        blocks.append(own)
+    return (blocks, far, by_depth[plan.slots, :1])
+
+
+def second_weights(plan, blocks):
+    slab = lax.axis_index("slab")
+    strips = []
+    for i in range(plan.inner):
+        place = lax.rem(slab + i, plan.inner)
+        strip = jnp.concatenate([lax.dynamic_slice_in_dim(b, place, 1, 0) for b in blocks], axis=0)
+        if i > 0:
+            pairs = []
+            for source in range(plan.slabs):
+                group = source // plan.inner * plan.inner
+                pairs.append((source, group + (source + i) % plan.inner))
+            strip = lax.ppermute(strip, "slab", pairs)
+        strips.append(strip)
+    return strips
 
 
 def per_device(charges, counts, projection, near_blocks, neighbours, spectrum):
@@ -541,36 +587,44 @@
     def exchange(pieces):
         return lax.all_to_all(pieces, axes, split_axis=0, concat_axis=0, tiled=True)
 
+    def values(*shapes):
+        return [pltpu.VMEM(shape, jnp.float32) for shape in shapes]
+
     rows_shape = (plan.ny, 2 * plan.x_chunk)
     freq_shape = (2 * plan.ny, plan.x_chunk)
     both_shape = (2 * plan.ny, plan.nx)
-    weights, far, near = spectrum_weights(plan, spectrum)
+    blocks, far, near = first_weights(plan, spectrum)
     slot = lax.broadcasted_iota(jnp.int32, charges.shape, 0)
     masked = jnp.where(slot < counts[None], charges, 0.0)
     left, right = extend_rows(plan, masked)
     pieces = [project(plan, i, charges, counts, split_projection, *depth_forward) for i in range(CHUNKS)]
-    pieces[0], far, left, right = lax.optimization_barrier((pieces[0], far, left, right))
+    pieces[0], blocks[1], far = lax.optimization_barrier((pieces[0], blocks[1], far))
+    even_pieces = exchange(pieces[0])
+    pieces[1], left, right, *blocks[2:] = lax.optimization_barrier(
+        (pieces[1], left, right, *blocks[2:])
+    )
+    odd_pieces = exchange(pieces[1])
+    strips = second_weights(plan, blocks)
+    (even,) = plane_call(
+        plan, first_plane_kernel, "even_planes", me, [even_pieces], [(y_forward, None), (x_forward, 0)], [],
+        [both_shape], values(rows_shape, freq_shape), 2,
+    )
     edge = jnp.concatenate([far, near], axis=0)
-    extended = extend_planes(plan, masked, left, right)
-    even_pieces = exchange(pieces[0])
-    pieces[1], extended = lax.optimization_barrier((pieces[1], extended))
-    odd_pieces = exchange(pieces[1])
-    (even,) = plane_call(
-        plan, first_plane_kernel, "even_planes", (None, 0), me, [even_pieces], [y_forward, x_forward],
-        [both_shape], [rows_shape, freq_shape], 2,
-    )
-    total = near_field(plan, extended, neighbours, near_blocks)
-    even, total = lax.optimization_barrier((even, total))
+    late = [even, x_backward[0][:1], x_backward[1][:1], *y_backward]
+    copies = [pltpu.VMEM(array.shape, array.dtype) for array in late]
+    copies.append(pltpu.SemaphoreType.DMA((len(late) + plan.slabs,)))
     back, rest = plane_call(
-        plan, middle_plane_kernel, "middle_planes", (None, 1, 0, None), me,
-        [odd_pieces, even, weights, edge], [y_forward, x_forward, x_backward, y_backward],
-        [piece_shape(plan), freq_shape], [rows_shape, freq_shape, freq_shape], 4,
+        plan, middle_plane_kernel, "middle_planes", me, [edge, odd_pieces],
+        [(y_forward, None), (x_forward, 1)], late + strips, [piece_shape(plan), freq_shape],
+        values(rows_shape, freq_shape, freq_shape, (plan.ny, plan.nx)) + copies, 4,
     )
     even_back = exchange(back)
     (back,) = plane_call(
-        plan, last_plane_kernel, "odd_planes", (1, None), me, [rest], [x_backward, y_backward],
-        [piece_shape(plan)], [rows_shape], 2,
-    )
+        plan, last_plane_kernel, "odd_planes", me, [rest], [(x_backward, 1), (y_backward, None)], [],
+        [piece_shape(plan)], values(rows_shape), 2,
+    )
+    total = near_field(plan, extend_planes(plan, masked, left, right), neighbours, near_blocks)
+    back, total = lax.optimization_barrier((back, total))
     odd_back = exchange(back)
     total = gather(plan, 0, counts, total, split_projection, *depth_backward, even_back)
     return gather(plan, 1, counts, total, split_projection, *depth_backward, odd_back)

time: 185 us -> 194 us (1.049)
  local copies, waits for them, and re-layouts: 26.4 us -> 2.92 us
  starting transfers between devices: 28.2 us -> 41.1 us
  Pallas kernels: 54.9 us -> 64.5 us
  waiting for transfers between devices: 71.6 us -> 80.6 us
    unnamed x66 -> x16, local copies, waits for them, and re-layouts: 21.7 us -> 1 us
    all_to_all x4, waiting for transfers between devices: 46.2 us -> 26.2 us  [exchange(): return lax.all_to_all(pieces, axes, split_axis=0, concat_axis=0, tiled=True)]
    ppermute x1 -> x7, waiting for transfers between devices: 16 us -> 35.9 us  [the longest x3 24.6 us: first_weights(): lax.ppermute(own, 'slab', [(i, (i + shift) % plan.slabs) for i in range(p...]
    ppermute x1 -> x7, starting transfers between devices: 1.28 us -> 11.9 us  [the longest x3 7.27 us: first_weights(): lax.ppermute(own, 'slab', [(i, (i + shift) % plan.slabs) for i in range(p...]
    all_to_all x4, starting transfers between devices: 13 us -> 22.7 us  [exchange(): return lax.all_to_all(pieces, axes, split_axis=0, concat_axis=0, tiled=True)]
    ppermute x1, waiting for transfers between devices: 9.38 us -> 18.5 us  [extend_planes(): before = lax.ppermute(wide[:, -1:], 'slab', up)]
    all_to_all x1 -> x0, starting transfers between devices: 7.37 us -> none  [spectrum_weights(): lax.all_to_all(own, 'slab', split_axis=0, concat_axis=0, tiled=True)]
    pallas_call x3, Pallas kernels: 15.8 us -> 22.7 us  [plane_call(): pl.pallas_call(functools.partial(kernel, plan), grid=(1,), in_specs=[pl.B...]
  transfers between devices with their start and end apart: 10 -> 15, of which waited for: 6 -> 7; matrix products, arithmetic and copies ran while one was open for 2% -> 2% of each run, Pallas kernels for 21% -> 24%
where the time goes in v4:
time: 194 us; the launch traced here: 193 us
  waiting for transfers between devices  80.6 us (42%)
  Pallas kernels  64.5 us (33%)
  starting transfers between devices  41.1 us (21%)
  other arithmetic  3.9 us (2%)
  local copies, waits for them, and re-layouts  2.92 us (2%)
    pallas_call x4, Pallas kernels, projection_call(): pl.pallas_call(kernel, grid=(1,), in_specs=[whole_spec(array.shape) for a...  26.2 us
    all_to_all x4, waiting for transfers between devices, exchange(): return lax.all_to_all(pieces, axes, split_axis=0, concat_axis=0, tiled=True)  26.2 us
    ppermute x3, waiting for transfers between devices, first_weights(): lax.ppermute(own, 'slab', [(i, (i + shift) % plan.slabs) for i in range(p...  24.6 us
    pallas_call x3, Pallas kernels, plane_call(): pl.pallas_call(functools.partial(kernel, plan), grid=(1,), in_specs=[pl.B...  22.7 us
    all_to_all x4, starting transfers between devices, exchange(): return lax.all_to_all(pieces, axes, split_axis=0, concat_axis=0, tiled=True)  22.7 us
    ppermute x1, waiting for transfers between devices, extend_planes(): before = lax.ppermute(wide[:, -1:], 'slab', up)  18.5 us
    pallas_call x1, Pallas kernels, near_field(): pl.pallas_call(functools.partial(near_kernel, plan), grid=(plan.cell_cols...  15.5 us
    ppermute x3, waiting for transfers between devices, second_weights(): strip = lax.ppermute(strip, 'slab', pairs)  11.3 us
  transfers between devices with their start and end apart: 15, of which 7 were waited for; matrix products, arithmetic and copies ran while one was open for 2% of the time, Pallas kernels for 24%

profile of v4, /device:TPU:0, one launch (start us, length us, event | category | flops | bytes accessed | tf_op | source)
XLA Modules:
  0.0 193.4 jit_solution(11002636995783183808)
XLA Ops:
  0.0 0.8 slice_bitcast_fusion
  0.9 1.3 bitcast_select_fusion
  2.2 3.1 %collective-permute-start = (f32[4,32,512]{2,1,0:T(8,128)S(1)}, f32[4,32,512]{2,1,0:T(8,128)S(1)}, u32[]{:S(2)}, u32[]{:S(2)}) collective-permute-start(f32[4,32,512]{2,1,0:T(8,128)S(1)} %get-tuple-element.31), channel_id=1, source_target_pairs={{0,8},{2,10},{4,12},{6,14},{8,16},{10,18},{12,20},{14,22},{16,24},... | collective-permute-start | bytes 786440 | tf_op jit(solution)/shard_map/ppermute | solution.py:545
  5.3 0.7 slice_bitcast_fusion.2
  6.0 1.3 collective-permute-start.1
  7.3 0.0 copy-start.2
  7.3 0.0 copy-start.4
  7.3 7.1 %project_depth.2 = f32[32,2,4,8,128]{4,3,2,1,0:T(8,128)} custom-call(f32[8,8,1024]{2,1,0:T(8,128)} %charges.3, s32[8,1024]{1,0:T(8,128)} %counts.7, bf16[512,512]{1,0:T(8,128)(2,1)} %constant.87.clone.high, bf16[512,512]{1,0:T(8,128)(2,1)} %constant.88.clone.low, f32[8,2,2,16,8,1024]{5,4,3,2,1,0:T(8,128)} %bitcast.26), custom_call_target="tpu_custom_call" | custom-call | flops 4194304 | bytes 8388608 | tf_op jit(solution)/shard_map/project_depth/pallas_call | solution.py:190
  14.4 0.0 collective-permute-done.1
  14.4 0.0 collective-permute-done
  14.4 4.9 %all-to-all-start.1 = ((f32[32,2,4,8,128]{4,3,2,1,0:T(8,128)}), f32[32,2,4,8,128]{4,3,2,1,0:T(8,128)S(1)}, u32[]{:S(2)}, u32[]{:S(2)}) async-start(f32[32,2,4,8,128]{4,3,2,1,0:T(8,128)} %project_depth.2), calls=%async_computation.1 | async-start | bytes 2097152 | tf_op jit(solution)/shard_map/all_to_all | solution.py:588
  19.3 2.7 %collective-permute-start.4 = (f32[4,32,512]{2,1,0:T(8,128)S(1)}, f32[4,32,512]{2,1,0:T(8,128)S(1)}, u32[]{:S(2)}, u32[]{:S(2)}) collective-permute-start(f32[4,32,512]{2,1,0:T(8,128)S(1)} %get-tuple-element.30), channel_id=1, source_target_pairs={{0,16},{2,18},{4,20},{6,22},{8,24},{10,26},{12,28},{14,30},{16,0},... | collective-permute-start | bytes 786440 | tf_op jit(solution)/shard_map/ppermute | solution.py:545
  22.0 1.5 collective-permute-start.5
  23.5 0.0 copy-done.2
  23.5 0.0 copy-done.4
  23.5 0.1 fusion.4
  23.6 1.5 collective-permute-start.3
  25.1 0.6 collective-permute-start.2
  25.6 7.0 %project_depth.3 = f32[32,2,4,8,128]{4,3,2,1,0:T(8,128)} custom-call(f32[8,8,1024]{2,1,0:T(8,128)} %charges.3, s32[8,1024]{1,0:T(8,128)} %counts.7, bf16[512,512]{1,0:T(8,128)(2,1)} %constant.87.clone.high, bf16[512,512]{1,0:T(8,128)(2,1)} %constant.88.clone.low, f32[8,2,2,16,8,1024]{5,4,3,2,1,0:T(8,128)} %bitcast.27), custom_call_target="tpu_custom_call" | custom-call | flops 4194304 | bytes 8388608 | tf_op jit(solution)/shard_map/project_depth/pallas_call | solution.py:190
  32.7 0.0 collective-permute-done.3
  32.7 0.0 collective-permute-done.2
  32.7 24.6 %collective-permute-done.4 = f32[4,32,512]{2,1,0:T(8,128)S(1)} collective-permute-done((f32[4,32,512]{2,1,0:T(8,128)S(1)}, f32[4,32,512]{2,1,0:T(8,128)S(1)}, u32[]{:S(2)}, u32[]{:S(2)}) %collective-permute-start.4) | collective-permute-done | bytes 262176 | tf_op jit(solution)/shard_map/ppermute | solution.py:545
  57.3 0.0 collective-permute-done.5
  57.3 0.0 all-to-all-done.1.pieces
  57.3 0.0 copy-start.3
  57.3 8.9 %all-to-all-start = ((f32[32,2,4,8,128]{4,3,2,1,0:T(8,128)}), f32[32,2,4,8,128]{4,3,2,1,0:T(8,128)}, u32[]{:S(2)}, u32[]{:S(2)}) async-start(f32[32,2,4,8,128]{4,3,2,1,0:T(8,128)} %project_depth.3), calls=%async_computation | async-start | bytes 2097152 | tf_op jit(solution)/shard_map/all_to_all | solution.py:588
  66.4 0.2 collective-permute-start.6
  66.6 1.7 collective-permute-start.7
  68.4 1.4 collective-permute-start.8
  69.7 0.7 pad_maximum_fusion.3.refs_5_
  70.5 0.6 pad_maximum_fusion.7.edge
  71.0 0.0 copy-done.3
  71.1 5.8 %even_planes.1.refs_0_ = f32[1024,512]{1,0:T(8,128)} custom-call(s32[1]{0:T(128)} %bitcast.me_ref, f32[32,2,4,8,128]{4,3,2,1,0:T(8,128)} %copy-done.3, bf16[2,512,256]{2,1,0:T(8,128)(2,1)} %constant.89.clone.y_high.yf_high, bf16[2,512,256]{2,1,0:T(8,128)(2,1)} %constant.90.clone.y_low.yf_low, bf16[2,256,512]{2,1,0:T(8,128)(2,1)} %constant.91.clone.x_high.xf_high, ...), custom_call_target="tpu_custom_call" | custom-call | flops 1610612736 | bytes 3145728 | tf_op jit(solution)/shard_map/even_planes/pallas_call | solution.py:392
  76.9 5.6 %collective-permute-done.6.refs_6_ = f32[4,32,512]{2,1,0:T(8,128)S(1)} collective-permute-done((f32[4,32,512]{2,1,0:T(8,128)S(1)}, f32[4,32,512]{2,1,0:T(8,128)S(1)}, u32[]{:S(2)}, u32[]{:S(2)}) %collective-permute-start.6) | collective-permute-done | bytes 262176 | tf_op jit(solution)/shard_map/ppermute | solution.py:561
  82.5 0.0 copy-start.5
  82.5 1.3 collective-permute-done.7.refs_7_
  83.8 0.0 copy-start.6
  83.8 4.5 %collective-permute-done.8.refs_8_ = f32[4,32,512]{2,1,0:T(8,128)S(1)} collective-permute-done((f32[4,32,512]{2,1,0:T(8,128)S(1)}, f32[4,32,512]{2,1,0:T(8,128)S(1)}, u32[]{:S(2)}, u32[]{:S(2)}) %collective-permute-start.8) | collective-permute-done | bytes 262176 | tf_op jit(solution)/shard_map/ppermute | solution.py:561
  88.2 0.0 copy-start.7
  88.2 5.1 %all-to-all-done.pieces = f32[32,2,4,8,128]{4,3,2,1,0:T(8,128)} async-done(((f32[32,2,4,8,128]{4,3,2,1,0:T(8,128)}), f32[32,2,4,8,128]{4,3,2,1,0:T(8,128)}, u32[]{:S(2)}, u32[]{:S(2)}) %all-to-all-start) | async-done | bytes 1048608 | tf_op jit(solution)/shard_map/all_to_all | solution.py:588
  93.3 0.0 copy-done.5
  93.3 0.0 copy-done.6
  93.3 0.0 copy-done.7
  93.3 11.2 %middle_planes.1 = (f32[32,2,4,8,128]{4,3,2,1,0:T(8,128)}, f32[1024,256]{1,0:T(8,128)}) custom-call(s32[1]{0:T(128)} %bitcast.me_ref, f32[2,512]{1,0:T(2,128)} %pad_maximum_fusion.7.edge, f32[32,2,4,8,128]{4,3,2,1,0:T(8,128)} %all-to-all-done.pieces, bf16[2,512,256]{2,1,0:T(8,128)(2,1)} %constant.89.clone.y_high.yf_high, ...), custom_call_target="tpu_custom_call" | custom-call | flops 3221225472 | bytes 9441280 | tf_op jit(solution)/shard_map/middle_planes/pallas_call | solution.py:392
  104.5 2.7 %all-to-all-start.2 = ((f32[32,2,4,8,128]{4,3,2,1,0:T(8,128)}), f32[32,2,4,8,128]{4,3,2,1,0:T(8,128)S(1)}, u32[]{:S(2)}, u32[]{:S(2)}) async-start(f32[32,2,4,8,128]{4,3,2,1,0:T(8,128)} %get-tuple-element.27), calls=%async_computation.2 | async-start | bytes 2097152 | tf_op jit(solution)/shard_map/all_to_all | solution.py:588
  107.2 0.1 concatenate.30
  107.3 0.1 fusion.3
  107.4 0.3 collective-permute-start.9
  107.7 4.2 %collective-permute-start.10 = (f32[8,1,1280]{2,1,0:T(1,128)S(1)}, f32[8,1,1280]{2,1,0:T(1,128)S(1)}, u32[]{:S(2)}, u32[]{:S(2)}) collective-permute-start(f32[8,1,1280]{2,1,0:T(1,128)S(1)} %get-tuple-element.38), channel_id=1, source_target_pairs={{2,0},{4,2},{6,4},{8,6},{10,8},{12,10},{14,12},{16,14},{18,16},{20... | collective-permute-start | bytes 122888 | tf_op jit(solution)/shard_map/ppermute | solution.py:526
  111.9 18.5 %collective-permute-done.9 = f32[8,1,1280]{2,1,0:T(1,128)S(1)} collective-permute-done((f32[8,1,1280]{2,1,0:T(1,128)S(1)}, f32[8,1,1280]{2,1,0:T(1,128)S(1)}, u32[]{:S(2)}, u32[]{:S(2)}) %collective-permute-start.9) | collective-permute-done | bytes 40992 | tf_op jit(solution)/shard_map/ppermute | solution.py:525
  130.4 0.0 collective-permute-done.10
  130.4 0.1 fusion.1
  130.5 1.0 pad_maximum_fusion.extended
  131.5 15.5 %near_blocks.1.before = f32[8,8,1024]{2,1,0:T(8,128)} custom-call(f32[8,3,8,1280]{3,2,1,0:T(8,128)} %pad_maximum_fusion.extended, s32[6,8,1024]{2,1,0:T(8,128)} %codes.1, f32[6,8,8,8,1024]{4,3,2,1,0:T(8,128)} %blocks_ref.1), custom_call_target="tpu_custom_call" | custom-call | flops 6291456 | bytes 12582912 | tf_op jit(solution)/shard_map/near_blocks/pallas_call | solution.py:488
  147.0 5.7 %odd_planes.1 = f32[32,2,4,8,128]{4,3,2,1,0:T(8,128)} custom-call(s32[1]{0:T(128)} %bitcast.me_ref, f32[1024,256]{1,0:T(8,128)} %get-tuple-element.23.freqs, bf16[2,256,512]{2,1,0:T(8,128)(2,1)} %constant.97.clone.x_high, bf16[2,256,512]{2,1,0:T(8,128)(2,1)} %constant.98.clone.x_low, bf16[2,512,256]{2,1,0:T(8,128)(2,1)} %constant.95.clone.refs_3_.y_high, ...), custom_call_target="tpu_custom_call" | custom-call | flops 1610612736 | bytes 3145728 | tf_op jit(solution)/shard_map/odd_planes/pallas_call | solution.py:392
  152.7 0.0 all-to-all-done.2.pieces
  152.7 0.0 copy-start
  152.7 6.3 %all-to-all-start.3 = ((f32[32,2,4,8,128]{4,3,2,1,0:T(8,128)}), f32[32,2,4,8,128]{4,3,2,1,0:T(8,128)S(1)}, u32[]{:S(2)}, u32[]{:S(2)}) async-start(f32[32,2,4,8,128]{4,3,2,1,0:T(8,128)} %odd_planes.1), calls=%async_computation.3 | async-start | bytes 2097152 | tf_op jit(solution)/shard_map/all_to_all | solution.py:588
  159.0 0.0 copy-done
  159.0 6.1 %depth_gather.2.before = f32[8,8,1024]{2,1,0:T(8,128)} custom-call(s32[8,1024]{1,0:T(8,128)} %counts.7, f32[8,8,1024]{2,1,0:T(8,128)} %near_blocks.1.before, f32[32,2,4,8,128]{4,3,2,1,0:T(8,128)} %copy-done, bf16[512,512]{1,0:T(8,128)(2,1)} %constant.99.clone.high, bf16[512,512]{1,0:T(8,128)(2,1)} %constant.100.clone.low, f32[8,2,2,16,8,1024]{5,4,3,2,1,0:T(8,128)} %bitcast.28), custom_call_target="tpu_custom_call" | custom-call | flops 4194304 | bytes 8388608 | tf_op jit(solution)/shard_map/depth_gather/pallas_call | solution.py:190
  165.1 21.1 %all-to-all-done.3.pieces = f32[32,2,4,8,128]{4,3,2,1,0:T(8,128)S(1)} async-done(((f32[32,2,4,8,128]{4,3,2,1,0:T(8,128)}), f32[32,2,4,8,128]{4,3,2,1,0:T(8,128)S(1)}, u32[]{:S(2)}, u32[]{:S(2)}) %all-to-all-start.3) | async-done | bytes 1048608 | tf_op jit(solution)/shard_map/all_to_all | solution.py:588
  186.2 0.0 copy-start.1
  186.2 1.0 copy-done.1
  187.2 6.1 %depth_gather.3 = f32[8,8,1024]{2,1,0:T(8,128)} custom-call(s32[8,1024]{1,0:T(8,128)} %counts.7, f32[8,8,1024]{2,1,0:T(8,128)} %depth_gather.2.before, f32[32,2,4,8,128]{4,3,2,1,0:T(8,128)} %copy-done.1, bf16[512,512]{1,0:T(8,128)(2,1)} %constant.99.clone.high, bf16[512,512]{1,0:T(8,128)(2,1)} %constant.100.clone.low, f32[8,2,2,16,8,1024]{5,4,3,2,1,0:T(8,128)} %bitcast.29), custom_call_target="tpu_custom_call" | custom-call | flops 4194304 | bytes 8388608 | tf_op jit(solution)/shard_map/depth_gather/pallas_call | solution.py:190
  (11 shorter events, 0.2 us)
Async XLA Ops:
  2.2 12.2 %collective-permute-start = (f32[4,32,512]{2,1,0:T(8,128)S(1)}, f32[4,32,512]{2,1,0:T(8,128)S(1)}, u32[]{:S(2)}, u32[]{:S(2)}) collective-permute-start(f32[4,32,512]{2,1,0:T(8,128)S(1)} %get-tuple-element.31), channel_id=1, source_target_pairs={{0,8},{2,10},{4,12},{6,14},{8,16},{10,18},{12,20},{14,22},{16,24},... | collective-permute-start | bytes 786440 | tf_op jit(solution)/shard_map/ppermute | solution.py:545
  6.0 8.4 %collective-permute-start.1 = (f32[1,512]{1,0:T(1,128)S(1)}, f32[1,512]{1,0:T(1,128)S(1)}, u32[]{:S(2)}, u32[]{:S(2)}) collective-permute-start(f32[1,512]{1,0:T(1,128)S(1)} %get-tuple-element.33), channel_id=1, source_target_pairs={{16,0},{17,1}} | collective-permute-start | bytes 6152 | tf_op jit(solution)/shard_map/ppermute | solution.py:535
  7.3 16.2 %copy-start.2 = (f32[8,8,1024]{2,1,0:T(8,128)S(1)}, f32[8,8,1024]{2,1,0:T(8,128)}, u32[]{:S(2)}) copy-start(f32[8,8,1024]{2,1,0:T(8,128)} %charges.3) | copy-start | bytes 786436
  7.3 16.2 %copy-start.4 = (s32[8,1024]{1,0:T(8,128)S(1)}, s32[8,1024]{1,0:T(8,128)}, u32[]{:S(2)}) copy-start(s32[8,1024]{1,0:T(8,128)} %counts.7) | copy-start | bytes 98308
  14.4 42.9 %all-to-all-start.1 = ((f32[32,2,4,8,128]{4,3,2,1,0:T(8,128)}), f32[32,2,4,8,128]{4,3,2,1,0:T(8,128)S(1)}, u32[]{:S(2)}, u32[]{:S(2)}) async-start(f32[32,2,4,8,128]{4,3,2,1,0:T(8,128)} %project_depth.2), calls=%async_computation.1 | async-start | bytes 2097152 | tf_op jit(solution)/shard_map/all_to_all | solution.py:588
  19.3 38.0 %collective-permute-start.4 = (f32[4,32,512]{2,1,0:T(8,128)S(1)}, f32[4,32,512]{2,1,0:T(8,128)S(1)}, u32[]{:S(2)}, u32[]{:S(2)}) collective-permute-start(f32[4,32,512]{2,1,0:T(8,128)S(1)} %get-tuple-element.30), channel_id=1, source_target_pairs={{0,16},{2,18},{4,20},{6,22},{8,24},{10,26},{12,28},{14,30},{16,0},... | collective-permute-start | bytes 786440 | tf_op jit(solution)/shard_map/ppermute | solution.py:545
  22.0 35.2 %collective-permute-start.5 = (f32[4,32,512]{2,1,0:T(8,128)S(1)}, f32[4,32,512]{2,1,0:T(8,128)S(1)}, u32[]{:S(2)}, u32[]{:S(2)}) collective-permute-start(f32[4,32,512]{2,1,0:T(8,128)S(1)} %get-tuple-element.32), channel_id=1, source_target_pairs={{0,24},{2,26},{4,28},{6,30},{8,0},{10,2},{12,4},{14,6},{16,8},{18,... | collective-permute-start | bytes 786440 | tf_op jit(solution)/shard_map/ppermute | solution.py:545
  23.6 9.1 %collective-permute-start.3 = (f32[8,8,16]{2,1,0:T(8,128)S(1)}, f32[8,8,16]{2,1,0:T(8,128)S(1)}, u32[]{:S(2)}, u32[]{:S(2)}) collective-permute-start(f32[8,8,16]{2,1,0:T(8,128)S(1)} %get-tuple-element.55), channel_id=1, source_target_pairs={{1,0},{0,1},{3,2},{2,3},{5,4},{4,5},{7,6},{6,7},{9,8},{8,9},{11,10... | collective-permute-start | bytes 12296 | tf_op jit(solution)/shard_map/ppermute | solution.py:517
  25.1 7.6 %collective-permute-start.2 = (f32[8,8,16]{2,1,0:T(8,128)S(1)}, f32[8,8,16]{2,1,0:T(8,128)S(1)}, u32[]{:S(2)}, u32[]{:S(2)}) collective-permute-start(f32[8,8,16]{2,1,0:T(8,128)S(1)} %get-tuple-element.56), channel_id=1, source_target_pairs={{0,1},{1,0},{2,3},{3,2},{4,5},{5,4},{6,7},{7,6},{8,9},{9,8},{10,11... | collective-permute-start | bytes 12296 | tf_op jit(solution)/shard_map/ppermute | solution.py:516
  57.3 13.8 %copy-start.3 = (f32[32,2,4,8,128]{4,3,2,1,0:T(8,128)}, f32[32,2,4,8,128]{4,3,2,1,0:T(8,128)S(1)}, u32[]{:S(2)}) copy-start(f32[32,2,4,8,128]{4,3,2,1,0:T(8,128)S(1)} %all-to-all-done.1.pieces) | copy-start | bytes 3145732
  57.3 36.0 %all-to-all-start = ((f32[32,2,4,8,128]{4,3,2,1,0:T(8,128)}), f32[32,2,4,8,128]{4,3,2,1,0:T(8,128)}, u32[]{:S(2)}, u32[]{:S(2)}) async-start(f32[32,2,4,8,128]{4,3,2,1,0:T(8,128)} %project_depth.3), calls=%async_computation | async-start | bytes 2097152 | tf_op jit(solution)/shard_map/all_to_all | solution.py:588
  66.4 16.1 %collective-permute-start.6 = (f32[4,32,512]{2,1,0:T(8,128)S(1)}, f32[4,32,512]{2,1,0:T(8,128)S(1)}, u32[]{:S(2)}, u32[]{:S(2)}) collective-permute-start(f32[4,32,512]{2,1,0:T(8,128)S(1)} %pad_maximum_fusion.4), channel_id=1, source_target_pairs={{0,2},{2,4},{4,6},{6,0},{8,10},{10,12},{12,14},{14,8},{16,18},{18,... | collective-permute-start | bytes 786440 | tf_op jit(solution)/shard_map/ppermute | solution.py:561
  66.6 17.1 %collective-permute-start.7 = (f32[4,32,512]{2,1,0:T(8,128)S(1)}, f32[4,32,512]{2,1,0:T(8,128)S(1)}, u32[]{:S(2)}, u32[]{:S(2)}) collective-permute-start(f32[4,32,512]{2,1,0:T(8,128)S(1)} %pad_maximum_fusion.5), channel_id=1, source_target_pairs={{0,4},{2,6},{4,0},{6,2},{8,12},{10,14},{12,8},{14,10},{16,20},{18,... | collective-permute-start | bytes 786440 | tf_op jit(solution)/shard_map/ppermute | solution.py:561
  68.4 19.9 %collective-permute-start.8 = (f32[4,32,512]{2,1,0:T(8,128)S(1)}, f32[4,32,512]{2,1,0:T(8,128)S(1)}, u32[]{:S(2)}, u32[]{:S(2)}) collective-permute-start(f32[4,32,512]{2,1,0:T(8,128)S(1)} %pad_maximum_fusion.6), channel_id=1, source_target_pairs={{0,6},{2,0},{4,2},{6,4},{8,14},{10,8},{12,10},{14,12},{16,22},{18,... | collective-permute-start | bytes 786440 | tf_op jit(solution)/shard_map/ppermute | solution.py:561
  82.5 10.8 %copy-start.5 = (f32[4,32,512]{2,1,0:T(8,128)}, f32[4,32,512]{2,1,0:T(8,128)S(1)}, u32[]{:S(2)}) copy-start(f32[4,32,512]{2,1,0:T(8,128)S(1)} %collective-permute-done.6.refs_6_) | copy-start | bytes 786436
  83.8 9.6 %copy-start.6 = (f32[4,32,512]{2,1,0:T(8,128)}, f32[4,32,512]{2,1,0:T(8,128)S(1)}, u32[]{:S(2)}) copy-start(f32[4,32,512]{2,1,0:T(8,128)S(1)} %collective-permute-done.7.refs_7_) | copy-start | bytes 786436
  88.2 5.1 %copy-start.7 = (f32[4,32,512]{2,1,0:T(8,128)}, f32[4,32,512]{2,1,0:T(8,128)S(1)}, u32[]{:S(2)}) copy-start(f32[4,32,512]{2,1,0:T(8,128)S(1)} %collective-permute-done.8.refs_8_) | copy-start | bytes 786436
  104.5 48.2 %all-to-all-start.2 = ((f32[32,2,4,8,128]{4,3,2,1,0:T(8,128)}), f32[32,2,4,8,128]{4,3,2,1,0:T(8,128)S(1)}, u32[]{:S(2)}, u32[]{:S(2)}) async-start(f32[32,2,4,8,128]{4,3,2,1,0:T(8,128)} %get-tuple-element.27), calls=%async_computation.2 | async-start | bytes 2097152 | tf_op jit(solution)/shard_map/all_to_all | solution.py:588
  107.4 22.9 %collective-permute-start.9 = (f32[8,1,1280]{2,1,0:T(1,128)S(1)}, f32[8,1,1280]{2,1,0:T(1,128)S(1)}, u32[]{:S(2)}, u32[]{:S(2)}) collective-permute-start(f32[8,1,1280]{2,1,0:T(1,128)S(1)} %get-tuple-element.37), channel_id=1, source_target_pairs={{0,2},{2,4},{4,6},{6,8},{8,10},{10,12},{12,14},{14,16},{16,18},{18... | collective-permute-start | bytes 122888 | tf_op jit(solution)/shard_map/ppermute | solution.py:525
  107.7 22.6 %collective-permute-start.10 = (f32[8,1,1280]{2,1,0:T(1,128)S(1)}, f32[8,1,1280]{2,1,0:T(1,128)S(1)}, u32[]{:S(2)}, u32[]{:S(2)}) collective-permute-start(f32[8,1,1280]{2,1,0:T(1,128)S(1)} %get-tuple-element.38), channel_id=1, source_target_pairs={{2,0},{4,2},{6,4},{8,6},{10,8},{12,10},{14,12},{16,14},{18,16},{20... | collective-permute-start | bytes 122888 | tf_op jit(solution)/shard_map/ppermute | solution.py:526
  152.7 6.3 %copy-start = (f32[32,2,4,8,128]{4,3,2,1,0:T(8,128)}, f32[32,2,4,8,128]{4,3,2,1,0:T(8,128)S(1)}, u32[]{:S(2)}) copy-start(f32[32,2,4,8,128]{4,3,2,1,0:T(8,128)S(1)} %all-to-all-done.2.pieces) | copy-start | bytes 3145732
  152.7 33.5 %all-to-all-start.3 = ((f32[32,2,4,8,128]{4,3,2,1,0:T(8,128)}), f32[32,2,4,8,128]{4,3,2,1,0:T(8,128)S(1)}, u32[]{:S(2)}, u32[]{:S(2)}) async-start(f32[32,2,4,8,128]{4,3,2,1,0:T(8,128)} %odd_planes.1), calls=%async_computation.3 | async-start | bytes 2097152 | tf_op jit(solution)/shard_map/all_to_all | solution.py:588
  186.2 1.0 copy-start.1

commit v5 on v4

--- a/solution.py
+++ b/solution.py
@@ -44,8 +44,9 @@
         self.steps = cell_cols // (LANES * self.step_blocks) if self.step_blocks else 0
         self.x_chunk = nx // CHUNKS
         self.ky_local = ny // slabs
-        self.outer = math.gcd(slabs, 4)
-        self.inner = slabs // self.outer
+        self.half = slabs // 2
+        self.outer = math.gcd(self.half, 2)
+        self.inner = self.half // self.outer
 
     def fits(self):
         return (
@@ -129,45 +130,37 @@
     return parts
 
 
-def lane_copies(plan, chunk, projection, held, sems):
-    width = plan.step_blocks * LANES
+def tile_copies(plan, chunk, projection, held, sems):
     return [
-        pltpu.make_async_copy(
-            projection.at[:, :, chunk, :, :, pl.ds(step * width, width)], held.at[step], sems.at[step]
-        )
-        for step in range(plan.steps)
+        pltpu.make_async_copy(projection.at[:, tx, chunk], held.at[tx], sems.at[tx])
+        for tx in range(plan.tx_chunk)
     ]
-
-
-def wait_lanes(held, sems, step):
-    pltpu.make_async_copy(held.at[step], held.at[step], sems.at[step]).wait()
 
 
 def project_kernel(plan, chunk, charges, counts, high, low, projection, out, scratch, held, sems):
     planes = plan.cell_planes
-    for copy in lane_copies(plan, chunk, projection, held, sems):
+    copies = tile_copies(plan, chunk, projection, held, sems)
+    for copy in copies:
         copy.start()
-
-    def body(step, carry):
-        wait_lanes(held, sems, step)
-        for block in range(plan.step_blocks):
-            start = pl.multiple_of((step * plan.step_blocks + block) * LANES, LANES)
-            count = counts[:, pl.ds(start, LANES)]
-            own = [jnp.where(count > p, charges[p, :, pl.ds(start, LANES)], 0.0) for p in range(plan.panels)]
-            lanes = slice(block * LANES, (block + 1) * LANES)
-            for tx in range(plan.tx_chunk):
-                for ty in range(TY):
-                    row = step * LANES + ((block * TY + ty) * plan.tx_chunk + tx) * planes
-                    rows = pl.ds(pl.multiple_of(row, planes), planes)
-                    for tz in range(TZ):
-                        t = ty * TZ + tz
-                        total = held[step, 0, tx, t, :, lanes] * own[0]
-                        for p in range(1, plan.panels):
-                            total = total + held[step, p, tx, t, :, lanes] * own[p]
-                        scratch[rows, tz * LANES : (tz + 1) * LANES] = total
-        return carry
-
-    lax.fori_loop(0, plan.steps, body, 0)
+    for tx, copy in enumerate(copies):
+        copy.wait()
+
+        def body(place, carry, tx=tx):
+            lanes = pl.ds(pl.multiple_of(place * LANES, LANES), LANES)
+            count = counts[:, lanes]
+            own = [jnp.where(count > p, charges[p, :, lanes], 0.0) for p in range(plan.panels)]
+            for ty in range(TY):
+                row = ((place * TY + ty) * plan.tx_chunk + tx) * planes
+                rows = pl.ds(pl.multiple_of(row, planes), planes)
+                for tz in range(TZ):
+                    t = ty * TZ + tz
+                    total = held[tx, 0, t, :, lanes] * own[0]
+                    for p in range(1, plan.panels):
+                        total = total + held[tx, p, t, :, lanes] * own[p]
+                    scratch[rows, tz * LANES : (tz + 1) * LANES] = total
+            return carry
+
+        lax.fori_loop(0, plan.steps * plan.step_blocks, body, 0)
     spectra = product((high[...], low[...]), split(scratch[...]), ((1,), (1,)))
     shape = (plan.slots, 2, plan.row_block, LANES)
     for step in range(plan.steps):
@@ -175,7 +168,8 @@
 
 
 def held_shape(plan):
-    return (plan.steps, plan.panels, plan.tx_chunk, TY * TZ, plan.cell_planes, plan.step_blocks * LANES)
+    cols = plan.steps * plan.step_blocks * LANES
+    return (plan.tx_chunk, plan.panels, TY * TZ, plan.cell_planes, cols)
 
 
 def piece_shape(plan):
@@ -196,7 +190,7 @@
         scratch_shapes=[
             pltpu.VMEM((plan.steps * LANES, TZ * LANES), jnp.float32),
             pltpu.VMEM(held_shape(plan), jnp.float32),
-            pltpu.SemaphoreType.DMA((plan.steps,)),
+            pltpu.SemaphoreType.DMA((plan.tx_chunk,)),
         ],
         compiler_params=pltpu.CompilerParams(vmem_limit_bytes=VMEM_LIMIT),
         cost_estimate=pl.CostEstimate(
@@ -214,7 +208,14 @@
     return projection_call(plan, kernel, "project_depth", arrays, projection, piece_shape(plan))
 
 
-def forward_plane(plan, special, pieces, y_table, x_table, rows_ref, freq_ref):
+def far_sign(plan, me_ref):
+    slab = lax.rem(me_ref[0], plan.slabs)
+    return jnp.where(slab >= plan.half, -1.0, 1.0)
+
+
+def forward_plane(plan, me_ref, pieces, y_table, x_table, rows_ref, freq_ref):
+    special = me_ref[0] == 0
+    sign = far_sign(plan, me_ref)
     rows = 2 * plan.steps * plan.row_block
     width = plan.x_chunk
     middle = plan.ny // 2
@@ -224,6 +225,8 @@
             parts = [pieces[first + i].reshape(rows, LANES) for i in range(plan.y_lanes)]
             parts = swap_groups(parts, plan.width)
             for place, value in enumerate(parts):
+                if place % 2 == 1:
+                    value = value * sign
                 for part in range(2):
                     for step in range(plan.steps):
                         source = (part * plan.steps + step) * plan.row_block
@@ -232,74 +235,58 @@
                         rows_ref[row : row + plan.row_block, col : col + LANES] = value[
                             source : source + plan.row_block
                         ]
-    high, low = y_table
-    even = product((high[0], low[0]), split(rows_ref[:middle]))
-    odd = product((high[1], low[1]), split(rows_ref[middle:]))
-    for upper, sums in ((0, even + odd), (1, even - odd)):
-        cosine, sine = (sums[:middle], sums[middle:])
-        start = upper * middle
-        freq_ref[start : start + middle] = cosine[:, :width] + sine[:, width:]
-        start += plan.ny
-        freq_ref[start : start + middle] = cosine[:, width:] - sine[:, :width]
+    sums = product((y_table[0][...], y_table[1][...]), split(rows_ref[...]))
+    cos_re, cos_im = (sums[:middle, :width], sums[:middle, width:])
+    sin_re, sin_im = (sums[middle:, :width], sums[middle:, width:])
+    first = lax.broadcasted_iota(jnp.int32, (middle, width), 0) == 0
+
+    @pl.when(jnp.logical_not(special))
+    def _():
+        freq_ref[:middle] = jnp.where(first, cos_re, cos_re + sin_im)
+        freq_ref[middle : 2 * middle] = jnp.where(first, cos_im, cos_im - sin_re)
+        freq_ref[2 * middle : 3 * middle] = jnp.where(first, sin_re, cos_re - sin_im)
+        freq_ref[3 * middle :] = jnp.where(first, sin_im, cos_im + sin_re)
 
     @pl.when(special)
     def _():
-        row = lax.broadcasted_iota(jnp.int32, (middle, width), 0)
-        below, above = (even + odd, even - odd)
-        for upper, sums, other in ((0, below, above), (1, above, below)):
-            cols = slice(upper * width, (upper + 1) * width)
-            start = upper * middle
-            freq_ref[start : start + middle] = sums[:middle, cols]
-            start += plan.ny
-            freq_ref[start : start + middle] = jnp.where(row == 0, other[0:1, cols], -sums[middle:, cols])
-
-    high, low = x_table
-    return product(split(freq_ref[...]), (high[0], low[0]))
-
-
-def backward_plane(plan, special, freqs, x_table, y_table, out, rows_ref):
+        freq_ref[:middle] = cos_re
+        freq_ref[middle : 2 * middle] = jnp.where(first, sin_re, -sin_re)
+        freq_ref[2 * middle : 3 * middle] = cos_im
+        freq_ref[3 * middle :] = sin_im
+
+    return product(split(freq_ref[...]), (x_table[0][0], x_table[1][0]))
+
+
+def backward_plane(plan, me_ref, freqs, x_table, y_table, out, rows_ref):
+    special = me_ref[0] == 0
+    sign = far_sign(plan, me_ref)
     width = plan.x_chunk
     middle = plan.ny // 2
-    high, low = x_table
-    sums = product(split(freqs), (high[0], low[0]))
-    real = sums[: plan.ny, :width] - sums[plan.ny :, width:]
-    imag = sums[plan.ny :, :width] + sums[: plan.ny, width:]
-    high, low = y_table
+    sums = product(split(freqs), (x_table[0][0], x_table[1][0]))
+    parts = []
+    for mirrored, turn in ((0, 1.0), (1, -1.0)):
+        re = slice(2 * mirrored * middle, (2 * mirrored + 1) * middle)
+        im = slice((2 * mirrored + 1) * middle, (2 * mirrored + 2) * middle)
+        parts.append(sums[re, :width] - turn * sums[im, width:])
+        parts.append(sums[im, :width] + turn * sums[re, width:])
+    re_n, im_n, re_m, im_m = parts
+    first = lax.broadcasted_iota(jnp.int32, (middle, width), 0) == 0
 
     @pl.when(jnp.logical_not(special))
     def _():
-        for parity in range(2):
-            joined = []
-            for value in (real, imag):
-                below, above = (value[:middle], value[middle:])
-                joined.append(below + above if parity == 0 else below - above)
-            pair = split(jnp.concatenate(joined, axis=1))
-            rows = product((high[parity], low[parity]), pair)
-            cosine, sine = (rows[:middle], rows[middle:])
-            start = parity * middle
-            rows_ref[start : start + middle, :width] = cosine[:, :width] - sine[:, width:]
-            rows_ref[start : start + middle, width:] = cosine[:, width:] + sine[:, :width]
+        rows_ref[:middle, :width] = jnp.where(first, re_n, re_n + re_m)
+        rows_ref[:middle, width:] = jnp.where(first, im_n, im_n + im_m)
+        rows_ref[middle:, :width] = jnp.where(first, -re_m, im_n - im_m)
+        rows_ref[middle:, width:] = jnp.where(first, -im_m, re_m - re_n)
 
     @pl.when(special)
     def _():
-        row = lax.broadcasted_iota(jnp.int32, (middle, width), 0)
-        columns, ends = ([], [])
-        for upper in range(2):
-            part = slice(upper * middle, (upper + 1) * middle)
-            stacked = [jnp.where(row == 0, value[part], 2.0 * value[part]) for value in (real, imag)]
-            columns.append(jnp.concatenate(stacked, axis=0))
-            ends.append(imag[upper * middle : upper * middle + 1])
-        pair = split(jnp.concatenate(columns, axis=1))
-        for parity in range(2):
-            table = tuple(
-                jnp.concatenate([t[parity, :middle], -t[parity, middle:]], axis=1) for t in (high, low)
-            )
-            rows = product(table, pair)
-            sign = 1.0 - 2.0 * parity
-            start = parity * middle
-            rows_ref[start : start + middle, :width] = rows[:, :width] + sign * ends[0]
-            rows_ref[start : start + middle, width:] = sign * rows[:, width:] + ends[1]
-
+        rows_ref[:middle, :width] = jnp.where(first, re_n, 2.0 * re_n)
+        rows_ref[:middle, width:] = jnp.where(first, re_m, 2.0 * re_m)
+        rows_ref[middle:, :width] = jnp.where(first, -im_n, 2.0 * im_n)
+        rows_ref[middle:, width:] = jnp.where(first, -im_m, -2.0 * im_m)
+
+    rows_ref[...] = product((y_table[0][...], y_table[1][...]), split(rows_ref[...]))
     for cell in range(plan.cells):
         for group in range(plan.slabs // plan.y_lanes):
             parts = []
@@ -310,7 +297,8 @@
                         row = plan.row_of(cell, step, place)
                         col = part * width + group * LANES
                         tiles.append(rows_ref[row : row + plan.row_block, col : col + LANES])
-                parts.append(jnp.concatenate(tiles, axis=0))
+                value = jnp.concatenate(tiles, axis=0)
+                parts.append(value * sign if place % 2 == 1 else value)
             parts = swap_groups(parts, plan.width)
             first = cell * plan.slabs + group * plan.y_lanes
             for i in range(plan.y_lanes):
@@ -318,17 +306,17 @@
 
 
 def first_plane_kernel(plan, me_ref, pieces, y_high, y_low, x_high, x_low, out, rows_ref, freq_ref):
-    special = me_ref[0] == 0
-    out[...] = forward_plane(plan, special, pieces, (y_high, y_low), (x_high, x_low), rows_ref, freq_ref)
+    out[...] = forward_plane(plan, me_ref, pieces, (y_high, y_low), (x_high, x_low), rows_ref, freq_ref)
 
 
 def middle_plane_kernel(plan, me_ref, edge, pieces, yf_high, yf_low, xf_high, xf_low, *refs):
     late, refs = (refs[:5], refs[5:])
     strips, refs = (refs[: plan.inner], refs[plan.inner :])
-    out, rest, rows_ref, freq_ref, sum_ref, weights = refs[:6]
-    even, xb_high, xb_low, yb_high, yb_low, sems = refs[6:]
+    out, rest, rows_ref, freq_ref, sum_ref, rest_ref, weights = refs[:7]
+    even, xb_high, xb_low, yb_high, yb_low, sems = refs[7:]
     slab = lax.rem(me_ref[0], plan.slabs)
-    outer_id, inner_id = (slab // plan.inner, lax.rem(slab, plan.inner))
+    place = lax.rem(slab, plan.half)
+    outer_id, inner_id = (place // plan.inner, lax.rem(place, plan.inner))
     held = (even, xb_high, xb_low, yb_high, yb_low)
     copies = [pltpu.make_async_copy(late[0], even, sems.at[0])]
     for i in range(plan.inner):
@@ -338,7 +326,7 @@
             rows = pl.ds(pl.multiple_of(owner * plan.ky_local, plan.ky_local), plan.ky_local)
             copies.append(
                 pltpu.make_async_copy(
-                    strips[i].at[j], weights.at[rows], sems.at[len(held) + i * plan.outer + j]
+                    strips[i].at[j], weights.at[:, rows], sems.at[len(held) + i * plan.outer + j]
                 )
             )
     early = len(copies)
@@ -348,34 +336,45 @@
         copy.start()
     special = me_ref[0] == 0
     width = plan.x_chunk
-    odd = forward_plane(plan, special, pieces, (yf_high, yf_low), (xf_high, xf_low), rows_ref, freq_ref)
+    middle = plan.ny // 2
+    odd = forward_plane(plan, me_ref, pieces, (yf_high, yf_low), (xf_high, xf_low), rows_ref, freq_ref)
     for copy in copies[:early]:
         copy.wait()
-    row = lax.broadcasted_iota(jnp.int32, (plan.ny, width), 0)
-    results = []
-    for upper in range(2):
-        sums = even[...] - odd if upper else even[...] + odd
-        cols = slice(upper * width, (upper + 1) * width)
-        weight = weights[:, cols]
-        second = jnp.where(special & (row == 0), edge[0:1, cols], weight)
-        second = jnp.where(special & (row == plan.ny // 2), edge[1:2, cols], second)
-        real = weight * sums[: plan.ny, :width] + second * sums[plan.ny :, width:]
-        imag = second * sums[plan.ny :, :width] - weight * sums[: plan.ny, width:]
-        results.append((real, imag))
-    for part in range(2):
-        rows = slice(part * plan.ny, (part + 1) * plan.ny)
-        below, above = (results[0][part], results[1][part])
-        sum_ref[rows] = below + above
-        rest[rows] = below - above
+    row = lax.broadcasted_iota(jnp.int32, (middle, width), 0)
+    at_first = row == 0
+    own_edge = edge[pl.ds(slab, 1)]
+    for mirrored, turn in ((0, 1.0), (1, -1.0)):
+        re = slice(2 * mirrored * middle, (2 * mirrored + 1) * middle)
+        im = slice((2 * mirrored + 1) * middle, (2 * mirrored + 2) * middle)
+        results = []
+        for upper in range(2):
+            cols = slice(upper * width, (upper + 1) * width)
+            plane = weights[mirrored, :, cols]
+            if mirrored:
+                weight = jnp.where(at_first & jnp.logical_not(special), own_edge[:, cols], plane)
+                second = jnp.where(at_first, own_edge[:, cols], plane)
+            else:
+                weight = plane
+                second = jnp.where(at_first & special, edge[plan.slabs : plan.slabs + 1, cols], plane)
+            re_sums = even[re] - odd[re] if upper else even[re] + odd[re]
+            im_sums = even[im] - odd[im] if upper else even[im] + odd[im]
+            real = weight * re_sums[:, :width] + (turn * second) * im_sums[:, width:]
+            imag = second * im_sums[:, :width] - (turn * weight) * re_sums[:, width:]
+            results.append((real, imag))
+        for part, rows in enumerate((re, im)):
+            below, above = (results[0][part], results[1][part])
+            sum_ref[rows] = below + above
+            rest_ref[rows] = below - above
+    last = pltpu.make_async_copy(rest_ref, rest, sems.at[len(held) + plan.half])
+    last.start()
     for copy in copies[early:]:
         copy.wait()
-    x_table = (xb_high.at[pl.ds(0, 1)], xb_low.at[pl.ds(0, 1)])
-    backward_plane(plan, special, sum_ref[...], x_table, (yb_high, yb_low), out, rows_ref)
+    backward_plane(plan, me_ref, sum_ref[...], (xb_high, xb_low), (yb_high, yb_low), out, rows_ref)
+    last.wait()
 
 
 def last_plane_kernel(plan, me_ref, freqs, x_high, x_low, y_high, y_low, out, rows_ref):
-    special = me_ref[0] == 0
-    backward_plane(plan, special, freqs[...], (x_high, x_low), (y_high, y_low), out, rows_ref)
+    backward_plane(plan, me_ref, freqs[...], (x_high, x_low), (y_high, y_low), out, rows_ref)
 
 
 def plane_call(plan, kernel, name, me, arrays, tables, late, out_shapes, scratch, work):
@@ -383,9 +382,10 @@
     flat = []
     for pair, chunk in tables:
         for table in pair:
-            shape = table.shape if chunk is None else (1,) + table.shape[1:]
-            first = 0 if chunk is None else chunk
-            specs.append(pl.BlockSpec(shape, lambda i, first=first: (first, 0, 0)))
+            if chunk is None:
+                specs.append(whole_spec(table.shape))
+            else:
+                specs.append(pl.BlockSpec((1,) + table.shape[1:], lambda i, chunk=chunk: (chunk, 0, 0)))
             flat.append(table)
     specs += [pl.BlockSpec(memory_space=pl.ANY)] * len(late)
     size = sum(4 * array.size for array in list(arrays) + list(late)) + sum(2 * t.size for t in flat)
@@ -393,7 +393,7 @@
         functools.partial(kernel, plan),
         grid=(1,),
         in_specs=[pl.BlockSpec(memory_space=pltpu.SMEM)] + specs,
-        out_specs=[whole_spec(shape) for shape in out_shapes],
+        out_specs=[whole_spec(out_shapes[0])] + [pl.BlockSpec(memory_space=pl.ANY)] * (len(out_shapes) - 1),
         out_shape=[jax.ShapeDtypeStruct(shape, jnp.float32) for shape in out_shapes],
         scratch_shapes=scratch,
         compiler_params=pltpu.CompilerParams(vmem_limit_bytes=VMEM_LIMIT),
@@ -407,32 +407,31 @@
 def gather_kernel(plan, chunk, counts, before, pieces, high, low, projection, out, scratch, held, sems):
     planes = plan.cell_planes
     rows = plan.slots * 2 * plan.row_block
-    for copy in lane_copies(plan, chunk, projection, held, sems):
+    copies = tile_copies(plan, chunk, projection, held, sems)
+    for copy in copies:
         copy.start()
     columns = [pieces[:, :, step].reshape(rows, LANES) for step in range(plan.steps)]
     scratch[...] = product(split(jnp.concatenate(columns, axis=1).T), (high[...], low[...]))
-
-    def body(step, carry):
-        wait_lanes(held, sems, step)
-        for block in range(plan.step_blocks):
-            cells = pl.ds(pl.multiple_of((step * plan.step_blocks + block) * LANES, LANES), LANES)
-            lanes = slice(block * LANES, (block + 1) * LANES)
-            far = [before[p, :, cells] for p in range(plan.panels)]
-            for tx in range(plan.tx_chunk):
-                for ty in range(TY):
-                    row = step * LANES + ((block * TY + ty) * plan.tx_chunk + tx) * planes
-                    rows_at = pl.ds(pl.multiple_of(row, planes), planes)
-                    for tz in range(TZ):
-                        t = ty * TZ + tz
-                        potential = scratch[rows_at, tz * LANES : (tz + 1) * LANES]
-                        for p in range(plan.panels):
-                            far[p] = far[p] + held[step, p, tx, t, :, lanes] * potential
+    for tx, copy in enumerate(copies):
+        copy.wait()
+        last = chunk == CHUNKS - 1 and tx == plan.tx_chunk - 1
+
+        def body(place, carry, tx=tx, last=last):
+            lanes = pl.ds(pl.multiple_of(place * LANES, LANES), LANES)
+            far = [(before if tx == 0 else out)[p, :, lanes] for p in range(plan.panels)]
+            for ty in range(TY):
+                row = ((place * TY + ty) * plan.tx_chunk + tx) * planes
+                rows_at = pl.ds(pl.multiple_of(row, planes), planes)
+                for tz in range(TZ):
+                    t = ty * TZ + tz
+                    potential = scratch[rows_at, tz * LANES : (tz + 1) * LANES]
+                    for p in range(plan.panels):
+                        far[p] = far[p] + held[tx, p, t, :, lanes] * potential
             for p in range(plan.panels):
-                value = jnp.where(counts[:, cells] > p, far[p], 0.0) if chunk == CHUNKS - 1 else far[p]
-                out[p, :, cells] = value
-        return carry
-
-    lax.fori_loop(0, plan.steps, body, 0)
+                out[p, :, lanes] = jnp.where(counts[:, lanes] > p, far[p], 0.0) if last else far[p]
+            return carry
+
+        lax.fori_loop(0, plan.steps * plan.step_blocks, body, 0)
 
 
 def gather(plan, chunk, counts, before, projection, high, low, pieces):
@@ -532,19 +531,38 @@
 def first_weights(plan, spectrum):
     slab, cell = (lax.axis_index("slab"), lax.axis_index("cell"))
     by_depth = jnp.transpose(spectrum, (1, 2, 0))
-    far = lax.ppermute(by_depth[0, :1], "slab", [(plan.slabs // 2, 0)])
+    half_id, place = (slab // plan.half, lax.rem(slab, plan.half))
     blocks = []
     for j in range(plan.outer):
-        group = lax.rem(slab // plan.inner + j, plan.outer)
-        own = lax.dynamic_slice_in_dim(by_depth, cell * plan.slabs + group * plan.inner, plan.inner, 0)
-        dest = lax.broadcasted_iota(jnp.int32, own.shape, 0)
-        swapped = (cell == 0) & (slab >= plan.slabs // 2) & (group == 0) & (dest == 0)
-        own = jnp.where(swapped, by_depth[plan.slots][None], own)
+        group = lax.rem(place // plan.inner + j, plan.outer)
+        base = cell * plan.slabs + half_id * plan.half + group * plan.inner
+        planes = []
+        for q in range(plan.inner):
+            freq = base + q
+            mirror = jnp.where(freq == 0, plan.nz // 2, plan.nz - freq)
+            for index in (freq, mirror):
+                planes.append(lax.dynamic_slice_in_dim(by_depth, index, 1, 0))
+        block = jnp.concatenate(planes, axis=0).reshape((plan.inner, 2) + by_depth.shape[1:])
         if j > 0:
-            shift = j * plan.inner
-            own = lax.ppermute(own, "slab", [(i, (i + shift) % plan.slabs) for i in range(plan.slabs)])
-        blocks.append(own)
-    return (blocks, far, by_depth[plan.slots, :1])
+            pairs = []
+            for source in range(plan.slabs):
+                base_id = source // plan.half * plan.half
+                pairs.append((source, base_id + (source - base_id + j * plan.inner) % plan.half))
+            block = lax.ppermute(block, "slab", pairs)
+        blocks.append(block)
+    return blocks
+
+
+def edge_weights(plan, spectrum):
+    slab, cell = (lax.axis_index("slab"), lax.axis_index("cell"))
+    rows = jnp.transpose(spectrum[:, :, 0], (1, 0))
+    turned = jnp.concatenate([rows[plan.nz // 2 : plan.nz // 2 + 1], jnp.flip(rows, 0)], axis=0)
+    own = lax.dynamic_slice_in_dim(turned, cell * plan.slabs, plan.slabs, 0)
+    own = jnp.concatenate([own, rows[:1]], axis=0)
+    dest = lax.broadcasted_iota(jnp.int32, own.shape, 0)
+    from_middle = (dest < plan.half) | (dest == plan.slabs)
+    keep = jnp.where(from_middle, slab == plan.half, slab == 0)
+    return lax.psum(jnp.where(keep, own, 0.0), "slab")
 
 
 def second_weights(plan, blocks):
@@ -572,11 +590,12 @@
         return plain_device(charges, counts, projection, near_blocks, neighbours, spectrum)
     me = (lax.axis_index("cell") * slabs + lax.axis_index("slab")).astype(jnp.int32).reshape(1)
     depth_forward, depth_backward = [halves(table) for table in plan.depth_tables()]
-    y_rows, x_cols, low_ids = (plan.y_rows(), plan.x_columns(), np.arange(plan.ny // 2))
-    y_waves = [wave(low_ids, rows, plan.ny) for rows in y_rows]
+    y_rows, x_cols, low_ids = (plan.y_rows().reshape(-1), plan.x_columns(), np.arange(plan.ny // 2))
+    cos_y, sin_y = wave(low_ids, y_rows, plan.ny)
+    sin_y[0] = 1.0 - 2.0 * (y_rows % 2)
+    y_forward = halves(np.concatenate([cos_y, sin_y], axis=0))
+    y_backward = halves(np.concatenate([cos_y.T, -sin_y.T], axis=1))
     x_waves = [wave(cols, low_ids, plan.nx) for cols in x_cols]
-    y_forward = halves(np.stack([np.concatenate(pair, axis=0) for pair in y_waves]))
-    y_backward = halves(np.stack([np.concatenate([t.T for t in pair], axis=0) for pair in y_waves]))
     x_forward = halves(np.stack([np.concatenate(pair, axis=1) for pair in x_waves]))
     x_backward = halves(np.stack([np.concatenate([t.T for t in pair], axis=1) for pair in x_waves]))
     split_projection = projection.reshape(
@@ -593,37 +612,36 @@
     rows_shape = (plan.ny, 2 * plan.x_chunk)
     freq_shape = (2 * plan.ny, plan.x_chunk)
     both_shape = (2 * plan.ny, plan.nx)
-    blocks, far, near = first_weights(plan, spectrum)
+    blocks = first_weights(plan, spectrum)
+    edge = edge_weights(plan, spectrum)
     slot = lax.broadcasted_iota(jnp.int32, charges.shape, 0)
     masked = jnp.where(slot < counts[None], charges, 0.0)
     left, right = extend_rows(plan, masked)
     pieces = [project(plan, i, charges, counts, split_projection, *depth_forward) for i in range(CHUNKS)]
-    pieces[0], blocks[1], far = lax.optimization_barrier((pieces[0], blocks[1], far))
+    pieces[0], left, right = lax.optimization_barrier((pieces[0], left, right))
     even_pieces = exchange(pieces[0])
-    pieces[1], left, right, *blocks[2:] = lax.optimization_barrier(
-        (pieces[1], left, right, *blocks[2:])
-    )
+    extended = extend_planes(plan, masked, left, right)
+    pieces[1], extended, *blocks = lax.optimization_barrier((pieces[1], extended, *blocks))
     odd_pieces = exchange(pieces[1])
     strips = second_weights(plan, blocks)
     (even,) = plane_call(
         plan, first_plane_kernel, "even_planes", me, [even_pieces], [(y_forward, None), (x_forward, 0)], [],
         [both_shape], values(rows_shape, freq_shape), 2,
     )
-    edge = jnp.concatenate([far, near], axis=0)
     late = [even, x_backward[0][:1], x_backward[1][:1], *y_backward]
     copies = [pltpu.VMEM(array.shape, array.dtype) for array in late]
-    copies.append(pltpu.SemaphoreType.DMA((len(late) + plan.slabs,)))
+    copies.append(pltpu.SemaphoreType.DMA((len(late) + plan.half + 1,)))
     back, rest = plane_call(
         plan, middle_plane_kernel, "middle_planes", me, [edge, odd_pieces],
         [(y_forward, None), (x_forward, 1)], late + strips, [piece_shape(plan), freq_shape],
-        values(rows_shape, freq_shape, freq_shape, (plan.ny, plan.nx)) + copies, 4,
+        values(rows_shape, freq_shape, freq_shape, freq_shape, (2, plan.ny // 2, plan.nx)) + copies, 4,
     )
     even_back = exchange(back)
     (back,) = plane_call(
         plan, last_plane_kernel, "odd_planes", me, [rest], [(x_backward, 1), (y_backward, None)], [],
         [piece_shape(plan)], values(rows_shape), 2,
     )
-    total = near_field(plan, extend_planes(plan, masked, left, right), neighbours, near_blocks)
+    total = near_field(plan, extended, neighbours, near_blocks)
     back, total = lax.optimization_barrier((back, total))
     odd_back = exchange(back)
     total = gather(plan, 0, counts, total, split_projection, *depth_backward, even_back)

time: 194 us -> 221 us (1.14)
  blocking collectives: 0 us -> 72 us
  waiting for transfers between devices: 80.6 us -> 37.6 us
  starting transfers between devices: 41.1 us -> 29.5 us
  local copies, waits for them, and re-layouts: 2.92 us -> 11.6 us
    psum x0 -> x1, blocking collectives: none -> 72 us  [edge_weights(): return lax.psum(jnp.where(keep, own, 0.0), 'slab')]
    ppermute x4 -> x1, waiting for transfers between devices: 24.6 us -> 7.02 us  [first_weights(): block = lax.ppermute(block, 'slab', pairs)]
    ppermute x1, waiting for transfers between devices: 18.5 us -> 3.75 us  [extend_planes(): before = lax.ppermute(wide[:, -1:], 'slab', up)]
    ppermute x3, waiting for transfers between devices: 11.3 us -> 1.22 us  [second_weights(): strip = lax.ppermute(strip, 'slab', pairs)]
    ppermute x4 -> x1, starting transfers between devices: 8.55 us -> 0.07 us  [first_weights(): block = lax.ppermute(block, 'slab', pairs)]
    unnamed x16 -> x22, local copies, waits for them, and re-layouts: 1 us -> 8.98 us
    all_to_all x4, starting transfers between devices: 22.7 us -> 20 us  [exchange(): return lax.all_to_all(pieces, axes, split_axis=0, concat_axis=0, tiled=True)]
  transfers between devices with their start and end apart: 15 -> 12, of which waited for: 7 -> 6; matrix products, arithmetic and copies ran while one was open for 2% -> 5% of each run, Pallas kernels for 24% -> 22%
where the time goes in v5:
time: 221 us; the launch traced here: 220 us
  blocking collectives  72 us (33%)
  Pallas kernels  65.6 us (30%)
  waiting for transfers between devices  37.6 us (17%)
  starting transfers between devices  29.5 us (13%)
  local copies, waits for them, and re-layouts  11.6 us (5%)
  other arithmetic  3 us (1%)
    psum x1, blocking collectives, edge_weights(): return lax.psum(jnp.where(keep, own, 0.0), 'slab')  72 us
    pallas_call x4, Pallas kernels, projection_call(): pl.pallas_call(kernel, grid=(1,), in_specs=[whole_spec(array.shape) for a...  27.7 us
    all_to_all x4, waiting for transfers between devices, exchange(): return lax.all_to_all(pieces, axes, split_axis=0, concat_axis=0, tiled=True)  25.6 us
    pallas_call x3, Pallas kernels, plane_call(): pl.pallas_call(functools.partial(kernel, plan), grid=(1,), in_specs=[pl.B...  22.4 us
    all_to_all x4, starting transfers between devices, exchange(): return lax.all_to_all(pieces, axes, split_axis=0, concat_axis=0, tiled=True)  20 us
    pallas_call x1, Pallas kernels, near_field(): pl.pallas_call(functools.partial(near_kernel, plan), grid=(plan.cell_cols...  15.5 us
    unnamed x22, local copies, waits for them, and re-layouts  8.98 us
    ppermute x1, waiting for transfers between devices, first_weights(): block = lax.ppermute(block, 'slab', pairs)  7.02 us
  transfers between devices with their start and end apart: 12, of which 6 were waited for; matrix products, arithmetic and copies ran while one was open for 5% of the time, Pallas kernels for 22%

profile of v5, /device:TPU:0, one launch (start us, length us, event | category | flops | bytes accessed | tf_op | source)
XLA Modules:
  0.0 220.0 jit_solution(2154158592108745570)
XLA Ops:
  0.0 1.0 fusion.2
  1.0 0.1 fusion.5
  1.1 3.0 %collective-permute-start.1 = (f32[8,8,16]{2,1,0:T(8,128)S(1)}, f32[8,8,16]{2,1,0:T(8,128)S(1)}, u32[]{:S(2)}, u32[]{:S(2)}) collective-permute-start(f32[8,8,16]{2,1,0:T(8,128)S(1)} %get-tuple-element.55), channel_id=1, source_target_pairs={{1,0},{0,1},{3,2},{2,3},{5,4},{4,5},{7,6},{6,7},{9,8},{8,9},{11,10... | collective-permute-start | bytes 12296 | tf_op jit(solution)/shard_map/ppermute | solution.py:516
  4.0 0.1 collective-permute-start
  4.1 7.4 %project_depth.3 = f32[32,2,4,8,128]{4,3,2,1,0:T(8,128)} custom-call(f32[8,8,1024]{2,1,0:T(8,128)} %charges.3, s32[8,1024]{1,0:T(8,128)} %counts.7, bf16[512,512]{1,0:T(8,128)(2,1)} %constant.103.clone.high, bf16[512,512]{1,0:T(8,128)(2,1)} %constant.104.clone.low, f32[8,2,2,16,8,1024]{5,4,3,2,1,0:T(8,128)} %bitcast.50), custom_call_target="tpu_custom_call" | custom-call | flops 4194304 | bytes 8388608 | tf_op jit(solution)/shard_map/project_depth/pallas_call | solution.py:184
  11.5 0.0 collective-permute-done.1
  11.5 0.0 collective-permute-done
  11.6 6.3 %all-to-all-start.1 = ((f32[32,2,4,8,128]{4,3,2,1,0:T(8,128)}), f32[32,2,4,8,128]{4,3,2,1,0:T(8,128)S(1)}, u32[]{:S(2)}, u32[]{:S(2)}) async-start(f32[32,2,4,8,128]{4,3,2,1,0:T(8,128)} %project_depth.3), calls=%async_computation.1 | async-start | bytes 2097152 | tf_op jit(solution)/shard_map/all_to_all | solution.py:607
  18.0 0.9 bitcast_dynamic-update-slice_fusion.7
  18.9 0.9 bitcast_dynamic-update-slice_fusion.6
  19.8 0.9 bitcast_dynamic-update-slice_fusion.5
  20.7 0.9 bitcast_dynamic-update-slice_fusion.4
  21.6 0.9 bitcast_dynamic-update-slice_fusion.3
  22.5 0.9 bitcast_dynamic-update-slice_fusion.2
  23.4 0.9 bitcast_dynamic-update-slice_fusion.1
  24.3 0.1 concatenate.36
  24.4 0.1 fusion.4
  24.4 0.3 collective-permute-start.2
  24.7 4.2 %collective-permute-start.3 = (f32[8,1,1280]{2,1,0:T(1,128)S(1)}, f32[8,1,1280]{2,1,0:T(1,128)S(1)}, u32[]{:S(2)}, u32[]{:S(2)}) collective-permute-start(f32[8,1,1280]{2,1,0:T(1,128)S(1)} %get-tuple-element.54), channel_id=1, source_target_pairs={{2,0},{4,2},{6,4},{8,6},{10,8},{12,10},{14,12},{16,14},{18,16},{20... | collective-permute-start | bytes 122888 | tf_op jit(solution)/shard_map/ppermute | solution.py:525
  28.9 0.9 bitcast_dynamic-update-slice_fusion
  29.8 0.1 collective-permute-start.4
  29.9 7.4 %project_depth.2 = f32[32,2,4,8,128]{4,3,2,1,0:T(8,128)} custom-call(f32[8,8,1024]{2,1,0:T(8,128)} %charges.3, s32[8,1024]{1,0:T(8,128)} %counts.7, bf16[512,512]{1,0:T(8,128)(2,1)} %constant.103.clone.high, bf16[512,512]{1,0:T(8,128)(2,1)} %constant.104.clone.low, f32[8,2,2,16,8,1024]{5,4,3,2,1,0:T(8,128)} %bitcast.51), custom_call_target="tpu_custom_call" | custom-call | flops 4194304 | bytes 8388608 | tf_op jit(solution)/shard_map/project_depth/pallas_call | solution.py:184
  37.3 3.7 %collective-permute-done.2 = f32[8,1,1280]{2,1,0:T(1,128)S(1)} collective-permute-done((f32[8,1,1280]{2,1,0:T(1,128)S(1)}, f32[8,1,1280]{2,1,0:T(1,128)S(1)}, u32[]{:S(2)}, u32[]{:S(2)}) %collective-permute-start.2) | collective-permute-done | bytes 40992 | tf_op jit(solution)/shard_map/ppermute | solution.py:524
  41.1 0.0 collective-permute-done.3
  41.1 0.1 fusion.1
  41.2 1.0 pad_maximum_fusion.extended
  42.2 7.0 %collective-permute-done.4 = f32[4,2,32,512]{3,2,1,0:T(8,128)S(1)} collective-permute-done((f32[4,2,32,512]{3,2,1,0:T(8,128)S(1)}, f32[4,2,32,512]{3,2,1,0:T(8,128)S(1)}, u32[]{:S(2)}, u32[]{:S(2)}) %collective-permute-start.4) | collective-permute-done | bytes 524320 | tf_op jit(solution)/shard_map/ppermute | solution.py:551
  49.2 0.0 all-to-all-done.1.pieces
  49.2 0.0 copy-start.2
  49.2 4.8 %all-to-all-start = ((f32[32,2,4,8,128]{4,3,2,1,0:T(8,128)}), f32[32,2,4,8,128]{4,3,2,1,0:T(8,128)S(1)}, u32[]{:S(2)}, u32[]{:S(2)}) async-start(f32[32,2,4,8,128]{4,3,2,1,0:T(8,128)} %project_depth.2), calls=%async_computation | async-start | bytes 2097152 | tf_op jit(solution)/shard_map/all_to_all | solution.py:607
  54.1 1.3 slice.29
  55.4 0.1 rev.4
  55.6 0.1 maximum_select_fusion
  55.7 72.0 %psum.7.edge = f32[17,512]{1,0:T(8,128)} all-reduce(f32[17,512]{1,0:T(8,128)S(1)} %maximum_select_fusion), channel_id=1, replica_groups=mesh['slab'=16,'cell'=2] {'slab'}, use_global_device_ids=true, to_apply=%region_0.1 | all-reduce | flops 8704 | bytes 69632 | tf_op jit(solution)/shard_map/psum | solution.py:565
  127.7 0.1 constant_dynamic-slice_fusion
  127.8 0.1 collective-permute-start.5
  127.9 0.1 collective-permute-start.6
  128.0 1.8 collective-permute-start.7
  129.8 0.7 pad_maximum_fusion.3.refs_5_
  130.5 0.0 copy-done.2
  130.5 5.7 %even_planes.1.refs_0_ = f32[1024,512]{1,0:T(8,128)} custom-call(s32[1]{0:T(128)} %bitcast.me_ref, f32[32,2,4,8,128]{4,3,2,1,0:T(8,128)} %copy-done.2, bf16[512,512]{1,0:T(8,128)(2,1)} %constant.105.clone.y_high.yf_high, bf16[512,512]{1,0:T(8,128)(2,1)} %constant.106.clone.y_low.yf_low, bf16[2,256,512]{2,1,0:T(8,128)(2,1)} %constant.107.clone.x_high.xf_high, ...), custom_call_target="tpu_custom_call" | custom-call | flops 1610612736 | bytes 3145728 | tf_op jit(solution)/shard_map/even_planes/pallas_call | solution.py:392
  136.3 0.0 collective-permute-done.5.refs_6_
  136.3 0.0 copy-start.4
  136.3 0.8 collective-permute-done.6.refs_7_
  137.1 0.4 collective-permute-done.7.refs_8_
  137.5 0.0 copy-start.6
  137.5 0.0 all-to-all-done.pieces
  137.5 0.0 copy-done.4
  137.5 0.3 copy-done.5
  137.8 0.4 copy-done.6
  138.2 0.0 copy-start.3
  138.2 1.0 copy-done.3
  139.3 10.0 %middle_planes.1 = (f32[32,2,4,8,128]{4,3,2,1,0:T(8,128)}, f32[1024,256]{1,0:T(8,128)}) custom-call(s32[1]{0:T(128)} %bitcast.me_ref, f32[17,512]{1,0:T(8,128)} %psum.7.edge, f32[32,2,4,8,128]{4,3,2,1,0:T(8,128)} %copy-done.3, bf16[512,512]{1,0:T(8,128)(2,1)} %constant.105.clone.y_high.yf_high, bf16[512,512]{1,0:T(8,128)(2,1)} %constant.106.clone.y_low.yf_low, ...), custom_call_target="tpu_custom_call" | custom-call | flops 3221225472 | bytes 9472000 | tf_op jit(solution)/shard_map/middle_planes/pallas_call | solution.py:392
  149.3 6.3 %all-to-all-start.2 = ((f32[32,2,4,8,128]{4,3,2,1,0:T(8,128)}), f32[32,2,4,8,128]{4,3,2,1,0:T(8,128)S(1)}, u32[]{:S(2)}, u32[]{:S(2)}) async-start(f32[32,2,4,8,128]{4,3,2,1,0:T(8,128)} %get-tuple-element.25), calls=%async_computation.2 | async-start | bytes 2097152 | tf_op jit(solution)/shard_map/all_to_all | solution.py:607
  155.5 15.5 %near_blocks.1.before = f32[8,8,1024]{2,1,0:T(8,128)} custom-call(f32[8,3,8,1280]{3,2,1,0:T(8,128)} %pad_maximum_fusion.extended, s32[6,8,1024]{2,1,0:T(8,128)} %codes.1, f32[6,8,8,8,1024]{4,3,2,1,0:T(8,128)} %blocks_ref.1), custom_call_target="tpu_custom_call" | custom-call | flops 6291456 | bytes 12582912 | tf_op jit(solution)/shard_map/near_blocks/pallas_call | solution.py:487
  171.0 6.6 %odd_planes.1 = f32[32,2,4,8,128]{4,3,2,1,0:T(8,128)} custom-call(s32[1]{0:T(128)} %bitcast.me_ref, f32[1024,256]{1,0:T(8,128)} %get-tuple-element.22.freqs, bf16[2,256,512]{2,1,0:T(8,128)(2,1)} %constant.113.clone.x_high, bf16[2,256,512]{2,1,0:T(8,128)(2,1)} %constant.114.clone.x_low, bf16[512,512]{1,0:T(8,128)(2,1)} %constant.111.clone.refs_3_.y_high, ...), custom_call_target="tpu_custom_call" | custom-call | flops 1610612736 | bytes 3145728 | tf_op jit(solution)/shard_map/odd_planes/pallas_call | solution.py:392
  177.7 4.9 %all-to-all-done.2.pieces = f32[32,2,4,8,128]{4,3,2,1,0:T(8,128)S(1)} async-done(((f32[32,2,4,8,128]{4,3,2,1,0:T(8,128)}), f32[32,2,4,8,128]{4,3,2,1,0:T(8,128)S(1)}, u32[]{:S(2)}, u32[]{:S(2)}) %all-to-all-start.2) | async-done | bytes 1048608 | tf_op jit(solution)/shard_map/all_to_all | solution.py:607
  182.5 0.0 copy-start
  182.5 2.6 %all-to-all-start.3 = ((f32[32,2,4,8,128]{4,3,2,1,0:T(8,128)}), f32[32,2,4,8,128]{4,3,2,1,0:T(8,128)S(1)}, u32[]{:S(2)}, u32[]{:S(2)}) async-start(f32[32,2,4,8,128]{4,3,2,1,0:T(8,128)} %odd_planes.1), calls=%async_computation.3 | async-start | bytes 2097152 | tf_op jit(solution)/shard_map/all_to_all | solution.py:607
  185.2 0.0 copy-done
  185.2 6.5 %depth_gather.2.before = f32[8,8,1024]{2,1,0:T(8,128)} custom-call(s32[8,1024]{1,0:T(8,128)} %counts.7, f32[8,8,1024]{2,1,0:T(8,128)} %near_blocks.1.before, f32[32,2,4,8,128]{4,3,2,1,0:T(8,128)} %copy-done, bf16[512,512]{1,0:T(8,128)(2,1)} %constant.115.clone.high, bf16[512,512]{1,0:T(8,128)(2,1)} %constant.116.clone.low, f32[8,2,2,16,8,1024]{5,4,3,2,1,0:T(8,128)} %bitcast.52), custom_call_target="tpu_custom_call" | custom-call | flops 4194304 | bytes 8388608 | tf_op jit(solution)/shard_map/depth_gather/pallas_call | solution.py:184
  191.7 20.7 %all-to-all-done.3.pieces = f32[32,2,4,8,128]{4,3,2,1,0:T(8,128)S(1)} async-done(((f32[32,2,4,8,128]{4,3,2,1,0:T(8,128)}), f32[32,2,4,8,128]{4,3,2,1,0:T(8,128)S(1)}, u32[]{:S(2)}, u32[]{:S(2)}) %all-to-all-start.3) | async-done | bytes 1048608 | tf_op jit(solution)/shard_map/all_to_all | solution.py:607
  212.4 1.0 copy-done.1
  213.4 6.5 %depth_gather.3 = f32[8,8,1024]{2,1,0:T(8,128)} custom-call(s32[8,1024]{1,0:T(8,128)} %counts.7, f32[8,8,1024]{2,1,0:T(8,128)} %depth_gather.2.before, f32[32,2,4,8,128]{4,3,2,1,0:T(8,128)} %copy-done.1, bf16[512,512]{1,0:T(8,128)(2,1)} %constant.115.clone.high, bf16[512,512]{1,0:T(8,128)(2,1)} %constant.116.clone.low, f32[8,2,2,16,8,1024]{5,4,3,2,1,0:T(8,128)} %bitcast.53), custom_call_target="tpu_custom_call" | custom-call | flops 4194304 | bytes 8388608 | tf_op jit(solution)/shard_map/depth_gather/pallas_call | solution.py:184
  (10 shorter events, 0.1 us)
Async XLA Ops:
  1.1 10.5 %collective-permute-start.1 = (f32[8,8,16]{2,1,0:T(8,128)S(1)}, f32[8,8,16]{2,1,0:T(8,128)S(1)}, u32[]{:S(2)}, u32[]{:S(2)}) collective-permute-start(f32[8,8,16]{2,1,0:T(8,128)S(1)} %get-tuple-element.55), channel_id=1, source_target_pairs={{1,0},{0,1},{3,2},{2,3},{5,4},{4,5},{7,6},{6,7},{9,8},{8,9},{11,10... | collective-permute-start | bytes 12296 | tf_op jit(solution)/shard_map/ppermute | solution.py:516
  4.0 7.5 %collective-permute-start = (f32[8,8,16]{2,1,0:T(8,128)S(1)}, f32[8,8,16]{2,1,0:T(8,128)S(1)}, u32[]{:S(2)}, u32[]{:S(2)}) collective-permute-start(f32[8,8,16]{2,1,0:T(8,128)S(1)} %get-tuple-element.56), channel_id=1, source_target_pairs={{0,1},{1,0},{2,3},{3,2},{4,5},{5,4},{6,7},{7,6},{8,9},{9,8},{10,11... | collective-permute-start | bytes 12296 | tf_op jit(solution)/shard_map/ppermute | solution.py:515
  11.6 37.7 %all-to-all-start.1 = ((f32[32,2,4,8,128]{4,3,2,1,0:T(8,128)}), f32[32,2,4,8,128]{4,3,2,1,0:T(8,128)S(1)}, u32[]{:S(2)}, u32[]{:S(2)}) async-start(f32[32,2,4,8,128]{4,3,2,1,0:T(8,128)} %project_depth.3), calls=%async_computation.1 | async-start | bytes 2097152 | tf_op jit(solution)/shard_map/all_to_all | solution.py:607
  24.4 16.6 %collective-permute-start.2 = (f32[8,1,1280]{2,1,0:T(1,128)S(1)}, f32[8,1,1280]{2,1,0:T(1,128)S(1)}, u32[]{:S(2)}, u32[]{:S(2)}) collective-permute-start(f32[8,1,1280]{2,1,0:T(1,128)S(1)} %get-tuple-element.53), channel_id=1, source_target_pairs={{0,2},{2,4},{4,6},{6,8},{8,10},{10,12},{12,14},{14,16},{16,18},{18... | collective-permute-start | bytes 122888 | tf_op jit(solution)/shard_map/ppermute | solution.py:524
  24.7 16.3 %collective-permute-start.3 = (f32[8,1,1280]{2,1,0:T(1,128)S(1)}, f32[8,1,1280]{2,1,0:T(1,128)S(1)}, u32[]{:S(2)}, u32[]{:S(2)}) collective-permute-start(f32[8,1,1280]{2,1,0:T(1,128)S(1)} %get-tuple-element.54), channel_id=1, source_target_pairs={{2,0},{4,2},{6,4},{8,6},{10,8},{12,10},{14,12},{16,14},{18,16},{20... | collective-permute-start | bytes 122888 | tf_op jit(solution)/shard_map/ppermute | solution.py:525
  29.8 19.4 %collective-permute-start.4 = (f32[4,2,32,512]{3,2,1,0:T(8,128)S(1)}, f32[4,2,32,512]{3,2,1,0:T(8,128)S(1)}, u32[]{:S(2)}, u32[]{:S(2)}) collective-permute-start(f32[4,2,32,512]{3,2,1,0:T(8,128)S(1)} %bitcast.58), channel_id=1, source_target_pairs={{0,8},{2,10},{4,12},{6,14},{8,0},{10,2},{12,4},{14,6},{16,24},{18,... | collective-permute-start | bytes 1572872 | tf_op jit(solution)/shard_map/ppermute | solution.py:551
  49.2 81.3 %copy-start.2 = (f32[32,2,4,8,128]{4,3,2,1,0:T(8,128)}, f32[32,2,4,8,128]{4,3,2,1,0:T(8,128)S(1)}, u32[]{:S(2)}) copy-start(f32[32,2,4,8,128]{4,3,2,1,0:T(8,128)S(1)} %all-to-all-done.1.pieces) | copy-start | bytes 3145732
  49.2 88.3 %all-to-all-start = ((f32[32,2,4,8,128]{4,3,2,1,0:T(8,128)}), f32[32,2,4,8,128]{4,3,2,1,0:T(8,128)S(1)}, u32[]{:S(2)}, u32[]{:S(2)}) async-start(f32[32,2,4,8,128]{4,3,2,1,0:T(8,128)} %project_depth.2), calls=%async_computation | async-start | bytes 2097152 | tf_op jit(solution)/shard_map/all_to_all | solution.py:607
  127.8 8.4 %collective-permute-start.5 = (f32[2,2,32,512]{3,2,1,0:T(8,128)S(1)}, f32[2,2,32,512]{3,2,1,0:T(8,128)S(1)}, u32[]{:S(2)}, u32[]{:S(2)}) collective-permute-start(f32[2,2,32,512]{3,2,1,0:T(8,128)S(1)} %pad_maximum_fusion.4), channel_id=1, source_target_pairs={{0,2},{2,4},{4,6},{6,0},{8,10},{10,12},{12,14},{14,8},{16,18},{18,... | collective-permute-start | bytes 786440 | tf_op jit(solution)/shard_map/ppermute | solution.py:579
  127.9 9.2 %collective-permute-start.6 = (f32[2,2,32,512]{3,2,1,0:T(8,128)S(1)}, f32[2,2,32,512]{3,2,1,0:T(8,128)S(1)}, u32[]{:S(2)}, u32[]{:S(2)}) collective-permute-start(f32[2,2,32,512]{3,2,1,0:T(8,128)S(1)} %pad_maximum_fusion.5), channel_id=1, source_target_pairs={{0,4},{2,6},{4,0},{6,2},{8,12},{10,14},{12,8},{14,10},{16,20},{18,... | collective-permute-start | bytes 786440 | tf_op jit(solution)/shard_map/ppermute | solution.py:579
  128.0 9.5 %collective-permute-start.7 = (f32[2,2,32,512]{3,2,1,0:T(8,128)S(1)}, f32[2,2,32,512]{3,2,1,0:T(8,128)S(1)}, u32[]{:S(2)}, u32[]{:S(2)}) collective-permute-start(f32[2,2,32,512]{3,2,1,0:T(8,128)S(1)} %pad_maximum_fusion.6), channel_id=1, source_target_pairs={{0,6},{2,0},{4,2},{6,4},{8,14},{10,8},{12,10},{14,12},{16,22},{18,... | collective-permute-start | bytes 786440 | tf_op jit(solution)/shard_map/ppermute | solution.py:579
  136.3 1.2 copy-start.4
  137.1 0.7 copy-start.5
  137.5 0.7 copy-start.6
  138.2 1.0 copy-start.3
  149.3 33.3 %all-to-all-start.2 = ((f32[32,2,4,8,128]{4,3,2,1,0:T(8,128)}), f32[32,2,4,8,128]{4,3,2,1,0:T(8,128)S(1)}, u32[]{:S(2)}, u32[]{:S(2)}) async-start(f32[32,2,4,8,128]{4,3,2,1,0:T(8,128)} %get-tuple-element.25), calls=%async_computation.2 | async-start | bytes 2097152 | tf_op jit(solution)/shard_map/all_to_all | solution.py:607
  182.5 2.7 %copy-start = (f32[32,2,4,8,128]{4,3,2,1,0:T(8,128)}, f32[32,2,4,8,128]{4,3,2,1,0:T(8,128)S(1)}, u32[]{:S(2)}) copy-start(f32[32,2,4,8,128]{4,3,2,1,0:T(8,128)S(1)} %all-to-all-done.2.pieces) | copy-start | bytes 3145732
  182.5 29.8 %all-to-all-start.3 = ((f32[32,2,4,8,128]{4,3,2,1,0:T(8,128)}), f32[32,2,4,8,128]{4,3,2,1,0:T(8,128)S(1)}, u32[]{:S(2)}, u32[]{:S(2)}) async-start(f32[32,2,4,8,128]{4,3,2,1,0:T(8,128)} %odd_planes.1), calls=%async_computation.3 | async-start | bytes 2097152 | tf_op jit(solution)/shard_map/all_to_all | solution.py:607
  212.4 1.0 copy-start.1

commit v6 on v5

--- a/solution.py
+++ b/solution.py
@@ -16,7 +16,7 @@
 NZC = 16
 LANES = 128
 CHUNKS = 2
-VMEM_LIMIT = 60 * 1024 * 1024
+VMEM_LIMIT = 62 * 1024 * 1024
 
 
 def halves(table):
@@ -180,32 +180,34 @@
     return pl.BlockSpec(shape, lambda i: (0,) * len(shape))
 
 
-def projection_call(plan, kernel, name, arrays, projection, out_shape):
+def projection_call(plan, kernel, name, arrays, late, out_shape, scratch):
     return pl.pallas_call(
         kernel,
         grid=(1,),
-        in_specs=[whole_spec(array.shape) for array in arrays] + [pl.BlockSpec(memory_space=pl.ANY)],
+        in_specs=[whole_spec(array.shape) for array in arrays]
+        + [pl.BlockSpec(memory_space=pl.ANY)] * len(late),
         out_specs=whole_spec(out_shape),
         out_shape=jax.ShapeDtypeStruct(out_shape, jnp.float32),
         scratch_shapes=[
             pltpu.VMEM((plan.steps * LANES, TZ * LANES), jnp.float32),
             pltpu.VMEM(held_shape(plan), jnp.float32),
-            pltpu.SemaphoreType.DMA((plan.tx_chunk,)),
-        ],
+            pltpu.SemaphoreType.DMA((plan.tx_chunk + 1,)),
+        ]
+        + scratch,
         compiler_params=pltpu.CompilerParams(vmem_limit_bytes=VMEM_LIMIT),
         cost_estimate=pl.CostEstimate(
-            flops=2 * projection.size // CHUNKS,
-            bytes_accessed=4 * projection.size // CHUNKS,
+            flops=2 * late[0].size // CHUNKS,
+            bytes_accessed=4 * late[0].size // CHUNKS,
             transcendentals=0,
         ),
         name=name,
-    )(*arrays, projection)
+    )(*arrays, *late)
 
 
 def project(plan, chunk, charges, counts, projection, high, low):
     kernel = functools.partial(project_kernel, plan, chunk)
     arrays = [charges, counts, high, low]
-    return projection_call(plan, kernel, "project_depth", arrays, projection, piece_shape(plan))
+    return projection_call(plan, kernel, "project_depth", arrays, [projection], piece_shape(plan), [])
 
 
 def far_sign(plan, me_ref):
@@ -309,16 +311,16 @@
     out[...] = forward_plane(plan, me_ref, pieces, (y_high, y_low), (x_high, x_low), rows_ref, freq_ref)
 
 
-def middle_plane_kernel(plan, me_ref, edge, pieces, yf_high, yf_low, xf_high, xf_low, *refs):
-    late, refs = (refs[:5], refs[5:])
+def middle_plane_kernel(plan, me_ref, edge, yf_high, yf_low, xf_high, xf_low, *refs):
+    late, refs = (refs[:6], refs[6:])
     strips, refs = (refs[: plan.inner], refs[plan.inner :])
     out, rest, rows_ref, freq_ref, sum_ref, rest_ref, weights = refs[:7]
-    even, xb_high, xb_low, yb_high, yb_low, sems = refs[7:]
+    pieces, even, xb_high, xb_low, yb_high, yb_low, sems = refs[7:]
     slab = lax.rem(me_ref[0], plan.slabs)
     place = lax.rem(slab, plan.half)
     outer_id, inner_id = (place // plan.inner, lax.rem(place, plan.inner))
-    held = (even, xb_high, xb_low, yb_high, yb_low)
-    copies = [pltpu.make_async_copy(late[0], even, sems.at[0])]
+    held = (pieces, even, xb_high, xb_low, yb_high, yb_low)
+    copies = [pltpu.make_async_copy(late[n], held[n], sems.at[n]) for n in range(2)]
     for i in range(plan.inner):
         for j in range(plan.outer):
             owner = lax.rem(outer_id - j + plan.outer, plan.outer) * plan.inner
@@ -330,19 +332,19 @@
                 )
             )
     early = len(copies)
-    for n in range(1, len(held)):
+    for n in range(2, len(held)):
         copies.append(pltpu.make_async_copy(late[n], held[n], sems.at[n]))
     for copy in copies:
         copy.start()
+    copies[0].wait()
     special = me_ref[0] == 0
     width = plan.x_chunk
     middle = plan.ny // 2
     odd = forward_plane(plan, me_ref, pieces, (yf_high, yf_low), (xf_high, xf_low), rows_ref, freq_ref)
-    for copy in copies[:early]:
+    for copy in copies[1:early]:
         copy.wait()
     row = lax.broadcasted_iota(jnp.int32, (middle, width), 0)
     at_first = row == 0
-    own_edge = edge[pl.ds(slab, 1)]
     for mirrored, turn in ((0, 1.0), (1, -1.0)):
         re = slice(2 * mirrored * middle, (2 * mirrored + 1) * middle)
         im = slice((2 * mirrored + 1) * middle, (2 * mirrored + 2) * middle)
@@ -350,12 +352,13 @@
         for upper in range(2):
             cols = slice(upper * width, (upper + 1) * width)
             plane = weights[mirrored, :, cols]
+            change = at_first & special
             if mirrored:
-                weight = jnp.where(at_first & jnp.logical_not(special), own_edge[:, cols], plane)
-                second = jnp.where(at_first, own_edge[:, cols], plane)
+                weight = jnp.where(change, edge[1:2, cols], plane)
+                second = plane
             else:
                 weight = plane
-                second = jnp.where(at_first & special, edge[plan.slabs : plan.slabs + 1, cols], plane)
+                second = jnp.where(change, edge[0:1, cols], plane)
             re_sums = even[re] - odd[re] if upper else even[re] + odd[re]
             im_sums = even[im] - odd[im] if upper else even[im] + odd[im]
             real = weight * re_sums[:, :width] + (turn * second) * im_sums[:, width:]
@@ -404,12 +407,17 @@
     )(me, *arrays, *flat, *late)
 
 
-def gather_kernel(plan, chunk, counts, before, pieces, high, low, projection, out, scratch, held, sems):
+def gather_kernel(
+    plan, chunk, counts, before, high, low, projection, sent, out, scratch, held, sems, pieces
+):
     planes = plan.cell_planes
     rows = plan.slots * 2 * plan.row_block
+    fetch = pltpu.make_async_copy(sent, pieces, sems.at[plan.tx_chunk])
+    fetch.start()
     copies = tile_copies(plan, chunk, projection, held, sems)
     for copy in copies:
         copy.start()
+    fetch.wait()
     columns = [pieces[:, :, step].reshape(rows, LANES) for step in range(plan.steps)]
     scratch[...] = product(split(jnp.concatenate(columns, axis=1).T), (high[...], low[...]))
     for tx, copy in enumerate(copies):
@@ -436,8 +444,11 @@
 
 def gather(plan, chunk, counts, before, projection, high, low, pieces):
     kernel = functools.partial(gather_kernel, plan, chunk)
-    arrays = [counts, before, pieces, high, low]
-    return projection_call(plan, kernel, "depth_gather", arrays, projection, before.shape)
+    arrays = [counts, before, high, low]
+    scratch = [pltpu.VMEM(pieces.shape, jnp.float32)]
+    return projection_call(
+        plan, kernel, "depth_gather", arrays, [projection, pieces], before.shape, scratch
+    )
 
 
 def near_kernel(plan, extended, codes, blocks_ref, out):
@@ -528,41 +539,69 @@
     return jnp.stack([whole[:, i : i + planes] for i in range(3)], axis=1)
 
 
-def first_weights(plan, spectrum):
-    slab, cell = (lax.axis_index("slab"), lax.axis_index("cell"))
-    by_depth = jnp.transpose(spectrum, (1, 2, 0))
+def pick_kernel(plan, ids_ref, turned, by_depth, out, sems):
+    cell, slab = (ids_ref[0], ids_ref[1])
     half_id, place = (slab // plan.half, lax.rem(slab, plan.half))
-    blocks = []
+    copies = []
     for j in range(plan.outer):
         group = lax.rem(place // plan.inner + j, plan.outer)
         base = cell * plan.slabs + half_id * plan.half + group * plan.inner
-        planes = []
         for q in range(plan.inner):
             freq = base + q
             mirror = jnp.where(freq == 0, plan.nz // 2, plan.nz - freq)
-            for index in (freq, mirror):
-                planes.append(lax.dynamic_slice_in_dim(by_depth, index, 1, 0))
-        block = jnp.concatenate(planes, axis=0).reshape((plan.inner, 2) + by_depth.shape[1:])
-        if j > 0:
-            pairs = []
-            for source in range(plan.slabs):
-                base_id = source // plan.half * plan.half
-                pairs.append((source, base_id + (source - base_id + j * plan.inner) % plan.half))
-            block = lax.ppermute(block, "slab", pairs)
-        blocks.append(block)
-    return blocks
+            for m, index in enumerate((freq, mirror)):
+                n = (j * plan.inner + q) * 2 + m
+                copies.append(pltpu.make_async_copy(by_depth.at[index], out.at[j, q, m], sems.at[n]))
+    for copy in copies:
+        copy.start()
+    for copy in copies:
+        copy.wait()
+
+    @pl.when(place == 0)
+    def _():
+        row = lax.broadcasted_iota(jnp.int32, (8, plan.nx), 0)
+        for j in range(plan.outer):
+            group = lax.rem(place // plan.inner + j, plan.outer)
+            for q in range(plan.inner):
+                value = turned[pl.ds(group * plan.inner + q, 1)]
+                out[j, q, 1, 0:8] = jnp.where(row == 0, value, out[j, q, 1, 0:8])
 
 
 def edge_weights(plan, spectrum):
     slab, cell = (lax.axis_index("slab"), lax.axis_index("cell"))
     rows = jnp.transpose(spectrum[:, :, 0], (1, 0))
-    turned = jnp.concatenate([rows[plan.nz // 2 : plan.nz // 2 + 1], jnp.flip(rows, 0)], axis=0)
-    own = lax.dynamic_slice_in_dim(turned, cell * plan.slabs, plan.slabs, 0)
-    own = jnp.concatenate([own, rows[:1]], axis=0)
-    dest = lax.broadcasted_iota(jnp.int32, own.shape, 0)
-    from_middle = (dest < plan.half) | (dest == plan.slabs)
-    keep = jnp.where(from_middle, slab == plan.half, slab == 0)
-    return lax.psum(jnp.where(keep, own, 0.0), "slab")
+    middle = plan.nz // 2
+    turned = jnp.concatenate([rows[middle : middle + 1], jnp.flip(rows, 0)], axis=0)
+    other = cell * plan.slabs + (1 - slab // plan.half) * plan.half
+    sent = jnp.concatenate([lax.dynamic_slice_in_dim(turned, other, plan.half, 0), rows[:1]], axis=0)
+    return (lax.ppermute(sent, "slab", [(0, plan.half), (plan.half, 0)]), rows[middle : middle + 1])
+
+
+def first_weights(plan, spectrum, turned):
+    slab, cell = (lax.axis_index("slab"), lax.axis_index("cell"))
+    by_depth = jnp.transpose(spectrum, (1, 2, 0))
+    shape = (plan.outer, plan.inner, 2) + by_depth.shape[1:]
+    picked = pl.pallas_call(
+        functools.partial(pick_kernel, plan),
+        in_specs=[
+            pl.BlockSpec(memory_space=pltpu.SMEM),
+            pl.BlockSpec(memory_space=pltpu.VMEM),
+            pl.BlockSpec(memory_space=pl.ANY),
+        ],
+        out_specs=pl.BlockSpec(memory_space=pltpu.VMEM),
+        out_shape=jax.ShapeDtypeStruct(shape, jnp.float32),
+        scratch_shapes=[pltpu.SemaphoreType.DMA((2 * plan.half,))],
+        cost_estimate=pl.CostEstimate(flops=0, bytes_accessed=8 * math.prod(shape), transcendentals=0),
+        name="pick_planes",
+    )(jnp.stack([cell, slab]).astype(jnp.int32), turned, by_depth)
+    blocks = [picked[0]]
+    for j in range(1, plan.outer):
+        pairs = []
+        for source in range(plan.slabs):
+            base_id = source // plan.half * plan.half
+            pairs.append((source, base_id + (source - base_id + j * plan.inner) % plan.half))
+        blocks.append(lax.ppermute(picked[j], "slab", pairs))
+    return blocks
 
 
 def second_weights(plan, blocks):
@@ -612,14 +651,15 @@
     rows_shape = (plan.ny, 2 * plan.x_chunk)
     freq_shape = (2 * plan.ny, plan.x_chunk)
     both_shape = (2 * plan.ny, plan.nx)
-    blocks = first_weights(plan, spectrum)
-    edge = edge_weights(plan, spectrum)
+    turned, own_row = edge_weights(plan, spectrum)
     slot = lax.broadcasted_iota(jnp.int32, charges.shape, 0)
     masked = jnp.where(slot < counts[None], charges, 0.0)
     left, right = extend_rows(plan, masked)
     pieces = [project(plan, i, charges, counts, split_projection, *depth_forward) for i in range(CHUNKS)]
-    pieces[0], left, right = lax.optimization_barrier((pieces[0], left, right))
+    pieces[0], left, right, turned = lax.optimization_barrier((pieces[0], left, right, turned))
     even_pieces = exchange(pieces[0])
+    blocks = first_weights(plan, spectrum, turned)
+    edge = jnp.concatenate([turned[plan.half :], own_row], axis=0)
     extended = extend_planes(plan, masked, left, right)
     pieces[1], extended, *blocks = lax.optimization_barrier((pieces[1], extended, *blocks))
     odd_pieces = exchange(pieces[1])
@@ -628,11 +668,11 @@
         plan, first_plane_kernel, "even_planes", me, [even_pieces], [(y_forward, None), (x_forward, 0)], [],
         [both_shape], values(rows_shape, freq_shape), 2,
     )
-    late = [even, x_backward[0][:1], x_backward[1][:1], *y_backward]
+    late = [odd_pieces, even, x_backward[0][:1], x_backward[1][:1], *y_backward]
     copies = [pltpu.VMEM(array.shape, array.dtype) for array in late]
     copies.append(pltpu.SemaphoreType.DMA((len(late) + plan.half + 1,)))
     back, rest = plane_call(
-        plan, middle_plane_kernel, "middle_planes", me, [edge, odd_pieces],
+        plan, middle_plane_kernel, "middle_planes", me, [edge],
         [(y_forward, None), (x_forward, 1)], late + strips, [piece_shape(plan), freq_shape],
         values(rows_shape, freq_shape, freq_shape, freq_shape, (2, plan.ny // 2, plan.nx)) + copies, 4,
     )

time: 221 us -> 163 us (0.74)
  blocking collectives: 72 us -> 0 us
  waiting for transfers between devices: 37.6 us -> 52.8 us
  local copies, waits for them, and re-layouts: 11.6 us -> 5.56 us
  Pallas kernels: 65.6 us -> 69.6 us
    psum x1 -> x0, blocking collectives: 72 us -> none  [edge_weights(): return lax.psum(jnp.where(keep, own, 0.0), 'slab')]
    ppermute x3, waiting for transfers between devices: 1.22 us -> 10.4 us  [second_weights(): strip = lax.ppermute(strip, 'slab', pairs)]
    unnamed x22 -> x7, local copies, waits for them, and re-layouts: 8.98 us -> 0.02 us
    all_to_all x4, starting transfers between devices: 20 us -> 13.9 us  [exchange(): return lax.all_to_all(pieces, axes, split_axis=0, concat_axis=0, tiled=True)]
    ppermute x1 -> x2, starting transfers between devices: 0.07 us -> 5.95 us  [the longest x1 5.94 us: edge_weights(): lax.ppermute(sent, 'slab', [(0, plan.half), (plan.half, 0)])]
    all_to_all x4, waiting for transfers between devices: 25.6 us -> 30.7 us  [exchange(): return lax.all_to_all(pieces, axes, split_axis=0, concat_axis=0, tiled=True)]
    pallas_call x0 -> x1, Pallas kernels: none -> 3.14 us  [first_weights(): pl.pallas_call(functools.partial(pick_kernel, plan), in_specs=[pl.BlockSp...]
    ppermute x1 -> x2, waiting for transfers between devices: 7.02 us -> 7.05 us  [the longest x1 7.05 us: first_weights(): blocks.append(lax.ppermute(picked[j], 'slab', pairs))]
  transfers between devices with their start and end apart: 12 -> 13, of which waited for: 6 -> 8; matrix products, arithmetic and copies ran while one was open for 5% -> 5% of each run, Pallas kernels for 22% -> 32%
where the time goes in v6:
time: 163 us; the launch traced here: 162 us
  Pallas kernels  69.6 us (43%)
  waiting for transfers between devices  52.8 us (32%)
  starting transfers between devices  29.7 us (18%)
  local copies, waits for them, and re-layouts  5.56 us (3%)
  other arithmetic  4.16 us (3%)
    all_to_all x4, waiting for transfers between devices, exchange(): return lax.all_to_all(pieces, axes, split_axis=0, concat_axis=0, tiled=True)  30.7 us
    pallas_call x4, Pallas kernels, projection_call(): pl.pallas_call(kernel, grid=(1,), in_specs=[whole_spec(array.shape) for a...  27.7 us
    pallas_call x3, Pallas kernels, plane_call(): pl.pallas_call(functools.partial(kernel, plan), grid=(1,), in_specs=[pl.B...  23.2 us
    pallas_call x1, Pallas kernels, near_field(): pl.pallas_call(functools.partial(near_kernel, plan), grid=(plan.cell_cols...  15.5 us
    all_to_all x4, starting transfers between devices, exchange(): return lax.all_to_all(pieces, axes, split_axis=0, concat_axis=0, tiled=True)  13.9 us
    ppermute x3, waiting for transfers between devices, second_weights(): strip = lax.ppermute(strip, 'slab', pairs)  10.4 us
    ppermute x1, waiting for transfers between devices, first_weights(): blocks.append(lax.ppermute(picked[j], 'slab', pairs))  7.05 us
    ppermute x1, starting transfers between devices, edge_weights(): lax.ppermute(sent, 'slab', [(0, plan.half), (plan.half, 0)])  5.94 us
  transfers between devices with their start and end apart: 13, of which 8 were waited for; matrix products, arithmetic and copies ran while one was open for 5% of the time, Pallas kernels for 32%

profile of v6, /device:TPU:0, one launch (start us, length us, event | category | flops | bytes accessed | tf_op | source)
XLA Modules:
  0.0 162.3 jit_solution(10988413909979352686)
XLA Ops:
  0.0 1.3 slice.41
  1.3 0.1 rev.4
  1.5 5.9 %collective-permute-start.2 = (f32[9,512]{1,0:T(8,128)S(1)}, f32[9,512]{1,0:T(8,128)S(1)}, u32[]{:S(2)}, u32[]{:S(2)}) collective-permute-start(f32[9,512]{1,0:T(8,128)S(1)} %pad_maximum_fusion.7), channel_id=1, source_target_pairs={{0,16},{16,0},{1,17},{17,1}} | collective-permute-start | bytes 55304 | tf_op jit(solution)/shard_map/ppermute | solution.py:577
  7.5 1.0 fusion.2
  8.5 0.1 fusion.5
  8.5 1.5 collective-permute-start.1
  10.1 0.5 collective-permute-start
  10.6 7.4 %project_depth.2 = f32[32,2,4,8,128]{4,3,2,1,0:T(8,128)} custom-call(f32[8,8,1024]{2,1,0:T(8,128)} %charges.3, s32[8,1024]{1,0:T(8,128)} %counts.7, bf16[512,512]{1,0:T(8,128)(2,1)} %constant.75.clone.high, bf16[512,512]{1,0:T(8,128)(2,1)} %constant.76.clone.low, f32[8,2,2,16,8,1024]{5,4,3,2,1,0:T(8,128)} %bitcast.23), custom_call_target="tpu_custom_call" | custom-call | flops 4194304 | bytes 8388608 | tf_op jit(solution)/shard_map/project_depth/pallas_call | solution.py:184
  18.0 0.0 collective-permute-done.1
  18.0 0.0 collective-permute-done
  18.0 0.0 collective-permute-done.2.turned
  18.0 0.0 copy-start.2
  18.1 2.7 %all-to-all-start.1 = ((f32[32,2,4,8,128]{4,3,2,1,0:T(8,128)}), f32[32,2,4,8,128]{4,3,2,1,0:T(8,128)S(1)}, u32[]{:S(2)}, u32[]{:S(2)}) async-start(f32[32,2,4,8,128]{4,3,2,1,0:T(8,128)} %project_depth.2), calls=%async_computation.1 | async-start | bytes 2097152 | tf_op jit(solution)/shard_map/all_to_all | solution.py:646
  20.7 0.7 pad_add_fusion.ids_ref
  21.4 0.1 concatenate.34
  21.5 0.7 fusion.4
  22.2 0.1 collective-permute-start.3
  22.3 4.3 %collective-permute-start.4 = (f32[8,1,1280]{2,1,0:T(1,128)S(1)}, f32[8,1,1280]{2,1,0:T(1,128)S(1)}, u32[]{:S(2)}, u32[]{:S(2)}) collective-permute-start(f32[8,1,1280]{2,1,0:T(1,128)S(1)} %get-tuple-element.42), channel_id=1, source_target_pairs={{2,0},{4,2},{6,4},{8,6},{10,8},{12,10},{14,12},{16,14},{18,16},{20... | collective-permute-start | bytes 122888 | tf_op jit(solution)/shard_map/ppermute | solution.py:536
  26.6 0.0 copy-done.2
  26.6 3.1 %pick_planes.1 = f32[2,4,2,32,512]{4,3,2,1,0:T(8,128)} custom-call(s32[2]{0:T(128)} %pad_add_fusion.ids_ref, f32[9,512]{1,0:T(8,128)} %copy-done.2, f32[64,32,512]{2,1,0:T(8,128)} %bitcast.27), custom_call_target="tpu_custom_call" | custom-call | bytes 2097152 | tf_op jit(solution)/shard_map/pick_planes/pallas_call | solution.py:584
  29.7 2.1 %slice_bitcast_fusion = (f32[4,2,32,512]{3,2,1,0:T(8,128)}, f32[4,2,32,512]{3,2,1,0:T(8,128)S(1)}) fusion(f32[2,4,2,32,512]{4,3,2,1,0:T(8,128)} %pick_planes.1), kind=kLoop, calls=%fused_computation.1 | loop fusion | bytes 2097152 | tf_op jit(solution)/shard_map/squeeze | solution.py:603
  31.9 0.0 slice-start
  31.9 0.0 collective-permute-start.5
  31.9 7.4 %project_depth.3 = f32[32,2,4,8,128]{4,3,2,1,0:T(8,128)} custom-call(f32[8,8,1024]{2,1,0:T(8,128)} %charges.3, s32[8,1024]{1,0:T(8,128)} %counts.7, bf16[512,512]{1,0:T(8,128)(2,1)} %constant.75.clone.high, bf16[512,512]{1,0:T(8,128)(2,1)} %constant.76.clone.low, f32[8,2,2,16,8,1024]{5,4,3,2,1,0:T(8,128)} %bitcast.24), custom_call_target="tpu_custom_call" | custom-call | flops 4194304 | bytes 8388608 | tf_op jit(solution)/shard_map/project_depth/pallas_call | solution.py:184
  39.3 4.7 %collective-permute-done.3 = f32[8,1,1280]{2,1,0:T(1,128)S(1)} collective-permute-done((f32[8,1,1280]{2,1,0:T(1,128)}, f32[8,1,1280]{2,1,0:T(1,128)S(1)}, u32[]{:S(2)}, u32[]{:S(2)}) %collective-permute-start.3) | collective-permute-done | bytes 40992 | tf_op jit(solution)/shard_map/ppermute | solution.py:535
  43.9 0.0 collective-permute-done.4
  43.9 0.1 fusion.1
  44.1 1.0 pad_maximum_fusion.extended
  45.1 7.0 %collective-permute-done.5 = f32[4,2,32,512]{3,2,1,0:T(8,128)} collective-permute-done((f32[4,2,32,512]{3,2,1,0:T(8,128)}, f32[4,2,32,512]{3,2,1,0:T(8,128)}, u32[]{:S(2)}, u32[]{:S(2)}) %collective-permute-start.5) | collective-permute-done | bytes 524320 | tf_op jit(solution)/shard_map/ppermute | solution.py:603
  52.1 0.0 all-to-all-done.1.pieces
  52.1 0.0 copy-start.1
  52.1 5.0 %all-to-all-start = ((f32[32,2,4,8,128]{4,3,2,1,0:T(8,128)}), f32[32,2,4,8,128]{4,3,2,1,0:T(8,128)}, u32[]{:S(2)}, u32[]{:S(2)}) async-start(f32[32,2,4,8,128]{4,3,2,1,0:T(8,128)} %project_depth.3), calls=%async_computation | async-start | bytes 2097152 | tf_op jit(solution)/shard_map/all_to_all | solution.py:646
  57.2 0.0 slice-done
  57.2 0.6 pad_maximum_fusion.8.edge
  57.8 1.2 constant_dynamic-slice_fusion
  59.0 0.2 collective-permute-start.6
  59.3 1.7 %collective-permute-start.7 = (f32[2,2,32,512]{3,2,1,0:T(8,128)S(1)}, f32[2,2,32,512]{3,2,1,0:T(8,128)}, u32[]{:S(2)}, u32[]{:S(2)}) collective-permute-start(f32[2,2,32,512]{3,2,1,0:T(8,128)S(1)} %pad_maximum_fusion.5), channel_id=1, source_target_pairs={{0,4},{2,6},{4,0},{6,2},{8,12},{10,14},{12,8},{14,10},{16,20},{18,... | collective-permute-start | bytes 786440 | tf_op jit(solution)/shard_map/ppermute | solution.py:618
  61.0 1.4 collective-permute-start.8
  62.4 0.7 pad_maximum_fusion.3.refs_6_
  63.1 0.0 copy-done.1
  63.1 5.7 %even_planes.1.refs_1_ = f32[1024,512]{1,0:T(8,128)} custom-call(s32[1]{0:T(128)} %bitcast.me_ref, f32[32,2,4,8,128]{4,3,2,1,0:T(8,128)} %copy-done.1, bf16[512,512]{1,0:T(8,128)(2,1)} %constant.77.clone.y_high.yf_high, bf16[512,512]{1,0:T(8,128)(2,1)} %constant.78.clone.y_low.yf_low, bf16[2,256,512]{2,1,0:T(8,128)(2,1)} %constant.79.clone.x_high.xf_high, ...), custom_call_target="tpu_custom_call" | custom-call | flops 1610612736 | bytes 3145728 | tf_op jit(solution)/shard_map/even_planes/pallas_call | solution.py:395
  68.8 4.8 %collective-permute-done.6.refs_7_ = f32[2,2,32,512]{3,2,1,0:T(8,128)} collective-permute-done((f32[2,2,32,512]{3,2,1,0:T(8,128)S(1)}, f32[2,2,32,512]{3,2,1,0:T(8,128)}, u32[]{:S(2)}, u32[]{:S(2)}) %collective-permute-start.6) | collective-permute-done | bytes 262176 | tf_op jit(solution)/shard_map/ppermute | solution.py:618
  73.6 1.3 collective-permute-done.7.refs_8_
  74.9 4.4 %collective-permute-done.8.refs_9_ = f32[2,2,32,512]{3,2,1,0:T(8,128)} collective-permute-done((f32[2,2,32,512]{3,2,1,0:T(8,128)S(1)}, f32[2,2,32,512]{3,2,1,0:T(8,128)}, u32[]{:S(2)}, u32[]{:S(2)}) %collective-permute-start.8) | collective-permute-done | bytes 262176 | tf_op jit(solution)/shard_map/ppermute | solution.py:618
  79.2 5.1 %all-to-all-done.refs_0_ = f32[32,2,4,8,128]{4,3,2,1,0:T(8,128)} async-done(((f32[32,2,4,8,128]{4,3,2,1,0:T(8,128)}), f32[32,2,4,8,128]{4,3,2,1,0:T(8,128)}, u32[]{:S(2)}, u32[]{:S(2)}) %all-to-all-start) | async-done | bytes 1048608 | tf_op jit(solution)/shard_map/all_to_all | solution.py:646
  84.3 10.9 %middle_planes.1 = (f32[32,2,4,8,128]{4,3,2,1,0:T(8,128)}, f32[1024,256]{1,0:T(8,128)}) custom-call(s32[1]{0:T(128)} %bitcast.me_ref, f32[2,512]{1,0:T(2,128)} %pad_maximum_fusion.8.edge, bf16[512,512]{1,0:T(8,128)(2,1)} %constant.77.clone.y_high.yf_high, bf16[512,512]{1,0:T(8,128)(2,1)} %constant.78.clone.y_low.yf_low, ...), custom_call_target="tpu_custom_call" | custom-call | flops 3221225472 | bytes 9441280 | tf_op jit(solution)/shard_map/middle_planes/pallas_call | solution.py:395
  95.2 2.8 %all-to-all-start.2 = ((f32[32,2,4,8,128]{4,3,2,1,0:T(8,128)}), f32[32,2,4,8,128]{4,3,2,1,0:T(8,128)S(1)}, u32[]{:S(2)}, u32[]{:S(2)}) async-start(f32[32,2,4,8,128]{4,3,2,1,0:T(8,128)} %get-tuple-element.27), calls=%async_computation.2 | async-start | bytes 2097152 | tf_op jit(solution)/shard_map/all_to_all | solution.py:646
  98.1 15.5 %near_blocks.1.before = f32[8,8,1024]{2,1,0:T(8,128)} custom-call(f32[8,3,8,1280]{3,2,1,0:T(8,128)} %pad_maximum_fusion.extended, s32[6,8,1024]{2,1,0:T(8,128)} %codes.1, f32[6,8,8,8,1024]{4,3,2,1,0:T(8,128)} %blocks_ref.1), custom_call_target="tpu_custom_call" | custom-call | flops 6291456 | bytes 12582912 | tf_op jit(solution)/shard_map/near_blocks/pallas_call | solution.py:498
  113.6 6.6 %odd_planes.1 = f32[32,2,4,8,128]{4,3,2,1,0:T(8,128)} custom-call(s32[1]{0:T(128)} %bitcast.me_ref, f32[1024,256]{1,0:T(8,128)} %get-tuple-element.24.freqs, bf16[2,256,512]{2,1,0:T(8,128)(2,1)} %constant.85.clone.x_high, bf16[2,256,512]{2,1,0:T(8,128)(2,1)} %constant.86.clone.x_low, bf16[512,512]{1,0:T(8,128)(2,1)} %constant.83.clone.refs_4_.y_high, ...), custom_call_target="tpu_custom_call" | custom-call | flops 1610612736 | bytes 3145728 | tf_op jit(solution)/shard_map/odd_planes/pallas_call | solution.py:395
  120.2 4.9 %all-to-all-done.2.sent = f32[32,2,4,8,128]{4,3,2,1,0:T(8,128)S(1)} async-done(((f32[32,2,4,8,128]{4,3,2,1,0:T(8,128)}), f32[32,2,4,8,128]{4,3,2,1,0:T(8,128)S(1)}, u32[]{:S(2)}, u32[]{:S(2)}) %all-to-all-start.2) | async-done | bytes 1048608 | tf_op jit(solution)/shard_map/all_to_all | solution.py:646
  125.1 0.0 copy-start
  125.1 3.4 %all-to-all-start.3 = ((f32[32,2,4,8,128]{4,3,2,1,0:T(8,128)}), f32[32,2,4,8,128]{4,3,2,1,0:T(8,128)}, u32[]{:S(2)}, u32[]{:S(2)}) async-start(f32[32,2,4,8,128]{4,3,2,1,0:T(8,128)} %odd_planes.1), calls=%async_computation.3 | async-start | bytes 2097152 | tf_op jit(solution)/shard_map/all_to_all | solution.py:646
  128.5 0.0 copy-done
  128.5 6.4 %depth_gather.2.before = f32[8,8,1024]{2,1,0:T(8,128)} custom-call(s32[8,1024]{1,0:T(8,128)} %counts.7, f32[8,8,1024]{2,1,0:T(8,128)} %near_blocks.1.before, bf16[512,512]{1,0:T(8,128)(2,1)} %constant.87.clone.high, bf16[512,512]{1,0:T(8,128)(2,1)} %constant.88.clone.low, f32[8,2,2,16,8,1024]{5,4,3,2,1,0:T(8,128)} %bitcast.25, f32[32,2,4,8,128]{4,3,2,1,0:T(8,128)} %copy-done), custom_call_target="tpu_custom_call" | custom-call | flops 4194304 | bytes 8388608 | tf_op jit(solution)/shard_map/depth_gather/pallas_call | solution.py:184
  134.9 20.7 %all-to-all-done.3.sent = f32[32,2,4,8,128]{4,3,2,1,0:T(8,128)} async-done(((f32[32,2,4,8,128]{4,3,2,1,0:T(8,128)}), f32[32,2,4,8,128]{4,3,2,1,0:T(8,128)}, u32[]{:S(2)}, u32[]{:S(2)}) %all-to-all-start.3) | async-done | bytes 1048608 | tf_op jit(solution)/shard_map/all_to_all | solution.py:646
  155.7 6.4 %depth_gather.3 = f32[8,8,1024]{2,1,0:T(8,128)} custom-call(s32[8,1024]{1,0:T(8,128)} %counts.7, f32[8,8,1024]{2,1,0:T(8,128)} %depth_gather.2.before, bf16[512,512]{1,0:T(8,128)(2,1)} %constant.87.clone.high, bf16[512,512]{1,0:T(8,128)(2,1)} %constant.88.clone.low, f32[8,2,2,16,8,1024]{5,4,3,2,1,0:T(8,128)} %bitcast.26, ...), custom_call_target="tpu_custom_call" | custom-call | flops 4194304 | bytes 8388608 | tf_op jit(solution)/shard_map/depth_gather/pallas_call | solution.py:184
  (8 shorter events, 0.1 us)
Async XLA Ops:
  1.5 16.5 %collective-permute-start.2 = (f32[9,512]{1,0:T(8,128)S(1)}, f32[9,512]{1,0:T(8,128)S(1)}, u32[]{:S(2)}, u32[]{:S(2)}) collective-permute-start(f32[9,512]{1,0:T(8,128)S(1)} %pad_maximum_fusion.7), channel_id=1, source_target_pairs={{0,16},{16,0},{1,17},{17,1}} | collective-permute-start | bytes 55304 | tf_op jit(solution)/shard_map/ppermute | solution.py:577
  8.5 9.5 %collective-permute-start.1 = (f32[8,8,16]{2,1,0:T(8,128)S(1)}, f32[8,8,16]{2,1,0:T(8,128)S(1)}, u32[]{:S(2)}, u32[]{:S(2)}) collective-permute-start(f32[8,8,16]{2,1,0:T(8,128)S(1)} %get-tuple-element.43), channel_id=1, source_target_pairs={{1,0},{0,1},{3,2},{2,3},{5,4},{4,5},{7,6},{6,7},{9,8},{8,9},{11,10... | collective-permute-start | bytes 12296 | tf_op jit(solution)/shard_map/ppermute | solution.py:527
  10.1 8.0 %collective-permute-start = (f32[8,8,16]{2,1,0:T(8,128)S(1)}, f32[8,8,16]{2,1,0:T(8,128)S(1)}, u32[]{:S(2)}, u32[]{:S(2)}) collective-permute-start(f32[8,8,16]{2,1,0:T(8,128)S(1)} %get-tuple-element.44), channel_id=1, source_target_pairs={{0,1},{1,0},{2,3},{3,2},{4,5},{5,4},{6,7},{7,6},{8,9},{9,8},{10,11... | collective-permute-start | bytes 12296 | tf_op jit(solution)/shard_map/ppermute | solution.py:526
  18.0 8.6 %copy-start.2 = (f32[9,512]{1,0:T(8,128)}, f32[9,512]{1,0:T(8,128)S(1)}, u32[]{:S(2)}) copy-start(f32[9,512]{1,0:T(8,128)S(1)} %collective-permute-done.2.turned) | copy-start | bytes 55300
  18.1 34.1 %all-to-all-start.1 = ((f32[32,2,4,8,128]{4,3,2,1,0:T(8,128)}), f32[32,2,4,8,128]{4,3,2,1,0:T(8,128)S(1)}, u32[]{:S(2)}, u32[]{:S(2)}) async-start(f32[32,2,4,8,128]{4,3,2,1,0:T(8,128)} %project_depth.2), calls=%async_computation.1 | async-start | bytes 2097152 | tf_op jit(solution)/shard_map/all_to_all | solution.py:646
  22.2 21.8 %collective-permute-start.3 = (f32[8,1,1280]{2,1,0:T(1,128)}, f32[8,1,1280]{2,1,0:T(1,128)S(1)}, u32[]{:S(2)}, u32[]{:S(2)}) collective-permute-start(f32[8,1,1280]{2,1,0:T(1,128)} %get-tuple-element.41), channel_id=1, source_target_pairs={{0,2},{2,4},{4,6},{6,8},{8,10},{10,12},{12,14},{14,16},{16,18},{18... | collective-permute-start | bytes 122888 | tf_op jit(solution)/shard_map/ppermute | solution.py:535
  22.3 21.7 %collective-permute-start.4 = (f32[8,1,1280]{2,1,0:T(1,128)S(1)}, f32[8,1,1280]{2,1,0:T(1,128)S(1)}, u32[]{:S(2)}, u32[]{:S(2)}) collective-permute-start(f32[8,1,1280]{2,1,0:T(1,128)S(1)} %get-tuple-element.42), channel_id=1, source_target_pairs={{2,0},{4,2},{6,4},{8,6},{10,8},{12,10},{14,12},{16,14},{18,16},{20... | collective-permute-start | bytes 122888 | tf_op jit(solution)/shard_map/ppermute | solution.py:536
  31.9 25.4 %slice-start = ((f32[9,512]{1,0:T(8,128)}), f32[1,512]{1,0:T(1,128)S(1)}, s32[]{:S(2)}) async-start(f32[9,512]{1,0:T(8,128)} %copy-done.2), calls=%async_computation.4 | async-start | bytes 4096 | tf_op jit(solution)/shard_map/slice | solution.py:662
  31.9 20.3 %collective-permute-start.5 = (f32[4,2,32,512]{3,2,1,0:T(8,128)}, f32[4,2,32,512]{3,2,1,0:T(8,128)}, u32[]{:S(2)}, u32[]{:S(2)}) collective-permute-start(f32[4,2,32,512]{3,2,1,0:T(8,128)} %get-tuple-element.29), channel_id=1, source_target_pairs={{0,8},{2,10},{4,12},{6,14},{8,0},{10,2},{12,4},{14,6},{16,24},{18,... | collective-permute-start | bytes 1572872 | tf_op jit(solution)/shard_map/ppermute | solution.py:603
  52.1 11.0 %copy-start.1 = (f32[32,2,4,8,128]{4,3,2,1,0:T(8,128)}, f32[32,2,4,8,128]{4,3,2,1,0:T(8,128)S(1)}, u32[]{:S(2)}) copy-start(f32[32,2,4,8,128]{4,3,2,1,0:T(8,128)S(1)} %all-to-all-done.1.pieces) | copy-start | bytes 3145732
  52.1 32.2 %all-to-all-start = ((f32[32,2,4,8,128]{4,3,2,1,0:T(8,128)}), f32[32,2,4,8,128]{4,3,2,1,0:T(8,128)}, u32[]{:S(2)}, u32[]{:S(2)}) async-start(f32[32,2,4,8,128]{4,3,2,1,0:T(8,128)} %project_depth.3), calls=%async_computation | async-start | bytes 2097152 | tf_op jit(solution)/shard_map/all_to_all | solution.py:646
  59.0 14.6 %collective-permute-start.6 = (f32[2,2,32,512]{3,2,1,0:T(8,128)S(1)}, f32[2,2,32,512]{3,2,1,0:T(8,128)}, u32[]{:S(2)}, u32[]{:S(2)}) collective-permute-start(f32[2,2,32,512]{3,2,1,0:T(8,128)S(1)} %pad_maximum_fusion.4), channel_id=1, source_target_pairs={{0,2},{2,4},{4,6},{6,0},{8,10},{10,12},{12,14},{14,8},{16,18},{18,... | collective-permute-start | bytes 786440 | tf_op jit(solution)/shard_map/ppermute | solution.py:618
  59.3 15.6 %collective-permute-start.7 = (f32[2,2,32,512]{3,2,1,0:T(8,128)S(1)}, f32[2,2,32,512]{3,2,1,0:T(8,128)}, u32[]{:S(2)}, u32[]{:S(2)}) collective-permute-start(f32[2,2,32,512]{3,2,1,0:T(8,128)S(1)} %pad_maximum_fusion.5), channel_id=1, source_target_pairs={{0,4},{2,6},{4,0},{6,2},{8,12},{10,14},{12,8},{14,10},{16,20},{18,... | collective-permute-start | bytes 786440 | tf_op jit(solution)/shard_map/ppermute | solution.py:618
  61.0 18.2 %collective-permute-start.8 = (f32[2,2,32,512]{3,2,1,0:T(8,128)S(1)}, f32[2,2,32,512]{3,2,1,0:T(8,128)}, u32[]{:S(2)}, u32[]{:S(2)}) collective-permute-start(f32[2,2,32,512]{3,2,1,0:T(8,128)S(1)} %pad_maximum_fusion.6), channel_id=1, source_target_pairs={{0,6},{2,0},{4,2},{6,4},{8,14},{10,8},{12,10},{14,12},{16,22},{18,... | collective-permute-start | bytes 786440 | tf_op jit(solution)/shard_map/ppermute | solution.py:618
  95.2 29.9 %all-to-all-start.2 = ((f32[32,2,4,8,128]{4,3,2,1,0:T(8,128)}), f32[32,2,4,8,128]{4,3,2,1,0:T(8,128)S(1)}, u32[]{:S(2)}, u32[]{:S(2)}) async-start(f32[32,2,4,8,128]{4,3,2,1,0:T(8,128)} %get-tuple-element.27), calls=%async_computation.2 | async-start | bytes 2097152 | tf_op jit(solution)/shard_map/all_to_all | solution.py:646
  125.1 3.4 %copy-start = (f32[32,2,4,8,128]{4,3,2,1,0:T(8,128)}, f32[32,2,4,8,128]{4,3,2,1,0:T(8,128)S(1)}, u32[]{:S(2)}) copy-start(f32[32,2,4,8,128]{4,3,2,1,0:T(8,128)S(1)} %all-to-all-done.2.sent) | copy-start | bytes 3145732
  125.1 30.6 %all-to-all-start.3 = ((f32[32,2,4,8,128]{4,3,2,1,0:T(8,128)}), f32[32,2,4,8,128]{4,3,2,1,0:T(8,128)}, u32[]{:S(2)}, u32[]{:S(2)}) async-start(f32[32,2,4,8,128]{4,3,2,1,0:T(8,128)} %odd_planes.1), calls=%async_computation.3 | async-start | bytes 2097152 | tf_op jit(solution)/shard_map/all_to_all | solution.py:646

commit v7 on v6

--- a/solution.py
+++ b/solution.py
@@ -161,7 +161,7 @@
             return carry
 
         lax.fori_loop(0, plan.steps * plan.step_blocks, body, 0)
-    spectra = product((high[...], low[...]), split(scratch[...]), ((1,), (1,)))
+    spectra = product(split(scratch[...]), (high[...], low[...])).T
     shape = (plan.slots, 2, plan.row_block, LANES)
     for step in range(plan.steps):
         out[:, :, step] = spectra[:, step * LANES : (step + 1) * LANES].reshape(shape)
@@ -539,7 +539,8 @@
     return jnp.stack([whole[:, i : i + planes] for i in range(3)], axis=1)
 
 
-def pick_kernel(plan, ids_ref, turned, by_depth, out, sems):
+def pick_kernel(plan, ids_ref, by_depth, *refs):
+    outs, sems = (refs[:-1], refs[-1])
     cell, slab = (ids_ref[0], ids_ref[1])
     half_id, place = (slab // plan.half, lax.rem(slab, plan.half))
     copies = []
@@ -551,20 +552,40 @@
             mirror = jnp.where(freq == 0, plan.nz // 2, plan.nz - freq)
             for m, index in enumerate((freq, mirror)):
                 n = (j * plan.inner + q) * 2 + m
-                copies.append(pltpu.make_async_copy(by_depth.at[index], out.at[j, q, m], sems.at[n]))
+                out = outs[2 * j + m]
+                copies.append(pltpu.make_async_copy(by_depth.at[index], out.at[q], sems.at[n]))
     for copy in copies:
         copy.start()
     for copy in copies:
         copy.wait()
 
-    @pl.when(place == 0)
-    def _():
-        row = lax.broadcasted_iota(jnp.int32, (8, plan.nx), 0)
-        for j in range(plan.outer):
-            group = lax.rem(place // plan.inner + j, plan.outer)
-            for q in range(plan.inner):
-                value = turned[pl.ds(group * plan.inner + q, 1)]
-                out[j, q, 1, 0:8] = jnp.where(row == 0, value, out[j, q, 1, 0:8])
+
+def pick_planes(plan, spectrum):
+    by_depth = jnp.transpose(spectrum, (1, 2, 0))
+    shape = (plan.inner,) + by_depth.shape[1:]
+    count = 2 * plan.outer
+    ids = jnp.stack([lax.axis_index("cell"), lax.axis_index("slab")]).astype(jnp.int32)
+    return pl.pallas_call(
+        functools.partial(pick_kernel, plan),
+        in_specs=[pl.BlockSpec(memory_space=pltpu.SMEM), pl.BlockSpec(memory_space=pl.ANY)],
+        out_specs=[pl.BlockSpec(memory_space=pl.ANY)] * count,
+        out_shape=[jax.ShapeDtypeStruct(shape, jnp.float32)] * count,
+        scratch_shapes=[pltpu.SemaphoreType.DMA((2 * plan.half,))],
+        cost_estimate=pl.CostEstimate(
+            flops=0, bytes_accessed=8 * count * math.prod(shape), transcendentals=0
+        ),
+        name="pick_planes",
+    )(ids, by_depth)
+
+
+def outer_shift(plan, value, j):
+    if j == 0:
+        return value
+    pairs = []
+    for source in range(plan.slabs):
+        base = source // plan.half * plan.half
+        pairs.append((source, base + (source - base + j * plan.inner) % plan.half))
+    return lax.ppermute(value, "slab", pairs)
 
 
 def edge_weights(plan, spectrum):
@@ -573,43 +594,26 @@
     middle = plan.nz // 2
     turned = jnp.concatenate([rows[middle : middle + 1], jnp.flip(rows, 0)], axis=0)
     other = cell * plan.slabs + (1 - slab // plan.half) * plan.half
-    sent = jnp.concatenate([lax.dynamic_slice_in_dim(turned, other, plan.half, 0), rows[:1]], axis=0)
-    return (lax.ppermute(sent, "slab", [(0, plan.half), (plan.half, 0)]), rows[middle : middle + 1])
-
-
-def first_weights(plan, spectrum, turned):
-    slab, cell = (lax.axis_index("slab"), lax.axis_index("cell"))
-    by_depth = jnp.transpose(spectrum, (1, 2, 0))
-    shape = (plan.outer, plan.inner, 2) + by_depth.shape[1:]
-    picked = pl.pallas_call(
-        functools.partial(pick_kernel, plan),
-        in_specs=[
-            pl.BlockSpec(memory_space=pltpu.SMEM),
-            pl.BlockSpec(memory_space=pltpu.VMEM),
-            pl.BlockSpec(memory_space=pl.ANY),
-        ],
-        out_specs=pl.BlockSpec(memory_space=pltpu.VMEM),
-        out_shape=jax.ShapeDtypeStruct(shape, jnp.float32),
-        scratch_shapes=[pltpu.SemaphoreType.DMA((2 * plan.half,))],
-        cost_estimate=pl.CostEstimate(flops=0, bytes_accessed=8 * math.prod(shape), transcendentals=0),
-        name="pick_planes",
-    )(jnp.stack([cell, slab]).astype(jnp.int32), turned, by_depth)
-    blocks = [picked[0]]
-    for j in range(1, plan.outer):
-        pairs = []
-        for source in range(plan.slabs):
-            base_id = source // plan.half * plan.half
-            pairs.append((source, base_id + (source - base_id + j * plan.inner) % plan.half))
-        blocks.append(lax.ppermute(picked[j], "slab", pairs))
-    return blocks
-
-
-def second_weights(plan, blocks):
+    total = 0.0
+    for j in range(plan.outer):
+        sent = lax.dynamic_slice_in_dim(turned, other + j * plan.inner, plan.inner, 0)
+        sent = jnp.concatenate([sent, rows[:1]], axis=0)
+        pairs = [(plan.half, j * plan.inner), (0, plan.half + j * plan.inner)]
+        total = total + lax.ppermute(sent, "slab", pairs)
+    return (total, rows[middle : middle + 1])
+
+
+def second_weights(plan, blocks, turned):
     slab = lax.axis_index("slab")
+    part = lax.rem(slab, plan.half) // plan.inner
     strips = []
     for i in range(plan.inner):
         place = lax.rem(slab + i, plan.inner)
-        strip = jnp.concatenate([lax.dynamic_slice_in_dim(b, place, 1, 0) for b in blocks], axis=0)
+        rows = [lax.dynamic_slice_in_dim(block, place, 1, 0) for pair in blocks for block in pair]
+        strip = jnp.stack(rows).reshape((plan.outer, 2) + blocks[0][0].shape[1:])
+        ids = [lax.broadcasted_iota(jnp.int32, strip.shape, n) for n in range(3)]
+        change = (ids[0] == part) & (ids[1] == 1) & (ids[2] == 0) & (slab % plan.inner == 0)
+        strip = jnp.where(change, lax.dynamic_slice_in_dim(turned, place, 1, 0), strip)
         if i > 0:
             pairs = []
             for source in range(plan.slabs):
@@ -628,7 +632,8 @@
     if not plan.fits():
         return plain_device(charges, counts, projection, near_blocks, neighbours, spectrum)
     me = (lax.axis_index("cell") * slabs + lax.axis_index("slab")).astype(jnp.int32).reshape(1)
-    depth_forward, depth_backward = [halves(table) for table in plan.depth_tables()]
+    forward_table, backward_table = plan.depth_tables()
+    depth_forward, depth_backward = (halves(forward_table.T), halves(backward_table))
     y_rows, x_cols, low_ids = (plan.y_rows().reshape(-1), plan.x_columns(), np.arange(plan.ny // 2))
     cos_y, sin_y = wave(low_ids, y_rows, plan.ny)
     sin_y[0] = 1.0 - 2.0 * (y_rows % 2)
@@ -651,23 +656,32 @@
     rows_shape = (plan.ny, 2 * plan.x_chunk)
     freq_shape = (2 * plan.ny, plan.x_chunk)
     both_shape = (2 * plan.ny, plan.nx)
-    turned, own_row = edge_weights(plan, spectrum)
+    picked = pick_planes(plan, spectrum)
+    start, *picked = lax.optimization_barrier((charges, *picked))
+    plain = [outer_shift(plan, picked[2 * j], j) for j in range(plan.outer)]
+    mirror = [outer_shift(plan, picked[2 * j + 1], j) for j in range(plan.outer)]
     slot = lax.broadcasted_iota(jnp.int32, charges.shape, 0)
     masked = jnp.where(slot < counts[None], charges, 0.0)
     left, right = extend_rows(plan, masked)
-    pieces = [project(plan, i, charges, counts, split_projection, *depth_forward) for i in range(CHUNKS)]
-    pieces[0], left, right, turned = lax.optimization_barrier((pieces[0], left, right, turned))
+    turned, own_row = edge_weights(plan, spectrum)
+    pieces = [
+        project(plan, i, part, counts, split_projection, *depth_forward)
+        for i, part in enumerate((start, charges))
+    ]
+    pieces[0], *plain = lax.optimization_barrier((pieces[0], *plain))
     even_pieces = exchange(pieces[0])
-    blocks = first_weights(plan, spectrum, turned)
-    edge = jnp.concatenate([turned[plan.half :], own_row], axis=0)
+    pieces[1], left, right, turned, *mirror = lax.optimization_barrier(
+        (pieces[1], left, right, turned, *mirror)
+    )
+    odd_pieces = exchange(pieces[1])
+    strips = second_weights(plan, list(zip(plain, mirror)), turned)
+    edge = jnp.concatenate([turned[plan.inner :], own_row], axis=0)
     extended = extend_planes(plan, masked, left, right)
-    pieces[1], extended, *blocks = lax.optimization_barrier((pieces[1], extended, *blocks))
-    odd_pieces = exchange(pieces[1])
-    strips = second_weights(plan, blocks)
     (even,) = plane_call(
         plan, first_plane_kernel, "even_planes", me, [even_pieces], [(y_forward, None), (x_forward, 0)], [],
         [both_shape], values(rows_shape, freq_shape), 2,
     )
+    even, extended = lax.optimization_barrier((even, extended))
     late = [odd_pieces, even, x_backward[0][:1], x_backward[1][:1], *y_backward]
     copies = [pltpu.VMEM(array.shape, array.dtype) for array in late]
     copies.append(pltpu.SemaphoreType.DMA((len(late) + plan.half + 1,)))

time: 163 us -> 194 us (1.19)
  Pallas kernels: 69.6 us -> 101 us
  starting transfers between devices: 29.7 us -> 36.2 us
  waiting for transfers between devices: 52.8 us -> 46.8 us
    pallas_call x1, Pallas kernels: 3.14 us -> 33.8 us  [pick_planes(): pl.pallas_call(functools.partial(pick_kernel, plan), in_specs=[pl.BlockSp...]
    ppermute x3, waiting for transfers between devices: 10.4 us -> 0.01 us  [second_weights(): strip = lax.ppermute(strip, 'slab', pairs)]
    ppermute x1, waiting for transfers between devices: 4.66 us -> 14.4 us  [extend_planes(): before = lax.ppermute(wide[:, -1:], 'slab', up)]
    ppermute x2 -> x4, starting transfers between devices: 5.95 us -> 11.2 us  [the longest x2 8.02 us: edge_weights(): total = total + lax.ppermute(sent, 'slab', pairs)]
    all_to_all x4, waiting for transfers between devices: 30.7 us -> 25.8 us  [exchange(): return lax.all_to_all(pieces, axes, split_axis=0, concat_axis=0, tiled=True)]
    all_to_all x4, starting transfers between devices: 13.9 us -> 18 us  [exchange(): return lax.all_to_all(pieces, axes, split_axis=0, concat_axis=0, tiled=True)]
    ppermute x3, starting transfers between devices: 3.33 us -> 0.51 us  [second_weights(): strip = lax.ppermute(strip, 'slab', pairs)]
    squeeze x1 -> x0, local copies, waits for them, and re-layouts: 2.1 us -> none  [first_weights(): blocks.append(lax.ppermute(picked[j], 'slab', pairs))]
  transfers between devices with their start and end apart: 13 -> 15, of which waited for: 8 -> 4; matrix products, arithmetic and copies ran while one was open for 5% -> 4% of each run, Pallas kernels for 32% -> 26%
where the time goes in v7:
time: 194 us; the launch traced here: 193 us
  Pallas kernels  101 us (52%)
  waiting for transfers between devices  46.8 us (24%)
  starting transfers between devices  36.2 us (19%)
  other arithmetic  4.7 us (2%)
  local copies, waits for them, and re-layouts  3.7 us (2%)
    pallas_call x1, Pallas kernels, pick_planes(): pl.pallas_call(functools.partial(pick_kernel, plan), in_specs=[pl.BlockSp...  33.8 us
    pallas_call x4, Pallas kernels, projection_call(): pl.pallas_call(kernel, grid=(1,), in_specs=[whole_spec(array.shape) for a...  28 us
    all_to_all x4, waiting for transfers between devices, exchange(): return lax.all_to_all(pieces, axes, split_axis=0, concat_axis=0, tiled=True)  25.8 us
    pallas_call x3, Pallas kernels, plane_call(): pl.pallas_call(functools.partial(kernel, plan), grid=(1,), in_specs=[pl.B...  23.5 us
    all_to_all x4, starting transfers between devices, exchange(): return lax.all_to_all(pieces, axes, split_axis=0, concat_axis=0, tiled=True)  18 us
    pallas_call x1, Pallas kernels, near_field(): pl.pallas_call(functools.partial(near_kernel, plan), grid=(plan.cell_cols...  15.5 us
    ppermute x1, waiting for transfers between devices, extend_planes(): before = lax.ppermute(wide[:, -1:], 'slab', up)  14.4 us
    ppermute x2, starting transfers between devices, edge_weights(): total = total + lax.ppermute(sent, 'slab', pairs)  8.02 us
  transfers between devices with their start and end apart: 15, of which 4 were waited for; matrix products, arithmetic and copies ran while one was open for 4% of the time, Pallas kernels for 26%

profile of v7, /device:TPU:0, one launch (start us, length us, event | category | flops | bytes accessed | tf_op | source)
XLA Modules:
  0.0 192.8 jit_solution(9771078923682665691)
XLA Ops:
  0.0 0.6 pad_add_fusion.ids_ref
  0.6 33.8 %pick_planes.1 = (f32[4,32,512]{2,1,0:T(8,128)}, f32[4,32,512]{2,1,0:T(8,128)}, f32[4,32,512]{2,1,0:T(8,128)}, f32[4,32,512]{2,1,0:T(8,128)}) custom-call(s32[2]{0:T(128)} %pad_add_fusion.ids_ref, f32[64,32,512]{2,1,0:T(8,128)} %bitcast.63), custom_call_target="tpu_custom_call" | custom-call | bytes 2097152 | tf_op jit(solution)/shard_map/pick_planes/pallas_call | solution.py:568
  34.4 3.1 %collective-permute-start.5 = (f32[4,32,512]{2,1,0:T(8,128)}, f32[4,32,512]{2,1,0:T(8,128)S(1)}, u32[]{:S(2)}, u32[]{:S(2)}) collective-permute-start(f32[4,32,512]{2,1,0:T(8,128)} %get-tuple-element.39), channel_id=1, source_target_pairs={{0,8},{2,10},{4,12},{6,14},{8,0},{10,2},{12,4},{14,6},{16,24},{18,... | collective-permute-start | bytes 786440 | tf_op jit(solution)/shard_map/ppermute | solution.py:588
  37.5 7.6 %project_depth.3 = f32[32,2,4,8,128]{4,3,2,1,0:T(8,128)} custom-call(f32[8,8,1024]{2,1,0:T(8,128)} %charges.2, s32[8,1024]{1,0:T(8,128)} %counts.7, bf16[512,512]{1,0:T(8,128)(2,1)} %constant.104.clone.high, bf16[512,512]{1,0:T(8,128)(2,1)} %constant.105.clone.low, f32[8,2,2,16,8,1024]{5,4,3,2,1,0:T(8,128)} %bitcast.59), custom_call_target="tpu_custom_call" | custom-call | flops 4194304 | bytes 8388608 | tf_op jit(solution)/shard_map/project_depth/pallas_call | solution.py:184
  45.1 0.0 collective-permute-done.5
  45.1 0.0 copy-start.5
  45.1 4.9 %all-to-all-start.1 = ((f32[32,2,4,8,128]{4,3,2,1,0:T(8,128)}), f32[32,2,4,8,128]{4,3,2,1,0:T(8,128)S(1)}, u32[]{:S(2)}, u32[]{:S(2)}) async-start(f32[32,2,4,8,128]{4,3,2,1,0:T(8,128)} %project_depth.3), calls=%async_computation.1 | async-start | bytes 2097152 | tf_op jit(solution)/shard_map/all_to_all | solution.py:651
  50.0 0.0 copy-start.4
  50.1 1.3 slice.36
  51.4 0.1 rev.4
  51.6 0.6 pad_maximum_fusion.7
  52.2 6.1 %collective-permute-start.3 = (f32[5,512]{1,0:T(8,128)}, f32[5,512]{1,0:T(8,128)}, u32[]{:S(2)}, u32[]{:S(2)}) collective-permute-start(f32[5,512]{1,0:T(8,128)} %get-tuple-element.84), channel_id=1, source_target_pairs={{16,8},{0,24},{17,9},{1,25}} | collective-permute-start | bytes 30728 | tf_op jit(solution)/shard_map/ppermute | solution.py:602
  58.3 1.9 collective-permute-start.2
  60.3 0.0 copy-done.5
  60.3 0.1 collective-permute-start.4
  60.3 0.0 copy-done.1
  60.4 0.0 copy-done.3
  60.4 0.0 copy-start.6
  60.4 0.1 fusion.6
  60.5 1.5 collective-permute-start.1
  62.0 0.5 collective-permute-start
  62.6 7.6 %project_depth.2 = f32[32,2,4,8,128]{4,3,2,1,0:T(8,128)} custom-call(f32[8,8,1024]{2,1,0:T(8,128)} %charges.2, s32[8,1024]{1,0:T(8,128)} %counts.7, bf16[512,512]{1,0:T(8,128)(2,1)} %constant.104.clone.high, bf16[512,512]{1,0:T(8,128)(2,1)} %constant.105.clone.low, f32[8,2,2,16,8,1024]{5,4,3,2,1,0:T(8,128)} %bitcast.60), custom_call_target="tpu_custom_call" | custom-call | flops 4194304 | bytes 8388608 | tf_op jit(solution)/shard_map/project_depth/pallas_call | solution.py:184
  70.2 0.0 collective-permute-done.3
  70.2 6.6 %collective-permute-done.2 = f32[5,512]{1,0:T(8,128)} collective-permute-done((f32[5,512]{1,0:T(8,128)S(1)}, f32[5,512]{1,0:T(8,128)}, u32[]{:S(2)}, u32[]{:S(2)}) %collective-permute-start.2) | collective-permute-done | bytes 10272 | tf_op jit(solution)/shard_map/ppermute | solution.py:602
  76.8 0.7 add.77
  77.5 0.0 collective-permute-done.1
  77.5 0.0 collective-permute-done
  77.5 0.0 collective-permute-done.4
  77.5 0.1 concatenate.26
  77.6 0.0 all-to-all-done.1.pieces
  77.6 0.0 copy-start.2
  77.7 3.4 %all-to-all-start = ((f32[32,2,4,8,128]{4,3,2,1,0:T(8,128)}), f32[32,2,4,8,128]{4,3,2,1,0:T(8,128)}, u32[]{:S(2)}, u32[]{:S(2)}) async-start(f32[32,2,4,8,128]{4,3,2,1,0:T(8,128)} %project_depth.2), calls=%async_computation | async-start | bytes 2097152 | tf_op jit(solution)/shard_map/all_to_all | solution.py:651
  81.1 0.1 fusion.5
  81.1 0.1 collective-permute-start.6
  81.2 4.4 %collective-permute-start.7 = (f32[8,1,1280]{2,1,0:T(1,128)S(1)}, f32[8,1,1280]{2,1,0:T(1,128)S(1)}, u32[]{:S(2)}, u32[]{:S(2)}) collective-permute-start(f32[8,1,1280]{2,1,0:T(1,128)S(1)} %get-tuple-element.56), channel_id=1, source_target_pairs={{2,0},{4,2},{6,4},{8,6},{10,8},{12,10},{14,12},{16,14},{18,16},{20... | collective-permute-start | bytes 122888 | tf_op jit(solution)/shard_map/ppermute | solution.py:536
  85.6 0.0 copy-done.6
  85.6 1.0 dynamic-slice_bitcast_fusion.1
  86.6 0.0 copy-done.4
  86.6 1.0 dynamic-slice_bitcast_fusion
  87.8 0.9 broadcast_select_fusion
  88.6 0.6 pad_maximum_fusion.9.edge
  89.2 0.0 collective-permute-start.10
  89.2 0.5 collective-permute-start.8
  89.7 0.0 collective-permute-start.9
  89.7 14.4 %collective-permute-done.6 = f32[8,1,1280]{2,1,0:T(1,128)S(1)} collective-permute-done((f32[8,1,1280]{2,1,0:T(1,128)S(1)}, f32[8,1,1280]{2,1,0:T(1,128)S(1)}, u32[]{:S(2)}, u32[]{:S(2)}) %collective-permute-start.6) | collective-permute-done | bytes 40992 | tf_op jit(solution)/shard_map/ppermute | solution.py:535
  104.2 0.0 collective-permute-done.7
  104.2 0.1 fusion.1
  104.3 1.1 pad_maximum_fusion.extended
  105.3 0.0 copy-done.2
  105.3 5.8 %even_planes.1.refs_1_ = f32[1024,512]{1,0:T(8,128)} custom-call(s32[1]{0:T(128)} %bitcast.me_ref, f32[32,2,4,8,128]{4,3,2,1,0:T(8,128)} %copy-done.2, bf16[512,512]{1,0:T(8,128)(2,1)} %constant.106.clone.y_high.yf_high, bf16[512,512]{1,0:T(8,128)(2,1)} %constant.107.clone.y_low.yf_low, bf16[2,256,512]{2,1,0:T(8,128)(2,1)} %constant.108.clone.x_high.xf_high, ...), custom_call_target="tpu_custom_call" | custom-call | flops 1610612736 | bytes 3145728 | tf_op jit(solution)/shard_map/even_planes/pallas_call | solution.py:395
  111.1 0.0 collective-permute-done.10.refs_9_
  111.1 0.0 collective-permute-done.8.refs_7_
  111.1 0.0 collective-permute-done.9.refs_8_
  111.1 0.0 all-to-all-done.refs_0_
  111.1 11.1 %middle_planes.1 = (f32[32,2,4,8,128]{4,3,2,1,0:T(8,128)}, f32[1024,256]{1,0:T(8,128)}) custom-call(s32[1]{0:T(128)} %bitcast.me_ref, f32[2,512]{1,0:T(2,128)} %pad_maximum_fusion.9.edge, bf16[512,512]{1,0:T(8,128)(2,1)} %constant.106.clone.y_high.yf_high, bf16[512,512]{1,0:T(8,128)(2,1)} %constant.107.clone.y_low.yf_low, ...), custom_call_target="tpu_custom_call" | custom-call | flops 3221225472 | bytes 9441280 | tf_op jit(solution)/shard_map/middle_planes/pallas_call | solution.py:395
  122.2 6.3 %all-to-all-start.2 = ((f32[32,2,4,8,128]{4,3,2,1,0:T(8,128)}), f32[32,2,4,8,128]{4,3,2,1,0:T(8,128)S(1)}, u32[]{:S(2)}, u32[]{:S(2)}) async-start(f32[32,2,4,8,128]{4,3,2,1,0:T(8,128)} %get-tuple-element.51), calls=%async_computation.2 | async-start | bytes 2097152 | tf_op jit(solution)/shard_map/all_to_all | solution.py:651
  128.5 15.5 %near_blocks.1.before = f32[8,8,1024]{2,1,0:T(8,128)} custom-call(f32[8,3,8,1280]{3,2,1,0:T(8,128)} %pad_maximum_fusion.extended, s32[6,8,1024]{2,1,0:T(8,128)} %codes.1, f32[6,8,8,8,1024]{4,3,2,1,0:T(8,128)} %blocks_ref.1), custom_call_target="tpu_custom_call" | custom-call | flops 6291456 | bytes 12582912 | tf_op jit(solution)/shard_map/near_blocks/pallas_call | solution.py:498
  144.0 6.6 %odd_planes.1 = f32[32,2,4,8,128]{4,3,2,1,0:T(8,128)} custom-call(s32[1]{0:T(128)} %bitcast.me_ref, f32[1024,256]{1,0:T(8,128)} %get-tuple-element.48.freqs, bf16[2,256,512]{2,1,0:T(8,128)(2,1)} %constant.114.clone.x_high, bf16[2,256,512]{2,1,0:T(8,128)(2,1)} %constant.115.clone.x_low, bf16[512,512]{1,0:T(8,128)(2,1)} %constant.112.clone.refs_4_.y_high, ...), custom_call_target="tpu_custom_call" | custom-call | flops 1610612736 | bytes 3145728 | tf_op jit(solution)/shard_map/odd_planes/pallas_call | solution.py:395
  150.6 5.0 %all-to-all-done.2.sent = f32[32,2,4,8,128]{4,3,2,1,0:T(8,128)S(1)} async-done(((f32[32,2,4,8,128]{4,3,2,1,0:T(8,128)}), f32[32,2,4,8,128]{4,3,2,1,0:T(8,128)S(1)}, u32[]{:S(2)}, u32[]{:S(2)}) %all-to-all-start.2) | async-done | bytes 1048608 | tf_op jit(solution)/shard_map/all_to_all | solution.py:651
  155.7 3.4 %all-to-all-start.3 = ((f32[32,2,4,8,128]{4,3,2,1,0:T(8,128)}), f32[32,2,4,8,128]{4,3,2,1,0:T(8,128)}, u32[]{:S(2)}, u32[]{:S(2)}) async-start(f32[32,2,4,8,128]{4,3,2,1,0:T(8,128)} %odd_planes.1), calls=%async_computation.3 | async-start | bytes 2097152 | tf_op jit(solution)/shard_map/all_to_all | solution.py:651
  159.0 0.0 copy-done
  159.1 6.4 %depth_gather.2.before = f32[8,8,1024]{2,1,0:T(8,128)} custom-call(s32[8,1024]{1,0:T(8,128)} %counts.7, f32[8,8,1024]{2,1,0:T(8,128)} %near_blocks.1.before, bf16[512,512]{1,0:T(8,128)(2,1)} %constant.116.clone.high, bf16[512,512]{1,0:T(8,128)(2,1)} %constant.117.clone.low, f32[8,2,2,16,8,1024]{5,4,3,2,1,0:T(8,128)} %bitcast.61, f32[32,2,4,8,128]{4,3,2,1,0:T(8,128)} %copy-done), custom_call_target="tpu_custom_call" | custom-call | flops 4194304 | bytes 8388608 | tf_op jit(solution)/shard_map/depth_gather/pallas_call | solution.py:184
  165.5 20.7 %all-to-all-done.3.sent = f32[32,2,4,8,128]{4,3,2,1,0:T(8,128)} async-done(((f32[32,2,4,8,128]{4,3,2,1,0:T(8,128)}), f32[32,2,4,8,128]{4,3,2,1,0:T(8,128)}, u32[]{:S(2)}, u32[]{:S(2)}) %all-to-all-start.3) | async-done | bytes 1048608 | tf_op jit(solution)/shard_map/all_to_all | solution.py:651
  186.2 6.4 %depth_gather.3 = f32[8,8,1024]{2,1,0:T(8,128)} custom-call(s32[8,1024]{1,0:T(8,128)} %counts.7, f32[8,8,1024]{2,1,0:T(8,128)} %depth_gather.2.before, bf16[512,512]{1,0:T(8,128)(2,1)} %constant.116.clone.high, bf16[512,512]{1,0:T(8,128)(2,1)} %constant.117.clone.low, f32[8,2,2,16,8,1024]{5,4,3,2,1,0:T(8,128)} %bitcast.62, ...), custom_call_target="tpu_custom_call" | custom-call | flops 4194304 | bytes 8388608 | tf_op jit(solution)/shard_map/depth_gather/pallas_call | solution.py:184
  (15 shorter events, 0.2 us)
Async XLA Ops:
  0.6 59.8 %copy-start.1 = (f32[8,8,1024]{2,1,0:T(8,128)S(1)}, f32[8,8,1024]{2,1,0:T(8,128)}, u32[]{:S(2)}) copy-start(f32[8,8,1024]{2,1,0:T(8,128)} %charges.2) | copy-start | bytes 786436
  0.6 59.8 %copy-start.3 = (s32[8,1024]{1,0:T(8,128)S(1)}, s32[8,1024]{1,0:T(8,128)}, u32[]{:S(2)}) copy-start(s32[8,1024]{1,0:T(8,128)} %counts.7) | copy-start | bytes 98308
  34.4 10.7 %collective-permute-start.5 = (f32[4,32,512]{2,1,0:T(8,128)}, f32[4,32,512]{2,1,0:T(8,128)S(1)}, u32[]{:S(2)}, u32[]{:S(2)}) collective-permute-start(f32[4,32,512]{2,1,0:T(8,128)} %get-tuple-element.39), channel_id=1, source_target_pairs={{0,8},{2,10},{4,12},{6,14},{8,0},{10,2},{12,4},{14,6},{16,24},{18,... | collective-permute-start | bytes 786440 | tf_op jit(solution)/shard_map/ppermute | solution.py:588
  45.1 15.2 %copy-start.5 = (f32[4,32,512]{2,1,0:T(8,128)}, f32[4,32,512]{2,1,0:T(8,128)S(1)}, u32[]{:S(2)}) copy-start(f32[4,32,512]{2,1,0:T(8,128)S(1)} %collective-permute-done.5) | copy-start | bytes 786436
  45.1 32.5 %all-to-all-start.1 = ((f32[32,2,4,8,128]{4,3,2,1,0:T(8,128)}), f32[32,2,4,8,128]{4,3,2,1,0:T(8,128)S(1)}, u32[]{:S(2)}, u32[]{:S(2)}) async-start(f32[32,2,4,8,128]{4,3,2,1,0:T(8,128)} %project_depth.3), calls=%async_computation.1 | async-start | bytes 2097152 | tf_op jit(solution)/shard_map/all_to_all | solution.py:651
  50.0 36.6 %copy-start.4 = (f32[4,32,512]{2,1,0:T(8,128)S(1)}, f32[4,32,512]{2,1,0:T(8,128)}, u32[]{:S(2)}) copy-start(f32[4,32,512]{2,1,0:T(8,128)} %get-tuple-element.45) | copy-start | bytes 786436
  52.2 18.0 %collective-permute-start.3 = (f32[5,512]{1,0:T(8,128)}, f32[5,512]{1,0:T(8,128)}, u32[]{:S(2)}, u32[]{:S(2)}) collective-permute-start(f32[5,512]{1,0:T(8,128)} %get-tuple-element.84), channel_id=1, source_target_pairs={{16,8},{0,24},{17,9},{1,25}} | collective-permute-start | bytes 30728 | tf_op jit(solution)/shard_map/ppermute | solution.py:602
  58.3 18.4 %collective-permute-start.2 = (f32[5,512]{1,0:T(8,128)S(1)}, f32[5,512]{1,0:T(8,128)}, u32[]{:S(2)}, u32[]{:S(2)}) collective-permute-start(f32[5,512]{1,0:T(8,128)S(1)} %get-tuple-element.85), channel_id=1, source_target_pairs={{16,0},{0,16},{17,1},{1,17}} | collective-permute-start | bytes 30728 | tf_op jit(solution)/shard_map/ppermute | solution.py:602
  60.3 17.3 %collective-permute-start.4 = (f32[4,32,512]{2,1,0:T(8,128)}, f32[4,32,512]{2,1,0:T(8,128)}, u32[]{:S(2)}, u32[]{:S(2)}) collective-permute-start(f32[4,32,512]{2,1,0:T(8,128)} %get-tuple-element.34), channel_id=1, source_target_pairs={{0,8},{2,10},{4,12},{6,14},{8,0},{10,2},{12,4},{14,6},{16,24},{18,... | collective-permute-start | bytes 786440 | tf_op jit(solution)/shard_map/ppermute | solution.py:588
  60.4 25.2 %copy-start.6 = (f32[4,32,512]{2,1,0:T(8,128)S(1)}, f32[4,32,512]{2,1,0:T(8,128)}, u32[]{:S(2)}) copy-start(f32[4,32,512]{2,1,0:T(8,128)} %copy-done.5) | copy-start | bytes 786436
  60.5 17.0 %collective-permute-start.1 = (f32[8,8,16]{2,1,0:T(8,128)S(1)}, f32[8,8,16]{2,1,0:T(8,128)S(1)}, u32[]{:S(2)}, u32[]{:S(2)}) collective-permute-start(f32[8,8,16]{2,1,0:T(8,128)S(1)} %get-tuple-element.73), channel_id=1, source_target_pairs={{1,0},{0,1},{3,2},{2,3},{5,4},{4,5},{7,6},{6,7},{9,8},{8,9},{11,10... | collective-permute-start | bytes 12296 | tf_op jit(solution)/shard_map/ppermute | solution.py:527
  62.0 15.5 %collective-permute-start = (f32[8,8,16]{2,1,0:T(8,128)S(1)}, f32[8,8,16]{2,1,0:T(8,128)S(1)}, u32[]{:S(2)}, u32[]{:S(2)}) collective-permute-start(f32[8,8,16]{2,1,0:T(8,128)S(1)} %get-tuple-element.74), channel_id=1, source_target_pairs={{0,1},{1,0},{2,3},{3,2},{4,5},{5,4},{6,7},{7,6},{8,9},{9,8},{10,11... | collective-permute-start | bytes 12296 | tf_op jit(solution)/shard_map/ppermute | solution.py:526
  77.6 27.7 %copy-start.2 = (f32[32,2,4,8,128]{4,3,2,1,0:T(8,128)}, f32[32,2,4,8,128]{4,3,2,1,0:T(8,128)S(1)}, u32[]{:S(2)}) copy-start(f32[32,2,4,8,128]{4,3,2,1,0:T(8,128)S(1)} %all-to-all-done.1.pieces) | copy-start | bytes 3145732
  77.7 33.5 %all-to-all-start = ((f32[32,2,4,8,128]{4,3,2,1,0:T(8,128)}), f32[32,2,4,8,128]{4,3,2,1,0:T(8,128)}, u32[]{:S(2)}, u32[]{:S(2)}) async-start(f32[32,2,4,8,128]{4,3,2,1,0:T(8,128)} %project_depth.2), calls=%async_computation | async-start | bytes 2097152 | tf_op jit(solution)/shard_map/all_to_all | solution.py:651
  81.1 23.0 %collective-permute-start.6 = (f32[8,1,1280]{2,1,0:T(1,128)S(1)}, f32[8,1,1280]{2,1,0:T(1,128)S(1)}, u32[]{:S(2)}, u32[]{:S(2)}) collective-permute-start(f32[8,1,1280]{2,1,0:T(1,128)S(1)} %get-tuple-element.55), channel_id=1, source_target_pairs={{0,2},{2,4},{4,6},{6,8},{8,10},{10,12},{12,14},{14,16},{16,18},{18... | collective-permute-start | bytes 122888 | tf_op jit(solution)/shard_map/ppermute | solution.py:535
  81.2 22.9 %collective-permute-start.7 = (f32[8,1,1280]{2,1,0:T(1,128)S(1)}, f32[8,1,1280]{2,1,0:T(1,128)S(1)}, u32[]{:S(2)}, u32[]{:S(2)}) collective-permute-start(f32[8,1,1280]{2,1,0:T(1,128)S(1)} %get-tuple-element.56), channel_id=1, source_target_pairs={{2,0},{4,2},{6,4},{8,6},{10,8},{12,10},{14,12},{16,14},{18,16},{20... | collective-permute-start | bytes 122888 | tf_op jit(solution)/shard_map/ppermute | solution.py:536
  89.2 21.9 %collective-permute-start.10 = (f32[2,2,32,512]{3,2,1,0:T(8,128)S(1)}, f32[2,2,32,512]{3,2,1,0:T(8,128)}, u32[]{:S(2)}, u32[]{:S(2)}) collective-permute-start(f32[2,2,32,512]{3,2,1,0:T(8,128)S(1)} %get-tuple-element.86), channel_id=1, source_target_pairs={{0,6},{2,0},{4,2},{6,4},{8,14},{10,8},{12,10},{14,12},{16,22},{18,... | collective-permute-start | bytes 786440 | tf_op jit(solution)/shard_map/ppermute | solution.py:622
  89.2 21.9 %collective-permute-start.8 = (f32[2,2,32,512]{3,2,1,0:T(8,128)S(1)}, f32[2,2,32,512]{3,2,1,0:T(8,128)}, u32[]{:S(2)}, u32[]{:S(2)}) collective-permute-start(f32[2,2,32,512]{3,2,1,0:T(8,128)S(1)} %get-tuple-element.87), channel_id=1, source_target_pairs={{0,2},{2,4},{4,6},{6,0},{8,10},{10,12},{12,14},{14,8},{16,18},{18,... | collective-permute-start | bytes 786440 | tf_op jit(solution)/shard_map/ppermute | solution.py:622
  89.7 21.4 %collective-permute-start.9 = (f32[2,2,32,512]{3,2,1,0:T(8,128)S(1)}, f32[2,2,32,512]{3,2,1,0:T(8,128)}, u32[]{:S(2)}, u32[]{:S(2)}) collective-permute-start(f32[2,2,32,512]{3,2,1,0:T(8,128)S(1)} %get-tuple-element.88), channel_id=1, source_target_pairs={{0,4},{2,6},{4,0},{6,2},{8,12},{10,14},{12,8},{14,10},{16,20},{18,... | collective-permute-start | bytes 786440 | tf_op jit(solution)/shard_map/ppermute | solution.py:622
  122.2 33.5 %all-to-all-start.2 = ((f32[32,2,4,8,128]{4,3,2,1,0:T(8,128)}), f32[32,2,4,8,128]{4,3,2,1,0:T(8,128)S(1)}, u32[]{:S(2)}, u32[]{:S(2)}) async-start(f32[32,2,4,8,128]{4,3,2,1,0:T(8,128)} %get-tuple-element.51), calls=%async_computation.2 | async-start | bytes 2097152 | tf_op jit(solution)/shard_map/all_to_all | solution.py:651
  155.6 3.4 %copy-start = (f32[32,2,4,8,128]{4,3,2,1,0:T(8,128)}, f32[32,2,4,8,128]{4,3,2,1,0:T(8,128)S(1)}, u32[]{:S(2)}) copy-start(f32[32,2,4,8,128]{4,3,2,1,0:T(8,128)S(1)} %all-to-all-done.2.sent) | copy-start | bytes 3145732
  155.7 30.6 %all-to-all-start.3 = ((f32[32,2,4,8,128]{4,3,2,1,0:T(8,128)}), f32[32,2,4,8,128]{4,3,2,1,0:T(8,128)}, u32[]{:S(2)}, u32[]{:S(2)}) async-start(f32[32,2,4,8,128]{4,3,2,1,0:T(8,128)} %odd_planes.1), calls=%async_computation.3 | async-start | bytes 2097152 | tf_op jit(solution)/shard_map/all_to_all | solution.py:651

commit v8 on v7

--- a/solution.py
+++ b/solution.py
@@ -137,11 +137,17 @@
     ]
 
 
-def project_kernel(plan, chunk, charges, counts, high, low, projection, out, scratch, held, sems):
+def project_kernel(plan, chunk, charges_in, counts_in, high_in, low_in, projection, out, scratch, held, sems,
+                   charges, counts, high, low):
     planes = plan.cell_planes
+    first = plan.tx_chunk
+    pairs = ((charges_in, charges), (counts_in, counts), (high_in, high), (low_in, low))
+    loads = [pltpu.make_async_copy(*pair, sems.at[first + n]) for n, pair in enumerate(pairs)]
     copies = tile_copies(plan, chunk, projection, held, sems)
-    for copy in copies:
+    for copy in loads[:2] + copies + loads[2:]:
         copy.start()
+    for copy in loads[:2]:
+        copy.wait()
     for tx, copy in enumerate(copies):
         copy.wait()
 
@@ -161,6 +167,8 @@
             return carry
 
         lax.fori_loop(0, plan.steps * plan.step_blocks, body, 0)
+    for copy in loads[2:]:
+        copy.wait()
     spectra = product(split(scratch[...]), (high[...], low[...])).T
     shape = (plan.slots, 2, plan.row_block, LANES)
     for step in range(plan.steps):
@@ -180,34 +188,58 @@
     return pl.BlockSpec(shape, lambda i: (0,) * len(shape))
 
 
-def projection_call(plan, kernel, name, arrays, late, out_shape, scratch):
+def projection_call(plan, kernel, name, arrays, projection, out_shape, fits_held):
+    scratch = [pltpu.VMEM((plan.steps * LANES, TZ * LANES), jnp.float32)]
+    space = pltpu.VMEM
+    limit = VMEM_LIMIT - 20 * 1024 * 1024
+    if fits_held:
+        scratch.append(pltpu.VMEM(held_shape(plan), jnp.float32))
+        space = pl.ANY
+        limit = VMEM_LIMIT
+    scratch.append(pltpu.SemaphoreType.DMA((plan.tx_chunk + len(arrays),)))
+    scratch += [pltpu.VMEM(array.shape, array.dtype) for array in arrays]
     return pl.pallas_call(
         kernel,
-        grid=(1,),
-        in_specs=[whole_spec(array.shape) for array in arrays]
-        + [pl.BlockSpec(memory_space=pl.ANY)] * len(late),
-        out_specs=whole_spec(out_shape),
+        in_specs=[pl.BlockSpec(memory_space=pl.ANY)] * len(arrays) + [pl.BlockSpec(memory_space=space)],
+        out_specs=pl.BlockSpec(memory_space=pltpu.VMEM),
         out_shape=jax.ShapeDtypeStruct(out_shape, jnp.float32),
-        scratch_shapes=[
-            pltpu.VMEM((plan.steps * LANES, TZ * LANES), jnp.float32),
-            pltpu.VMEM(held_shape(plan), jnp.float32),
-            pltpu.SemaphoreType.DMA((plan.tx_chunk + 1,)),
-        ]
-        + scratch,
-        compiler_params=pltpu.CompilerParams(vmem_limit_bytes=VMEM_LIMIT),
+        scratch_shapes=scratch,
+        compiler_params=pltpu.CompilerParams(vmem_limit_bytes=limit),
         cost_estimate=pl.CostEstimate(
-            flops=2 * late[0].size // CHUNKS,
-            bytes_accessed=4 * late[0].size // CHUNKS,
+            flops=2 * math.prod(held_shape(plan)),
+            bytes_accessed=4 * math.prod(held_shape(plan)),
             transcendentals=0,
         ),
         name=name,
-    )(*arrays, *late)
+    )(*arrays, projection)
 
 
 def project(plan, chunk, charges, counts, projection, high, low):
     kernel = functools.partial(project_kernel, plan, chunk)
     arrays = [charges, counts, high, low]
-    return projection_call(plan, kernel, "project_depth", arrays, [projection], piece_shape(plan), [])
+    return projection_call(plan, kernel, "project_depth", arrays, projection, piece_shape(plan), True)
+
+
+def hold_kernel(plan, chunk, projection, after, out, sems):
+    copies = tile_copies(plan, chunk, projection, out, sems)
+    for copy in copies:
+        copy.start()
+    for copy in copies:
+        copy.wait()
+
+
+def hold_projection(plan, chunk, projection, after):
+    return pl.pallas_call(
+        functools.partial(hold_kernel, plan, chunk),
+        in_specs=[pl.BlockSpec(memory_space=pl.ANY)] * 2,
+        out_specs=pl.BlockSpec(memory_space=pltpu.VMEM),
+        out_shape=jax.ShapeDtypeStruct(held_shape(plan), jnp.float32),
+        scratch_shapes=[pltpu.SemaphoreType.DMA((plan.tx_chunk,))],
+        cost_estimate=pl.CostEstimate(
+            flops=0, bytes_accessed=8 * math.prod(held_shape(plan)), transcendentals=0
+        ),
+        name="hold_projection",
+    )(projection, after)
 
 
 def far_sign(plan, me_ref):
@@ -215,7 +247,7 @@
     return jnp.where(slab >= plan.half, -1.0, 1.0)
 
 
-def forward_plane(plan, me_ref, pieces, y_table, x_table, rows_ref, freq_ref):
+def forward_plane(plan, me_ref, pieces, y_table, x_table, rows_ref, freq_ref, waits=()):
     special = me_ref[0] == 0
     sign = far_sign(plan, me_ref)
     rows = 2 * plan.steps * plan.row_block
@@ -237,6 +269,8 @@
                         rows_ref[row : row + plan.row_block, col : col + LANES] = value[
                             source : source + plan.row_block
                         ]
+    for copy in waits:
+        copy.wait()
     sums = product((y_table[0][...], y_table[1][...]), split(rows_ref[...]))
     cos_re, cos_im = (sums[:middle, :width], sums[:middle, width:])
     sin_re, sin_im = (sums[middle:, :width], sums[middle:, width:])
@@ -311,16 +345,16 @@
     out[...] = forward_plane(plan, me_ref, pieces, (y_high, y_low), (x_high, x_low), rows_ref, freq_ref)
 
 
-def middle_plane_kernel(plan, me_ref, edge, yf_high, yf_low, xf_high, xf_low, *refs):
-    late, refs = (refs[:6], refs[6:])
+def middle_plane_kernel(plan, me_ref, edge, *refs):
+    late, refs = (refs[:10], refs[10:])
     strips, refs = (refs[: plan.inner], refs[plan.inner :])
     out, rest, rows_ref, freq_ref, sum_ref, rest_ref, weights = refs[:7]
-    pieces, even, xb_high, xb_low, yb_high, yb_low, sems = refs[7:]
+    pieces, yf_high, yf_low, xf_high, xf_low, even, xb_high, xb_low, yb_high, yb_low, sems = refs[7:]
     slab = lax.rem(me_ref[0], plan.slabs)
     place = lax.rem(slab, plan.half)
     outer_id, inner_id = (place // plan.inner, lax.rem(place, plan.inner))
-    held = (pieces, even, xb_high, xb_low, yb_high, yb_low)
-    copies = [pltpu.make_async_copy(late[n], held[n], sems.at[n]) for n in range(2)]
+    held = (pieces, yf_high, yf_low, xf_high, xf_low, even, xb_high, xb_low, yb_high, yb_low)
+    copies = [pltpu.make_async_copy(late[n], held[n], sems.at[n]) for n in range(6)]
     for i in range(plan.inner):
         for j in range(plan.outer):
             owner = lax.rem(outer_id - j + plan.outer, plan.outer) * plan.inner
@@ -332,7 +366,7 @@
                 )
             )
     early = len(copies)
-    for n in range(2, len(held)):
+    for n in range(6, len(held)):
         copies.append(pltpu.make_async_copy(late[n], held[n], sems.at[n]))
     for copy in copies:
         copy.start()
@@ -340,8 +374,11 @@
     special = me_ref[0] == 0
     width = plan.x_chunk
     middle = plan.ny // 2
-    odd = forward_plane(plan, me_ref, pieces, (yf_high, yf_low), (xf_high, xf_low), rows_ref, freq_ref)
-    for copy in copies[1:early]:
+    x_table = (xf_high.at[pl.ds(0, 1)], xf_low.at[pl.ds(0, 1)])
+    odd = forward_plane(
+        plan, me_ref, pieces, (yf_high, yf_low), x_table, rows_ref, freq_ref, copies[1:5]
+    )
+    for copy in copies[5:early]:
         copy.wait()
     row = lax.broadcasted_iota(jnp.int32, (middle, width), 0)
     at_first = row == 0
@@ -407,21 +444,27 @@
     )(me, *arrays, *flat, *late)
 
 
-def gather_kernel(
-    plan, chunk, counts, before, high, low, projection, sent, out, scratch, held, sems, pieces
-):
+def gather_kernel(plan, chunk, sent, high_in, low_in, before_in, counts_in, *refs):
     planes = plan.cell_planes
     rows = plan.slots * 2 * plan.row_block
-    fetch = pltpu.make_async_copy(sent, pieces, sems.at[plan.tx_chunk])
-    fetch.start()
-    copies = tile_copies(plan, chunk, projection, held, sems)
-    for copy in copies:
+    first = plan.tx_chunk
+    if chunk == CHUNKS - 1:
+        held, out, scratch, sems, pieces, high, low, before, counts = refs
+        copies = []
+    else:
+        projection, out, scratch, held, sems, pieces, high, low, before, counts = refs
+        copies = tile_copies(plan, chunk, projection, held, sems)
+    pairs = ((sent, pieces), (high_in, high), (low_in, low), (before_in, before), (counts_in, counts))
+    loads = [pltpu.make_async_copy(*pair, sems.at[first + n]) for n, pair in enumerate(pairs)]
+    for copy in loads + copies:
         copy.start()
-    fetch.wait()
+    for copy in loads:
+        copy.wait()
     columns = [pieces[:, :, step].reshape(rows, LANES) for step in range(plan.steps)]
     scratch[...] = product(split(jnp.concatenate(columns, axis=1).T), (high[...], low[...]))
-    for tx, copy in enumerate(copies):
-        copy.wait()
+    for tx in range(plan.tx_chunk):
+        if copies:
+            copies[tx].wait()
         last = chunk == CHUNKS - 1 and tx == plan.tx_chunk - 1
 
         def body(place, carry, tx=tx, last=last):
@@ -444,11 +487,9 @@
 
 def gather(plan, chunk, counts, before, projection, high, low, pieces):
     kernel = functools.partial(gather_kernel, plan, chunk)
-    arrays = [counts, before, high, low]
-    scratch = [pltpu.VMEM(pieces.shape, jnp.float32)]
-    return projection_call(
-        plan, kernel, "depth_gather", arrays, [projection, pieces], before.shape, scratch
-    )
+    arrays = [pieces, high, low, before, counts]
+    held_here = chunk < CHUNKS - 1
+    return projection_call(plan, kernel, "depth_gather", arrays, projection, before.shape, held_here)
 
 
 def near_kernel(plan, extended, codes, blocks_ref, out):
@@ -560,15 +601,14 @@
         copy.wait()
 
 
-def pick_planes(plan, spectrum):
+def pick_planes(plan, ids, spectrum):
     by_depth = jnp.transpose(spectrum, (1, 2, 0))
     shape = (plan.inner,) + by_depth.shape[1:]
     count = 2 * plan.outer
-    ids = jnp.stack([lax.axis_index("cell"), lax.axis_index("slab")]).astype(jnp.int32)
     return pl.pallas_call(
         functools.partial(pick_kernel, plan),
         in_specs=[pl.BlockSpec(memory_space=pltpu.SMEM), pl.BlockSpec(memory_space=pl.ANY)],
-        out_specs=[pl.BlockSpec(memory_space=pl.ANY)] * count,
+        out_specs=[pl.BlockSpec(memory_space=pltpu.VMEM)] * count,
         out_shape=[jax.ShapeDtypeStruct(shape, jnp.float32)] * count,
         scratch_shapes=[pltpu.SemaphoreType.DMA((2 * plan.half,))],
         cost_estimate=pl.CostEstimate(
@@ -588,9 +628,8 @@
     return lax.ppermute(value, "slab", pairs)
 
 
-def edge_weights(plan, spectrum):
+def edge_weights(plan, rows):
     slab, cell = (lax.axis_index("slab"), lax.axis_index("cell"))
-    rows = jnp.transpose(spectrum[:, :, 0], (1, 0))
     middle = plan.nz // 2
     turned = jnp.concatenate([rows[middle : middle + 1], jnp.flip(rows, 0)], axis=0)
     other = cell * plan.slabs + (1 - slab // plan.half) * plan.half
@@ -656,38 +695,37 @@
     rows_shape = (plan.ny, 2 * plan.x_chunk)
     freq_shape = (2 * plan.ny, plan.x_chunk)
     both_shape = (2 * plan.ny, plan.nx)
-    picked = pick_planes(plan, spectrum)
-    start, *picked = lax.optimization_barrier((charges, *picked))
+    ids = jnp.stack([lax.axis_index("cell"), lax.axis_index("slab")]).astype(jnp.int32)
+    slot = lax.broadcasted_iota(jnp.int32, charges.shape, 0)
+    masked = jnp.where(slot < counts[None], charges, 0.0)
+    rows = jnp.transpose(spectrum[:, :, 0], (1, 0))
+    pieces = [project(plan, i, charges, counts, split_projection, *depth_forward) for i in range(CHUNKS)]
+    pieces[0], ids = lax.optimization_barrier((pieces[0], ids))
+    even_pieces = exchange(pieces[0])
+    picked = pick_planes(plan, ids, spectrum)
+    masked, rows, *picked = lax.optimization_barrier((masked, rows, *picked))
     plain = [outer_shift(plan, picked[2 * j], j) for j in range(plan.outer)]
     mirror = [outer_shift(plan, picked[2 * j + 1], j) for j in range(plan.outer)]
-    slot = lax.broadcasted_iota(jnp.int32, charges.shape, 0)
-    masked = jnp.where(slot < counts[None], charges, 0.0)
+    turned, own_row = edge_weights(plan, rows)
     left, right = extend_rows(plan, masked)
-    turned, own_row = edge_weights(plan, spectrum)
-    pieces = [
-        project(plan, i, part, counts, split_projection, *depth_forward)
-        for i, part in enumerate((start, charges))
-    ]
-    pieces[0], *plain = lax.optimization_barrier((pieces[0], *plain))
-    even_pieces = exchange(pieces[0])
-    pieces[1], left, right, turned, *mirror = lax.optimization_barrier(
-        (pieces[1], left, right, turned, *mirror)
-    )
+    pieces[1], left, right, turned, *moved = lax.optimization_barrier(
+        (pieces[1], left, right, turned, *plain, *mirror)
+    )
+    plain, mirror = (moved[: plan.outer], moved[plan.outer :])
     odd_pieces = exchange(pieces[1])
     strips = second_weights(plan, list(zip(plain, mirror)), turned)
     edge = jnp.concatenate([turned[plan.inner :], own_row], axis=0)
-    extended = extend_planes(plan, masked, left, right)
     (even,) = plane_call(
         plan, first_plane_kernel, "even_planes", me, [even_pieces], [(y_forward, None), (x_forward, 0)], [],
         [both_shape], values(rows_shape, freq_shape), 2,
     )
-    even, extended = lax.optimization_barrier((even, extended))
-    late = [odd_pieces, even, x_backward[0][:1], x_backward[1][:1], *y_backward]
+    late = [odd_pieces, *y_forward, x_forward[0][1:], x_forward[1][1:], even]
+    late += [x_backward[0][:1], x_backward[1][:1], *y_backward]
     copies = [pltpu.VMEM(array.shape, array.dtype) for array in late]
     copies.append(pltpu.SemaphoreType.DMA((len(late) + plan.half + 1,)))
     back, rest = plane_call(
         plan, middle_plane_kernel, "middle_planes", me, [edge],
-        [(y_forward, None), (x_forward, 1)], late + strips, [piece_shape(plan), freq_shape],
+        [], late + strips, [piece_shape(plan), freq_shape],
         values(rows_shape, freq_shape, freq_shape, freq_shape, (2, plan.ny // 2, plan.nx)) + copies, 4,
     )
     even_back = exchange(back)
@@ -695,11 +733,13 @@
         plan, last_plane_kernel, "odd_planes", me, [rest], [(x_backward, 1), (y_backward, None)], [],
         [piece_shape(plan)], values(rows_shape), 2,
     )
+    extended = extend_planes(plan, masked, left, right)
+    back, extended = lax.optimization_barrier((back, extended))
+    odd_back = exchange(back)
     total = near_field(plan, extended, neighbours, near_blocks)
-    back, total = lax.optimization_barrier((back, total))
-    odd_back = exchange(back)
     total = gather(plan, 0, counts, total, split_projection, *depth_backward, even_back)
-    return gather(plan, 1, counts, total, split_projection, *depth_backward, odd_back)
+    held = hold_projection(plan, 1, split_projection, total)
+    return gather(plan, 1, counts, total, held, *depth_backward, odd_back)
 
 
 def padded(value, sides, width):

time: 194 us -> 173 us (0.89)
  Pallas kernels: 101 us -> 70.1 us
  local copies, waits for them, and re-layouts: 3.7 us -> 9.75 us
  starting transfers between devices: 36.2 us -> 40.8 us
    pallas_call x1, Pallas kernels: 33.8 us -> 3.02 us  [pick_planes(): pl.pallas_call(functools.partial(pick_kernel, plan), in_specs=[pl.BlockSp...]
    all_to_all x4, waiting for transfers between devices: 25.8 us -> 3.23 us  [exchange(): return lax.all_to_all(pieces, axes, split_axis=0, concat_axis=0, tiled=True)]
    ppermute x3, waiting for transfers between devices: 0.01 us -> 12.1 us  [second_weights(): strip = lax.ppermute(strip, 'slab', pairs)]
    ppermute x2, waiting for transfers between devices: 6.58 us -> 13.5 us  [edge_weights(): total = total + lax.ppermute(sent, 'slab', pairs)]
    unnamed x15 -> x23, local copies, waits for them, and re-layouts: 0.04 us -> 6.13 us
    ppermute x1, waiting for transfers between devices: 14.4 us -> 18.4 us  [extend_planes(): before = lax.ppermute(wide[:, -1:], 'slab', up)]
    all_to_all x4, starting transfers between devices: 18 us -> 21.3 us  [exchange(): return lax.all_to_all(pieces, axes, split_axis=0, concat_axis=0, tiled=True)]
    pallas_call x4 -> x5, Pallas kernels: 28 us -> 28.5 us  [the longest x4 21.7 us: projection_call(): pl.pallas_call(kernel, in_specs=[pl.BlockSpec(memory_space=pl.ANY)] * len...]
  transfers between devices with their start and end apart: 15 -> 15, of which waited for: 4 -> 6; matrix products, arithmetic and copies ran while one was open for 4% -> 4% of each run, Pallas kernels for 26% -> 29%
where the time goes in v8:
time: 173 us; the launch traced here: 172 us
  Pallas kernels  70.1 us (41%)
  waiting for transfers between devices  47.2 us (27%)
  starting transfers between devices  40.8 us (24%)
  local copies, waits for them, and re-layouts  9.75 us (6%)
  other arithmetic  3.52 us (2%)
    pallas_call x3, Pallas kernels, plane_call(): pl.pallas_call(functools.partial(kernel, plan), grid=(1,), in_specs=[pl.B...  23 us
    pallas_call x4, Pallas kernels, projection_call(): pl.pallas_call(kernel, in_specs=[pl.BlockSpec(memory_space=pl.ANY)] * len...  21.7 us
    all_to_all x4, starting transfers between devices, exchange(): return lax.all_to_all(pieces, axes, split_axis=0, concat_axis=0, tiled=True)  21.3 us
    ppermute x1, waiting for transfers between devices, extend_planes(): before = lax.ppermute(wide[:, -1:], 'slab', up)  18.4 us
    pallas_call x1, Pallas kernels, near_field(): pl.pallas_call(functools.partial(near_kernel, plan), grid=(plan.cell_cols...  15.5 us
    ppermute x2, waiting for transfers between devices, edge_weights(): total = total + lax.ppermute(sent, 'slab', pairs)  13.5 us
    ppermute x3, waiting for transfers between devices, second_weights(): strip = lax.ppermute(strip, 'slab', pairs)  12.1 us
    ppermute x2, starting transfers between devices, edge_weights(): total = total + lax.ppermute(sent, 'slab', pairs)  7.4 us
  transfers between devices with their start and end apart: 15, of which 6 were waited for; matrix products, arithmetic and copies ran while one was open for 4% of the time, Pallas kernels for 29%

profile of v8, /device:TPU:0, one launch (start us, length us, event | category | flops | bytes accessed | tf_op | source)
XLA Modules:
  0.0 171.9 jit_solution(8837193139675644143)
XLA Ops:
  0.0 0.6 pad_add_fusion.ids_ref
  0.6 6.4 %project_depth.3 = f32[32,2,4,8,128]{4,3,2,1,0:T(8,128)} custom-call(f32[8,8,1024]{2,1,0:T(8,128)} %charges_in.3, s32[8,1024]{1,0:T(8,128)} %counts_in.7, bf16[512,512]{1,0:T(8,128)(2,1)} %constant.108.clone.high_in, bf16[512,512]{1,0:T(8,128)(2,1)} %constant.109.clone.low_in, f32[8,2,2,16,8,1024]{5,4,3,2,1,0:T(8,128)} %bitcast.59), custom_call_target="tpu_custom_call" | custom-call | flops 4194304 | bytes 8388608 | tf_op jit(solution)/shard_map/project_depth/pallas_call | solution.py:201
  7.1 7.4 %all-to-all-start.1 = ((f32[32,2,4,8,128]{4,3,2,1,0:T(8,128)}), f32[32,2,4,8,128]{4,3,2,1,0:T(8,128)}, u32[]{:S(2)}, u32[]{:S(2)}) async-start(f32[32,2,4,8,128]{4,3,2,1,0:T(8,128)} %project_depth.3), calls=%async_computation.1 | async-start | bytes 2097152 | tf_op jit(solution)/shard_map/all_to_all | solution.py:690
  14.5 1.3 slice.34
  15.8 3.0 %pick_planes.1 = (f32[4,32,512]{2,1,0:T(8,128)}, f32[4,32,512]{2,1,0:T(8,128)}, f32[4,32,512]{2,1,0:T(8,128)}, f32[4,32,512]{2,1,0:T(8,128)}) custom-call(s32[2]{0:T(128)} %pad_add_fusion.ids_ref, f32[64,32,512]{2,1,0:T(8,128)} %bitcast.63), custom_call_target="tpu_custom_call" | custom-call | bytes 2097152 | tf_op jit(solution)/shard_map/pick_planes/pallas_call | solution.py:608
  18.9 0.0 copy-done.4
  18.9 0.0 copy-done.7
  18.9 1.8 %collective-permute-start.4 = (f32[4,32,512]{2,1,0:T(8,128)}, f32[4,32,512]{2,1,0:T(8,128)S(1)}, u32[]{:S(2)}, u32[]{:S(2)}) collective-permute-start(f32[4,32,512]{2,1,0:T(8,128)} %get-tuple-element.37), channel_id=1, source_target_pairs={{0,8},{2,10},{4,12},{6,14},{8,0},{10,2},{12,4},{14,6},{16,24},{18,... | collective-permute-start | bytes 786440 | tf_op jit(solution)/shard_map/ppermute | solution.py:628
  20.7 0.3 collective-permute-start.5
  21.0 0.1 rev.4
  21.2 5.5 %collective-permute-start.3 = (f32[5,512]{1,0:T(8,128)S(1)}, f32[5,512]{1,0:T(8,128)S(1)}, u32[]{:S(2)}, u32[]{:S(2)}) collective-permute-start(f32[5,512]{1,0:T(8,128)S(1)} %get-tuple-element.84), channel_id=1, source_target_pairs={{16,8},{0,24},{17,9},{1,25}} | collective-permute-start | bytes 30728 | tf_op jit(solution)/shard_map/ppermute | solution.py:641
  26.7 1.9 %collective-permute-start.2 = (f32[5,512]{1,0:T(8,128)S(1)}, f32[5,512]{1,0:T(8,128)S(1)}, u32[]{:S(2)}, u32[]{:S(2)}) collective-permute-start(f32[5,512]{1,0:T(8,128)S(1)} %get-tuple-element.85), channel_id=1, source_target_pairs={{16,0},{0,16},{17,1},{1,17}} | collective-permute-start | bytes 30728 | tf_op jit(solution)/shard_map/ppermute | solution.py:641
  28.6 0.1 fusion.6
  28.7 1.5 collective-permute-start.1
  30.2 13.5 %collective-permute-done.3 = f32[5,512]{1,0:T(8,128)S(1)} collective-permute-done((f32[5,512]{1,0:T(8,128)S(1)}, f32[5,512]{1,0:T(8,128)S(1)}, u32[]{:S(2)}, u32[]{:S(2)}) %collective-permute-start.3) | collective-permute-done | bytes 10272 | tf_op jit(solution)/shard_map/ppermute | solution.py:641
  43.6 1.7 collective-permute-start
  45.3 6.4 %project_depth.2 = f32[32,2,4,8,128]{4,3,2,1,0:T(8,128)} custom-call(f32[8,8,1024]{2,1,0:T(8,128)} %charges_in.3, s32[8,1024]{1,0:T(8,128)} %counts_in.7, bf16[512,512]{1,0:T(8,128)(2,1)} %constant.108.clone.high_in, bf16[512,512]{1,0:T(8,128)(2,1)} %constant.109.clone.low_in, f32[8,2,2,16,8,1024]{5,4,3,2,1,0:T(8,128)} %bitcast.60), custom_call_target="tpu_custom_call" | custom-call | flops 4194304 | bytes 8388608 | tf_op jit(solution)/shard_map/project_depth/pallas_call | solution.py:201
  51.7 0.0 collective-permute-done.2
  51.7 0.0 collective-permute-done.1
  51.8 0.0 collective-permute-done
  51.8 0.0 collective-permute-done.4
  51.8 0.0 collective-permute-done.5
  51.8 0.0 copy-start.10
  51.8 0.0 all-to-all-done.1.pieces
  51.8 0.7 copy-done.10
  52.5 4.6 %all-to-all-start = ((f32[32,2,4,8,128]{4,3,2,1,0:T(8,128)}), f32[32,2,4,8,128]{4,3,2,1,0:T(8,128)S(1)}, u32[]{:S(2)}, u32[]{:S(2)}) async-start(f32[32,2,4,8,128]{4,3,2,1,0:T(8,128)} %project_depth.2), calls=%async_computation | async-start | bytes 2097152 | tf_op jit(solution)/shard_map/all_to_all | solution.py:690
  57.3 0.0 copy-done.9
  57.3 1.0 dynamic-slice_bitcast_fusion.2
  58.3 1.0 dynamic-slice_bitcast_fusion
  59.4 1.0 broadcast_select_fusion
  60.4 1.5 collective-permute-start.8
  61.9 0.0 collective-permute-start.6
  61.9 0.8 collective-permute-start.7
  62.7 0.6 pad_maximum_fusion.9.edge
  63.3 5.8 %even_planes.1.refs_5_ = f32[1024,512]{1,0:T(8,128)} custom-call(s32[1]{0:T(128)} %bitcast.me_ref, f32[32,2,4,8,128]{4,3,2,1,0:T(8,128)} %all-to-all-done.1.pieces, bf16[512,512]{1,0:T(8,128)(2,1)} %constant.110.clone.y_high.refs_1_, bf16[512,512]{1,0:T(8,128)(2,1)} %constant.111.clone.y_low.refs_2_, bf16[2,256,512]{2,1,0:T(8,128)(2,1)} %constant.112.clone.x_high, ...), custom_call_target="tpu_custom_call" | custom-call | flops 1610612736 | bytes 3145728 | tf_op jit(solution)/shard_map/even_planes/pallas_call | solution.py:432
  69.0 3.1 %collective-permute-done.8.refs_13_ = f32[2,2,32,512]{3,2,1,0:T(8,128)} collective-permute-done((f32[2,2,32,512]{3,2,1,0:T(8,128)}, f32[2,2,32,512]{3,2,1,0:T(8,128)}, u32[]{:S(2)}, u32[]{:S(2)}) %collective-permute-start.8) | collective-permute-done | bytes 262176 | tf_op jit(solution)/shard_map/ppermute | solution.py:661
  72.1 2.8 %collective-permute-done.6.refs_11_ = f32[2,2,32,512]{3,2,1,0:T(8,128)} collective-permute-done((f32[2,2,32,512]{3,2,1,0:T(8,128)S(1)}, f32[2,2,32,512]{3,2,1,0:T(8,128)}, u32[]{:S(2)}, u32[]{:S(2)}) %collective-permute-start.6) | collective-permute-done | bytes 262176 | tf_op jit(solution)/shard_map/ppermute | solution.py:661
  74.9 6.2 %collective-permute-done.7.refs_12_ = f32[2,2,32,512]{3,2,1,0:T(8,128)} collective-permute-done((f32[2,2,32,512]{3,2,1,0:T(8,128)S(1)}, f32[2,2,32,512]{3,2,1,0:T(8,128)}, u32[]{:S(2)}, u32[]{:S(2)}) %collective-permute-start.7) | collective-permute-done | bytes 262176 | tf_op jit(solution)/shard_map/ppermute | solution.py:661
  81.1 3.2 %all-to-all-done.refs_0_ = f32[32,2,4,8,128]{4,3,2,1,0:T(8,128)S(1)} async-done(((f32[32,2,4,8,128]{4,3,2,1,0:T(8,128)}), f32[32,2,4,8,128]{4,3,2,1,0:T(8,128)S(1)}, u32[]{:S(2)}, u32[]{:S(2)}) %all-to-all-start) | async-done | bytes 1048608 | tf_op jit(solution)/shard_map/all_to_all | solution.py:690
  84.4 1.0 copy-done.8
  85.4 10.6 %middle_planes.1 = (f32[32,2,4,8,128]{4,3,2,1,0:T(8,128)}, f32[1024,256]{1,0:T(8,128)}) custom-call(s32[1]{0:T(128)} %bitcast.me_ref, f32[2,512]{1,0:T(2,128)} %pad_maximum_fusion.9.edge, f32[32,2,4,8,128]{4,3,2,1,0:T(8,128)} %copy-done.8, bf16[512,512]{1,0:T(8,128)(2,1)} %constant.110.clone.y_high.refs_1_, bf16[512,512]{1,0:T(8,128)(2,1)} %constant.111.clone.y_low.refs_2_, ...), custom_call_target="tpu_custom_call" | custom-call | flops 3221225472 | bytes 10489856 | tf_op jit(solution)/shard_map/middle_planes/pallas_call | solution.py:432
  96.0 2.9 %all-to-all-start.3 = ((f32[32,2,4,8,128]{4,3,2,1,0:T(8,128)}), f32[32,2,4,8,128]{4,3,2,1,0:T(8,128)S(1)}, u32[]{:S(2)}, u32[]{:S(2)}) async-start(f32[32,2,4,8,128]{4,3,2,1,0:T(8,128)} %get-tuple-element.51), calls=%async_computation.3 | async-start | bytes 2097152 | tf_op jit(solution)/shard_map/all_to_all | solution.py:690
  98.9 0.1 concatenate.26
  99.0 0.1 fusion.5
  99.1 0.3 collective-permute-start.9
  99.4 4.3 %collective-permute-start.10 = (f32[8,1,1280]{2,1,0:T(1,128)S(1)}, f32[8,1,1280]{2,1,0:T(1,128)S(1)}, u32[]{:S(2)}, u32[]{:S(2)}) collective-permute-start(f32[8,1,1280]{2,1,0:T(1,128)S(1)} %get-tuple-element.56), channel_id=1, source_target_pairs={{2,0},{4,2},{6,4},{8,6},{10,8},{12,10},{14,12},{16,14},{18,16},{20... | collective-permute-start | bytes 122888 | tf_op jit(solution)/shard_map/ppermute | solution.py:577
  103.7 18.4 %collective-permute-done.9 = f32[8,1,1280]{2,1,0:T(1,128)S(1)} collective-permute-done((f32[8,1,1280]{2,1,0:T(1,128)S(1)}, f32[8,1,1280]{2,1,0:T(1,128)S(1)}, u32[]{:S(2)}, u32[]{:S(2)}) %collective-permute-start.9) | collective-permute-done | bytes 40992 | tf_op jit(solution)/shard_map/ppermute | solution.py:576
  122.0 0.0 collective-permute-done.10
  122.0 0.1 fusion.1
  122.1 1.0 pad_maximum_fusion.extended
  123.2 6.6 %odd_planes.1 = f32[32,2,4,8,128]{4,3,2,1,0:T(8,128)} custom-call(s32[1]{0:T(128)} %bitcast.me_ref, f32[1024,256]{1,0:T(8,128)} %get-tuple-element.47.freqs, bf16[2,256,512]{2,1,0:T(8,128)(2,1)} %constant.120.clone.x_high, bf16[2,256,512]{2,1,0:T(8,128)(2,1)} %constant.121.clone.x_low, bf16[512,512]{1,0:T(8,128)(2,1)} %constant.118.clone.refs_8_.y_high, ...), custom_call_target="tpu_custom_call" | custom-call | flops 1610612736 | bytes 3145728 | tf_op jit(solution)/shard_map/odd_planes/pallas_call | solution.py:432
  129.8 0.0 all-to-all-done.3.sent
  129.8 1.0 copy-done.6
  130.8 6.3 %all-to-all-start.2 = ((f32[32,2,4,8,128]{4,3,2,1,0:T(8,128)}), f32[32,2,4,8,128]{4,3,2,1,0:T(8,128)S(1)}, u32[]{:S(2)}, u32[]{:S(2)}) async-start(f32[32,2,4,8,128]{4,3,2,1,0:T(8,128)} %odd_planes.1), calls=%async_computation.2 | async-start | bytes 2097152 | tf_op jit(solution)/shard_map/all_to_all | solution.py:690
  137.1 15.5 %near_blocks.1.before_in = f32[8,8,1024]{2,1,0:T(8,128)} custom-call(f32[8,3,8,1280]{3,2,1,0:T(8,128)} %pad_maximum_fusion.extended, s32[6,8,1024]{2,1,0:T(8,128)} %codes.1, f32[6,8,8,8,1024]{4,3,2,1,0:T(8,128)} %blocks_ref.1), custom_call_target="tpu_custom_call" | custom-call | flops 6291456 | bytes 12582912 | tf_op jit(solution)/shard_map/near_blocks/pallas_call | solution.py:539
  152.6 5.5 %depth_gather.2.after.before_in = f32[8,8,1024]{2,1,0:T(8,128)} custom-call(f32[32,2,4,8,128]{4,3,2,1,0:T(8,128)} %copy-done.6, bf16[512,512]{1,0:T(8,128)(2,1)} %constant.122.clone.high_in, bf16[512,512]{1,0:T(8,128)(2,1)} %constant.123.clone.low_in, f32[8,8,1024]{2,1,0:T(8,128)} %near_blocks.1.before_in, s32[8,1024]{1,0:T(8,128)} %counts_in.7, ...), custom_call_target="tpu_custom_call" | custom-call | flops 4194304 | bytes 8388608 | tf_op jit(solution)/shard_map/depth_gather/pallas_call | solution.py:201
  158.2 0.0 copy-start.1
  158.2 0.0 copy-start.2
  158.2 0.0 copy-start.3
  158.2 0.0 copy-start.5
  158.2 6.9 %hold_projection.1.refs_0_ = f32[2,8,16,8,1024]{4,3,2,1,0:T(8,128)} custom-call(f32[8,2,2,16,8,1024]{5,4,3,2,1,0:T(8,128)} %bitcast.62, f32[8,8,1024]{2,1,0:T(8,128)} %depth_gather.2.after.before_in), custom_call_target="tpu_custom_call" | custom-call | bytes 16777216 | tf_op jit(solution)/shard_map/hold_projection/pallas_call | solution.py:232
  165.1 0.0 all-to-all-done.2.sent
  165.1 3.4 %copy-done = f32[2,8,16,8,1024]{4,3,2,1,0:T(8,128)S(1)} copy-done((f32[2,8,16,8,1024]{4,3,2,1,0:T(8,128)S(1)}, f32[2,8,16,8,1024]{4,3,2,1,0:T(8,128)}, u32[]{:S(2)}) %copy-start) | copy-done | bytes 8388632
  168.5 3.3 %depth_gather.3 = f32[8,8,1024]{2,1,0:T(8,128)} custom-call(f32[32,2,4,8,128]{4,3,2,1,0:T(8,128)S(1)} %all-to-all-done.2.sent, bf16[512,512]{1,0:T(8,128)(2,1)S(1)} %copy-done.3, bf16[512,512]{1,0:T(8,128)(2,1)S(1)} %copy-done.2, f32[8,8,1024]{2,1,0:T(8,128)S(1)} %copy-done.1, s32[8,1024]{1,0:T(8,128)S(1)} %copy-done.5, f32[2,8,16,8,1024]{4,3,2,1,0:T(8,128)S(1)} %copy-done), custom_call_target="tpu_custom_call" | custom-call | flops 4194304 | bytes 8388608 | tf_op jit(solution)/shard_map/depth_gather/pallas_call | solution.py:201
  (24 shorter events, 0.2 us)
Async XLA Ops:
  0.6 18.2 %copy-start.4 = (s32[8,1024]{1,0:T(8,128)S(1)}, s32[8,1024]{1,0:T(8,128)}, u32[]{:S(2)}) copy-start(s32[8,1024]{1,0:T(8,128)} %counts_in.7) | copy-start | bytes 98308
  0.6 18.3 %copy-start.7 = (f32[8,8,1024]{2,1,0:T(8,128)S(1)}, f32[8,8,1024]{2,1,0:T(8,128)}, u32[]{:S(2)}) copy-start(f32[8,8,1024]{2,1,0:T(8,128)} %charges_in.3) | copy-start | bytes 786436
  7.1 44.7 %all-to-all-start.1 = ((f32[32,2,4,8,128]{4,3,2,1,0:T(8,128)}), f32[32,2,4,8,128]{4,3,2,1,0:T(8,128)}, u32[]{:S(2)}, u32[]{:S(2)}) async-start(f32[32,2,4,8,128]{4,3,2,1,0:T(8,128)} %project_depth.3), calls=%async_computation.1 | async-start | bytes 2097152 | tf_op jit(solution)/shard_map/all_to_all | solution.py:690
  18.9 32.9 %collective-permute-start.4 = (f32[4,32,512]{2,1,0:T(8,128)}, f32[4,32,512]{2,1,0:T(8,128)S(1)}, u32[]{:S(2)}, u32[]{:S(2)}) collective-permute-start(f32[4,32,512]{2,1,0:T(8,128)} %get-tuple-element.37), channel_id=1, source_target_pairs={{0,8},{2,10},{4,12},{6,14},{8,0},{10,2},{12,4},{14,6},{16,24},{18,... | collective-permute-start | bytes 786440 | tf_op jit(solution)/shard_map/ppermute | solution.py:628
  20.7 31.1 %collective-permute-start.5 = (f32[4,32,512]{2,1,0:T(8,128)}, f32[4,32,512]{2,1,0:T(8,128)S(1)}, u32[]{:S(2)}, u32[]{:S(2)}) collective-permute-start(f32[4,32,512]{2,1,0:T(8,128)} %get-tuple-element.39), channel_id=1, source_target_pairs={{0,8},{2,10},{4,12},{6,14},{8,0},{10,2},{12,4},{14,6},{16,24},{18,... | collective-permute-start | bytes 786440 | tf_op jit(solution)/shard_map/ppermute | solution.py:628
  21.2 22.4 %collective-permute-start.3 = (f32[5,512]{1,0:T(8,128)S(1)}, f32[5,512]{1,0:T(8,128)S(1)}, u32[]{:S(2)}, u32[]{:S(2)}) collective-permute-start(f32[5,512]{1,0:T(8,128)S(1)} %get-tuple-element.84), channel_id=1, source_target_pairs={{16,8},{0,24},{17,9},{1,25}} | collective-permute-start | bytes 30728 | tf_op jit(solution)/shard_map/ppermute | solution.py:641
  26.7 25.1 %collective-permute-start.2 = (f32[5,512]{1,0:T(8,128)S(1)}, f32[5,512]{1,0:T(8,128)S(1)}, u32[]{:S(2)}, u32[]{:S(2)}) collective-permute-start(f32[5,512]{1,0:T(8,128)S(1)} %get-tuple-element.85), channel_id=1, source_target_pairs={{16,0},{0,16},{17,1},{1,17}} | collective-permute-start | bytes 30728 | tf_op jit(solution)/shard_map/ppermute | solution.py:641
  28.7 23.1 %collective-permute-start.1 = (f32[8,8,16]{2,1,0:T(8,128)S(1)}, f32[8,8,16]{2,1,0:T(8,128)S(1)}, u32[]{:S(2)}, u32[]{:S(2)}) collective-permute-start(f32[8,8,16]{2,1,0:T(8,128)S(1)} %get-tuple-element.73), channel_id=1, source_target_pairs={{1,0},{0,1},{3,2},{2,3},{5,4},{4,5},{7,6},{6,7},{9,8},{8,9},{11,10... | collective-permute-start | bytes 12296 | tf_op jit(solution)/shard_map/ppermute | solution.py:568
  43.6 13.6 %copy-start.9 = (f32[4,32,512]{2,1,0:T(8,128)S(1)}, f32[4,32,512]{2,1,0:T(8,128)}, u32[]{:S(2)}) copy-start(f32[4,32,512]{2,1,0:T(8,128)} %get-tuple-element.43) | copy-start | bytes 786436
  43.6 8.1 %collective-permute-start = (f32[8,8,16]{2,1,0:T(8,128)S(1)}, f32[8,8,16]{2,1,0:T(8,128)S(1)}, u32[]{:S(2)}, u32[]{:S(2)}) collective-permute-start(f32[8,8,16]{2,1,0:T(8,128)S(1)} %get-tuple-element.74), channel_id=1, source_target_pairs={{0,1},{1,0},{2,3},{3,2},{4,5},{5,4},{6,7},{7,6},{8,9},{9,8},{10,11... | collective-permute-start | bytes 12296 | tf_op jit(solution)/shard_map/ppermute | solution.py:567
  51.8 0.7 copy-start.10
  52.5 31.8 %all-to-all-start = ((f32[32,2,4,8,128]{4,3,2,1,0:T(8,128)}), f32[32,2,4,8,128]{4,3,2,1,0:T(8,128)S(1)}, u32[]{:S(2)}, u32[]{:S(2)}) async-start(f32[32,2,4,8,128]{4,3,2,1,0:T(8,128)} %project_depth.2), calls=%async_computation | async-start | bytes 2097152 | tf_op jit(solution)/shard_map/all_to_all | solution.py:690
  60.4 11.7 %collective-permute-start.8 = (f32[2,2,32,512]{3,2,1,0:T(8,128)}, f32[2,2,32,512]{3,2,1,0:T(8,128)}, u32[]{:S(2)}, u32[]{:S(2)}) collective-permute-start(f32[2,2,32,512]{3,2,1,0:T(8,128)} %get-tuple-element.86), channel_id=1, source_target_pairs={{0,6},{2,0},{4,2},{6,4},{8,14},{10,8},{12,10},{14,12},{16,22},{18,... | collective-permute-start | bytes 786440 | tf_op jit(solution)/shard_map/ppermute | solution.py:661
  61.9 13.0 %collective-permute-start.6 = (f32[2,2,32,512]{3,2,1,0:T(8,128)S(1)}, f32[2,2,32,512]{3,2,1,0:T(8,128)}, u32[]{:S(2)}, u32[]{:S(2)}) collective-permute-start(f32[2,2,32,512]{3,2,1,0:T(8,128)S(1)} %get-tuple-element.87), channel_id=1, source_target_pairs={{0,2},{2,4},{4,6},{6,0},{8,10},{10,12},{12,14},{14,8},{16,18},{18,... | collective-permute-start | bytes 786440 | tf_op jit(solution)/shard_map/ppermute | solution.py:661
  61.9 19.2 %collective-permute-start.7 = (f32[2,2,32,512]{3,2,1,0:T(8,128)S(1)}, f32[2,2,32,512]{3,2,1,0:T(8,128)}, u32[]{:S(2)}, u32[]{:S(2)}) collective-permute-start(f32[2,2,32,512]{3,2,1,0:T(8,128)S(1)} %get-tuple-element.88), channel_id=1, source_target_pairs={{0,4},{2,6},{4,0},{6,2},{8,12},{10,14},{12,8},{14,10},{16,20},{18,... | collective-permute-start | bytes 786440 | tf_op jit(solution)/shard_map/ppermute | solution.py:661
  84.3 1.0 copy-start.8
  96.0 33.8 %all-to-all-start.3 = ((f32[32,2,4,8,128]{4,3,2,1,0:T(8,128)}), f32[32,2,4,8,128]{4,3,2,1,0:T(8,128)S(1)}, u32[]{:S(2)}, u32[]{:S(2)}) async-start(f32[32,2,4,8,128]{4,3,2,1,0:T(8,128)} %get-tuple-element.51), calls=%async_computation.3 | async-start | bytes 2097152 | tf_op jit(solution)/shard_map/all_to_all | solution.py:690
  99.1 22.9 %collective-permute-start.9 = (f32[8,1,1280]{2,1,0:T(1,128)S(1)}, f32[8,1,1280]{2,1,0:T(1,128)S(1)}, u32[]{:S(2)}, u32[]{:S(2)}) collective-permute-start(f32[8,1,1280]{2,1,0:T(1,128)S(1)} %get-tuple-element.55), channel_id=1, source_target_pairs={{0,2},{2,4},{4,6},{6,8},{8,10},{10,12},{12,14},{14,16},{16,18},{18... | collective-permute-start | bytes 122888 | tf_op jit(solution)/shard_map/ppermute | solution.py:576
  99.4 22.6 %collective-permute-start.10 = (f32[8,1,1280]{2,1,0:T(1,128)S(1)}, f32[8,1,1280]{2,1,0:T(1,128)S(1)}, u32[]{:S(2)}, u32[]{:S(2)}) collective-permute-start(f32[8,1,1280]{2,1,0:T(1,128)S(1)} %get-tuple-element.56), channel_id=1, source_target_pairs={{2,0},{4,2},{6,4},{8,6},{10,8},{12,10},{14,12},{16,14},{18,16},{20... | collective-permute-start | bytes 122888 | tf_op jit(solution)/shard_map/ppermute | solution.py:577
  129.8 1.0 copy-start.6
  130.8 34.3 %all-to-all-start.2 = ((f32[32,2,4,8,128]{4,3,2,1,0:T(8,128)}), f32[32,2,4,8,128]{4,3,2,1,0:T(8,128)S(1)}, u32[]{:S(2)}, u32[]{:S(2)}) async-start(f32[32,2,4,8,128]{4,3,2,1,0:T(8,128)} %odd_planes.1), calls=%async_computation.2 | async-start | bytes 2097152 | tf_op jit(solution)/shard_map/all_to_all | solution.py:690
  158.2 6.9 %copy-start.1 = (f32[8,8,1024]{2,1,0:T(8,128)S(1)}, f32[8,8,1024]{2,1,0:T(8,128)}, u32[]{:S(2)}) copy-start(f32[8,8,1024]{2,1,0:T(8,128)} %depth_gather.2.after.before_in) | copy-start | bytes 786436
  158.2 6.9 %copy-start.2 = (bf16[512,512]{1,0:T(8,128)(2,1)S(1)}, bf16[512,512]{1,0:T(8,128)(2,1)}, u32[]{:S(2)}) copy-start(bf16[512,512]{1,0:T(8,128)(2,1)} %constant.123.clone.low_in) | copy-start | bytes 1572868
  158.2 6.9 %copy-start.3 = (bf16[512,512]{1,0:T(8,128)(2,1)S(1)}, bf16[512,512]{1,0:T(8,128)(2,1)}, u32[]{:S(2)}) copy-start(bf16[512,512]{1,0:T(8,128)(2,1)} %constant.122.clone.high_in) | copy-start | bytes 1572868
  158.2 6.9 %copy-start.5 = (s32[8,1024]{1,0:T(8,128)S(1)}, s32[8,1024]{1,0:T(8,128)}, u32[]{:S(2)}) copy-start(s32[8,1024]{1,0:T(8,128)} %counts_in.7) | copy-start | bytes 98308
  165.1 3.4 %copy-start = (f32[2,8,16,8,1024]{4,3,2,1,0:T(8,128)S(1)}, f32[2,8,16,8,1024]{4,3,2,1,0:T(8,128)}, u32[]{:S(2)}) copy-start(f32[2,8,16,8,1024]{4,3,2,1,0:T(8,128)} %hold_projection.1.refs_0_) | copy-start | bytes 25165828

commit v9 on v8

--- a/solution.py
+++ b/solution.py
@@ -16,7 +16,7 @@
 NZC = 16
 LANES = 128
 CHUNKS = 2
-VMEM_LIMIT = 62 * 1024 * 1024
+VMEM_LIMIT = 60 * 1024 * 1024
 
 
 def halves(table):
@@ -188,58 +188,33 @@
     return pl.BlockSpec(shape, lambda i: (0,) * len(shape))
 
 
-def projection_call(plan, kernel, name, arrays, projection, out_shape, fits_held):
-    scratch = [pltpu.VMEM((plan.steps * LANES, TZ * LANES), jnp.float32)]
-    space = pltpu.VMEM
-    limit = VMEM_LIMIT - 20 * 1024 * 1024
-    if fits_held:
-        scratch.append(pltpu.VMEM(held_shape(plan), jnp.float32))
-        space = pl.ANY
-        limit = VMEM_LIMIT
-    scratch.append(pltpu.SemaphoreType.DMA((plan.tx_chunk + len(arrays),)))
-    scratch += [pltpu.VMEM(array.shape, array.dtype) for array in arrays]
+def projection_call(plan, kernel, name, ready, arrays, projection, out_shape):
     return pl.pallas_call(
         kernel,
-        in_specs=[pl.BlockSpec(memory_space=pl.ANY)] * len(arrays) + [pl.BlockSpec(memory_space=space)],
+        in_specs=[pl.BlockSpec(memory_space=pltpu.VMEM)] * len(ready)
+        + [pl.BlockSpec(memory_space=pl.ANY)] * (len(arrays) + 1),
         out_specs=pl.BlockSpec(memory_space=pltpu.VMEM),
         out_shape=jax.ShapeDtypeStruct(out_shape, jnp.float32),
-        scratch_shapes=scratch,
-        compiler_params=pltpu.CompilerParams(vmem_limit_bytes=limit),
+        scratch_shapes=[
+            pltpu.VMEM((plan.steps * LANES, TZ * LANES), jnp.float32),
+            pltpu.VMEM(held_shape(plan), jnp.float32),
+            pltpu.SemaphoreType.DMA((plan.tx_chunk + len(arrays),)),
+        ]
+        + [pltpu.VMEM(array.shape, array.dtype) for array in arrays],
+        compiler_params=pltpu.CompilerParams(vmem_limit_bytes=VMEM_LIMIT),
         cost_estimate=pl.CostEstimate(
             flops=2 * math.prod(held_shape(plan)),
             bytes_accessed=4 * math.prod(held_shape(plan)),
             transcendentals=0,
         ),
         name=name,
-    )(*arrays, projection)
+    )(*ready, *arrays, projection)
 
 
 def project(plan, chunk, charges, counts, projection, high, low):
     kernel = functools.partial(project_kernel, plan, chunk)
     arrays = [charges, counts, high, low]
-    return projection_call(plan, kernel, "project_depth", arrays, projection, piece_shape(plan), True)
-
-
-def hold_kernel(plan, chunk, projection, after, out, sems):
-    copies = tile_copies(plan, chunk, projection, out, sems)
-    for copy in copies:
-        copy.start()
-    for copy in copies:
-        copy.wait()
-
-
-def hold_projection(plan, chunk, projection, after):
-    return pl.pallas_call(
-        functools.partial(hold_kernel, plan, chunk),
-        in_specs=[pl.BlockSpec(memory_space=pl.ANY)] * 2,
-        out_specs=pl.BlockSpec(memory_space=pltpu.VMEM),
-        out_shape=jax.ShapeDtypeStruct(held_shape(plan), jnp.float32),
-        scratch_shapes=[pltpu.SemaphoreType.DMA((plan.tx_chunk,))],
-        cost_estimate=pl.CostEstimate(
-            flops=0, bytes_accessed=8 * math.prod(held_shape(plan)), transcendentals=0
-        ),
-        name="hold_projection",
-    )(projection, after)
+    return projection_call(plan, kernel, "project_depth", [], arrays, projection, piece_shape(plan))
 
 
 def far_sign(plan, me_ref):
@@ -345,16 +320,16 @@
     out[...] = forward_plane(plan, me_ref, pieces, (y_high, y_low), (x_high, x_low), rows_ref, freq_ref)
 
 
-def middle_plane_kernel(plan, me_ref, edge, *refs):
-    late, refs = (refs[:10], refs[10:])
+def middle_plane_kernel(plan, me_ref, pieces, edge, *refs):
+    late, refs = (refs[:9], refs[9:])
     strips, refs = (refs[: plan.inner], refs[plan.inner :])
     out, rest, rows_ref, freq_ref, sum_ref, rest_ref, weights = refs[:7]
-    pieces, yf_high, yf_low, xf_high, xf_low, even, xb_high, xb_low, yb_high, yb_low, sems = refs[7:]
+    yf_high, yf_low, xf_high, xf_low, even, xb_high, xb_low, yb_high, yb_low, sems = refs[7:]
     slab = lax.rem(me_ref[0], plan.slabs)
     place = lax.rem(slab, plan.half)
     outer_id, inner_id = (place // plan.inner, lax.rem(place, plan.inner))
-    held = (pieces, yf_high, yf_low, xf_high, xf_low, even, xb_high, xb_low, yb_high, yb_low)
-    copies = [pltpu.make_async_copy(late[n], held[n], sems.at[n]) for n in range(6)]
+    held = (yf_high, yf_low, xf_high, xf_low, even, xb_high, xb_low, yb_high, yb_low)
+    copies = [pltpu.make_async_copy(late[n], held[n], sems.at[n]) for n in range(5)]
     for i in range(plan.inner):
         for j in range(plan.outer):
             owner = lax.rem(outer_id - j + plan.outer, plan.outer) * plan.inner
@@ -366,19 +341,18 @@
                 )
             )
     early = len(copies)
-    for n in range(6, len(held)):
+    for n in range(5, len(held)):
         copies.append(pltpu.make_async_copy(late[n], held[n], sems.at[n]))
     for copy in copies:
         copy.start()
-    copies[0].wait()
     special = me_ref[0] == 0
     width = plan.x_chunk
     middle = plan.ny // 2
     x_table = (xf_high.at[pl.ds(0, 1)], xf_low.at[pl.ds(0, 1)])
     odd = forward_plane(
-        plan, me_ref, pieces, (yf_high, yf_low), x_table, rows_ref, freq_ref, copies[1:5]
-    )
-    for copy in copies[5:early]:
+        plan, me_ref, pieces, (yf_high, yf_low), x_table, rows_ref, freq_ref, copies[:4]
+    )
+    for copy in copies[4:early]:
         copy.wait()
     row = lax.broadcasted_iota(jnp.int32, (middle, width), 0)
     at_first = row == 0
@@ -417,8 +391,9 @@
     backward_plane(plan, me_ref, freqs[...], (x_high, x_low), (y_high, y_low), out, rows_ref)
 
 
-def plane_call(plan, kernel, name, me, arrays, tables, late, out_shapes, scratch, work):
-    specs = [whole_spec(array.shape) for array in arrays]
+def plane_call(plan, kernel, name, me, ready, arrays, tables, late, out_shapes, scratch, work):
+    specs = [pl.BlockSpec(memory_space=pltpu.VMEM)] * len(ready)
+    specs += [whole_spec(array.shape) for array in arrays]
     flat = []
     for pair, chunk in tables:
         for table in pair:
@@ -428,7 +403,7 @@
                 specs.append(pl.BlockSpec((1,) + table.shape[1:], lambda i, chunk=chunk: (chunk, 0, 0)))
             flat.append(table)
     specs += [pl.BlockSpec(memory_space=pl.ANY)] * len(late)
-    size = sum(4 * array.size for array in list(arrays) + list(late)) + sum(2 * t.size for t in flat)
+    size = sum(4 * array.size for array in list(ready) + list(arrays) + list(late)) + sum(2 * t.size for t in flat)
     return pl.pallas_call(
         functools.partial(kernel, plan),
         grid=(1,),
@@ -441,30 +416,29 @@
             flops=work * 12 * plan.nx * plan.ny * plan.x_chunk, bytes_accessed=size, transcendentals=0
         ),
         name=name,
-    )(me, *arrays, *flat, *late)
-
-
-def gather_kernel(plan, chunk, sent, high_in, low_in, before_in, counts_in, *refs):
+    )(me, *ready, *arrays, *flat, *late)
+
+
+def gather_kernel(
+    plan, chunk, pieces, high_in, low_in, before_in, counts_in, projection, out, scratch, held, sems,
+    high, low, before, counts
+):
     planes = plan.cell_planes
     rows = plan.slots * 2 * plan.row_block
     first = plan.tx_chunk
-    if chunk == CHUNKS - 1:
-        held, out, scratch, sems, pieces, high, low, before, counts = refs
-        copies = []
-    else:
-        projection, out, scratch, held, sems, pieces, high, low, before, counts = refs
-        copies = tile_copies(plan, chunk, projection, held, sems)
-    pairs = ((sent, pieces), (high_in, high), (low_in, low), (before_in, before), (counts_in, counts))
+    copies = tile_copies(plan, chunk, projection, held, sems)
+    pairs = ((high_in, high), (low_in, low), (before_in, before), (counts_in, counts))
     loads = [pltpu.make_async_copy(*pair, sems.at[first + n]) for n, pair in enumerate(pairs)]
-    for copy in loads + copies:
+    for copy in loads[:2] + copies + loads[2:]:
         copy.start()
-    for copy in loads:
+    for copy in loads[:2]:
         copy.wait()
     columns = [pieces[:, :, step].reshape(rows, LANES) for step in range(plan.steps)]
     scratch[...] = product(split(jnp.concatenate(columns, axis=1).T), (high[...], low[...]))
+    for copy in loads[2:]:
+        copy.wait()
     for tx in range(plan.tx_chunk):
-        if copies:
-            copies[tx].wait()
+        copies[tx].wait()
         last = chunk == CHUNKS - 1 and tx == plan.tx_chunk - 1
 
         def body(place, carry, tx=tx, last=last):
@@ -487,9 +461,8 @@
 
 def gather(plan, chunk, counts, before, projection, high, low, pieces):
     kernel = functools.partial(gather_kernel, plan, chunk)
-    arrays = [pieces, high, low, before, counts]
-    held_here = chunk < CHUNKS - 1
-    return projection_call(plan, kernel, "depth_gather", arrays, projection, before.shape, held_here)
+    arrays = [high, low, before, counts]
+    return projection_call(plan, kernel, "depth_gather", [pieces], arrays, projection, before.shape)
 
 
 def near_kernel(plan, extended, codes, blocks_ref, out):
@@ -703,9 +676,9 @@
     pieces[0], ids = lax.optimization_barrier((pieces[0], ids))
     even_pieces = exchange(pieces[0])
     picked = pick_planes(plan, ids, spectrum)
-    masked, rows, *picked = lax.optimization_barrier((masked, rows, *picked))
     plain = [outer_shift(plan, picked[2 * j], j) for j in range(plan.outer)]
     mirror = [outer_shift(plan, picked[2 * j + 1], j) for j in range(plan.outer)]
+    pieces[1], masked, rows = lax.optimization_barrier((pieces[1], masked, rows))
     turned, own_row = edge_weights(plan, rows)
     left, right = extend_rows(plan, masked)
     pieces[1], left, right, turned, *moved = lax.optimization_barrier(
@@ -716,30 +689,31 @@
     strips = second_weights(plan, list(zip(plain, mirror)), turned)
     edge = jnp.concatenate([turned[plan.inner :], own_row], axis=0)
     (even,) = plane_call(
-        plan, first_plane_kernel, "even_planes", me, [even_pieces], [(y_forward, None), (x_forward, 0)], [],
+        plan, first_plane_kernel, "even_planes", me, [even_pieces], [], [(y_forward, None), (x_forward, 0)], [],
         [both_shape], values(rows_shape, freq_shape), 2,
     )
-    late = [odd_pieces, *y_forward, x_forward[0][1:], x_forward[1][1:], even]
+    even, masked = lax.optimization_barrier((even, masked))
+    extended = extend_planes(plan, masked, left, right)
+    odd_pieces, extended = lax.optimization_barrier((odd_pieces, extended))
+    late = [*y_forward, x_forward[0][1:], x_forward[1][1:], even]
     late += [x_backward[0][:1], x_backward[1][:1], *y_backward]
     copies = [pltpu.VMEM(array.shape, array.dtype) for array in late]
     copies.append(pltpu.SemaphoreType.DMA((len(late) + plan.half + 1,)))
     back, rest = plane_call(
-        plan, middle_plane_kernel, "middle_planes", me, [edge],
+        plan, middle_plane_kernel, "middle_planes", me, [odd_pieces], [edge],
         [], late + strips, [piece_shape(plan), freq_shape],
         values(rows_shape, freq_shape, freq_shape, freq_shape, (2, plan.ny // 2, plan.nx)) + copies, 4,
     )
     even_back = exchange(back)
     (back,) = plane_call(
-        plan, last_plane_kernel, "odd_planes", me, [rest], [(x_backward, 1), (y_backward, None)], [],
+        plan, last_plane_kernel, "odd_planes", me, [], [rest], [(x_backward, 1), (y_backward, None)], [],
         [piece_shape(plan)], values(rows_shape), 2,
     )
-    extended = extend_planes(plan, masked, left, right)
-    back, extended = lax.optimization_barrier((back, extended))
+    total = near_field(plan, extended, neighbours, near_blocks)
+    back, total = lax.optimization_barrier((back, total))
     odd_back = exchange(back)
-    total = near_field(plan, extended, neighbours, near_blocks)
     total = gather(plan, 0, counts, total, split_projection, *depth_backward, even_back)
-    held = hold_projection(plan, 1, split_projection, total)
-    return gather(plan, 1, counts, total, held, *depth_backward, odd_back)
+    return gather(plan, 1, counts, total, split_projection, *depth_backward, odd_back)
 
 
 def padded(value, sides, width):

time: 173 us -> 164 us (0.948)
  local copies, waits for them, and re-layouts: 9.75 us -> 3.82 us
  starting transfers between devices: 40.8 us -> 38.3 us
    all_to_all x4, waiting for transfers between devices: 3.23 us -> 28.1 us  [exchange(): return lax.all_to_all(pieces, axes, split_axis=0, concat_axis=0, tiled=True)]
    ppermute x3, waiting for transfers between devices: 12.1 us -> 0.05 us  [second_weights(): strip = lax.ppermute(strip, 'slab', pairs)]
    ppermute x1, waiting for transfers between devices: 18.4 us -> 10.7 us  [extend_planes(): before = lax.ppermute(wide[:, -1:], 'slab', up)]
    ppermute x2, waiting for transfers between devices: 13.5 us -> 7.02 us  [edge_weights(): total = total + lax.ppermute(sent, 'slab', pairs)]
    unnamed x23 -> x19, local copies, waits for them, and re-layouts: 6.13 us -> 2.06 us
    ppermute x1, waiting for transfers between devices: 0.01 us -> 2.22 us  [extend_rows(): left = lax.ppermute(masked[:, :, -NZC:], 'cell', up)]
    another operation x2, local copies, waits for them, and re-layouts: 1.98 us -> 0.1 us  [second_weights(): strip = jnp.stack(rows).reshape((plan.outer, 2) + blocks[0][0].shape[1:])]
    pallas_call x5 -> x4, Pallas kernels: 28.5 us -> 26.7 us  [projection_call(): pl.pallas_call(kernel, in_specs=[pl.BlockSpec(memory_space=pltpu.VMEM)] *...]
  transfers between devices with their start and end apart: 15 -> 15, of which waited for: 6 -> 6; matrix products, arithmetic and copies ran while one was open for 4% -> 3% of each run, Pallas kernels for 29% -> 27%
where the time goes in v9:
time: 164 us; the launch traced here: 163 us
  Pallas kernels  68.6 us (42%)
  waiting for transfers between devices  48 us (29%)
  starting transfers between devices  38.3 us (23%)
  local copies, waits for them, and re-layouts  3.82 us (2%)
  other arithmetic  3.43 us (2%)
    all_to_all x4, waiting for transfers between devices, exchange(): return lax.all_to_all(pieces, axes, split_axis=0, concat_axis=0, tiled=True)  28.1 us
    pallas_call x4, Pallas kernels, projection_call(): pl.pallas_call(kernel, in_specs=[pl.BlockSpec(memory_space=pltpu.VMEM)] *...  26.7 us
    pallas_call x3, Pallas kernels, plane_call(): pl.pallas_call(functools.partial(kernel, plan), grid=(1,), in_specs=[pl.B...  23.4 us
    all_to_all x4, starting transfers between devices, exchange(): return lax.all_to_all(pieces, axes, split_axis=0, concat_axis=0, tiled=True)  20.6 us
    pallas_call x1, Pallas kernels, near_field(): pl.pallas_call(functools.partial(near_kernel, plan), grid=(plan.cell_cols...  15.5 us
    ppermute x1, waiting for transfers between devices, extend_planes(): before = lax.ppermute(wide[:, -1:], 'slab', up)  10.7 us
    ppermute x2, starting transfers between devices, edge_weights(): total = total + lax.ppermute(sent, 'slab', pairs)  7.47 us
    ppermute x2, waiting for transfers between devices, edge_weights(): total = total + lax.ppermute(sent, 'slab', pairs)  7.02 us
  transfers between devices with their start and end apart: 15, of which 6 were waited for; matrix products, arithmetic and copies ran while one was open for 3% of the time, Pallas kernels for 27%

profile of v9, /device:TPU:0, one launch (start us, length us, event | category | flops | bytes accessed | tf_op | source)
XLA Modules:
  0.0 162.8 jit_solution(6319793346538791473)
XLA Ops:
  0.0 0.6 pad_add_fusion.ids_ref
  0.6 6.4 %project_depth.3 = f32[32,2,4,8,128]{4,3,2,1,0:T(8,128)} custom-call(f32[8,8,1024]{2,1,0:T(8,128)} %charges_in.3, s32[8,1024]{1,0:T(8,128)} %counts_in.7, bf16[512,512]{1,0:T(8,128)(2,1)} %constant.108.clone.high_in, bf16[512,512]{1,0:T(8,128)(2,1)} %constant.109.clone.low_in, f32[8,2,2,16,8,1024]{5,4,3,2,1,0:T(8,128)} %bitcast.59), custom_call_target="tpu_custom_call" | custom-call | flops 4194304 | bytes 8388608 | tf_op jit(solution)/shard_map/project_depth/pallas_call | solution.py:192
  7.0 0.0 copy-start.2
  7.0 0.0 copy-start.5
  7.0 7.3 %all-to-all-start.1 = ((f32[32,2,4,8,128]{4,3,2,1,0:T(8,128)}), f32[32,2,4,8,128]{4,3,2,1,0:T(8,128)S(1)}, u32[]{:S(2)}, u32[]{:S(2)}) async-start(f32[32,2,4,8,128]{4,3,2,1,0:T(8,128)} %project_depth.3), calls=%async_computation.1 | async-start | bytes 2097152 | tf_op jit(solution)/shard_map/all_to_all | solution.py:663
  14.3 3.0 %pick_planes.1 = (f32[4,32,512]{2,1,0:T(8,128)}, f32[4,32,512]{2,1,0:T(8,128)}, f32[4,32,512]{2,1,0:T(8,128)}, f32[4,32,512]{2,1,0:T(8,128)}) custom-call(s32[2]{0:T(128)} %pad_add_fusion.ids_ref, f32[64,32,512]{2,1,0:T(8,128)} %bitcast.63), custom_call_target="tpu_custom_call" | custom-call | bytes 2097152 | tf_op jit(solution)/shard_map/pick_planes/pallas_call | solution.py:581
  17.4 0.0 copy-start.6
  17.4 0.0 copy-start.7
  17.4 1.8 %collective-permute-start.4 = (f32[4,32,512]{2,1,0:T(8,128)}, f32[4,32,512]{2,1,0:T(8,128)S(1)}, u32[]{:S(2)}, u32[]{:S(2)}) collective-permute-start(f32[4,32,512]{2,1,0:T(8,128)} %get-tuple-element.35), channel_id=1, source_target_pairs={{0,8},{2,10},{4,12},{6,14},{8,0},{10,2},{12,4},{14,6},{16,24},{18,... | collective-permute-start | bytes 786440 | tf_op jit(solution)/shard_map/ppermute | solution.py:601
  19.2 0.3 collective-permute-start.5
  19.5 1.3 slice.34
  20.8 6.4 %project_depth.2 = f32[32,2,4,8,128]{4,3,2,1,0:T(8,128)} custom-call(f32[8,8,1024]{2,1,0:T(8,128)} %charges_in.3, s32[8,1024]{1,0:T(8,128)} %counts_in.7, bf16[512,512]{1,0:T(8,128)(2,1)} %constant.108.clone.high_in, bf16[512,512]{1,0:T(8,128)(2,1)} %constant.109.clone.low_in, f32[8,2,2,16,8,1024]{5,4,3,2,1,0:T(8,128)} %bitcast.60), custom_call_target="tpu_custom_call" | custom-call | flops 4194304 | bytes 8388608 | tf_op jit(solution)/shard_map/project_depth/pallas_call | solution.py:192
  27.2 0.0 copy-done.2
  27.2 0.0 copy-done.5
  27.3 0.1 rev.4
  27.5 5.5 %collective-permute-start.3 = (f32[5,512]{1,0:T(8,128)S(1)}, f32[5,512]{1,0:T(8,128)S(1)}, u32[]{:S(2)}, u32[]{:S(2)}) collective-permute-start(f32[5,512]{1,0:T(8,128)S(1)} %get-tuple-element.86), channel_id=1, source_target_pairs={{16,8},{0,24},{17,9},{1,25}} | collective-permute-start | bytes 30728 | tf_op jit(solution)/shard_map/ppermute | solution.py:614
  33.1 1.9 %collective-permute-start.2 = (f32[5,512]{1,0:T(8,128)S(1)}, f32[5,512]{1,0:T(8,128)S(1)}, u32[]{:S(2)}, u32[]{:S(2)}) collective-permute-start(f32[5,512]{1,0:T(8,128)S(1)} %get-tuple-element.87), channel_id=1, source_target_pairs={{16,0},{0,16},{17,1},{1,17}} | collective-permute-start | bytes 30728 | tf_op jit(solution)/shard_map/ppermute | solution.py:614
  35.0 0.1 fusion.6
  35.1 1.5 collective-permute-start.1
  36.6 7.0 %collective-permute-done.3 = f32[5,512]{1,0:T(8,128)S(1)} collective-permute-done((f32[5,512]{1,0:T(8,128)S(1)}, f32[5,512]{1,0:T(8,128)S(1)}, u32[]{:S(2)}, u32[]{:S(2)}) %collective-permute-start.3) | collective-permute-done | bytes 10272 | tf_op jit(solution)/shard_map/ppermute | solution.py:614
  43.6 1.7 %collective-permute-start = (f32[8,8,16]{2,1,0:T(8,128)S(1)}, f32[8,8,16]{2,1,0:T(8,128)S(1)}, u32[]{:S(2)}, u32[]{:S(2)}) collective-permute-start(f32[8,8,16]{2,1,0:T(8,128)S(1)} %get-tuple-element.76), channel_id=1, source_target_pairs={{0,1},{1,0},{2,3},{3,2},{4,5},{5,4},{6,7},{7,6},{8,9},{9,8},{10,11... | collective-permute-start | bytes 12296 | tf_op jit(solution)/shard_map/ppermute | solution.py:540
  45.3 0.0 collective-permute-done.2
  45.3 0.0 collective-permute-done.1
  45.3 2.2 %collective-permute-done = f32[8,8,16]{2,1,0:T(8,128)S(1)} collective-permute-done((f32[8,8,16]{2,1,0:T(8,128)S(1)}, f32[8,8,16]{2,1,0:T(8,128)S(1)}, u32[]{:S(2)}, u32[]{:S(2)}) %collective-permute-start) | collective-permute-done | bytes 4128 | tf_op jit(solution)/shard_map/ppermute | solution.py:540
  47.5 0.0 collective-permute-done.4
  47.5 0.0 collective-permute-done.5
  47.5 0.0 copy-done.6
  47.5 0.0 copy-done.7
  47.7 0.0 all-to-all-done.1.pieces
  47.7 0.0 copy-start.3
  47.7 5.8 %all-to-all-start = ((f32[32,2,4,8,128]{4,3,2,1,0:T(8,128)}), f32[32,2,4,8,128]{4,3,2,1,0:T(8,128)S(1)}, u32[]{:S(2)}, u32[]{:S(2)}) async-start(f32[32,2,4,8,128]{4,3,2,1,0:T(8,128)} %project_depth.2), calls=%async_computation | async-start | bytes 2097152 | tf_op jit(solution)/shard_map/all_to_all | solution.py:663
  53.6 0.9 broadcast_select_fusion
  54.4 0.0 copy-done.3
  54.4 5.8 %even_planes.1.refs_4_ = f32[1024,512]{1,0:T(8,128)} custom-call(s32[1]{0:T(128)} %bitcast.me_ref, f32[32,2,4,8,128]{4,3,2,1,0:T(8,128)} %copy-done.3, bf16[512,512]{1,0:T(8,128)(2,1)} %constant.110.clone.y_high.refs_0_, bf16[512,512]{1,0:T(8,128)(2,1)} %constant.111.clone.y_low.refs_1_, bf16[2,256,512]{2,1,0:T(8,128)(2,1)} %constant.112.clone.x_high, ...), custom_call_target="tpu_custom_call" | custom-call | flops 1610612736 | bytes 3145728 | tf_op jit(solution)/shard_map/even_planes/pallas_call | solution.py:407
  60.2 0.1 concatenate.25
  60.3 0.1 fusion.5
  60.4 0.3 collective-permute-start.6
  60.7 4.2 %collective-permute-start.7 = (f32[8,1,1280]{2,1,0:T(1,128)S(1)}, f32[8,1,1280]{2,1,0:T(1,128)S(1)}, u32[]{:S(2)}, u32[]{:S(2)}) collective-permute-start(f32[8,1,1280]{2,1,0:T(1,128)S(1)} %get-tuple-element.58), channel_id=1, source_target_pairs={{2,0},{4,2},{6,4},{8,6},{10,8},{12,10},{14,12},{16,14},{18,16},{20... | collective-permute-start | bytes 122888 | tf_op jit(solution)/shard_map/ppermute | solution.py:550
  64.9 0.6 pad_maximum_fusion.9.edge
  65.5 0.0 collective-permute-start.10
  65.5 0.5 collective-permute-start.8
  66.0 0.0 collective-permute-start.9
  66.0 10.7 %collective-permute-done.6 = f32[8,1,1280]{2,1,0:T(1,128)S(1)} collective-permute-done((f32[8,1,1280]{2,1,0:T(1,128)S(1)}, f32[8,1,1280]{2,1,0:T(1,128)S(1)}, u32[]{:S(2)}, u32[]{:S(2)}) %collective-permute-start.6) | collective-permute-done | bytes 40992 | tf_op jit(solution)/shard_map/ppermute | solution.py:549
  76.7 0.0 collective-permute-done.7
  76.7 0.1 fusion.1
  76.8 1.1 pad_maximum_fusion.extended
  77.8 2.8 %all-to-all-done.pieces = f32[32,2,4,8,128]{4,3,2,1,0:T(8,128)S(1)} async-done(((f32[32,2,4,8,128]{4,3,2,1,0:T(8,128)}), f32[32,2,4,8,128]{4,3,2,1,0:T(8,128)S(1)}, u32[]{:S(2)}, u32[]{:S(2)}) %all-to-all-start) | async-done | bytes 1048608 | tf_op jit(solution)/shard_map/all_to_all | solution.py:663
  80.6 0.0 copy-start.4
  80.6 0.0 collective-permute-done.10.refs_12_
  80.6 0.0 collective-permute-done.8.refs_10_
  80.6 0.0 collective-permute-done.9.refs_11_
  80.7 1.0 copy-done.4
  81.6 0.1 copy-done.8
  81.7 11.0 %middle_planes.1 = (f32[32,2,4,8,128]{4,3,2,1,0:T(8,128)}, f32[1024,256]{1,0:T(8,128)}) custom-call(s32[1]{0:T(128)} %bitcast.me_ref, f32[32,2,4,8,128]{4,3,2,1,0:T(8,128)} %copy-done.4, f32[2,512]{1,0:T(2,128)} %pad_maximum_fusion.9.edge, bf16[512,512]{1,0:T(8,128)(2,1)} %constant.110.clone.y_high.refs_0_, bf16[512,512]{1,0:T(8,128)(2,1)} %constant.111.clone.y_low.refs_1_, ...), custom_call_target="tpu_custom_call" | custom-call | flops 3221225472 | bytes 10489856 | tf_op jit(solution)/shard_map/middle_planes/pallas_call | solution.py:407
  92.7 4.9 %all-to-all-start.3 = ((f32[32,2,4,8,128]{4,3,2,1,0:T(8,128)}), f32[32,2,4,8,128]{4,3,2,1,0:T(8,128)S(1)}, u32[]{:S(2)}, u32[]{:S(2)}) async-start(f32[32,2,4,8,128]{4,3,2,1,0:T(8,128)} %get-tuple-element.53), calls=%async_computation.3 | async-start | bytes 2097152 | tf_op jit(solution)/shard_map/all_to_all | solution.py:663
  97.6 15.5 %near_blocks.1.before_in = f32[8,8,1024]{2,1,0:T(8,128)} custom-call(f32[8,3,8,1280]{3,2,1,0:T(8,128)} %pad_maximum_fusion.extended, s32[6,8,1024]{2,1,0:T(8,128)} %codes.1, f32[6,8,8,8,1024]{4,3,2,1,0:T(8,128)} %blocks_ref.1), custom_call_target="tpu_custom_call" | custom-call | flops 6291456 | bytes 12582912 | tf_op jit(solution)/shard_map/near_blocks/pallas_call | solution.py:512
  113.1 6.6 %odd_planes.1 = f32[32,2,4,8,128]{4,3,2,1,0:T(8,128)} custom-call(s32[1]{0:T(128)} %bitcast.me_ref, f32[1024,256]{1,0:T(8,128)} %get-tuple-element.50.freqs, bf16[2,256,512]{2,1,0:T(8,128)(2,1)} %constant.120.clone.x_high, bf16[2,256,512]{2,1,0:T(8,128)(2,1)} %constant.121.clone.x_low, bf16[512,512]{1,0:T(8,128)(2,1)} %constant.118.clone.refs_7_.y_high, ...), custom_call_target="tpu_custom_call" | custom-call | flops 1610612736 | bytes 3145728 | tf_op jit(solution)/shard_map/odd_planes/pallas_call | solution.py:407
  119.7 5.1 %all-to-all-done.3.pieces = f32[32,2,4,8,128]{4,3,2,1,0:T(8,128)S(1)} async-done(((f32[32,2,4,8,128]{4,3,2,1,0:T(8,128)}), f32[32,2,4,8,128]{4,3,2,1,0:T(8,128)S(1)}, u32[]{:S(2)}, u32[]{:S(2)}) %all-to-all-start.3) | async-done | bytes 1048608 | tf_op jit(solution)/shard_map/all_to_all | solution.py:663
  124.8 2.6 %all-to-all-start.2 = ((f32[32,2,4,8,128]{4,3,2,1,0:T(8,128)}), f32[32,2,4,8,128]{4,3,2,1,0:T(8,128)S(1)}, u32[]{:S(2)}, u32[]{:S(2)}) async-start(f32[32,2,4,8,128]{4,3,2,1,0:T(8,128)} %odd_planes.1), calls=%async_computation.2 | async-start | bytes 2097152 | tf_op jit(solution)/shard_map/all_to_all | solution.py:663
  127.5 0.0 copy-done
  127.5 7.0 %depth_gather.2.before_in = f32[8,8,1024]{2,1,0:T(8,128)} custom-call(f32[32,2,4,8,128]{4,3,2,1,0:T(8,128)} %copy-done, bf16[512,512]{1,0:T(8,128)(2,1)} %constant.122.clone.high_in, bf16[512,512]{1,0:T(8,128)(2,1)} %constant.123.clone.low_in, f32[8,8,1024]{2,1,0:T(8,128)} %near_blocks.1.before_in, s32[8,1024]{1,0:T(8,128)} %counts_in.7, ...), custom_call_target="tpu_custom_call" | custom-call | flops 4194304 | bytes 8388608 | tf_op jit(solution)/shard_map/depth_gather/pallas_call | solution.py:192
  134.4 20.2 %all-to-all-done.2.pieces = f32[32,2,4,8,128]{4,3,2,1,0:T(8,128)S(1)} async-done(((f32[32,2,4,8,128]{4,3,2,1,0:T(8,128)}), f32[32,2,4,8,128]{4,3,2,1,0:T(8,128)S(1)}, u32[]{:S(2)}, u32[]{:S(2)}) %all-to-all-start.2) | async-done | bytes 1048608 | tf_op jit(solution)/shard_map/all_to_all | solution.py:663
  154.6 1.0 copy-done.1
  155.6 7.0 %depth_gather.3 = f32[8,8,1024]{2,1,0:T(8,128)} custom-call(f32[32,2,4,8,128]{4,3,2,1,0:T(8,128)} %copy-done.1, bf16[512,512]{1,0:T(8,128)(2,1)} %constant.122.clone.high_in, bf16[512,512]{1,0:T(8,128)(2,1)} %constant.123.clone.low_in, f32[8,8,1024]{2,1,0:T(8,128)} %depth_gather.2.before_in, s32[8,1024]{1,0:T(8,128)} %counts_in.7, ...), custom_call_target="tpu_custom_call" | custom-call | flops 4194304 | bytes 8388608 | tf_op jit(solution)/shard_map/depth_gather/pallas_call | solution.py:192
  (19 shorter events, 0.3 us)
Async XLA Ops:
  7.0 20.2 %copy-start.2 = (f32[8,8,1024]{2,1,0:T(8,128)S(1)}, f32[8,8,1024]{2,1,0:T(8,128)}, u32[]{:S(2)}) copy-start(f32[8,8,1024]{2,1,0:T(8,128)} %charges_in.3) | copy-start | bytes 786436
  7.0 20.2 %copy-start.5 = (s32[8,1024]{1,0:T(8,128)S(1)}, s32[8,1024]{1,0:T(8,128)}, u32[]{:S(2)}) copy-start(s32[8,1024]{1,0:T(8,128)} %counts_in.7) | copy-start | bytes 98308
  7.0 40.6 %all-to-all-start.1 = ((f32[32,2,4,8,128]{4,3,2,1,0:T(8,128)}), f32[32,2,4,8,128]{4,3,2,1,0:T(8,128)S(1)}, u32[]{:S(2)}, u32[]{:S(2)}) async-start(f32[32,2,4,8,128]{4,3,2,1,0:T(8,128)} %project_depth.3), calls=%async_computation.1 | async-start | bytes 2097152 | tf_op jit(solution)/shard_map/all_to_all | solution.py:663
  17.4 30.1 %copy-start.6 = (f32[4,32,512]{2,1,0:T(8,128)S(1)}, f32[4,32,512]{2,1,0:T(8,128)}, u32[]{:S(2)}) copy-start(f32[4,32,512]{2,1,0:T(8,128)} %get-tuple-element.46) | copy-start | bytes 786436
  17.4 30.1 %copy-start.7 = (f32[4,32,512]{2,1,0:T(8,128)S(1)}, f32[4,32,512]{2,1,0:T(8,128)}, u32[]{:S(2)}) copy-start(f32[4,32,512]{2,1,0:T(8,128)} %get-tuple-element.47) | copy-start | bytes 786436
  17.4 30.1 %collective-permute-start.4 = (f32[4,32,512]{2,1,0:T(8,128)}, f32[4,32,512]{2,1,0:T(8,128)S(1)}, u32[]{:S(2)}, u32[]{:S(2)}) collective-permute-start(f32[4,32,512]{2,1,0:T(8,128)} %get-tuple-element.35), channel_id=1, source_target_pairs={{0,8},{2,10},{4,12},{6,14},{8,0},{10,2},{12,4},{14,6},{16,24},{18,... | collective-permute-start | bytes 786440 | tf_op jit(solution)/shard_map/ppermute | solution.py:601
  19.2 28.3 %collective-permute-start.5 = (f32[4,32,512]{2,1,0:T(8,128)}, f32[4,32,512]{2,1,0:T(8,128)S(1)}, u32[]{:S(2)}, u32[]{:S(2)}) collective-permute-start(f32[4,32,512]{2,1,0:T(8,128)} %get-tuple-element.37), channel_id=1, source_target_pairs={{0,8},{2,10},{4,12},{6,14},{8,0},{10,2},{12,4},{14,6},{16,24},{18,... | collective-permute-start | bytes 786440 | tf_op jit(solution)/shard_map/ppermute | solution.py:601
  27.5 16.1 %collective-permute-start.3 = (f32[5,512]{1,0:T(8,128)S(1)}, f32[5,512]{1,0:T(8,128)S(1)}, u32[]{:S(2)}, u32[]{:S(2)}) collective-permute-start(f32[5,512]{1,0:T(8,128)S(1)} %get-tuple-element.86), channel_id=1, source_target_pairs={{16,8},{0,24},{17,9},{1,25}} | collective-permute-start | bytes 30728 | tf_op jit(solution)/shard_map/ppermute | solution.py:614
  33.1 12.2 %collective-permute-start.2 = (f32[5,512]{1,0:T(8,128)S(1)}, f32[5,512]{1,0:T(8,128)S(1)}, u32[]{:S(2)}, u32[]{:S(2)}) collective-permute-start(f32[5,512]{1,0:T(8,128)S(1)} %get-tuple-element.87), channel_id=1, source_target_pairs={{16,0},{0,16},{17,1},{1,17}} | collective-permute-start | bytes 30728 | tf_op jit(solution)/shard_map/ppermute | solution.py:614
  35.1 10.2 %collective-permute-start.1 = (f32[8,8,16]{2,1,0:T(8,128)S(1)}, f32[8,8,16]{2,1,0:T(8,128)S(1)}, u32[]{:S(2)}, u32[]{:S(2)}) collective-permute-start(f32[8,8,16]{2,1,0:T(8,128)S(1)} %get-tuple-element.75), channel_id=1, source_target_pairs={{1,0},{0,1},{3,2},{2,3},{5,4},{4,5},{7,6},{6,7},{9,8},{8,9},{11,10... | collective-permute-start | bytes 12296 | tf_op jit(solution)/shard_map/ppermute | solution.py:541
  43.6 3.9 %collective-permute-start = (f32[8,8,16]{2,1,0:T(8,128)S(1)}, f32[8,8,16]{2,1,0:T(8,128)S(1)}, u32[]{:S(2)}, u32[]{:S(2)}) collective-permute-start(f32[8,8,16]{2,1,0:T(8,128)S(1)} %get-tuple-element.76), channel_id=1, source_target_pairs={{0,1},{1,0},{2,3},{3,2},{4,5},{5,4},{6,7},{7,6},{8,9},{9,8},{10,11... | collective-permute-start | bytes 12296 | tf_op jit(solution)/shard_map/ppermute | solution.py:540
  47.7 6.8 %copy-start.3 = (f32[32,2,4,8,128]{4,3,2,1,0:T(8,128)}, f32[32,2,4,8,128]{4,3,2,1,0:T(8,128)S(1)}, u32[]{:S(2)}) copy-start(f32[32,2,4,8,128]{4,3,2,1,0:T(8,128)S(1)} %all-to-all-done.1.pieces) | copy-start | bytes 3145732
  47.7 33.0 %all-to-all-start = ((f32[32,2,4,8,128]{4,3,2,1,0:T(8,128)}), f32[32,2,4,8,128]{4,3,2,1,0:T(8,128)S(1)}, u32[]{:S(2)}, u32[]{:S(2)}) async-start(f32[32,2,4,8,128]{4,3,2,1,0:T(8,128)} %project_depth.2), calls=%async_computation | async-start | bytes 2097152 | tf_op jit(solution)/shard_map/all_to_all | solution.py:663
  60.4 16.3 %collective-permute-start.6 = (f32[8,1,1280]{2,1,0:T(1,128)S(1)}, f32[8,1,1280]{2,1,0:T(1,128)S(1)}, u32[]{:S(2)}, u32[]{:S(2)}) collective-permute-start(f32[8,1,1280]{2,1,0:T(1,128)S(1)} %get-tuple-element.57), channel_id=1, source_target_pairs={{0,2},{2,4},{4,6},{6,8},{8,10},{10,12},{12,14},{14,16},{16,18},{18... | collective-permute-start | bytes 122888 | tf_op jit(solution)/shard_map/ppermute | solution.py:549
  60.7 16.0 %collective-permute-start.7 = (f32[8,1,1280]{2,1,0:T(1,128)S(1)}, f32[8,1,1280]{2,1,0:T(1,128)S(1)}, u32[]{:S(2)}, u32[]{:S(2)}) collective-permute-start(f32[8,1,1280]{2,1,0:T(1,128)S(1)} %get-tuple-element.58), channel_id=1, source_target_pairs={{2,0},{4,2},{6,4},{8,6},{10,8},{12,10},{14,12},{16,14},{18,16},{20... | collective-permute-start | bytes 122888 | tf_op jit(solution)/shard_map/ppermute | solution.py:550
  65.5 15.2 %collective-permute-start.10 = (f32[2,2,32,512]{3,2,1,0:T(8,128)S(1)}, f32[2,2,32,512]{3,2,1,0:T(8,128)S(1)}, u32[]{:S(2)}, u32[]{:S(2)}) collective-permute-start(f32[2,2,32,512]{3,2,1,0:T(8,128)S(1)} %get-tuple-element.88), channel_id=1, source_target_pairs={{0,6},{2,0},{4,2},{6,4},{8,14},{10,8},{12,10},{14,12},{16,22},{18,... | collective-permute-start | bytes 786440 | tf_op jit(solution)/shard_map/ppermute | solution.py:634
  65.5 15.2 %collective-permute-start.8 = (f32[2,2,32,512]{3,2,1,0:T(8,128)S(1)}, f32[2,2,32,512]{3,2,1,0:T(8,128)}, u32[]{:S(2)}, u32[]{:S(2)}) collective-permute-start(f32[2,2,32,512]{3,2,1,0:T(8,128)S(1)} %get-tuple-element.89), channel_id=1, source_target_pairs={{0,2},{2,4},{4,6},{6,0},{8,10},{10,12},{12,14},{14,8},{16,18},{18,... | collective-permute-start | bytes 786440 | tf_op jit(solution)/shard_map/ppermute | solution.py:634
  66.0 14.7 %collective-permute-start.9 = (f32[2,2,32,512]{3,2,1,0:T(8,128)S(1)}, f32[2,2,32,512]{3,2,1,0:T(8,128)}, u32[]{:S(2)}, u32[]{:S(2)}) collective-permute-start(f32[2,2,32,512]{3,2,1,0:T(8,128)S(1)} %get-tuple-element.90), channel_id=1, source_target_pairs={{0,4},{2,6},{4,0},{6,2},{8,12},{10,14},{12,8},{14,10},{16,20},{18,... | collective-permute-start | bytes 786440 | tf_op jit(solution)/shard_map/ppermute | solution.py:634
  80.6 1.0 copy-start.4
  80.6 1.1 copy-start.8
  92.7 32.1 %all-to-all-start.3 = ((f32[32,2,4,8,128]{4,3,2,1,0:T(8,128)}), f32[32,2,4,8,128]{4,3,2,1,0:T(8,128)S(1)}, u32[]{:S(2)}, u32[]{:S(2)}) async-start(f32[32,2,4,8,128]{4,3,2,1,0:T(8,128)} %get-tuple-element.53), calls=%async_computation.3 | async-start | bytes 2097152 | tf_op jit(solution)/shard_map/all_to_all | solution.py:663
  124.8 2.7 %copy-start = (f32[32,2,4,8,128]{4,3,2,1,0:T(8,128)}, f32[32,2,4,8,128]{4,3,2,1,0:T(8,128)S(1)}, u32[]{:S(2)}) copy-start(f32[32,2,4,8,128]{4,3,2,1,0:T(8,128)S(1)} %all-to-all-done.3.pieces) | copy-start | bytes 3145732
  124.8 29.8 %all-to-all-start.2 = ((f32[32,2,4,8,128]{4,3,2,1,0:T(8,128)}), f32[32,2,4,8,128]{4,3,2,1,0:T(8,128)S(1)}, u32[]{:S(2)}, u32[]{:S(2)}) async-start(f32[32,2,4,8,128]{4,3,2,1,0:T(8,128)} %odd_planes.1), calls=%async_computation.2 | async-start | bytes 2097152 | tf_op jit(solution)/shard_map/all_to_all | solution.py:663
  154.6 1.0 copy-start.1

commit v10 on v9

--- a/solution.py
+++ b/solution.py
@@ -17,6 +17,7 @@
 LANES = 128
 CHUNKS = 2
 VMEM_LIMIT = 60 * 1024 * 1024
+PLANE_LIMIT = 50 * 1024 * 1024
 
 
 def halves(table):
@@ -201,7 +202,7 @@
             pltpu.SemaphoreType.DMA((plan.tx_chunk + len(arrays),)),
         ]
         + [pltpu.VMEM(array.shape, array.dtype) for array in arrays],
-        compiler_params=pltpu.CompilerParams(vmem_limit_bytes=VMEM_LIMIT),
+        compiler_params=pltpu.CompilerParams(vmem_limit_bytes=PLANE_LIMIT),
         cost_estimate=pl.CostEstimate(
             flops=2 * math.prod(held_shape(plan)),
             bytes_accessed=4 * math.prod(held_shape(plan)),
@@ -320,31 +321,33 @@
     out[...] = forward_plane(plan, me_ref, pieces, (y_high, y_low), (x_high, x_low), rows_ref, freq_ref)
 
 
-def middle_plane_kernel(plan, me_ref, pieces, edge, *refs):
-    late, refs = (refs[:9], refs[9:])
+def middle_plane_kernel(plan, me_ref, pieces, even, edge, *refs):
     strips, refs = (refs[: plan.inner], refs[plan.inner :])
+    blocks, refs = (refs[: plan.outer], refs[plan.outer :])
+    late, refs = (refs[:8], refs[8:])
     out, rest, rows_ref, freq_ref, sum_ref, rest_ref, weights = refs[:7]
-    yf_high, yf_low, xf_high, xf_low, even, xb_high, xb_low, yb_high, yb_low, sems = refs[7:]
+    held, sems = (refs[7:15], refs[15])
+    yf_high, yf_low, xf_high, xf_low, xb_high, xb_low, yb_high, yb_low = held
     slab = lax.rem(me_ref[0], plan.slabs)
     place = lax.rem(slab, plan.half)
     outer_id, inner_id = (place // plan.inner, lax.rem(place, plan.inner))
-    held = (yf_high, yf_low, xf_high, xf_low, even, xb_high, xb_low, yb_high, yb_low)
-    copies = [pltpu.make_async_copy(late[n], held[n], sems.at[n]) for n in range(5)]
+    copies = [pltpu.make_async_copy(late[n], held[n], sems.at[n]) for n in range(len(held))]
+    count = plan.ky_local
     for i in range(plan.inner):
         for j in range(plan.outer):
             owner = lax.rem(outer_id - j + plan.outer, plan.outer) * plan.inner
             owner = owner + lax.rem(inner_id - i + plan.inner, plan.inner)
-            rows = pl.ds(pl.multiple_of(owner * plan.ky_local, plan.ky_local), plan.ky_local)
-            copies.append(
-                pltpu.make_async_copy(
-                    strips[i].at[j], weights.at[:, rows], sems.at[len(held) + i * plan.outer + j]
-                )
-            )
-    early = len(copies)
-    for n in range(5, len(held)):
-        copies.append(pltpu.make_async_copy(late[n], held[n], sems.at[n]))
+            rows = pl.ds(pl.multiple_of(owner * count, count), count)
+            n = len(copies)
+            source = strips[i].at[pl.ds(j * count, count)]
+            copies.append(pltpu.make_async_copy(source, weights.at[0, rows], sems.at[n]))
+            copies.append(pltpu.make_async_copy(blocks[j].at[i], weights.at[1, rows], sems.at[n + 1]))
     for copy in copies:
         copy.start()
+    own_edge = strips[0][plan.outer * count : plan.outer * count + 1]
+    for i in range(1, plan.inner):
+        row = strips[i][plan.outer * count : plan.outer * count + 1]
+        own_edge = jnp.where(inner_id == i, row, own_edge)
     special = me_ref[0] == 0
     width = plan.x_chunk
     middle = plan.ny // 2
@@ -352,7 +355,7 @@
     odd = forward_plane(
         plan, me_ref, pieces, (yf_high, yf_low), x_table, rows_ref, freq_ref, copies[:4]
     )
-    for copy in copies[4:early]:
+    for copy in copies[len(held) :]:
         copy.wait()
     row = lax.broadcasted_iota(jnp.int32, (middle, width), 0)
     at_first = row == 0
@@ -363,13 +366,12 @@
         for upper in range(2):
             cols = slice(upper * width, (upper + 1) * width)
             plane = weights[mirrored, :, cols]
-            change = at_first & special
             if mirrored:
-                weight = jnp.where(change, edge[1:2, cols], plane)
-                second = plane
+                second = jnp.where(at_first, own_edge[:, cols], plane)
+                weight = jnp.where(special, plane, second)
             else:
                 weight = plane
-                second = jnp.where(change, edge[0:1, cols], plane)
+                second = jnp.where(at_first & special, edge[0:1, cols], plane)
             re_sums = even[re] - odd[re] if upper else even[re] + odd[re]
             im_sums = even[im] - odd[im] if upper else even[im] + odd[im]
             real = weight * re_sums[:, :width] + (turn * second) * im_sums[:, width:]
@@ -379,9 +381,9 @@
             below, above = (results[0][part], results[1][part])
             sum_ref[rows] = below + above
             rest_ref[rows] = below - above
-    last = pltpu.make_async_copy(rest_ref, rest, sems.at[len(held) + plan.half])
+    last = pltpu.make_async_copy(rest_ref, rest, sems.at[len(held) + 2 * plan.half])
     last.start()
-    for copy in copies[early:]:
+    for copy in copies[4 : len(held)]:
         copy.wait()
     backward_plane(plan, me_ref, sum_ref[...], (xb_high, xb_low), (yb_high, yb_low), out, rows_ref)
     last.wait()
@@ -391,7 +393,7 @@
     backward_plane(plan, me_ref, freqs[...], (x_high, x_low), (y_high, y_low), out, rows_ref)
 
 
-def plane_call(plan, kernel, name, me, ready, arrays, tables, late, out_shapes, scratch, work):
+def plane_call(plan, kernel, name, me, ready, arrays, tables, late, out_specs, out_shapes, scratch, work):
     specs = [pl.BlockSpec(memory_space=pltpu.VMEM)] * len(ready)
     specs += [whole_spec(array.shape) for array in arrays]
     flat = []
@@ -403,17 +405,19 @@
                 specs.append(pl.BlockSpec((1,) + table.shape[1:], lambda i, chunk=chunk: (chunk, 0, 0)))
             flat.append(table)
     specs += [pl.BlockSpec(memory_space=pl.ANY)] * len(late)
-    size = sum(4 * array.size for array in list(ready) + list(arrays) + list(late)) + sum(2 * t.size for t in flat)
+    size = sum(4 * array.size for array in list(ready) + list(arrays) + list(late))
     return pl.pallas_call(
         functools.partial(kernel, plan),
-        grid=(1,),
+        grid=(1,) if tables else (),
         in_specs=[pl.BlockSpec(memory_space=pltpu.SMEM)] + specs,
-        out_specs=[whole_spec(out_shapes[0])] + [pl.BlockSpec(memory_space=pl.ANY)] * (len(out_shapes) - 1),
+        out_specs=out_specs,
         out_shape=[jax.ShapeDtypeStruct(shape, jnp.float32) for shape in out_shapes],
         scratch_shapes=scratch,
-        compiler_params=pltpu.CompilerParams(vmem_limit_bytes=VMEM_LIMIT),
+        compiler_params=pltpu.CompilerParams(vmem_limit_bytes=PLANE_LIMIT),
         cost_estimate=pl.CostEstimate(
-            flops=work * 12 * plan.nx * plan.ny * plan.x_chunk, bytes_accessed=size, transcendentals=0
+            flops=work * 12 * plan.nx * plan.ny * plan.x_chunk,
+            bytes_accessed=size + sum(2 * table.size for table in flat),
+            transcendentals=0,
         ),
         name=name,
     )(me, *ready, *arrays, *flat, *late)
@@ -557,17 +561,20 @@
     outs, sems = (refs[:-1], refs[-1])
     cell, slab = (ids_ref[0], ids_ref[1])
     half_id, place = (slab // plan.half, lax.rem(slab, plan.half))
+    first = cell * plan.slabs + half_id * plan.half
     copies = []
     for j in range(plan.outer):
-        group = lax.rem(place // plan.inner + j, plan.outer)
-        base = cell * plan.slabs + half_id * plan.half + group * plan.inner
-        for q in range(plan.inner):
-            freq = base + q
+        part = lax.rem(place // plan.inner + j, plan.outer) * plan.inner
+        for i in range(plan.inner):
+            n = len(copies)
+            copies.append(
+                pltpu.make_async_copy(by_depth.at[first + part + i], outs[j].at[i], sems.at[n])
+            )
+            freq = first + part + lax.rem(place + i, plan.inner)
             mirror = jnp.where(freq == 0, plan.nz // 2, plan.nz - freq)
-            for m, index in enumerate((freq, mirror)):
-                n = (j * plan.inner + q) * 2 + m
-                out = outs[2 * j + m]
-                copies.append(pltpu.make_async_copy(by_depth.at[index], out.at[q], sems.at[n]))
+            copies.append(
+                pltpu.make_async_copy(by_depth.at[mirror], outs[plan.outer + i].at[j], sems.at[n + 1])
+            )
     for copy in copies:
         copy.start()
     for copy in copies:
@@ -576,19 +583,20 @@
 
 def pick_planes(plan, ids, spectrum):
     by_depth = jnp.transpose(spectrum, (1, 2, 0))
-    shape = (plan.inner,) + by_depth.shape[1:]
-    count = 2 * plan.outer
-    return pl.pallas_call(
+    shapes = [(plan.inner,) + by_depth.shape[1:]] * plan.outer
+    shapes += [(plan.outer,) + by_depth.shape[1:]] * plan.inner
+    picked = pl.pallas_call(
         functools.partial(pick_kernel, plan),
         in_specs=[pl.BlockSpec(memory_space=pltpu.SMEM), pl.BlockSpec(memory_space=pl.ANY)],
-        out_specs=[pl.BlockSpec(memory_space=pltpu.VMEM)] * count,
-        out_shape=[jax.ShapeDtypeStruct(shape, jnp.float32)] * count,
+        out_specs=[pl.BlockSpec(memory_space=pltpu.VMEM)] * len(shapes),
+        out_shape=[jax.ShapeDtypeStruct(shape, jnp.float32) for shape in shapes],
         scratch_shapes=[pltpu.SemaphoreType.DMA((2 * plan.half,))],
         cost_estimate=pl.CostEstimate(
-            flops=0, bytes_accessed=8 * count * math.prod(shape), transcendentals=0
+            flops=0, bytes_accessed=8 * sum(math.prod(shape) for shape in shapes), transcendentals=0
         ),
         name="pick_planes",
     )(ids, by_depth)
+    return (picked[: plan.outer], picked[plan.outer :])
 
 
 def outer_shift(plan, value, j):
@@ -598,6 +606,16 @@
     for source in range(plan.slabs):
         base = source // plan.half * plan.half
         pairs.append((source, base + (source - base + j * plan.inner) % plan.half))
+    return lax.ppermute(value, "slab", pairs)
+
+
+def inner_shift(plan, value, i):
+    if i == 0:
+        return value
+    pairs = []
+    for source in range(plan.slabs):
+        base = source // plan.inner * plan.inner
+        pairs.append((source, base + (source + i) % plan.inner))
     return lax.ppermute(value, "slab", pairs)
 
 
@@ -612,28 +630,20 @@
         sent = jnp.concatenate([sent, rows[:1]], axis=0)
         pairs = [(plan.half, j * plan.inner), (0, plan.half + j * plan.inner)]
         total = total + lax.ppermute(sent, "slab", pairs)
-    return (total, rows[middle : middle + 1])
-
-
-def second_weights(plan, blocks, turned):
+    return total
+
+
+def second_weights(plan, plain, mirror, turned):
     slab = lax.axis_index("slab")
-    part = lax.rem(slab, plan.half) // plan.inner
     strips = []
     for i in range(plan.inner):
         place = lax.rem(slab + i, plan.inner)
-        rows = [lax.dynamic_slice_in_dim(block, place, 1, 0) for pair in blocks for block in pair]
-        strip = jnp.stack(rows).reshape((plan.outer, 2) + blocks[0][0].shape[1:])
-        ids = [lax.broadcasted_iota(jnp.int32, strip.shape, n) for n in range(3)]
-        change = (ids[0] == part) & (ids[1] == 1) & (ids[2] == 0) & (slab % plan.inner == 0)
-        strip = jnp.where(change, lax.dynamic_slice_in_dim(turned, place, 1, 0), strip)
-        if i > 0:
-            pairs = []
-            for source in range(plan.slabs):
-                group = source // plan.inner * plan.inner
-                pairs.append((source, group + (source + i) % plan.inner))
-            strip = lax.ppermute(strip, "slab", pairs)
-        strips.append(strip)
-    return strips
+        rows = [lax.dynamic_slice_in_dim(block, place, 1, 0)[0] for block in plain]
+        last = lax.dynamic_slice_in_dim(turned, place, 1, 0)
+        rows.append(jnp.broadcast_to(last, (8,) + last.shape[1:]))
+        strips.append(inner_shift(plan, jnp.concatenate(rows, axis=0), i))
+    blocks = [outer_shift(plan, jnp.stack([m[j] for m in mirror]), j) for j in range(plan.outer)]
+    return strips + blocks
 
 
 def per_device(charges, counts, projection, near_blocks, neighbours, spectrum):
@@ -675,39 +685,42 @@
     pieces = [project(plan, i, charges, counts, split_projection, *depth_forward) for i in range(CHUNKS)]
     pieces[0], ids = lax.optimization_barrier((pieces[0], ids))
     even_pieces = exchange(pieces[0])
-    picked = pick_planes(plan, ids, spectrum)
-    plain = [outer_shift(plan, picked[2 * j], j) for j in range(plan.outer)]
-    mirror = [outer_shift(plan, picked[2 * j + 1], j) for j in range(plan.outer)]
+    plain, mirror = pick_planes(plan, ids, spectrum)
+    plain = [outer_shift(plan, value, j) for j, value in enumerate(plain)]
+    mirror = [inner_shift(plan, value, i) for i, value in enumerate(mirror)]
     pieces[1], masked, rows = lax.optimization_barrier((pieces[1], masked, rows))
-    turned, own_row = edge_weights(plan, rows)
+    turned = edge_weights(plan, rows)
     left, right = extend_rows(plan, masked)
     pieces[1], left, right, turned, *moved = lax.optimization_barrier(
         (pieces[1], left, right, turned, *plain, *mirror)
     )
     plain, mirror = (moved[: plan.outer], moved[plan.outer :])
     odd_pieces = exchange(pieces[1])
-    strips = second_weights(plan, list(zip(plain, mirror)), turned)
-    edge = jnp.concatenate([turned[plan.inner :], own_row], axis=0)
+    strips = second_weights(plan, plain, mirror, turned)
+    in_vmem = pl.BlockSpec(memory_space=pltpu.VMEM)
+    in_place = pl.BlockSpec(memory_space=pl.ANY)
     (even,) = plane_call(
-        plan, first_plane_kernel, "even_planes", me, [even_pieces], [], [(y_forward, None), (x_forward, 0)], [],
-        [both_shape], values(rows_shape, freq_shape), 2,
+        plan, first_plane_kernel, "even_planes", me, [even_pieces], [],
+        [(y_forward, None), (x_forward, 0)], [], [in_vmem], [both_shape],
+        values(rows_shape, freq_shape), 2,
     )
     even, masked = lax.optimization_barrier((even, masked))
     extended = extend_planes(plan, masked, left, right)
     odd_pieces, extended = lax.optimization_barrier((odd_pieces, extended))
-    late = [*y_forward, x_forward[0][1:], x_forward[1][1:], even]
+    late = [*y_forward, x_forward[0][1:], x_forward[1][1:]]
     late += [x_backward[0][:1], x_backward[1][:1], *y_backward]
     copies = [pltpu.VMEM(array.shape, array.dtype) for array in late]
-    copies.append(pltpu.SemaphoreType.DMA((len(late) + plan.half + 1,)))
+    copies.append(pltpu.SemaphoreType.DMA((len(late) + 2 * plan.half + 1,)))
     back, rest = plane_call(
-        plan, middle_plane_kernel, "middle_planes", me, [odd_pieces], [edge],
-        [], late + strips, [piece_shape(plan), freq_shape],
+        plan, middle_plane_kernel, "middle_planes", me, [odd_pieces, even, turned[plan.inner :]] + strips,
+        [], [], late, [in_vmem, in_place], [piece_shape(plan), freq_shape],
         values(rows_shape, freq_shape, freq_shape, freq_shape, (2, plan.ny // 2, plan.nx)) + copies, 4,
     )
     even_back = exchange(back)
     (back,) = plane_call(
-        plan, last_plane_kernel, "odd_planes", me, [], [rest], [(x_backward, 1), (y_backward, None)], [],
-        [piece_shape(plan)], values(rows_shape), 2,
+        plan, last_plane_kernel, "odd_planes", me, [], [rest],
+        [(x_backward, 1), (y_backward, None)], [], [whole_spec(piece_shape(plan))], [piece_shape(plan)],
+        values(rows_shape), 2,
     )
     total = near_field(plan, extended, neighbours, near_blocks)
     back, total = lax.optimization_barrier((back, total))

time: 164 us -> 176 us (1.073)
  local copies, waits for them, and re-layouts: 3.82 us -> 22.4 us
  Pallas kernels: 68.6 us -> 62.6 us
  waiting for transfers between devices: 48 us -> 45 us
    unnamed x19 -> x57, local copies, waits for them, and re-layouts: 2.06 us -> 16.9 us
    ppermute x1, waiting for transfers between devices: 10.7 us -> 4.28 us  [extend_planes(): before = lax.ppermute(wide[:, -1:], 'slab', up)]
    pallas_call x4, Pallas kernels: 26.7 us -> 22 us  [projection_call(): pl.pallas_call(kernel, in_specs=[pl.BlockSpec(memory_space=pltpu.VMEM)] *...]
    ppermute x3 -> x6, starting transfers between devices: 0.51 us -> 5.01 us  [inner_shift(): return lax.ppermute(value, 'slab', pairs)]
    ppermute x1, waiting for transfers between devices: 0.01 us -> 2.56 us  [extend_rows(): right = lax.ppermute(masked[:, :, :NZC], 'cell', down)]
    slice x0 -> x2, local copies, waits for them, and re-layouts: none -> 1.91 us  [second_weights(): m[j]]
  transfers between devices with their start and end apart: 15 -> 18, of which waited for: 6 -> 8; matrix products, arithmetic and copies ran while one was open for 3% -> 5% of each run, Pallas kernels for 27% -> 22%
where the time goes in v10:
time: 176 us; the launch traced here: 175 us
  Pallas kernels  62.6 us (36%)
  waiting for transfers between devices  45 us (26%)
  starting transfers between devices  39.6 us (22%)
  local copies, waits for them, and re-layouts  22.4 us (13%)
  other arithmetic  4.68 us (3%)
    all_to_all x4, waiting for transfers between devices, exchange(): return lax.all_to_all(pieces, axes, split_axis=0, concat_axis=0, tiled=True)  29.3 us
    pallas_call x4, Pallas kernels, projection_call(): pl.pallas_call(kernel, in_specs=[pl.BlockSpec(memory_space=pltpu.VMEM)] *...  22 us
    pallas_call x3, Pallas kernels, plane_call(): pl.pallas_call(functools.partial(kernel, plan), grid=(1,) if tables else...  22 us
    all_to_all x4, starting transfers between devices, exchange(): return lax.all_to_all(pieces, axes, split_axis=0, concat_axis=0, tiled=True)  19.6 us
    unnamed x57, local copies, waits for them, and re-layouts  16.9 us
    pallas_call x1, Pallas kernels, near_field(): pl.pallas_call(functools.partial(near_kernel, plan), grid=(plan.cell_cols...  15.6 us
    ppermute x2, starting transfers between devices, edge_weights(): total = total + lax.ppermute(sent, 'slab', pairs)  6.55 us
    ppermute x2, waiting for transfers between devices, edge_weights(): total = total + lax.ppermute(sent, 'slab', pairs)  5.98 us
  transfers between devices with their start and end apart: 18, of which 8 were waited for; matrix products, arithmetic and copies ran while one was open for 5% of the time, Pallas kernels for 22%

profile of v10, /device:TPU:0, one launch (start us, length us, event | category | flops | bytes accessed | tf_op | source)
XLA Modules:
  0.0 174.9 jit_solution(5431803499393653109)
XLA Ops:
  0.0 0.7 pad_add_fusion.ids_ref
  0.7 0.9 copy-done
  1.6 1.0 copy-done.4
  2.7 1.0 copy-done.6
  3.7 0.8 copy-done.10
  4.5 6.5 %project_depth.3 = f32[32,2,4,8,128]{4,3,2,1,0:T(8,128)} custom-call(f32[8,8,1024]{2,1,0:T(8,128)S(1)} %copy-done, s32[8,1024]{1,0:T(8,128)S(1)} %copy-done.10, bf16[512,512]{1,0:T(8,128)(2,1)S(1)} %copy-done.6, bf16[512,512]{1,0:T(8,128)(2,1)S(1)} %copy-done.4, f32[8,2,2,16,8,1024]{5,4,3,2,1,0:T(8,128)} %bitcast.39), custom_call_target="tpu_custom_call" | custom-call | flops 4194304 | bytes 8388608 | tf_op jit(solution)/shard_map/project_depth/pallas_call | solution.py:193
  11.0 7.3 %all-to-all-start.1 = ((f32[32,2,4,8,128]{4,3,2,1,0:T(8,128)}), f32[32,2,4,8,128]{4,3,2,1,0:T(8,128)S(1)}, u32[]{:S(2)}, u32[]{:S(2)}) async-start(f32[32,2,4,8,128]{4,3,2,1,0:T(8,128)} %project_depth.3), calls=%async_computation.1 | async-start | bytes 2097152 | tf_op jit(solution)/shard_map/all_to_all | solution.py:673
  18.3 3.0 %pick_planes.1 = (f32[4,32,512]{2,1,0:T(8,128)}, f32[4,32,512]{2,1,0:T(8,128)}, f32[2,32,512]{2,1,0:T(8,128)}, f32[2,32,512]{2,1,0:T(8,128)}, f32[2,32,512]{2,1,0:T(8,128)}, /*index=5*/f32[2,32,512]{2,1,0:T(8,128)}) custom-call(s32[2]{0:T(128)} %pad_add_fusion.ids_ref, f32[64,32,512]{2,1,0:T(8,128)} %bitcast.43), custom_call_target="tpu_custom_call" | custom-call | bytes 2097152 | tf_op jit(solution)/shard_map/pick_planes/pallas_call | solution.py:588
  21.3 0.3 collective-permute-start.5
  21.6 1.7 collective-permute-start.6
  23.3 1.3 collective-permute-start.7
  24.6 1.5 collective-permute-start.4
  26.0 1.3 slice.57
  27.4 6.4 %project_depth.2 = f32[32,2,4,8,128]{4,3,2,1,0:T(8,128)} custom-call(f32[8,8,1024]{2,1,0:T(8,128)S(1)} %copy-done.1, s32[8,1024]{1,0:T(8,128)S(1)} %copy-done.11, bf16[512,512]{1,0:T(8,128)(2,1)S(1)} %copy-done.7, bf16[512,512]{1,0:T(8,128)(2,1)S(1)} %copy-done.5, f32[8,2,2,16,8,1024]{5,4,3,2,1,0:T(8,128)} %bitcast.40), custom_call_target="tpu_custom_call" | custom-call | flops 4194304 | bytes 8388608 | tf_op jit(solution)/shard_map/project_depth/pallas_call | solution.py:193
  33.9 0.1 fusion.6
  33.9 1.5 collective-permute-start.1
  35.4 0.1 rev.4
  35.6 2.6 %collective-permute-done.1 = f32[8,8,16]{2,1,0:T(8,128)S(1)} collective-permute-done((f32[8,8,16]{2,1,0:T(8,128)S(1)}, f32[8,8,16]{2,1,0:T(8,128)S(1)}, u32[]{:S(2)}, u32[]{:S(2)}) %collective-permute-start.1) | collective-permute-done | bytes 4128 | tf_op jit(solution)/shard_map/ppermute | solution.py:545
  38.2 4.5 %collective-permute-start.3 = (f32[5,512]{1,0:T(8,128)S(1)}, f32[5,512]{1,0:T(8,128)S(1)}, u32[]{:S(2)}, u32[]{:S(2)}) collective-permute-start(f32[5,512]{1,0:T(8,128)S(1)} %get-tuple-element.94), channel_id=1, source_target_pairs={{16,8},{0,24},{17,9},{1,25}} | collective-permute-start | bytes 30728 | tf_op jit(solution)/shard_map/ppermute | solution.py:632
  42.7 1.4 collective-permute-done.3
  44.1 2.1 %collective-permute-start.2 = (f32[5,512]{1,0:T(8,128)S(1)}, f32[5,512]{1,0:T(8,128)S(1)}, u32[]{:S(2)}, u32[]{:S(2)}) collective-permute-start(f32[5,512]{1,0:T(8,128)S(1)} %get-tuple-element.95), channel_id=1, source_target_pairs={{16,0},{0,16},{17,1},{1,17}} | collective-permute-start | bytes 30728 | tf_op jit(solution)/shard_map/ppermute | solution.py:632
  46.2 4.6 %collective-permute-done.2 = f32[5,512]{1,0:T(8,128)S(1)} collective-permute-done((f32[5,512]{1,0:T(8,128)S(1)}, f32[5,512]{1,0:T(8,128)S(1)}, u32[]{:S(2)}, u32[]{:S(2)}) %collective-permute-start.2) | collective-permute-done | bytes 10272 | tf_op jit(solution)/shard_map/ppermute | solution.py:632
  50.7 1.1 collective-permute-start
  51.8 2.8 %collective-permute-done = f32[8,8,16]{2,1,0:T(8,128)S(1)} collective-permute-done((f32[8,8,16]{2,1,0:T(8,128)S(1)}, f32[8,8,16]{2,1,0:T(8,128)S(1)}, u32[]{:S(2)}, u32[]{:S(2)}) %collective-permute-start) | collective-permute-done | bytes 4128 | tf_op jit(solution)/shard_map/ppermute | solution.py:544
  54.7 1.0 fusion.7
  55.6 1.0 fusion.9
  56.6 0.7 pad_maximum_fusion.4
  57.3 3.4 %all-to-all-start = ((f32[32,2,4,8,128]{4,3,2,1,0:T(8,128)}), f32[32,2,4,8,128]{4,3,2,1,0:T(8,128)}, u32[]{:S(2)}, u32[]{:S(2)}) async-start(f32[32,2,4,8,128]{4,3,2,1,0:T(8,128)} %project_depth.2), calls=%async_computation | async-start | bytes 2097152 | tf_op jit(solution)/shard_map/all_to_all | solution.py:673
  60.7 1.0 dynamic-slice_bitcast_fusion
  61.8 0.7 pad_maximum_fusion.6
  62.5 0.7 pad_maximum_fusion.7
  63.1 1.7 collective-permute-start.11
  64.8 0.7 pad_maximum_fusion.8
  65.5 1.0 copy-done.16
  66.6 1.0 copy-done.18
  67.6 1.0 copy-done.20
  68.7 1.0 copy-done.21
  69.7 4.1 %even_planes.1.even = f32[1024,512]{1,0:T(8,128)} custom-call(s32[1]{0:T(128)} %bitcast.me_ref, f32[32,2,4,8,128]{4,3,2,1,0:T(8,128)S(1)} %all-to-all-done.1.pieces, bf16[512,512]{1,0:T(8,128)(2,1)S(1)} %copy-done.18, bf16[512,512]{1,0:T(8,128)(2,1)S(1)} %copy-done.16, bf16[2,256,512]{2,1,0:T(8,128)(2,1)S(1)} %copy-done.21, bf16[2,256,512]{2,1,0:T(8,128)(2,1)S(1)} %copy-done.20), custom_call_target="tpu_custom_call" | custom-call | flops 1610612736 | bytes 3145728 | tf_op jit(solution)/shard_map/even_planes/pallas_call | solution.py:409
  73.8 1.0 concatenate.34
  74.8 0.1 fusion.5
  74.9 0.2 collective-permute-start.8
  75.2 4.2 %collective-permute-start.9 = (f32[8,1,1280]{2,1,0:T(1,128)S(1)}, f32[8,1,1280]{2,1,0:T(1,128)S(1)}, u32[]{:S(2)}, u32[]{:S(2)}) collective-permute-start(f32[8,1,1280]{2,1,0:T(1,128)S(1)} %get-tuple-element.66), channel_id=1, source_target_pairs={{2,0},{4,2},{6,4},{8,6},{10,8},{12,10},{14,12},{16,14},{18,16},{20... | collective-permute-start | bytes 122888 | tf_op jit(solution)/shard_map/ppermute | solution.py:554
  79.4 4.3 %collective-permute-done.8 = f32[8,1,1280]{2,1,0:T(1,128)S(1)} collective-permute-done((f32[8,1,1280]{2,1,0:T(1,128)S(1)}, f32[8,1,1280]{2,1,0:T(1,128)S(1)}, u32[]{:S(2)}, u32[]{:S(2)}) %collective-permute-start.8) | collective-permute-done | bytes 40992 | tf_op jit(solution)/shard_map/ppermute | solution.py:553
  83.7 0.1 fusion.1
  83.8 1.0 pad_maximum_fusion.extended
  84.9 3.0 %all-to-all-done.pieces = f32[32,2,4,8,128]{4,3,2,1,0:T(8,128)} async-done(((f32[32,2,4,8,128]{4,3,2,1,0:T(8,128)}), f32[32,2,4,8,128]{4,3,2,1,0:T(8,128)}, u32[]{:S(2)}, u32[]{:S(2)}) %all-to-all-start) | async-done | bytes 1048608 | tf_op jit(solution)/shard_map/all_to_all | solution.py:673
  87.9 1.0 copy-done.17
  89.0 1.0 copy-done.19
  90.0 0.9 copy-done.22
  91.0 0.9 copy-done.23
  91.9 0.9 copy-done.24
  92.9 0.9 copy-done.25
  93.8 12.6 %middle_planes.1 = (f32[32,2,4,8,128]{4,3,2,1,0:T(8,128)}, f32[1024,256]{1,0:T(8,128)}) custom-call(s32[1]{0:T(128)} %bitcast.me_ref, f32[32,2,4,8,128]{4,3,2,1,0:T(8,128)} %all-to-all-done.pieces, f32[1024,512]{1,0:T(8,128)} %even_planes.1.even, f32[1,512]{1,0:T(1,128)S(1)} %get-tuple-element.93.edge, f32[72,512]{1,0:T(8,128)S(1)} %pad_maximum_fusion.5.refs_0_, ...), custom_call_target="tpu_custom_call" | custom-call | flops 3221225472 | bytes 10553344 | tf_op jit(solution)/shard_map/middle_planes/pallas_call | solution.py:409
  106.5 6.2 %all-to-all-start.3 = ((f32[32,2,4,8,128]{4,3,2,1,0:T(8,128)}), f32[32,2,4,8,128]{4,3,2,1,0:T(8,128)S(1)}, u32[]{:S(2)}, u32[]{:S(2)}) async-start(f32[32,2,4,8,128]{4,3,2,1,0:T(8,128)} %get-tuple-element.61), calls=%async_computation.3 | async-start | bytes 2097152 | tf_op jit(solution)/shard_map/all_to_all | solution.py:673
  112.7 15.6 %near_blocks.1.before_in = f32[8,8,1024]{2,1,0:T(8,128)} custom-call(f32[8,3,8,1280]{3,2,1,0:T(8,128)} %pad_maximum_fusion.extended, s32[6,8,1024]{2,1,0:T(8,128)} %codes.1, f32[6,8,8,8,1024]{4,3,2,1,0:T(8,128)} %blocks_ref.1), custom_call_target="tpu_custom_call" | custom-call | flops 6291456 | bytes 12582912 | tf_op jit(solution)/shard_map/near_blocks/pallas_call | solution.py:516
  128.3 1.0 copy-done.15
  129.4 5.2 %odd_planes.1 = f32[32,2,4,8,128]{4,3,2,1,0:T(8,128)S(1)} custom-call(s32[1]{0:T(128)} %bitcast.me_ref, f32[1024,256]{1,0:T(8,128)} %get-tuple-element.58.freqs, bf16[2,256,512]{2,1,0:T(8,128)(2,1)S(1)} %copy-done.15, bf16[2,256,512]{2,1,0:T(8,128)(2,1)S(1)} %copy-done.14, bf16[512,512]{1,0:T(8,128)(2,1)S(1)} %copy-done.13, bf16[512,512]{1,0:T(8,128)(2,1)S(1)} %copy-done.12), custom_call_target="tpu_custom_call" | custom-call | flops 1610612736 | bytes 3145728 | tf_op jit(solution)/shard_map/odd_planes/pallas_call | solution.py:409
  134.6 1.0 copy-done.9
  135.6 4.3 %all-to-all-done.3.pieces = f32[32,2,4,8,128]{4,3,2,1,0:T(8,128)S(1)} async-done(((f32[32,2,4,8,128]{4,3,2,1,0:T(8,128)}), f32[32,2,4,8,128]{4,3,2,1,0:T(8,128)S(1)}, u32[]{:S(2)}, u32[]{:S(2)}) %all-to-all-start.3) | async-done | bytes 1048608 | tf_op jit(solution)/shard_map/all_to_all | solution.py:673
  139.9 2.6 %all-to-all-start.2 = ((f32[32,2,4,8,128]{4,3,2,1,0:T(8,128)}), f32[32,2,4,8,128]{4,3,2,1,0:T(8,128)S(1)}, u32[]{:S(2)}, u32[]{:S(2)}) async-start(f32[32,2,4,8,128]{4,3,2,1,0:T(8,128)} %copy-done.9), calls=%async_computation.2 | async-start | bytes 2097152 | tf_op jit(solution)/shard_map/all_to_all | solution.py:673
  142.6 0.9 copy-done.8
  143.5 4.2 %depth_gather.2.before_in = f32[8,8,1024]{2,1,0:T(8,128)S(1)} custom-call(f32[32,2,4,8,128]{4,3,2,1,0:T(8,128)S(1)} %all-to-all-done.3.pieces, bf16[512,512]{1,0:T(8,128)(2,1)S(1)} %copy-done.3, bf16[512,512]{1,0:T(8,128)(2,1)S(1)} %copy-done.2, f32[8,8,1024]{2,1,0:T(8,128)S(1)} %copy-done.8, s32[8,1024]{1,0:T(8,128)S(1)} %copy-done.11, ...), custom_call_target="tpu_custom_call" | custom-call | flops 4194304 | bytes 8388608 | tf_op jit(solution)/shard_map/depth_gather/pallas_call | solution.py:193
  147.8 22.0 %all-to-all-done.2.pieces = f32[32,2,4,8,128]{4,3,2,1,0:T(8,128)S(1)} async-done(((f32[32,2,4,8,128]{4,3,2,1,0:T(8,128)}), f32[32,2,4,8,128]{4,3,2,1,0:T(8,128)S(1)}, u32[]{:S(2)}, u32[]{:S(2)}) %all-to-all-start.2) | async-done | bytes 1048608 | tf_op jit(solution)/shard_map/all_to_all | solution.py:673
  169.8 4.9 %depth_gather.3 = f32[8,8,1024]{2,1,0:T(8,128)} custom-call(f32[32,2,4,8,128]{4,3,2,1,0:T(8,128)S(1)} %all-to-all-done.2.pieces, bf16[512,512]{1,0:T(8,128)(2,1)S(1)} %copy-done.3, bf16[512,512]{1,0:T(8,128)(2,1)S(1)} %copy-done.2, f32[8,8,1024]{2,1,0:T(8,128)S(1)} %depth_gather.2.before_in, s32[8,1024]{1,0:T(8,128)S(1)} %copy-done.11, ...), custom_call_target="tpu_custom_call" | custom-call | flops 4194304 | bytes 8388608 | tf_op jit(solution)/shard_map/depth_gather/pallas_call | solution.py:193
  (66 shorter events, 0.3 us)
Async XLA Ops:
  0.7 0.9 copy-start
  1.6 1.0 copy-start.4
  2.7 1.0 copy-start.6
  3.7 0.8 copy-start.10
  4.5 22.9 %copy-start.1 = (f32[8,8,1024]{2,1,0:T(8,128)S(1)}, f32[8,8,1024]{2,1,0:T(8,128)}, u32[]{:S(2)}) copy-start(f32[8,8,1024]{2,1,0:T(8,128)} %charges_in.3) | copy-start | bytes 786436
  4.5 22.9 %copy-start.5 = (bf16[512,512]{1,0:T(8,128)(2,1)S(1)}, bf16[512,512]{1,0:T(8,128)(2,1)}, u32[]{:S(2)}) copy-start(bf16[512,512]{1,0:T(8,128)(2,1)} %constant.84.clone.low_in) | copy-start | bytes 1572868
  4.5 22.9 %copy-start.7 = (bf16[512,512]{1,0:T(8,128)(2,1)S(1)}, bf16[512,512]{1,0:T(8,128)(2,1)}, u32[]{:S(2)}) copy-start(bf16[512,512]{1,0:T(8,128)(2,1)} %constant.83.clone.high_in) | copy-start | bytes 1572868
  4.5 22.9 %copy-start.11 = (s32[8,1024]{1,0:T(8,128)S(1)}, s32[8,1024]{1,0:T(8,128)}, u32[]{:S(2)}) copy-start(s32[8,1024]{1,0:T(8,128)} %counts_in.7) | copy-start | bytes 98308
  11.0 46.4 %all-to-all-start.1 = ((f32[32,2,4,8,128]{4,3,2,1,0:T(8,128)}), f32[32,2,4,8,128]{4,3,2,1,0:T(8,128)S(1)}, u32[]{:S(2)}, u32[]{:S(2)}) async-start(f32[32,2,4,8,128]{4,3,2,1,0:T(8,128)} %project_depth.3), calls=%async_computation.1 | async-start | bytes 2097152 | tf_op jit(solution)/shard_map/all_to_all | solution.py:673
  21.3 33.3 %collective-permute-start.5 = (f32[2,32,512]{2,1,0:T(8,128)}, f32[2,32,512]{2,1,0:T(8,128)}, u32[]{:S(2)}, u32[]{:S(2)}) collective-permute-start(f32[2,32,512]{2,1,0:T(8,128)} %get-tuple-element.41), channel_id=1, source_target_pairs={{0,2},{2,4},{4,6},{6,0},{8,10},{10,12},{12,14},{14,8},{16,18},{18,... | collective-permute-start | bytes 393224 | tf_op jit(solution)/shard_map/ppermute | solution.py:619
  21.6 33.0 %collective-permute-start.6 = (f32[2,32,512]{2,1,0:T(8,128)}, f32[2,32,512]{2,1,0:T(8,128)}, u32[]{:S(2)}, u32[]{:S(2)}) collective-permute-start(f32[2,32,512]{2,1,0:T(8,128)} %get-tuple-element.42), channel_id=1, source_target_pairs={{0,4},{2,6},{4,0},{6,2},{8,12},{10,14},{12,8},{14,10},{16,20},{18,... | collective-permute-start | bytes 393224 | tf_op jit(solution)/shard_map/ppermute | solution.py:619
  23.3 31.4 %collective-permute-start.7 = (f32[2,32,512]{2,1,0:T(8,128)}, f32[2,32,512]{2,1,0:T(8,128)}, u32[]{:S(2)}, u32[]{:S(2)}) collective-permute-start(f32[2,32,512]{2,1,0:T(8,128)} %get-tuple-element.43), channel_id=1, source_target_pairs={{0,6},{2,0},{4,2},{6,4},{8,14},{10,8},{12,10},{14,12},{16,22},{18,... | collective-permute-start | bytes 393224 | tf_op jit(solution)/shard_map/ppermute | solution.py:619
  24.6 30.1 %collective-permute-start.4 = (f32[4,32,512]{2,1,0:T(8,128)}, f32[4,32,512]{2,1,0:T(8,128)}, u32[]{:S(2)}, u32[]{:S(2)}) collective-permute-start(f32[4,32,512]{2,1,0:T(8,128)} %get-tuple-element.39), channel_id=1, source_target_pairs={{0,8},{2,10},{4,12},{6,14},{8,0},{10,2},{12,4},{14,6},{16,24},{18,... | collective-permute-start | bytes 786440 | tf_op jit(solution)/shard_map/ppermute | solution.py:609
  27.4 33.3 %copy-start.27 = (f32[4,32,512]{2,1,0:T(8,128)S(1)}, f32[4,32,512]{2,1,0:T(8,128)}, u32[]{:S(2)}) copy-start(f32[4,32,512]{2,1,0:T(8,128)} %get-tuple-element.52) | copy-start | bytes 786436
  33.8 54.1 %copy-start.13 = (bf16[512,512]{1,0:T(8,128)(2,1)S(1)}, bf16[512,512]{1,0:T(8,128)(2,1)}, u32[]{:S(2)}) copy-start(bf16[512,512]{1,0:T(8,128)(2,1)} %constant.93.clone.refs_12_.y_high) | copy-start | bytes 1572868
  33.9 22.7 %copy-start.26 = (f32[8,8,1024]{2,1,0:T(8,128)}, f32[8,8,1024]{2,1,0:T(8,128)S(1)}, u32[]{:S(2)}) copy-start(f32[8,8,1024]{2,1,0:T(8,128)S(1)} %fusion.2) | copy-start | bytes 786436
  33.9 4.2 %collective-permute-start.1 = (f32[8,8,16]{2,1,0:T(8,128)S(1)}, f32[8,8,16]{2,1,0:T(8,128)S(1)}, u32[]{:S(2)}, u32[]{:S(2)}) collective-permute-start(f32[8,8,16]{2,1,0:T(8,128)S(1)} %get-tuple-element.75), channel_id=1, source_target_pairs={{1,0},{0,1},{3,2},{2,3},{5,4},{4,5},{7,6},{6,7},{9,8},{8,9},{11,10... | collective-permute-start | bytes 12296 | tf_op jit(solution)/shard_map/ppermute | solution.py:545
  38.2 5.9 %collective-permute-start.3 = (f32[5,512]{1,0:T(8,128)S(1)}, f32[5,512]{1,0:T(8,128)S(1)}, u32[]{:S(2)}, u32[]{:S(2)}) collective-permute-start(f32[5,512]{1,0:T(8,128)S(1)} %get-tuple-element.94), channel_id=1, source_target_pairs={{16,8},{0,24},{17,9},{1,25}} | collective-permute-start | bytes 30728 | tf_op jit(solution)/shard_map/ppermute | solution.py:632
  44.1 6.6 %collective-permute-start.2 = (f32[5,512]{1,0:T(8,128)S(1)}, f32[5,512]{1,0:T(8,128)S(1)}, u32[]{:S(2)}, u32[]{:S(2)}) collective-permute-start(f32[5,512]{1,0:T(8,128)S(1)} %get-tuple-element.95), channel_id=1, source_target_pairs={{16,0},{0,16},{17,1},{1,17}} | collective-permute-start | bytes 30728 | tf_op jit(solution)/shard_map/ppermute | solution.py:632
  50.7 3.9 %collective-permute-start = (f32[8,8,16]{2,1,0:T(8,128)S(1)}, f32[8,8,16]{2,1,0:T(8,128)S(1)}, u32[]{:S(2)}, u32[]{:S(2)}) collective-permute-start(f32[8,8,16]{2,1,0:T(8,128)S(1)} %get-tuple-element.76), channel_id=1, source_target_pairs={{0,1},{1,0},{2,3},{3,2},{4,5},{5,4},{6,7},{7,6},{8,9},{9,8},{10,11... | collective-permute-start | bytes 12296 | tf_op jit(solution)/shard_map/ppermute | solution.py:544
  57.3 30.6 %collective-permute-start.13 = (f32[4,32,512]{2,1,0:T(8,128)}, f32[4,32,512]{2,1,0:T(8,128)S(1)}, u32[]{:S(2)}, u32[]{:S(2)}) collective-permute-start(f32[4,32,512]{2,1,0:T(8,128)} %pad_maximum_fusion.4), channel_id=1, source_target_pairs={{0,8},{2,10},{4,12},{6,14},{8,0},{10,2},{12,4},{14,6},{16,24},{18,... | collective-permute-start | bytes 786440 | tf_op jit(solution)/shard_map/ppermute | solution.py:609
  57.3 30.6 %all-to-all-start = ((f32[32,2,4,8,128]{4,3,2,1,0:T(8,128)}), f32[32,2,4,8,128]{4,3,2,1,0:T(8,128)}, u32[]{:S(2)}, u32[]{:S(2)}) async-start(f32[32,2,4,8,128]{4,3,2,1,0:T(8,128)} %project_depth.2), calls=%async_computation | async-start | bytes 2097152 | tf_op jit(solution)/shard_map/all_to_all | solution.py:673
  62.4 25.5 %collective-permute-start.10 = (f32[72,512]{1,0:T(8,128)}, f32[72,512]{1,0:T(8,128)S(1)}, u32[]{:S(2)}, u32[]{:S(2)}) collective-permute-start(f32[72,512]{1,0:T(8,128)} %pad_maximum_fusion.6), channel_id=1, source_target_pairs={{0,2},{2,4},{4,6},{6,0},{8,10},{10,12},{12,14},{14,8},{16,18},{18,... | collective-permute-start | bytes 442376 | tf_op jit(solution)/shard_map/ppermute | solution.py:619
  63.1 24.7 %collective-permute-start.11 = (f32[72,512]{1,0:T(8,128)}, f32[72,512]{1,0:T(8,128)S(1)}, u32[]{:S(2)}, u32[]{:S(2)}) collective-permute-start(f32[72,512]{1,0:T(8,128)} %pad_maximum_fusion.7), channel_id=1, source_target_pairs={{0,4},{2,6},{4,0},{6,2},{8,12},{10,14},{12,8},{14,10},{16,20},{18,... | collective-permute-start | bytes 442376 | tf_op jit(solution)/shard_map/ppermute | solution.py:619
  65.5 1.0 copy-start.16
  66.6 1.0 copy-start.18
  67.6 1.0 copy-start.20
  68.7 1.0 copy-start.21
  74.9 8.8 %collective-permute-start.8 = (f32[8,1,1280]{2,1,0:T(1,128)S(1)}, f32[8,1,1280]{2,1,0:T(1,128)S(1)}, u32[]{:S(2)}, u32[]{:S(2)}) collective-permute-start(f32[8,1,1280]{2,1,0:T(1,128)S(1)} %get-tuple-element.65), channel_id=1, source_target_pairs={{0,2},{2,4},{4,6},{6,8},{8,10},{10,12},{12,14},{14,16},{16,18},{18... | collective-permute-start | bytes 122888 | tf_op jit(solution)/shard_map/ppermute | solution.py:553
  75.2 8.6 %collective-permute-start.9 = (f32[8,1,1280]{2,1,0:T(1,128)S(1)}, f32[8,1,1280]{2,1,0:T(1,128)S(1)}, u32[]{:S(2)}, u32[]{:S(2)}) collective-permute-start(f32[8,1,1280]{2,1,0:T(1,128)S(1)} %get-tuple-element.66), channel_id=1, source_target_pairs={{2,0},{4,2},{6,4},{8,6},{10,8},{12,10},{14,12},{16,14},{18,16},{20... | collective-permute-start | bytes 122888 | tf_op jit(solution)/shard_map/ppermute | solution.py:554
  83.7 4.2 %collective-permute-start.12 = (f32[72,512]{1,0:T(8,128)}, f32[72,512]{1,0:T(8,128)S(1)}, u32[]{:S(2)}, u32[]{:S(2)}) collective-permute-start(f32[72,512]{1,0:T(8,128)} %pad_maximum_fusion.8), channel_id=1, source_target_pairs={{0,6},{2,0},{4,2},{6,4},{8,14},{10,8},{12,10},{14,12},{16,22},{18,... | collective-permute-start | bytes 442376 | tf_op jit(solution)/shard_map/ppermute | solution.py:619
  87.9 1.0 copy-start.17
  89.0 1.0 copy-start.19
  90.0 0.9 copy-start.22
  91.0 0.9 copy-start.23
  91.9 0.9 copy-start.24
  92.9 0.9 copy-start.25
  93.8 34.5 %copy-start.12 = (bf16[512,512]{1,0:T(8,128)(2,1)S(1)}, bf16[512,512]{1,0:T(8,128)(2,1)}, u32[]{:S(2)}) copy-start(bf16[512,512]{1,0:T(8,128)(2,1)} %constant.94.clone.refs_13_.y_low) | copy-start | bytes 1572868
  106.4 36.1 %copy-start.2 = (bf16[512,512]{1,0:T(8,128)(2,1)S(1)}, bf16[512,512]{1,0:T(8,128)(2,1)}, u32[]{:S(2)}) copy-start(bf16[512,512]{1,0:T(8,128)(2,1)} %constant.98.clone.low_in) | copy-start | bytes 1572868
  106.5 36.1 %copy-start.3 = (bf16[512,512]{1,0:T(8,128)(2,1)S(1)}, bf16[512,512]{1,0:T(8,128)(2,1)}, u32[]{:S(2)}) copy-start(bf16[512,512]{1,0:T(8,128)(2,1)} %constant.97.clone.high_in) | copy-start | bytes 1572868
  106.5 33.4 %all-to-all-start.3 = ((f32[32,2,4,8,128]{4,3,2,1,0:T(8,128)}), f32[32,2,4,8,128]{4,3,2,1,0:T(8,128)S(1)}, u32[]{:S(2)}, u32[]{:S(2)}) async-start(f32[32,2,4,8,128]{4,3,2,1,0:T(8,128)} %get-tuple-element.61), calls=%async_computation.3 | async-start | bytes 2097152 | tf_op jit(solution)/shard_map/all_to_all | solution.py:673
  112.7 15.6 %copy-start.14 = (bf16[2,256,512]{2,1,0:T(8,128)(2,1)S(1)}, bf16[2,256,512]{2,1,0:T(8,128)(2,1)}, u32[]{:S(2)}) copy-start(bf16[2,256,512]{2,1,0:T(8,128)(2,1)} %constant.96.clone.x_low) | copy-start | bytes 1572868
  128.3 1.0 copy-start.15
  134.6 1.0 copy-start.9
  139.9 29.8 %all-to-all-start.2 = ((f32[32,2,4,8,128]{4,3,2,1,0:T(8,128)}), f32[32,2,4,8,128]{4,3,2,1,0:T(8,128)S(1)}, u32[]{:S(2)}, u32[]{:S(2)}) async-start(f32[32,2,4,8,128]{4,3,2,1,0:T(8,128)} %copy-done.9), calls=%async_computation.2 | async-start | bytes 2097152 | tf_op jit(solution)/shard_map/all_to_all | solution.py:673
  142.6 1.0 copy-start.8

commit v11 on v10

--- a/solution.py
+++ b/solution.py
@@ -16,8 +16,7 @@
 NZC = 16
 LANES = 128
 CHUNKS = 2
-VMEM_LIMIT = 60 * 1024 * 1024
-PLANE_LIMIT = 50 * 1024 * 1024
+VMEM_LIMIT = 62 * 1024 * 1024
 
 
 def halves(table):
@@ -45,6 +44,7 @@
         self.steps = cell_cols // (LANES * self.step_blocks) if self.step_blocks else 0
         self.x_chunk = nx // CHUNKS
         self.ky_local = ny // slabs
+        self.piece_rows = 2 * self.steps * self.row_block
         self.half = slabs // 2
         self.outer = math.gcd(self.half, 2)
         self.inner = self.half // self.outer
@@ -58,6 +58,7 @@
             and self.ky_local % 8 == 0
             and self.steps * self.step_blocks * LANES == self.cell_cols
             and self.x_chunk % LANES == 0
+            and self.nx == self.ny == 4 * LANES
             and self.ny % 1024 == self.nx % 1024 == 512
         )
 
@@ -138,12 +139,19 @@
     ]
 
 
-def project_kernel(plan, chunk, charges_in, counts_in, high_in, low_in, projection, out, scratch, held, sems,
-                   charges, counts, high, low):
+def project_kernel(plan, chunk, *refs):
+    edges = chunk == CHUNKS - 1
+    count_in = 5 if edges else 4
+    arrays_in, projection, out = (refs[:count_in], refs[count_in], refs[count_in + 1])
+    scratch, held, sems = refs[count_in + 2 : count_in + 5]
+    arrays = refs[count_in + 5 :]
+    charges, counts, high, low = arrays[:4]
     planes = plan.cell_planes
     first = plan.tx_chunk
-    pairs = ((charges_in, charges), (counts_in, counts), (high_in, high), (low_in, low))
-    loads = [pltpu.make_async_copy(*pair, sems.at[first + n]) for n, pair in enumerate(pairs)]
+    loads = [
+        pltpu.make_async_copy(source, place, sems.at[first + n])
+        for n, (source, place) in enumerate(zip(arrays_in, arrays))
+    ]
     copies = tile_copies(plan, chunk, projection, held, sems)
     for copy in loads[:2] + copies + loads[2:]:
         copy.start()
@@ -173,7 +181,12 @@
     spectra = product(split(scratch[...]), (high[...], low[...])).T
     shape = (plan.slots, 2, plan.row_block, LANES)
     for step in range(plan.steps):
-        out[:, :, step] = spectra[:, step * LANES : (step + 1) * LANES].reshape(shape)
+        value = spectra[:, step * LANES : (step + 1) * LANES].reshape(shape)
+        for part in range(2):
+            row = (part * plan.steps + step) * plan.row_block
+            out[:, row : row + plan.row_block] = value[:, part]
+    if edges:
+        out[:, plan.piece_rows :] = arrays[4][...]
 
 
 def held_shape(plan):
@@ -189,11 +202,10 @@
     return pl.BlockSpec(shape, lambda i: (0,) * len(shape))
 
 
-def projection_call(plan, kernel, name, ready, arrays, projection, out_shape):
+def projection_call(plan, kernel, name, arrays, projection, out_shape):
     return pl.pallas_call(
         kernel,
-        in_specs=[pl.BlockSpec(memory_space=pltpu.VMEM)] * len(ready)
-        + [pl.BlockSpec(memory_space=pl.ANY)] * (len(arrays) + 1),
+        in_specs=[pl.BlockSpec(memory_space=pl.ANY)] * (len(arrays) + 1),
         out_specs=pl.BlockSpec(memory_space=pltpu.VMEM),
         out_shape=jax.ShapeDtypeStruct(out_shape, jnp.float32),
         scratch_shapes=[
@@ -202,20 +214,21 @@
             pltpu.SemaphoreType.DMA((plan.tx_chunk + len(arrays),)),
         ]
         + [pltpu.VMEM(array.shape, array.dtype) for array in arrays],
-        compiler_params=pltpu.CompilerParams(vmem_limit_bytes=PLANE_LIMIT),
+        compiler_params=pltpu.CompilerParams(vmem_limit_bytes=VMEM_LIMIT),
         cost_estimate=pl.CostEstimate(
             flops=2 * math.prod(held_shape(plan)),
             bytes_accessed=4 * math.prod(held_shape(plan)),
             transcendentals=0,
         ),
         name=name,
-    )(*ready, *arrays, projection)
-
-
-def project(plan, chunk, charges, counts, projection, high, low):
+    )(*arrays, projection)
+
+
+def project(plan, chunk, charges, counts, projection, high, low, edges):
     kernel = functools.partial(project_kernel, plan, chunk)
-    arrays = [charges, counts, high, low]
-    return projection_call(plan, kernel, "project_depth", [], arrays, projection, piece_shape(plan))
+    arrays = [charges, counts, high, low] + ([] if edges is None else [edges])
+    rows = plan.piece_rows + (0 if edges is None else edges.shape[1])
+    return projection_call(plan, kernel, "project_depth", arrays, projection, (plan.slots, rows, LANES))
 
 
 def far_sign(plan, me_ref):
@@ -232,7 +245,7 @@
     for cell in range(plan.cells):
         for group in range(plan.slabs // plan.y_lanes):
             first = cell * plan.slabs + group * plan.y_lanes
-            parts = [pieces[first + i].reshape(rows, LANES) for i in range(plan.y_lanes)]
+            parts = [pieces[first + i, :rows] for i in range(plan.y_lanes)]
             parts = swap_groups(parts, plan.width)
             for place, value in enumerate(parts):
                 if place % 2 == 1:
@@ -321,41 +334,43 @@
     out[...] = forward_plane(plan, me_ref, pieces, (y_high, y_low), (x_high, x_low), rows_ref, freq_ref)
 
 
-def middle_plane_kernel(plan, me_ref, pieces, even, edge, *refs):
+def middle_plane_kernel(plan, me_ref, *refs):
+    late, refs = (refs[:10], refs[10:])
     strips, refs = (refs[: plan.inner], refs[plan.inner :])
     blocks, refs = (refs[: plan.outer], refs[plan.outer :])
-    late, refs = (refs[:8], refs[8:])
     out, rest, rows_ref, freq_ref, sum_ref, rest_ref, weights = refs[:7]
-    held, sems = (refs[7:15], refs[15])
-    yf_high, yf_low, xf_high, xf_low, xb_high, xb_low, yb_high, yb_low = held
+    held, sems = (refs[7:17], refs[17])
+    pieces, yf_high, yf_low, xf_high, xf_low, even, xb_high, xb_low, yb_high, yb_low = held
     slab = lax.rem(me_ref[0], plan.slabs)
     place = lax.rem(slab, plan.half)
     outer_id, inner_id = (place // plan.inner, lax.rem(place, plan.inner))
     copies = [pltpu.make_async_copy(late[n], held[n], sems.at[n]) for n in range(len(held))]
     count = plan.ky_local
+    placed = []
     for i in range(plan.inner):
         for j in range(plan.outer):
             owner = lax.rem(outer_id - j + plan.outer, plan.outer) * plan.inner
             owner = owner + lax.rem(inner_id - i + plan.inner, plan.inner)
             rows = pl.ds(pl.multiple_of(owner * count, count), count)
-            n = len(copies)
-            source = strips[i].at[pl.ds(j * count, count)]
-            copies.append(pltpu.make_async_copy(source, weights.at[0, rows], sems.at[n]))
-            copies.append(pltpu.make_async_copy(blocks[j].at[i], weights.at[1, rows], sems.at[n + 1]))
-    for copy in copies:
+            for m, source in enumerate((strips[i].at[j], blocks[j].at[i])):
+                sem = sems.at[len(held) + len(placed)]
+                placed.append(pltpu.make_async_copy(source, weights.at[m, rows], sem))
+    for copy in copies[:6] + placed + copies[6:]:
         copy.start()
-    own_edge = strips[0][plan.outer * count : plan.outer * count + 1]
-    for i in range(1, plan.inner):
-        row = strips[i][plan.outer * count : plan.outer * count + 1]
-        own_edge = jnp.where(inner_id == i, row, own_edge)
+    copies[0].wait()
+    cell_first = me_ref[0] - slab
+    tile = pieces[cell_first + jnp.where(slab < plan.half, plan.half, 0), plan.piece_rows :]
+    parts = plan.nx // LANES
+    own_edge = jnp.concatenate([tile[n : n + 1] for n in range(parts)], axis=1)
+    edge = jnp.concatenate([tile[n : n + 1] for n in range(parts, 2 * parts)], axis=1)
     special = me_ref[0] == 0
     width = plan.x_chunk
     middle = plan.ny // 2
     x_table = (xf_high.at[pl.ds(0, 1)], xf_low.at[pl.ds(0, 1)])
     odd = forward_plane(
-        plan, me_ref, pieces, (yf_high, yf_low), x_table, rows_ref, freq_ref, copies[:4]
-    )
-    for copy in copies[len(held) :]:
+        plan, me_ref, pieces, (yf_high, yf_low), x_table, rows_ref, freq_ref, copies[1:5]
+    )
+    for copy in copies[5:6] + placed:
         copy.wait()
     row = lax.broadcasted_iota(jnp.int32, (middle, width), 0)
     at_first = row == 0
@@ -383,7 +398,7 @@
             rest_ref[rows] = below - above
     last = pltpu.make_async_copy(rest_ref, rest, sems.at[len(held) + 2 * plan.half])
     last.start()
-    for copy in copies[4 : len(held)]:
+    for copy in copies[6:]:
         copy.wait()
     backward_plane(plan, me_ref, sum_ref[...], (xb_high, xb_low), (yb_high, yb_low), out, rows_ref)
     last.wait()
@@ -413,7 +428,7 @@
         out_specs=out_specs,
         out_shape=[jax.ShapeDtypeStruct(shape, jnp.float32) for shape in out_shapes],
         scratch_shapes=scratch,
-        compiler_params=pltpu.CompilerParams(vmem_limit_bytes=PLANE_LIMIT),
+        compiler_params=pltpu.CompilerParams(vmem_limit_bytes=VMEM_LIMIT),
         cost_estimate=pl.CostEstimate(
             flops=work * 12 * plan.nx * plan.ny * plan.x_chunk,
             bytes_accessed=size + sum(2 * table.size for table in flat),
@@ -424,22 +439,22 @@
 
 
 def gather_kernel(
-    plan, chunk, pieces, high_in, low_in, before_in, counts_in, projection, out, scratch, held, sems,
-    high, low, before, counts
+    plan, chunk, sent, high_in, low_in, before_in, counts_in, projection, out, scratch, held, sems,
+    pieces, high, low, before, counts
 ):
     planes = plan.cell_planes
     rows = plan.slots * 2 * plan.row_block
     first = plan.tx_chunk
     copies = tile_copies(plan, chunk, projection, held, sems)
-    pairs = ((high_in, high), (low_in, low), (before_in, before), (counts_in, counts))
+    pairs = ((sent, pieces), (high_in, high), (low_in, low), (before_in, before), (counts_in, counts))
     loads = [pltpu.make_async_copy(*pair, sems.at[first + n]) for n, pair in enumerate(pairs)]
-    for copy in loads[:2] + copies + loads[2:]:
+    for copy in loads[:3] + copies + loads[3:]:
         copy.start()
-    for copy in loads[:2]:
+    for copy in loads[:3]:
         copy.wait()
     columns = [pieces[:, :, step].reshape(rows, LANES) for step in range(plan.steps)]
     scratch[...] = product(split(jnp.concatenate(columns, axis=1).T), (high[...], low[...]))
-    for copy in loads[2:]:
+    for copy in loads[3:]:
         copy.wait()
     for tx in range(plan.tx_chunk):
         copies[tx].wait()
@@ -465,8 +480,8 @@
 
 def gather(plan, chunk, counts, before, projection, high, low, pieces):
     kernel = functools.partial(gather_kernel, plan, chunk)
-    arrays = [high, low, before, counts]
-    return projection_call(plan, kernel, "depth_gather", [pieces], arrays, projection, before.shape)
+    arrays = [pieces, high, low, before, counts]
+    return projection_call(plan, kernel, "depth_gather", arrays, projection, before.shape)
 
 
 def near_kernel(plan, extended, codes, blocks_ref, out):
@@ -620,27 +635,19 @@
 
 
 def edge_weights(plan, rows):
-    slab, cell = (lax.axis_index("slab"), lax.axis_index("cell"))
     middle = plan.nz // 2
-    turned = jnp.concatenate([rows[middle : middle + 1], jnp.flip(rows, 0)], axis=0)
-    other = cell * plan.slabs + (1 - slab // plan.half) * plan.half
-    total = 0.0
-    for j in range(plan.outer):
-        sent = lax.dynamic_slice_in_dim(turned, other + j * plan.inner, plan.inner, 0)
-        sent = jnp.concatenate([sent, rows[:1]], axis=0)
-        pairs = [(plan.half, j * plan.inner), (0, plan.half + j * plan.inner)]
-        total = total + lax.ppermute(sent, "slab", pairs)
-    return total
-
-
-def second_weights(plan, plain, mirror, turned):
+    turned = jnp.concatenate([rows[middle : middle + 1], jnp.flip(rows, 0)], axis=0)[: plan.slots]
+    shape = (plan.slots, plan.nx // LANES, LANES)
+    plane = jnp.broadcast_to(rows[0].reshape(shape[1:]), shape)
+    return jnp.concatenate([turned.reshape(shape), plane], axis=1)
+
+
+def second_weights(plan, plain, mirror):
     slab = lax.axis_index("slab")
     strips = []
     for i in range(plan.inner):
         place = lax.rem(slab + i, plan.inner)
-        rows = [lax.dynamic_slice_in_dim(block, place, 1, 0)[0] for block in plain]
-        last = lax.dynamic_slice_in_dim(turned, place, 1, 0)
-        rows.append(jnp.broadcast_to(last, (8,) + last.shape[1:]))
+        rows = [lax.dynamic_slice_in_dim(block, place, 1, 0) for block in plain]
         strips.append(inner_shift(plan, jnp.concatenate(rows, axis=0), i))
     blocks = [outer_shift(plan, jnp.stack([m[j] for m in mirror]), j) for j in range(plan.outer)]
     return strips + blocks
@@ -682,38 +689,36 @@
     slot = lax.broadcasted_iota(jnp.int32, charges.shape, 0)
     masked = jnp.where(slot < counts[None], charges, 0.0)
     rows = jnp.transpose(spectrum[:, :, 0], (1, 0))
-    pieces = [project(plan, i, charges, counts, split_projection, *depth_forward) for i in range(CHUNKS)]
-    pieces[0], ids = lax.optimization_barrier((pieces[0], ids))
-    even_pieces = exchange(pieces[0])
+    first = project(plan, 0, charges, counts, split_projection, *depth_forward, None)
+    first, ids = lax.optimization_barrier((first, ids))
+    even_pieces = exchange(first)
+    edges = edge_weights(plan, rows)
+    second = project(plan, 1, charges, counts, split_projection, *depth_forward, edges)
     plain, mirror = pick_planes(plan, ids, spectrum)
     plain = [outer_shift(plan, value, j) for j, value in enumerate(plain)]
     mirror = [inner_shift(plan, value, i) for i, value in enumerate(mirror)]
-    pieces[1], masked, rows = lax.optimization_barrier((pieces[1], masked, rows))
-    turned = edge_weights(plan, rows)
+    second, masked = lax.optimization_barrier((second, masked))
     left, right = extend_rows(plan, masked)
-    pieces[1], left, right, turned, *moved = lax.optimization_barrier(
-        (pieces[1], left, right, turned, *plain, *mirror)
-    )
+    second, left, right, *moved = lax.optimization_barrier((second, left, right, *plain, *mirror))
     plain, mirror = (moved[: plan.outer], moved[plan.outer :])
-    odd_pieces = exchange(pieces[1])
-    strips = second_weights(plan, plain, mirror, turned)
+    odd_pieces = exchange(second)
+    strips = second_weights(plan, plain, mirror)
     in_vmem = pl.BlockSpec(memory_space=pltpu.VMEM)
     in_place = pl.BlockSpec(memory_space=pl.ANY)
     (even,) = plane_call(
-        plan, first_plane_kernel, "even_planes", me, [even_pieces], [],
-        [(y_forward, None), (x_forward, 0)], [], [in_vmem], [both_shape],
+        plan, first_plane_kernel, "even_planes", me, [], [even_pieces],
+        [(y_forward, None), (x_forward, 0)], [], [whole_spec(both_shape)], [both_shape],
         values(rows_shape, freq_shape), 2,
     )
     even, masked = lax.optimization_barrier((even, masked))
     extended = extend_planes(plan, masked, left, right)
     odd_pieces, extended = lax.optimization_barrier((odd_pieces, extended))
-    late = [*y_forward, x_forward[0][1:], x_forward[1][1:]]
+    late = [odd_pieces, *y_forward, x_forward[0][1:], x_forward[1][1:], even]
     late += [x_backward[0][:1], x_backward[1][:1], *y_backward]
     copies = [pltpu.VMEM(array.shape, array.dtype) for array in late]
     copies.append(pltpu.SemaphoreType.DMA((len(late) + 2 * plan.half + 1,)))
     back, rest = plane_call(
-        plan, middle_plane_kernel, "middle_planes", me, [odd_pieces, even, turned[plan.inner :]] + strips,
-        [], [], late, [in_vmem, in_place], [piece_shape(plan), freq_shape],
+        plan, middle_plane_kernel, "middle_planes", me, [], [], [], late + strips, [in_vmem, in_place], [piece_shape(plan), freq_shape],
         values(rows_shape, freq_shape, freq_shape, freq_shape, (2, plan.ny // 2, plan.nx)) + copies, 4,
     )
     even_back = exchange(back)

time: 176 us -> 158 us (0.90)
  local copies, waits for them, and re-layouts: 22.4 us -> 6.1 us
  starting transfers between devices: 39.6 us -> 32.2 us
  Pallas kernels: 62.6 us -> 66.1 us
  waiting for transfers between devices: 45 us -> 47 us
    unnamed x57 -> x23, local copies, waits for them, and re-layouts: 16.9 us -> 1.68 us
    ppermute x1, waiting for transfers between devices: 4.28 us -> 11.5 us  [extend_planes(): before = lax.ppermute(wide[:, -1:], 'slab', up)]
    ppermute x2 -> x0, starting transfers between devices: 6.55 us -> none  [edge_weights(): total = total + lax.ppermute(sent, 'slab', pairs)]
    ppermute x2 -> x0, waiting for transfers between devices: 5.98 us -> none  [edge_weights(): total = total + lax.ppermute(sent, 'slab', pairs)]
    pallas_call x4, Pallas kernels: 22 us -> 25 us  [projection_call(): pl.pallas_call(kernel, in_specs=[pl.BlockSpec(memory_space=pl.ANY)] * (le...]
    all_to_all x4, starting transfers between devices: 19.6 us -> 16.8 us  [exchange(): return lax.all_to_all(pieces, axes, split_axis=0, concat_axis=0, tiled=True)]
    ppermute x2, starting transfers between devices: 1.46 us -> 3.29 us  [outer_shift(): return lax.ppermute(value, 'slab', pairs)]
  transfers between devices with their start and end apart: 18 -> 16, of which waited for: 8 -> 7; matrix products, arithmetic and copies ran while one was open for 5% -> 6% of each run, Pallas kernels for 22% -> 28%
where the time goes in v11:
time: 158 us; the launch traced here: 157 us
  Pallas kernels  66.1 us (42%)
  waiting for transfers between devices  47 us (30%)
  starting transfers between devices  32.2 us (20%)
  local copies, waits for them, and re-layouts  6.1 us (4%)
  other arithmetic  5.18 us (3%)
    all_to_all x4, waiting for transfers between devices, exchange(): return lax.all_to_all(pieces, axes, split_axis=0, concat_axis=0, tiled=True)  28.7 us
    pallas_call x4, Pallas kernels, projection_call(): pl.pallas_call(kernel, in_specs=[pl.BlockSpec(memory_space=pl.ANY)] * (le...  25 us
    pallas_call x3, Pallas kernels, plane_call(): pl.pallas_call(functools.partial(kernel, plan), grid=(1,) if tables else...  22.6 us
    all_to_all x4, starting transfers between devices, exchange(): return lax.all_to_all(pieces, axes, split_axis=0, concat_axis=0, tiled=True)  16.8 us
    pallas_call x1, Pallas kernels, near_field(): pl.pallas_call(functools.partial(near_kernel, plan), grid=(plan.cell_cols...  15.5 us
    ppermute x1, waiting for transfers between devices, extend_planes(): before = lax.ppermute(wide[:, -1:], 'slab', up)  11.5 us
    ppermute x6, starting transfers between devices, inner_shift(): return lax.ppermute(value, 'slab', pairs)  4.82 us
    ppermute x1, starting transfers between devices, extend_planes(): after = lax.ppermute(wide[:, :1], 'slab', down)  4.03 us
  transfers between devices with their start and end apart: 16, of which 7 were waited for; matrix products, arithmetic and copies ran while one was open for 6% of the time, Pallas kernels for 28%

profile of v11, /device:TPU:0, one launch (start us, length us, event | category | flops | bytes accessed | tf_op | source)
XLA Modules:
  0.0 157.1 jit_solution(7276332446189556255)
XLA Ops:
  0.0 0.6 pad_add_fusion.ids_ref
  0.6 6.4 %project_depth.3 = f32[32,64,128]{2,1,0:T(8,128)} custom-call(f32[8,8,1024]{2,1,0:T(8,128)} %refs_0_.3, s32[8,1024]{1,0:T(8,128)} %counts_in.3, bf16[512,512]{1,0:T(8,128)(2,1)} %constant.63.clone.refs_2_, bf16[512,512]{1,0:T(8,128)(2,1)} %constant.64.clone.refs_3_, f32[8,2,2,16,8,1024]{5,4,3,2,1,0:T(8,128)} %bitcast.20), custom_call_target="tpu_custom_call" | custom-call | flops 4194304 | bytes 8388608 | tf_op jit(solution)/shard_map/project_depth/pallas_call | solution.py:206
  7.0 0.0 copy-start.1
  7.0 0.0 copy-start.4
  7.0 7.3 %all-to-all-start.1 = ((f32[32,64,128]{2,1,0:T(8,128)}), f32[32,64,128]{2,1,0:T(8,128)S(1)}, u32[]{:S(2)}, u32[]{:S(2)}) async-start(f32[32,64,128]{2,1,0:T(8,128)} %project_depth.3), calls=%async_computation.1 | async-start | bytes 2097152 | tf_op jit(solution)/shard_map/all_to_all | solution.py:680
  14.3 3.0 %pick_planes.1 = (f32[4,32,512]{2,1,0:T(8,128)}, f32[4,32,512]{2,1,0:T(8,128)}, f32[2,32,512]{2,1,0:T(8,128)}, f32[2,32,512]{2,1,0:T(8,128)}, f32[2,32,512]{2,1,0:T(8,128)}, /*index=5*/f32[2,32,512]{2,1,0:T(8,128)}) custom-call(s32[2]{0:T(128)} %pad_add_fusion.ids_ref, f32[64,32,512]{2,1,0:T(8,128)} %bitcast.24), custom_call_target="tpu_custom_call" | custom-call | bytes 2097152 | tf_op jit(solution)/shard_map/pick_planes/pallas_call | solution.py:603
  17.3 0.3 collective-permute-start.3
  17.7 1.7 %collective-permute-start.4 = (f32[2,32,512]{2,1,0:T(8,128)}, f32[2,32,512]{2,1,0:T(8,128)S(1)}, u32[]{:S(2)}, u32[]{:S(2)}) collective-permute-start(f32[2,32,512]{2,1,0:T(8,128)} %get-tuple-element.39), channel_id=1, source_target_pairs={{0,4},{2,6},{4,0},{6,2},{8,12},{10,14},{12,8},{14,10},{16,20},{18,... | collective-permute-start | bytes 393224 | tf_op jit(solution)/shard_map/ppermute | solution.py:634
  19.3 1.3 collective-permute-start.5
  20.6 1.5 collective-permute-start.2
  22.1 1.3 slice.56
  23.4 0.1 rev.4
  23.7 0.7 pad_maximum_fusion.5.refs_4_
  24.3 6.5 %project_depth.2 = f32[32,72,128]{2,1,0:T(8,128)} custom-call(f32[8,8,1024]{2,1,0:T(8,128)} %refs_0_.3, s32[8,1024]{1,0:T(8,128)} %counts_in.3, bf16[512,512]{1,0:T(8,128)(2,1)} %constant.63.clone.refs_2_, bf16[512,512]{1,0:T(8,128)(2,1)} %constant.64.clone.refs_3_, f32[32,8,128]{2,1,0:T(8,128)} %pad_maximum_fusion.5.refs_4_, f32[8,2,2,16,8,1024]{5,4,3,2,1,0:T(8,128)} %bitcast.21), custom_call_target="tpu_custom_call" | custom-call | flops 4194304 | bytes 8388608 | tf_op jit(solution)/shard_map/project_depth/pallas_call | solution.py:206
  30.9 0.0 copy-start.5
  30.9 0.1 fusion.4
  30.9 1.5 collective-permute-start.1
  32.4 2.6 %collective-permute-done.1 = f32[8,8,16]{2,1,0:T(8,128)S(1)} collective-permute-done((f32[8,8,16]{2,1,0:T(8,128)S(1)}, f32[8,8,16]{2,1,0:T(8,128)S(1)}, u32[]{:S(2)}, u32[]{:S(2)}) %collective-permute-start.1) | collective-permute-done | bytes 4128 | tf_op jit(solution)/shard_map/ppermute | solution.py:560
  35.0 1.4 collective-permute-start
  36.3 2.6 %collective-permute-done = f32[8,8,16]{2,1,0:T(8,128)S(1)} collective-permute-done((f32[8,8,16]{2,1,0:T(8,128)S(1)}, f32[8,8,16]{2,1,0:T(8,128)S(1)}, u32[]{:S(2)}, u32[]{:S(2)}) %collective-permute-start) | collective-permute-done | bytes 4128 | tf_op jit(solution)/shard_map/ppermute | solution.py:559
  39.0 0.0 collective-permute-done.3
  39.0 0.0 collective-permute-done.4
  39.0 0.0 collective-permute-done.5
  39.0 0.0 collective-permute-done.2
  39.0 2.5 %all-to-all-done.1.pieces = f32[32,64,128]{2,1,0:T(8,128)S(1)} async-done(((f32[32,64,128]{2,1,0:T(8,128)}), f32[32,64,128]{2,1,0:T(8,128)S(1)}, u32[]{:S(2)}, u32[]{:S(2)}) %all-to-all-start.1) | async-done | bytes 1048608 | tf_op jit(solution)/shard_map/all_to_all | solution.py:680
  41.5 0.0 copy-done.8
  41.5 1.0 copy-done.3
  42.5 3.0 %all-to-all-start = ((f32[32,72,128]{2,1,0:T(8,128)}), f32[32,72,128]{2,1,0:T(8,128)S(1)}, u32[]{:S(2)}, u32[]{:S(2)}) async-start(f32[32,72,128]{2,1,0:T(8,128)} %project_depth.2), calls=%async_computation | async-start | bytes 2359296 | tf_op jit(solution)/shard_map/all_to_all | solution.py:680
  45.5 0.9 fusion.5
  46.4 0.9 fusion.7
  47.3 0.0 copy-done.6
  47.4 1.8 %collective-permute-start.11 = (f32[4,32,512]{2,1,0:T(8,128)S(1)}, f32[4,32,512]{2,1,0:T(8,128)}, u32[]{:S(2)}, u32[]{:S(2)}) collective-permute-start(f32[4,32,512]{2,1,0:T(8,128)S(1)} %pad_maximum_fusion.4), channel_id=1, source_target_pairs={{0,8},{2,10},{4,12},{6,14},{8,0},{10,2},{12,4},{14,6},{16,24},{18,... | collective-permute-start | bytes 786440 | tf_op jit(solution)/shard_map/ppermute | solution.py:624
  49.2 1.0 constant_dynamic-slice_fusion
  50.2 0.1 collective-permute-start.8
  50.3 0.7 pad_maximum_fusion.8
  50.9 1.5 collective-permute-start.9
  52.4 0.7 pad_maximum_fusion.9
  53.0 0.7 pad_maximum_fusion.3.refs_14_
  53.8 5.8 %even_planes.1.refs_5_ = f32[1024,512]{1,0:T(8,128)} custom-call(s32[1]{0:T(128)} %bitcast.me_ref, f32[32,64,128]{2,1,0:T(8,128)} %copy-done.3, bf16[512,512]{1,0:T(8,128)(2,1)} %constant.65.clone.y_high.refs_1_, bf16[512,512]{1,0:T(8,128)(2,1)} %constant.66.clone.y_low.refs_2_, bf16[2,256,512]{2,1,0:T(8,128)(2,1)} %constant.67.clone.x_high, ...), custom_call_target="tpu_custom_call" | custom-call | flops 1610612736 | bytes 3145728 | tf_op jit(solution)/shard_map/even_planes/pallas_call | solution.py:424
  59.5 0.1 concatenate.30
  59.6 0.1 fusion.3
  59.7 0.5 collective-permute-start.6
  60.1 4.0 %collective-permute-start.7 = (f32[8,1,1280]{2,1,0:T(1,128)S(1)}, f32[8,1,1280]{2,1,0:T(1,128)S(1)}, u32[]{:S(2)}, u32[]{:S(2)}) collective-permute-start(f32[8,1,1280]{2,1,0:T(1,128)S(1)} %get-tuple-element.62), channel_id=1, source_target_pairs={{2,0},{4,2},{6,4},{8,6},{10,8},{12,10},{14,12},{16,14},{18,16},{20... | collective-permute-start | bytes 122888 | tf_op jit(solution)/shard_map/ppermute | solution.py:569
  64.2 0.7 pad_maximum_fusion.6.refs_10_
  64.8 11.5 %collective-permute-done.6 = f32[8,1,1280]{2,1,0:T(1,128)S(1)} collective-permute-done((f32[8,1,1280]{2,1,0:T(1,128)S(1)}, f32[8,1,1280]{2,1,0:T(1,128)S(1)}, u32[]{:S(2)}, u32[]{:S(2)}) %collective-permute-start.6) | collective-permute-done | bytes 40992 | tf_op jit(solution)/shard_map/ppermute | solution.py:568
  76.3 0.0 collective-permute-start.10
  76.3 0.0 collective-permute-done.7
  76.3 0.1 fusion.1
  76.4 1.0 pad_maximum_fusion.extended
  77.5 0.0 all-to-all-done.refs_0_
  77.5 0.0 collective-permute-done.8.refs_11_
  77.5 0.0 collective-permute-done.9.refs_12_
  77.5 1.6 %collective-permute-done.10.refs_13_ = f32[2,32,512]{2,1,0:T(8,128)S(1)} collective-permute-done((f32[2,32,512]{2,1,0:T(8,128)}, f32[2,32,512]{2,1,0:T(8,128)S(1)}, u32[]{:S(2)}, u32[]{:S(2)}) %collective-permute-start.10) | collective-permute-done | bytes 131104 | tf_op jit(solution)/shard_map/ppermute | solution.py:634
  79.1 0.0 collective-permute-done.11.refs_15_
  79.1 0.6 copy-done.10
  79.8 10.2 %middle_planes.1 = (f32[32,2,4,8,128]{4,3,2,1,0:T(8,128)}, f32[1024,256]{1,0:T(8,128)}) custom-call(s32[1]{0:T(128)} %bitcast.me_ref, f32[32,72,128]{2,1,0:T(8,128)} %copy-done.2, bf16[512,512]{1,0:T(8,128)(2,1)} %constant.65.clone.y_high.refs_1_, bf16[512,512]{1,0:T(8,128)(2,1)} %constant.66.clone.y_low.refs_2_, ...), custom_call_target="tpu_custom_call" | custom-call | flops 3221225472 | bytes 10616832 | tf_op jit(solution)/shard_map/middle_planes/pallas_call | solution.py:424
  90.0 3.1 %all-to-all-start.3 = ((f32[32,2,4,8,128]{4,3,2,1,0:T(8,128)}), f32[32,2,4,8,128]{4,3,2,1,0:T(8,128)S(1)}, u32[]{:S(2)}, u32[]{:S(2)}) async-start(f32[32,2,4,8,128]{4,3,2,1,0:T(8,128)} %get-tuple-element.57), calls=%async_computation.3 | async-start | bytes 2097152 | tf_op jit(solution)/shard_map/all_to_all | solution.py:680
  93.2 15.5 %near_blocks.1.before_in = f32[8,8,1024]{2,1,0:T(8,128)} custom-call(f32[8,3,8,1280]{3,2,1,0:T(8,128)} %pad_maximum_fusion.extended, s32[6,8,1024]{2,1,0:T(8,128)} %codes.1, f32[6,8,8,8,1024]{4,3,2,1,0:T(8,128)} %blocks_ref.1), custom_call_target="tpu_custom_call" | custom-call | flops 6291456 | bytes 12582912 | tf_op jit(solution)/shard_map/near_blocks/pallas_call | solution.py:531
  108.7 6.6 %odd_planes.1 = f32[32,2,4,8,128]{4,3,2,1,0:T(8,128)} custom-call(s32[1]{0:T(128)} %bitcast.me_ref, f32[1024,256]{1,0:T(8,128)} %get-tuple-element.54.freqs, bf16[2,256,512]{2,1,0:T(8,128)(2,1)} %constant.75.clone.x_high, bf16[2,256,512]{2,1,0:T(8,128)(2,1)} %constant.76.clone.x_low, bf16[512,512]{1,0:T(8,128)(2,1)} %constant.73.clone.refs_8_.y_high, ...), custom_call_target="tpu_custom_call" | custom-call | flops 1610612736 | bytes 3145728 | tf_op jit(solution)/shard_map/odd_planes/pallas_call | solution.py:424
  115.3 5.0 %all-to-all-done.3.sent = f32[32,2,4,8,128]{4,3,2,1,0:T(8,128)S(1)} async-done(((f32[32,2,4,8,128]{4,3,2,1,0:T(8,128)}), f32[32,2,4,8,128]{4,3,2,1,0:T(8,128)S(1)}, u32[]{:S(2)}, u32[]{:S(2)}) %all-to-all-start.3) | async-done | bytes 1048608 | tf_op jit(solution)/shard_map/all_to_all | solution.py:680
  120.3 3.4 %all-to-all-start.2 = ((f32[32,2,4,8,128]{4,3,2,1,0:T(8,128)}), f32[32,2,4,8,128]{4,3,2,1,0:T(8,128)}, u32[]{:S(2)}, u32[]{:S(2)}) async-start(f32[32,2,4,8,128]{4,3,2,1,0:T(8,128)} %odd_planes.1), calls=%async_computation.2 | async-start | bytes 2097152 | tf_op jit(solution)/shard_map/all_to_all | solution.py:680
  123.7 6.0 %depth_gather.2.before_in = f32[8,8,1024]{2,1,0:T(8,128)} custom-call(f32[32,2,4,8,128]{4,3,2,1,0:T(8,128)} %copy-done, bf16[512,512]{1,0:T(8,128)(2,1)} %constant.77.clone.high_in, bf16[512,512]{1,0:T(8,128)(2,1)} %constant.78.clone.low_in, f32[8,8,1024]{2,1,0:T(8,128)} %near_blocks.1.before_in, s32[8,1024]{1,0:T(8,128)} %counts_in.3, ...), custom_call_target="tpu_custom_call" | custom-call | flops 4194304 | bytes 8388608 | tf_op jit(solution)/shard_map/depth_gather/pallas_call | solution.py:206
  129.8 21.1 %all-to-all-done.2.sent = f32[32,2,4,8,128]{4,3,2,1,0:T(8,128)} async-done(((f32[32,2,4,8,128]{4,3,2,1,0:T(8,128)}), f32[32,2,4,8,128]{4,3,2,1,0:T(8,128)}, u32[]{:S(2)}, u32[]{:S(2)}) %all-to-all-start.2) | async-done | bytes 1048608 | tf_op jit(solution)/shard_map/all_to_all | solution.py:680
  150.9 6.0 %depth_gather.3 = f32[8,8,1024]{2,1,0:T(8,128)} custom-call(f32[32,2,4,8,128]{4,3,2,1,0:T(8,128)} %all-to-all-done.2.sent, bf16[512,512]{1,0:T(8,128)(2,1)} %constant.77.clone.high_in, bf16[512,512]{1,0:T(8,128)(2,1)} %constant.78.clone.low_in, f32[8,8,1024]{2,1,0:T(8,128)} %depth_gather.2.before_in, s32[8,1024]{1,0:T(8,128)} %counts_in.3, ...), custom_call_target="tpu_custom_call" | custom-call | flops 4194304 | bytes 8388608 | tf_op jit(solution)/shard_map/depth_gather/pallas_call | solution.py:206
  (24 shorter events, 0.1 us)
Async XLA Ops:
  7.0 16.6 %copy-start.1 = (f32[8,8,1024]{2,1,0:T(8,128)S(1)}, f32[8,8,1024]{2,1,0:T(8,128)}, u32[]{:S(2)}) copy-start(f32[8,8,1024]{2,1,0:T(8,128)} %refs_0_.3) | copy-start | bytes 786436
  7.0 16.6 %copy-start.4 = (s32[8,1024]{1,0:T(8,128)S(1)}, s32[8,1024]{1,0:T(8,128)}, u32[]{:S(2)}) copy-start(s32[8,1024]{1,0:T(8,128)} %counts_in.3) | copy-start | bytes 98308
  7.0 34.5 %all-to-all-start.1 = ((f32[32,64,128]{2,1,0:T(8,128)}), f32[32,64,128]{2,1,0:T(8,128)S(1)}, u32[]{:S(2)}, u32[]{:S(2)}) async-start(f32[32,64,128]{2,1,0:T(8,128)} %project_depth.3), calls=%async_computation.1 | async-start | bytes 2097152 | tf_op jit(solution)/shard_map/all_to_all | solution.py:680
  17.3 21.6 %collective-permute-start.3 = (f32[2,32,512]{2,1,0:T(8,128)}, f32[2,32,512]{2,1,0:T(8,128)}, u32[]{:S(2)}, u32[]{:S(2)}) collective-permute-start(f32[2,32,512]{2,1,0:T(8,128)} %get-tuple-element.38), channel_id=1, source_target_pairs={{0,2},{2,4},{4,6},{6,0},{8,10},{10,12},{12,14},{14,8},{16,18},{18,... | collective-permute-start | bytes 393224 | tf_op jit(solution)/shard_map/ppermute | solution.py:634
  17.7 21.3 %collective-permute-start.4 = (f32[2,32,512]{2,1,0:T(8,128)}, f32[2,32,512]{2,1,0:T(8,128)S(1)}, u32[]{:S(2)}, u32[]{:S(2)}) collective-permute-start(f32[2,32,512]{2,1,0:T(8,128)} %get-tuple-element.39), channel_id=1, source_target_pairs={{0,4},{2,6},{4,0},{6,2},{8,12},{10,14},{12,8},{14,10},{16,20},{18,... | collective-permute-start | bytes 393224 | tf_op jit(solution)/shard_map/ppermute | solution.py:634
  19.3 19.7 %collective-permute-start.5 = (f32[2,32,512]{2,1,0:T(8,128)}, f32[2,32,512]{2,1,0:T(8,128)}, u32[]{:S(2)}, u32[]{:S(2)}) collective-permute-start(f32[2,32,512]{2,1,0:T(8,128)} %get-tuple-element.40), channel_id=1, source_target_pairs={{0,6},{2,0},{4,2},{6,4},{8,14},{10,8},{12,10},{14,12},{16,22},{18,... | collective-permute-start | bytes 393224 | tf_op jit(solution)/shard_map/ppermute | solution.py:634
  20.6 18.4 %collective-permute-start.2 = (f32[4,32,512]{2,1,0:T(8,128)}, f32[4,32,512]{2,1,0:T(8,128)S(1)}, u32[]{:S(2)}, u32[]{:S(2)}) collective-permute-start(f32[4,32,512]{2,1,0:T(8,128)} %get-tuple-element.36), channel_id=1, source_target_pairs={{0,8},{2,10},{4,12},{6,14},{8,0},{10,2},{12,4},{14,6},{16,24},{18,... | collective-permute-start | bytes 786440 | tf_op jit(solution)/shard_map/ppermute | solution.py:624
  24.3 21.2 %copy-start.7 = (f32[2,32,512]{2,1,0:T(8,128)S(1)}, f32[2,32,512]{2,1,0:T(8,128)}, u32[]{:S(2)}) copy-start(f32[2,32,512]{2,1,0:T(8,128)} %get-tuple-element.50) | copy-start | bytes 393220
  30.9 18.3 %copy-start.5 = (f32[4,32,512]{2,1,0:T(8,128)S(1)}, f32[4,32,512]{2,1,0:T(8,128)}, u32[]{:S(2)}) copy-start(f32[4,32,512]{2,1,0:T(8,128)} %get-tuple-element.48) | copy-start | bytes 786436
  30.9 4.0 %collective-permute-start.1 = (f32[8,8,16]{2,1,0:T(8,128)S(1)}, f32[8,8,16]{2,1,0:T(8,128)S(1)}, u32[]{:S(2)}, u32[]{:S(2)}) collective-permute-start(f32[8,8,16]{2,1,0:T(8,128)S(1)} %get-tuple-element.71), channel_id=1, source_target_pairs={{1,0},{0,1},{3,2},{2,3},{5,4},{4,5},{7,6},{6,7},{9,8},{8,9},{11,10... | collective-permute-start | bytes 12296 | tf_op jit(solution)/shard_map/ppermute | solution.py:560
  35.0 4.0 %collective-permute-start = (f32[8,8,16]{2,1,0:T(8,128)S(1)}, f32[8,8,16]{2,1,0:T(8,128)S(1)}, u32[]{:S(2)}, u32[]{:S(2)}) collective-permute-start(f32[8,8,16]{2,1,0:T(8,128)S(1)} %get-tuple-element.72), channel_id=1, source_target_pairs={{0,1},{1,0},{2,3},{3,2},{4,5},{5,4},{6,7},{7,6},{8,9},{9,8},{10,11... | collective-permute-start | bytes 12296 | tf_op jit(solution)/shard_map/ppermute | solution.py:559
  39.0 2.5 %copy-start.8 = (f32[8,8,16]{2,1,0:T(8,128)}, f32[8,8,16]{2,1,0:T(8,128)S(1)}, u32[]{:S(2)}) copy-start(f32[8,8,16]{2,1,0:T(8,128)S(1)} %collective-permute-done) | copy-start | bytes 12292
  39.0 8.3 %copy-start.6 = (f32[4,32,512]{2,1,0:T(8,128)}, f32[4,32,512]{2,1,0:T(8,128)S(1)}, u32[]{:S(2)}) copy-start(f32[4,32,512]{2,1,0:T(8,128)S(1)} %collective-permute-done.2) | copy-start | bytes 786436
  41.5 1.0 copy-start.3
  42.5 35.0 %all-to-all-start = ((f32[32,72,128]{2,1,0:T(8,128)}), f32[32,72,128]{2,1,0:T(8,128)S(1)}, u32[]{:S(2)}, u32[]{:S(2)}) async-start(f32[32,72,128]{2,1,0:T(8,128)} %project_depth.2), calls=%async_computation | async-start | bytes 2359296 | tf_op jit(solution)/shard_map/all_to_all | solution.py:680
  47.3 12.2 %copy-start.9 = (f32[8,8,16]{2,1,0:T(8,128)S(1)}, f32[8,8,16]{2,1,0:T(8,128)}, u32[]{:S(2)}) copy-start(f32[8,8,16]{2,1,0:T(8,128)} %copy-done.8) | copy-start | bytes 12292
  47.4 31.8 %collective-permute-start.11 = (f32[4,32,512]{2,1,0:T(8,128)S(1)}, f32[4,32,512]{2,1,0:T(8,128)}, u32[]{:S(2)}, u32[]{:S(2)}) collective-permute-start(f32[4,32,512]{2,1,0:T(8,128)S(1)} %pad_maximum_fusion.4), channel_id=1, source_target_pairs={{0,8},{2,10},{4,12},{6,14},{8,0},{10,2},{12,4},{14,6},{16,24},{18,... | collective-permute-start | bytes 786440 | tf_op jit(solution)/shard_map/ppermute | solution.py:624
  50.2 27.3 %collective-permute-start.8 = (f32[2,32,512]{2,1,0:T(8,128)S(1)}, f32[2,32,512]{2,1,0:T(8,128)}, u32[]{:S(2)}, u32[]{:S(2)}) collective-permute-start(f32[2,32,512]{2,1,0:T(8,128)S(1)} %pad_maximum_fusion.7), channel_id=1, source_target_pairs={{0,2},{2,4},{4,6},{6,0},{8,10},{10,12},{12,14},{14,8},{16,18},{18,... | collective-permute-start | bytes 393224 | tf_op jit(solution)/shard_map/ppermute | solution.py:634
  50.9 26.6 %collective-permute-start.9 = (f32[2,32,512]{2,1,0:T(8,128)}, f32[2,32,512]{2,1,0:T(8,128)}, u32[]{:S(2)}, u32[]{:S(2)}) collective-permute-start(f32[2,32,512]{2,1,0:T(8,128)} %pad_maximum_fusion.8), channel_id=1, source_target_pairs={{0,4},{2,6},{4,0},{6,2},{8,12},{10,14},{12,8},{14,10},{16,20},{18,... | collective-permute-start | bytes 393224 | tf_op jit(solution)/shard_map/ppermute | solution.py:634
  59.7 16.6 %collective-permute-start.6 = (f32[8,1,1280]{2,1,0:T(1,128)S(1)}, f32[8,1,1280]{2,1,0:T(1,128)S(1)}, u32[]{:S(2)}, u32[]{:S(2)}) collective-permute-start(f32[8,1,1280]{2,1,0:T(1,128)S(1)} %get-tuple-element.61), channel_id=1, source_target_pairs={{0,2},{2,4},{4,6},{6,8},{8,10},{10,12},{12,14},{14,16},{16,18},{18... | collective-permute-start | bytes 122888 | tf_op jit(solution)/shard_map/ppermute | solution.py:568
  60.1 16.2 %collective-permute-start.7 = (f32[8,1,1280]{2,1,0:T(1,128)S(1)}, f32[8,1,1280]{2,1,0:T(1,128)S(1)}, u32[]{:S(2)}, u32[]{:S(2)}) collective-permute-start(f32[8,1,1280]{2,1,0:T(1,128)S(1)} %get-tuple-element.62), channel_id=1, source_target_pairs={{2,0},{4,2},{6,4},{8,6},{10,8},{12,10},{14,12},{16,14},{18,16},{20... | collective-permute-start | bytes 122888 | tf_op jit(solution)/shard_map/ppermute | solution.py:569
  76.3 2.8 %collective-permute-start.10 = (f32[2,32,512]{2,1,0:T(8,128)}, f32[2,32,512]{2,1,0:T(8,128)S(1)}, u32[]{:S(2)}, u32[]{:S(2)}) collective-permute-start(f32[2,32,512]{2,1,0:T(8,128)} %pad_maximum_fusion.9), channel_id=1, source_target_pairs={{0,6},{2,0},{4,2},{6,4},{8,14},{10,8},{12,10},{14,12},{16,22},{18,... | collective-permute-start | bytes 393224 | tf_op jit(solution)/shard_map/ppermute | solution.py:634
  77.5 1.7 %copy-start.2 = (f32[32,72,128]{2,1,0:T(8,128)}, f32[32,72,128]{2,1,0:T(8,128)S(1)}, u32[]{:S(2)}) copy-start(f32[32,72,128]{2,1,0:T(8,128)S(1)} %all-to-all-done.refs_0_) | copy-start | bytes 3538948
  79.1 0.7 copy-start.10
  90.0 30.3 %all-to-all-start.3 = ((f32[32,2,4,8,128]{4,3,2,1,0:T(8,128)}), f32[32,2,4,8,128]{4,3,2,1,0:T(8,128)S(1)}, u32[]{:S(2)}, u32[]{:S(2)}) async-start(f32[32,2,4,8,128]{4,3,2,1,0:T(8,128)} %get-tuple-element.57), calls=%async_computation.3 | async-start | bytes 2097152 | tf_op jit(solution)/shard_map/all_to_all | solution.py:680
  120.3 3.4 %copy-start = (f32[32,2,4,8,128]{4,3,2,1,0:T(8,128)}, f32[32,2,4,8,128]{4,3,2,1,0:T(8,128)S(1)}, u32[]{:S(2)}) copy-start(f32[32,2,4,8,128]{4,3,2,1,0:T(8,128)S(1)} %all-to-all-done.3.sent) | copy-start | bytes 3145732
  120.3 30.6 %all-to-all-start.2 = ((f32[32,2,4,8,128]{4,3,2,1,0:T(8,128)}), f32[32,2,4,8,128]{4,3,2,1,0:T(8,128)}, u32[]{:S(2)}, u32[]{:S(2)}) async-start(f32[32,2,4,8,128]{4,3,2,1,0:T(8,128)} %odd_planes.1), calls=%async_computation.2 | async-start | bytes 2097152 | tf_op jit(solution)/shard_map/all_to_all | solution.py:680

commit v12 on v11

--- a/solution.py
+++ b/solution.py
@@ -16,7 +16,7 @@
 NZC = 16
 LANES = 128
 CHUNKS = 2
-VMEM_LIMIT = 62 * 1024 * 1024
+VMEM_LIMIT = 127 * 512 * 1024
 
 
 def halves(table):
@@ -132,11 +132,15 @@
     return parts
 
 
-def tile_copies(plan, chunk, projection, held, sems):
-    return [
-        pltpu.make_async_copy(projection.at[:, tx, chunk], held.at[tx], sems.at[tx])
-        for tx in range(plan.tx_chunk)
-    ]
+def tile_copies(plan, chunk, projection, held, sems, parts):
+    count = TY * TZ // parts
+    copies = []
+    for tx in range(plan.tx_chunk):
+        for part in range(parts):
+            rows = pl.ds(part * count, count)
+            source = projection.at[:, tx, chunk, rows]
+            copies.append(pltpu.make_async_copy(source, held.at[tx, :, rows], sems.at[len(copies)]))
+    return copies
 
 
 def project_kernel(plan, chunk, *refs):
@@ -147,32 +151,30 @@
     arrays = refs[count_in + 5 :]
     charges, counts, high, low = arrays[:4]
     planes = plan.cell_planes
-    first = plan.tx_chunk
+    copies = tile_copies(plan, chunk, projection, held, sems, TY)
     loads = [
-        pltpu.make_async_copy(source, place, sems.at[first + n])
+        pltpu.make_async_copy(source, place, sems.at[len(copies) + n])
         for n, (source, place) in enumerate(zip(arrays_in, arrays))
     ]
-    copies = tile_copies(plan, chunk, projection, held, sems)
     for copy in loads[:2] + copies + loads[2:]:
         copy.start()
     for copy in loads[:2]:
         copy.wait()
-    for tx, copy in enumerate(copies):
+    for n, copy in enumerate(copies):
         copy.wait()
 
-        def body(place, carry, tx=tx):
+        def body(place, carry, tx=n // TY, ty=n % TY):
             lanes = pl.ds(pl.multiple_of(place * LANES, LANES), LANES)
             count = counts[:, lanes]
             own = [jnp.where(count > p, charges[p, :, lanes], 0.0) for p in range(plan.panels)]
-            for ty in range(TY):
-                row = ((place * TY + ty) * plan.tx_chunk + tx) * planes
-                rows = pl.ds(pl.multiple_of(row, planes), planes)
-                for tz in range(TZ):
-                    t = ty * TZ + tz
-                    total = held[tx, 0, t, :, lanes] * own[0]
-                    for p in range(1, plan.panels):
-                        total = total + held[tx, p, t, :, lanes] * own[p]
-                    scratch[rows, tz * LANES : (tz + 1) * LANES] = total
+            row = ((place * TY + ty) * plan.tx_chunk + tx) * planes
+            rows = pl.ds(pl.multiple_of(row, planes), planes)
+            for tz in range(TZ):
+                t = ty * TZ + tz
+                total = held[tx, 0, t, :, lanes] * own[0]
+                for p in range(1, plan.panels):
+                    total = total + held[tx, p, t, :, lanes] * own[p]
+                scratch[rows, tz * LANES : (tz + 1) * LANES] = total
             return carry
 
         lax.fori_loop(0, plan.steps * plan.step_blocks, body, 0)
@@ -211,7 +213,7 @@
         scratch_shapes=[
             pltpu.VMEM((plan.steps * LANES, TZ * LANES), jnp.float32),
             pltpu.VMEM(held_shape(plan), jnp.float32),
-            pltpu.SemaphoreType.DMA((plan.tx_chunk + len(arrays),)),
+            pltpu.SemaphoreType.DMA((plan.tx_chunk * TY + len(arrays),)),
         ]
         + [pltpu.VMEM(array.shape, array.dtype) for array in arrays],
         compiler_params=pltpu.CompilerParams(vmem_limit_bytes=VMEM_LIMIT),
@@ -445,7 +447,7 @@
     planes = plan.cell_planes
     rows = plan.slots * 2 * plan.row_block
     first = plan.tx_chunk
-    copies = tile_copies(plan, chunk, projection, held, sems)
+    copies = tile_copies(plan, chunk, projection, held, sems, 1)
     pairs = ((sent, pieces), (high_in, high), (low_in, low), (before_in, before), (counts_in, counts))
     loads = [pltpu.make_async_copy(*pair, sems.at[first + n]) for n, pair in enumerate(pairs)]
     for copy in loads[:3] + copies + loads[3:]:
@@ -574,9 +576,8 @@
 
 def pick_kernel(plan, ids_ref, by_depth, *refs):
     outs, sems = (refs[:-1], refs[-1])
-    cell, slab = (ids_ref[0], ids_ref[1])
-    half_id, place = (slab // plan.half, lax.rem(slab, plan.half))
-    first = cell * plan.slabs + half_id * plan.half
+    place = lax.rem(ids_ref[0], plan.half)
+    first = ids_ref[0] - place
     copies = []
     for j in range(plan.outer):
         part = lax.rem(place // plan.inner + j, plan.outer) * plan.inner
@@ -685,16 +686,15 @@
     rows_shape = (plan.ny, 2 * plan.x_chunk)
     freq_shape = (2 * plan.ny, plan.x_chunk)
     both_shape = (2 * plan.ny, plan.nx)
-    ids = jnp.stack([lax.axis_index("cell"), lax.axis_index("slab")]).astype(jnp.int32)
     slot = lax.broadcasted_iota(jnp.int32, charges.shape, 0)
     masked = jnp.where(slot < counts[None], charges, 0.0)
     rows = jnp.transpose(spectrum[:, :, 0], (1, 0))
     first = project(plan, 0, charges, counts, split_projection, *depth_forward, None)
-    first, ids = lax.optimization_barrier((first, ids))
+    first, late_me = lax.optimization_barrier((first, me))
     even_pieces = exchange(first)
     edges = edge_weights(plan, rows)
     second = project(plan, 1, charges, counts, split_projection, *depth_forward, edges)
-    plain, mirror = pick_planes(plan, ids, spectrum)
+    plain, mirror = pick_planes(plan, late_me, spectrum)
     plain = [outer_shift(plan, value, j) for j, value in enumerate(plain)]
     mirror = [inner_shift(plan, value, i) for i, value in enumerate(mirror)]
     second, masked = lax.optimization_barrier((second, masked))
@@ -710,9 +710,6 @@
         [(y_forward, None), (x_forward, 0)], [], [whole_spec(both_shape)], [both_shape],
         values(rows_shape, freq_shape), 2,
     )
-    even, masked = lax.optimization_barrier((even, masked))
-    extended = extend_planes(plan, masked, left, right)
-    odd_pieces, extended = lax.optimization_barrier((odd_pieces, extended))
     late = [odd_pieces, *y_forward, x_forward[0][1:], x_forward[1][1:], even]
     late += [x_backward[0][:1], x_backward[1][:1], *y_backward]
     copies = [pltpu.VMEM(array.shape, array.dtype) for array in late]
@@ -727,9 +724,11 @@
         [(x_backward, 1), (y_backward, None)], [], [whole_spec(piece_shape(plan))], [piece_shape(plan)],
         values(rows_shape), 2,
     )
+    back, masked = lax.optimization_barrier((back, masked))
+    extended = extend_planes(plan, masked, left, right)
+    back, extended = lax.optimization_barrier((back, extended))
+    odd_back = exchange(back)
     total = near_field(plan, extended, neighbours, near_blocks)
-    back, total = lax.optimization_barrier((back, total))
-    odd_back = exchange(back)
     total = gather(plan, 0, counts, total, split_projection, *depth_backward, even_back)
     return gather(plan, 1, counts, total, split_projection, *depth_backward, odd_back)
 

time: 158 us -> 152 us (0.962)
  waiting for transfers between devices: 47 us -> 42.7 us
    all_to_all x4, waiting for transfers between devices: 28.7 us -> 15.8 us  [exchange(): return lax.all_to_all(pieces, axes, split_axis=0, concat_axis=0, tiled=True)]
    ppermute x2, waiting for transfers between devices: 0.01 us -> 6.67 us  [outer_shift(): return lax.ppermute(value, 'slab', pairs)]
    unnamed x23 -> x11, local copies, waits for them, and re-layouts: 1.68 us -> 0.04 us
    ppermute x6, waiting for transfers between devices: 1.66 us -> 3.3 us  [inner_shift(): return lax.ppermute(value, 'slab', pairs)]
  transfers between devices with their start and end apart: 16 -> 16, of which waited for: 7 -> 10; matrix products, arithmetic and copies ran while one was open for 6% -> 7% of each run, Pallas kernels for 28% -> 28%
where the time goes in v12:
time: 152 us
  Pallas kernels  64.7 us (43%)
  waiting for transfers between devices  42.7 us (28%)
  starting transfers between devices  33.2 us (22%)
  other arithmetic  6.06 us (4%)
  local copies, waits for them, and re-layouts  4.53 us (3%)
    pallas_call x4, Pallas kernels, projection_call(): pl.pallas_call(kernel, in_specs=[pl.BlockSpec(memory_space=pl.ANY)] * (le...  24.4 us
    pallas_call x3, Pallas kernels, plane_call(): pl.pallas_call(functools.partial(kernel, plan), grid=(1,) if tables else...  22.4 us
    all_to_all x4, starting transfers between devices, exchange(): return lax.all_to_all(pieces, axes, split_axis=0, concat_axis=0, tiled=True)  17.8 us
    all_to_all x4, waiting for transfers between devices, exchange(): return lax.all_to_all(pieces, axes, split_axis=0, concat_axis=0, tiled=True)  15.8 us
    pallas_call x1, Pallas kernels, near_field(): pl.pallas_call(functools.partial(near_kernel, plan), grid=(plan.cell_cols...  15.5 us
    ppermute x1, waiting for transfers between devices, extend_planes(): before = lax.ppermute(wide[:, -1:], 'slab', up)  11.5 us
    ppermute x2, waiting for transfers between devices, outer_shift(): return lax.ppermute(value, 'slab', pairs)  6.67 us
    ppermute x6, starting transfers between devices, inner_shift(): return lax.ppermute(value, 'slab', pairs)  4.69 us
  transfers between devices with their start and end apart: 16, of which 10 were waited for; matrix products, arithmetic and copies ran while one was open for 7% of the time, Pallas kernels for 28%

profile of v12, /device:TPU:0, one launch (start us, length us, event | category | flops | bytes accessed | tf_op | source)
XLA Modules:
  0.0 151.5 jit_solution(6786580067117416567)
XLA Ops:
  0.0 6.0 %project_depth.3 = f32[32,64,128]{2,1,0:T(8,128)} custom-call(f32[8,8,1024]{2,1,0:T(8,128)} %refs_0_.3, s32[8,1024]{1,0:T(8,128)} %counts_in.3, bf16[512,512]{1,0:T(8,128)(2,1)} %constant.63.clone.refs_2_, bf16[512,512]{1,0:T(8,128)(2,1)} %constant.64.clone.refs_3_, f32[8,2,2,16,8,1024]{5,4,3,2,1,0:T(8,128)} %bitcast.18), custom_call_target="tpu_custom_call" | custom-call | flops 4194304 | bytes 8388608 | tf_op jit(solution)/shard_map/project_depth/pallas_call | solution.py:208
  6.1 0.0 copy-start
  6.1 0.0 copy-start.2
  6.1 7.4 %all-to-all-start.1 = ((f32[32,64,128]{2,1,0:T(8,128)}), f32[32,64,128]{2,1,0:T(8,128)}, u32[]{:S(2)}, u32[]{:S(2)}) async-start(f32[32,64,128]{2,1,0:T(8,128)} %project_depth.3), calls=%async_computation.1 | async-start | bytes 2097152 | tf_op jit(solution)/shard_map/all_to_all | solution.py:681
  13.5 2.3 %pick_planes.1 = (f32[4,32,512]{2,1,0:T(8,128)}, f32[4,32,512]{2,1,0:T(8,128)}, f32[2,32,512]{2,1,0:T(8,128)}, f32[2,32,512]{2,1,0:T(8,128)}, f32[2,32,512]{2,1,0:T(8,128)}, /*index=5*/f32[2,32,512]{2,1,0:T(8,128)}) custom-call(s32[1]{0:T(128)} %bitcast.ids_ref.me_ref, f32[64,32,512]{2,1,0:T(8,128)} %bitcast.22), custom_call_target="tpu_custom_call" | custom-call | bytes 2097152 | tf_op jit(solution)/shard_map/pick_planes/pallas_call | solution.py:604
  15.9 1.8 %collective-permute-start.2 = (f32[4,32,512]{2,1,0:T(8,128)}, f32[4,32,512]{2,1,0:T(8,128)}, u32[]{:S(2)}, u32[]{:S(2)}) collective-permute-start(f32[4,32,512]{2,1,0:T(8,128)} %get-tuple-element.34), channel_id=1, source_target_pairs={{0,8},{2,10},{4,12},{6,14},{8,0},{10,2},{12,4},{14,6},{16,24},{18,... | collective-permute-start | bytes 786440 | tf_op jit(solution)/shard_map/ppermute | solution.py:625
  17.6 0.0 collective-permute-start.3
  17.6 1.5 collective-permute-start.4
  19.1 1.4 collective-permute-start.5
  20.6 1.3 slice.56
  21.9 0.1 rev.4
  22.1 0.0 copy-done
  22.1 0.0 copy-done.2
  22.1 0.7 fusion.2
  22.8 0.7 pad_maximum_fusion.5.refs_4_
  23.5 6.1 %project_depth.2 = f32[32,72,128]{2,1,0:T(8,128)} custom-call(f32[8,8,1024]{2,1,0:T(8,128)} %refs_0_.3, s32[8,1024]{1,0:T(8,128)} %counts_in.3, bf16[512,512]{1,0:T(8,128)(2,1)} %constant.63.clone.refs_2_, bf16[512,512]{1,0:T(8,128)(2,1)} %constant.64.clone.refs_3_, f32[32,8,128]{2,1,0:T(8,128)} %pad_maximum_fusion.5.refs_4_, f32[8,2,2,16,8,1024]{5,4,3,2,1,0:T(8,128)} %bitcast.19), custom_call_target="tpu_custom_call" | custom-call | flops 4194304 | bytes 8388608 | tf_op jit(solution)/shard_map/project_depth/pallas_call | solution.py:208
  29.7 0.0 copy-start.3
  29.7 0.1 fusion.4
  29.8 1.5 collective-permute-start
  31.3 2.6 %collective-permute-done = f32[8,8,16]{2,1,0:T(8,128)S(1)} collective-permute-done((f32[8,8,16]{2,1,0:T(8,128)S(1)}, f32[8,8,16]{2,1,0:T(8,128)S(1)}, u32[]{:S(2)}, u32[]{:S(2)}) %collective-permute-start) | collective-permute-done | bytes 4128 | tf_op jit(solution)/shard_map/ppermute | solution.py:561
  33.8 1.4 collective-permute-start.1
  35.2 2.8 %collective-permute-done.1 = f32[8,8,16]{2,1,0:T(8,128)S(1)} collective-permute-done((f32[8,8,16]{2,1,0:T(8,128)S(1)}, f32[8,8,16]{2,1,0:T(8,128)S(1)}, u32[]{:S(2)}, u32[]{:S(2)}) %collective-permute-start.1) | collective-permute-done | bytes 4128 | tf_op jit(solution)/shard_map/ppermute | solution.py:562
  37.9 0.0 collective-permute-done.3
  38.0 0.0 collective-permute-done.4
  38.0 0.0 collective-permute-done.5
  38.0 0.0 collective-permute-done.2
  38.0 2.7 %all-to-all-done.1.pieces = f32[32,64,128]{2,1,0:T(8,128)} async-done(((f32[32,64,128]{2,1,0:T(8,128)}), f32[32,64,128]{2,1,0:T(8,128)}, u32[]{:S(2)}, u32[]{:S(2)}) %all-to-all-start.1) | async-done | bytes 1048608 | tf_op jit(solution)/shard_map/all_to_all | solution.py:681
  40.7 3.4 %all-to-all-start = ((f32[32,72,128]{2,1,0:T(8,128)}), f32[32,72,128]{2,1,0:T(8,128)}, u32[]{:S(2)}, u32[]{:S(2)}) async-start(f32[32,72,128]{2,1,0:T(8,128)} %project_depth.2), calls=%async_computation | async-start | bytes 2359296 | tf_op jit(solution)/shard_map/all_to_all | solution.py:681
  44.1 0.0 copy-done.4
  44.1 0.9 fusion.5
  45.0 1.0 fusion.7
  46.0 0.7 pad_maximum_fusion.4
  46.7 1.6 %collective-permute-start.9 = (f32[4,32,512]{2,1,0:T(8,128)}, f32[4,32,512]{2,1,0:T(8,128)}, u32[]{:S(2)}, u32[]{:S(2)}) collective-permute-start(f32[4,32,512]{2,1,0:T(8,128)} %pad_maximum_fusion.4), channel_id=1, source_target_pairs={{0,8},{2,10},{4,12},{6,14},{8,0},{10,2},{12,4},{14,6},{16,24},{18,... | collective-permute-start | bytes 786440 | tf_op jit(solution)/shard_map/ppermute | solution.py:625
  48.3 1.0 constant_dynamic-slice_fusion
  49.3 1.0 collective-permute-start.8
  50.3 0.7 pad_maximum_fusion.8
  51.0 0.5 collective-permute-start.7
  51.5 0.7 pad_maximum_fusion.7
  52.2 0.2 collective-permute-start.6
  52.4 0.7 pad_maximum_fusion.3.refs_14_
  53.1 0.7 pad_maximum_fusion.6.refs_10_
  53.8 5.7 %even_planes.1.refs_5_ = f32[1024,512]{1,0:T(8,128)} custom-call(s32[1]{0:T(128)} %bitcast.ids_ref.me_ref, f32[32,64,128]{2,1,0:T(8,128)} %all-to-all-done.1.pieces, bf16[512,512]{1,0:T(8,128)(2,1)} %constant.65.clone.y_high.refs_1_, bf16[512,512]{1,0:T(8,128)(2,1)} %constant.66.clone.y_low.refs_2_, bf16[2,256,512]{2,1,0:T(8,128)(2,1)} %constant.67.clone.x_high, ...), custom_call_target="tpu_custom_call" | custom-call | flops 1610612736 | bytes 3145728 | tf_op jit(solution)/shard_map/even_planes/pallas_call | solution.py:426
  59.5 0.0 collective-permute-done.8.refs_13_
  59.5 2.4 %collective-permute-done.7.refs_12_ = f32[2,32,512]{2,1,0:T(8,128)} collective-permute-done((f32[2,32,512]{2,1,0:T(8,128)}, f32[2,32,512]{2,1,0:T(8,128)}, u32[]{:S(2)}, u32[]{:S(2)}) %collective-permute-start.7) | collective-permute-done | bytes 131104 | tf_op jit(solution)/shard_map/ppermute | solution.py:635
  61.9 0.9 collective-permute-done.6.refs_11_
  62.8 6.7 %collective-permute-done.9.refs_15_ = f32[4,32,512]{2,1,0:T(8,128)} collective-permute-done((f32[4,32,512]{2,1,0:T(8,128)}, f32[4,32,512]{2,1,0:T(8,128)}, u32[]{:S(2)}, u32[]{:S(2)}) %collective-permute-start.9) | collective-permute-done | bytes 262176 | tf_op jit(solution)/shard_map/ppermute | solution.py:625
  69.5 4.6 %all-to-all-done.refs_0_ = f32[32,72,128]{2,1,0:T(8,128)} async-done(((f32[32,72,128]{2,1,0:T(8,128)}), f32[32,72,128]{2,1,0:T(8,128)}, u32[]{:S(2)}, u32[]{:S(2)}) %all-to-all-start) | async-done | bytes 1179680 | tf_op jit(solution)/shard_map/all_to_all | solution.py:681
  74.1 10.1 %middle_planes.1 = (f32[32,2,4,8,128]{4,3,2,1,0:T(8,128)}, f32[1024,256]{1,0:T(8,128)}) custom-call(s32[1]{0:T(128)} %bitcast.ids_ref.me_ref, f32[32,72,128]{2,1,0:T(8,128)} %all-to-all-done.refs_0_, bf16[512,512]{1,0:T(8,128)(2,1)} %constant.65.clone.y_high.refs_1_, bf16[512,512]{1,0:T(8,128)(2,1)} %constant.66.clone.y_low.refs_2_, ...), custom_call_target="tpu_custom_call" | custom-call | flops 3221225472 | bytes 10616832 | tf_op jit(solution)/shard_map/middle_planes/pallas_call | solution.py:426
  84.1 3.6 %all-to-all-start.3 = ((f32[32,2,4,8,128]{4,3,2,1,0:T(8,128)}), f32[32,2,4,8,128]{4,3,2,1,0:T(8,128)}, u32[]{:S(2)}, u32[]{:S(2)}) async-start(f32[32,2,4,8,128]{4,3,2,1,0:T(8,128)} %get-tuple-element.53), calls=%async_computation.3 | async-start | bytes 2097152 | tf_op jit(solution)/shard_map/all_to_all | solution.py:681
  87.7 6.6 %odd_planes.1 = f32[32,2,4,8,128]{4,3,2,1,0:T(8,128)} custom-call(s32[1]{0:T(128)} %bitcast.ids_ref.me_ref, f32[1024,256]{1,0:T(8,128)} %get-tuple-element.47.freqs, bf16[2,256,512]{2,1,0:T(8,128)(2,1)} %constant.75.clone.x_high, bf16[2,256,512]{2,1,0:T(8,128)(2,1)} %constant.76.clone.x_low, bf16[512,512]{1,0:T(8,128)(2,1)} %constant.73.clone.refs_8_.y_high, ...), custom_call_target="tpu_custom_call" | custom-call | flops 1610612736 | bytes 3145728 | tf_op jit(solution)/shard_map/odd_planes/pallas_call | solution.py:426
  94.4 0.1 concatenate.34
  94.5 0.1 fusion.3
  94.5 0.1 collective-permute-start.10
  94.6 4.4 %collective-permute-start.11 = (f32[8,1,1280]{2,1,0:T(1,128)S(1)}, f32[8,1,1280]{2,1,0:T(1,128)S(1)}, u32[]{:S(2)}, u32[]{:S(2)}) collective-permute-start(f32[8,1,1280]{2,1,0:T(1,128)S(1)} %get-tuple-element.58), channel_id=1, source_target_pairs={{2,0},{4,2},{6,4},{8,6},{10,8},{12,10},{14,12},{16,14},{18,16},{20... | collective-permute-start | bytes 122888 | tf_op jit(solution)/shard_map/ppermute | solution.py:571
  99.0 11.5 %collective-permute-done.10 = f32[8,1,1280]{2,1,0:T(1,128)S(1)} collective-permute-done((f32[8,1,1280]{2,1,0:T(1,128)S(1)}, f32[8,1,1280]{2,1,0:T(1,128)S(1)}, u32[]{:S(2)}, u32[]{:S(2)}) %collective-permute-start.10) | collective-permute-done | bytes 40992 | tf_op jit(solution)/shard_map/ppermute | solution.py:570
  110.5 0.0 collective-permute-done.11
  110.5 0.1 fusion.1
  110.7 1.1 pad_maximum_fusion.extended
  111.7 3.0 %all-to-all-done.3.sent = f32[32,2,4,8,128]{4,3,2,1,0:T(8,128)} async-done(((f32[32,2,4,8,128]{4,3,2,1,0:T(8,128)}), f32[32,2,4,8,128]{4,3,2,1,0:T(8,128)}, u32[]{:S(2)}, u32[]{:S(2)}) %all-to-all-start.3) | async-done | bytes 1048608 | tf_op jit(solution)/shard_map/all_to_all | solution.py:681
  114.7 3.4 %all-to-all-start.2 = ((f32[32,2,4,8,128]{4,3,2,1,0:T(8,128)}), f32[32,2,4,8,128]{4,3,2,1,0:T(8,128)}, u32[]{:S(2)}, u32[]{:S(2)}) async-start(f32[32,2,4,8,128]{4,3,2,1,0:T(8,128)} %odd_planes.1), calls=%async_computation.2 | async-start | bytes 2097152 | tf_op jit(solution)/shard_map/all_to_all | solution.py:681
  118.1 15.5 %near_blocks.1.before_in = f32[8,8,1024]{2,1,0:T(8,128)} custom-call(f32[8,3,8,1280]{3,2,1,0:T(8,128)} %pad_maximum_fusion.extended, s32[6,8,1024]{2,1,0:T(8,128)} %codes.1, f32[6,8,8,8,1024]{4,3,2,1,0:T(8,128)} %blocks_ref.1), custom_call_target="tpu_custom_call" | custom-call | flops 6291456 | bytes 12582912 | tf_op jit(solution)/shard_map/near_blocks/pallas_call | solution.py:533
  133.6 6.1 %depth_gather.2.before_in = f32[8,8,1024]{2,1,0:T(8,128)} custom-call(f32[32,2,4,8,128]{4,3,2,1,0:T(8,128)} %all-to-all-done.3.sent, bf16[512,512]{1,0:T(8,128)(2,1)} %constant.77.clone.high_in, bf16[512,512]{1,0:T(8,128)(2,1)} %constant.78.clone.low_in, f32[8,8,1024]{2,1,0:T(8,128)} %near_blocks.1.before_in, s32[8,1024]{1,0:T(8,128)} %counts_in.3, ...), custom_call_target="tpu_custom_call" | custom-call | flops 4194304 | bytes 8388608 | tf_op jit(solution)/shard_map/depth_gather/pallas_call | solution.py:208
  139.7 5.6 %all-to-all-done.2.sent = f32[32,2,4,8,128]{4,3,2,1,0:T(8,128)} async-done(((f32[32,2,4,8,128]{4,3,2,1,0:T(8,128)}), f32[32,2,4,8,128]{4,3,2,1,0:T(8,128)}, u32[]{:S(2)}, u32[]{:S(2)}) %all-to-all-start.2) | async-done | bytes 1048608 | tf_op jit(solution)/shard_map/all_to_all | solution.py:681
  145.3 6.1 %depth_gather.3 = f32[8,8,1024]{2,1,0:T(8,128)} custom-call(f32[32,2,4,8,128]{4,3,2,1,0:T(8,128)} %all-to-all-done.2.sent, bf16[512,512]{1,0:T(8,128)(2,1)} %constant.77.clone.high_in, bf16[512,512]{1,0:T(8,128)(2,1)} %constant.78.clone.low_in, f32[8,8,1024]{2,1,0:T(8,128)} %depth_gather.2.before_in, s32[8,1024]{1,0:T(8,128)} %counts_in.3, ...), custom_call_target="tpu_custom_call" | custom-call | flops 4194304 | bytes 8388608 | tf_op jit(solution)/shard_map/depth_gather/pallas_call | solution.py:208
  (11 shorter events, 0.1 us)
Async XLA Ops:
  6.1 16.0 %copy-start = (f32[8,8,1024]{2,1,0:T(8,128)S(1)}, f32[8,8,1024]{2,1,0:T(8,128)}, u32[]{:S(2)}) copy-start(f32[8,8,1024]{2,1,0:T(8,128)} %refs_0_.3) | copy-start | bytes 786436
  6.1 16.0 %copy-start.2 = (s32[8,1024]{1,0:T(8,128)S(1)}, s32[8,1024]{1,0:T(8,128)}, u32[]{:S(2)}) copy-start(s32[8,1024]{1,0:T(8,128)} %counts_in.3) | copy-start | bytes 98308
  6.1 34.6 %all-to-all-start.1 = ((f32[32,64,128]{2,1,0:T(8,128)}), f32[32,64,128]{2,1,0:T(8,128)}, u32[]{:S(2)}, u32[]{:S(2)}) async-start(f32[32,64,128]{2,1,0:T(8,128)} %project_depth.3), calls=%async_computation.1 | async-start | bytes 2097152 | tf_op jit(solution)/shard_map/all_to_all | solution.py:681
  15.9 22.1 %collective-permute-start.2 = (f32[4,32,512]{2,1,0:T(8,128)}, f32[4,32,512]{2,1,0:T(8,128)}, u32[]{:S(2)}, u32[]{:S(2)}) collective-permute-start(f32[4,32,512]{2,1,0:T(8,128)} %get-tuple-element.34), channel_id=1, source_target_pairs={{0,8},{2,10},{4,12},{6,14},{8,0},{10,2},{12,4},{14,6},{16,24},{18,... | collective-permute-start | bytes 786440 | tf_op jit(solution)/shard_map/ppermute | solution.py:625
  17.6 20.3 %collective-permute-start.3 = (f32[2,32,512]{2,1,0:T(8,128)}, f32[2,32,512]{2,1,0:T(8,128)}, u32[]{:S(2)}, u32[]{:S(2)}) collective-permute-start(f32[2,32,512]{2,1,0:T(8,128)} %get-tuple-element.36), channel_id=1, source_target_pairs={{0,2},{2,4},{4,6},{6,0},{8,10},{10,12},{12,14},{14,8},{16,18},{18,... | collective-permute-start | bytes 393224 | tf_op jit(solution)/shard_map/ppermute | solution.py:635
  17.6 20.3 %collective-permute-start.4 = (f32[2,32,512]{2,1,0:T(8,128)}, f32[2,32,512]{2,1,0:T(8,128)}, u32[]{:S(2)}, u32[]{:S(2)}) collective-permute-start(f32[2,32,512]{2,1,0:T(8,128)} %get-tuple-element.37), channel_id=1, source_target_pairs={{0,4},{2,6},{4,0},{6,2},{8,12},{10,14},{12,8},{14,10},{16,20},{18,... | collective-permute-start | bytes 393224 | tf_op jit(solution)/shard_map/ppermute | solution.py:635
  19.1 18.8 %collective-permute-start.5 = (f32[2,32,512]{2,1,0:T(8,128)}, f32[2,32,512]{2,1,0:T(8,128)}, u32[]{:S(2)}, u32[]{:S(2)}) collective-permute-start(f32[2,32,512]{2,1,0:T(8,128)} %get-tuple-element.38), channel_id=1, source_target_pairs={{0,6},{2,0},{4,2},{6,4},{8,14},{10,8},{12,10},{14,12},{16,22},{18,... | collective-permute-start | bytes 393224 | tf_op jit(solution)/shard_map/ppermute | solution.py:635
  23.5 6.2 %copy-start.1 = (f32[8,8,1024]{2,1,0:T(8,128)S(1)}, f32[8,8,1024]{2,1,0:T(8,128)}, u32[]{:S(2)}) copy-start(f32[8,8,1024]{2,1,0:T(8,128)} %fusion.2) | copy-start | bytes 786436
  23.5 20.6 %copy-start.4 = (f32[2,32,512]{2,1,0:T(8,128)S(1)}, f32[2,32,512]{2,1,0:T(8,128)}, u32[]{:S(2)}) copy-start(f32[2,32,512]{2,1,0:T(8,128)} %get-tuple-element.43) | copy-start | bytes 393220
  29.7 18.6 %copy-start.3 = (f32[4,32,512]{2,1,0:T(8,128)S(1)}, f32[4,32,512]{2,1,0:T(8,128)}, u32[]{:S(2)}) copy-start(f32[4,32,512]{2,1,0:T(8,128)} %get-tuple-element.41) | copy-start | bytes 786436
  29.8 4.0 %collective-permute-start = (f32[8,8,16]{2,1,0:T(8,128)S(1)}, f32[8,8,16]{2,1,0:T(8,128)S(1)}, u32[]{:S(2)}, u32[]{:S(2)}) collective-permute-start(f32[8,8,16]{2,1,0:T(8,128)S(1)} %get-tuple-element.68), channel_id=1, source_target_pairs={{0,1},{1,0},{2,3},{3,2},{4,5},{5,4},{6,7},{7,6},{8,9},{9,8},{10,11... | collective-permute-start | bytes 12296 | tf_op jit(solution)/shard_map/ppermute | solution.py:561
  33.8 4.1 %collective-permute-start.1 = (f32[8,8,16]{2,1,0:T(8,128)S(1)}, f32[8,8,16]{2,1,0:T(8,128)S(1)}, u32[]{:S(2)}, u32[]{:S(2)}) collective-permute-start(f32[8,8,16]{2,1,0:T(8,128)S(1)} %get-tuple-element.67), channel_id=1, source_target_pairs={{1,0},{0,1},{3,2},{2,3},{5,4},{4,5},{7,6},{6,7},{9,8},{8,9},{11,10... | collective-permute-start | bytes 12296 | tf_op jit(solution)/shard_map/ppermute | solution.py:562
  40.7 33.4 %all-to-all-start = ((f32[32,72,128]{2,1,0:T(8,128)}), f32[32,72,128]{2,1,0:T(8,128)}, u32[]{:S(2)}, u32[]{:S(2)}) async-start(f32[32,72,128]{2,1,0:T(8,128)} %project_depth.2), calls=%async_computation | async-start | bytes 2359296 | tf_op jit(solution)/shard_map/all_to_all | solution.py:681
  46.7 22.8 %collective-permute-start.9 = (f32[4,32,512]{2,1,0:T(8,128)}, f32[4,32,512]{2,1,0:T(8,128)}, u32[]{:S(2)}, u32[]{:S(2)}) collective-permute-start(f32[4,32,512]{2,1,0:T(8,128)} %pad_maximum_fusion.4), channel_id=1, source_target_pairs={{0,8},{2,10},{4,12},{6,14},{8,0},{10,2},{12,4},{14,6},{16,24},{18,... | collective-permute-start | bytes 786440 | tf_op jit(solution)/shard_map/ppermute | solution.py:625
  49.3 10.2 %collective-permute-start.8 = (f32[2,32,512]{2,1,0:T(8,128)S(1)}, f32[2,32,512]{2,1,0:T(8,128)}, u32[]{:S(2)}, u32[]{:S(2)}) collective-permute-start(f32[2,32,512]{2,1,0:T(8,128)S(1)} %pad_maximum_fusion.9), channel_id=1, source_target_pairs={{0,6},{2,0},{4,2},{6,4},{8,14},{10,8},{12,10},{14,12},{16,22},{18,... | collective-permute-start | bytes 393224 | tf_op jit(solution)/shard_map/ppermute | solution.py:635
  51.0 10.9 %collective-permute-start.7 = (f32[2,32,512]{2,1,0:T(8,128)}, f32[2,32,512]{2,1,0:T(8,128)}, u32[]{:S(2)}, u32[]{:S(2)}) collective-permute-start(f32[2,32,512]{2,1,0:T(8,128)} %pad_maximum_fusion.8), channel_id=1, source_target_pairs={{0,4},{2,6},{4,0},{6,2},{8,12},{10,14},{12,8},{14,10},{16,20},{18,... | collective-permute-start | bytes 393224 | tf_op jit(solution)/shard_map/ppermute | solution.py:635
  52.2 10.6 %collective-permute-start.6 = (f32[2,32,512]{2,1,0:T(8,128)}, f32[2,32,512]{2,1,0:T(8,128)}, u32[]{:S(2)}, u32[]{:S(2)}) collective-permute-start(f32[2,32,512]{2,1,0:T(8,128)} %pad_maximum_fusion.7), channel_id=1, source_target_pairs={{0,2},{2,4},{4,6},{6,0},{8,10},{10,12},{12,14},{14,8},{16,18},{18,... | collective-permute-start | bytes 393224 | tf_op jit(solution)/shard_map/ppermute | solution.py:635
  84.1 30.6 %all-to-all-start.3 = ((f32[32,2,4,8,128]{4,3,2,1,0:T(8,128)}), f32[32,2,4,8,128]{4,3,2,1,0:T(8,128)}, u32[]{:S(2)}, u32[]{:S(2)}) async-start(f32[32,2,4,8,128]{4,3,2,1,0:T(8,128)} %get-tuple-element.53), calls=%async_computation.3 | async-start | bytes 2097152 | tf_op jit(solution)/shard_map/all_to_all | solution.py:681
  94.5 16.0 %collective-permute-start.10 = (f32[8,1,1280]{2,1,0:T(1,128)S(1)}, f32[8,1,1280]{2,1,0:T(1,128)S(1)}, u32[]{:S(2)}, u32[]{:S(2)}) collective-permute-start(f32[8,1,1280]{2,1,0:T(1,128)S(1)} %get-tuple-element.57), channel_id=1, source_target_pairs={{0,2},{2,4},{4,6},{6,8},{8,10},{10,12},{12,14},{14,16},{16,18},{18... | collective-permute-start | bytes 122888 | tf_op jit(solution)/shard_map/ppermute | solution.py:570
  94.6 16.0 %collective-permute-start.11 = (f32[8,1,1280]{2,1,0:T(1,128)S(1)}, f32[8,1,1280]{2,1,0:T(1,128)S(1)}, u32[]{:S(2)}, u32[]{:S(2)}) collective-permute-start(f32[8,1,1280]{2,1,0:T(1,128)S(1)} %get-tuple-element.58), channel_id=1, source_target_pairs={{2,0},{4,2},{6,4},{8,6},{10,8},{12,10},{14,12},{16,14},{18,16},{20... | collective-permute-start | bytes 122888 | tf_op jit(solution)/shard_map/ppermute | solution.py:571
  114.7 30.5 %all-to-all-start.2 = ((f32[32,2,4,8,128]{4,3,2,1,0:T(8,128)}), f32[32,2,4,8,128]{4,3,2,1,0:T(8,128)}, u32[]{:S(2)}, u32[]{:S(2)}) async-start(f32[32,2,4,8,128]{4,3,2,1,0:T(8,128)} %odd_planes.1), calls=%async_computation.2 | async-start | bytes 2097152 | tf_op jit(solution)/shard_map/all_to_all | solution.py:681

commit v13 on v12

--- a/solution.py
+++ b/solution.py
@@ -177,7 +177,7 @@
                 scratch[rows, tz * LANES : (tz + 1) * LANES] = total
             return carry
 
-        lax.fori_loop(0, plan.steps * plan.step_blocks, body, 0)
+        lax.fori_loop(0, plan.steps * plan.step_blocks, body, 0, unroll=True)
     for copy in loads[2:]:
         copy.wait()
     spectra = product(split(scratch[...]), (high[...], low[...])).T
@@ -238,7 +238,17 @@
     return jnp.where(slab >= plan.half, -1.0, 1.0)
 
 
-def forward_plane(plan, me_ref, pieces, y_table, x_table, rows_ref, freq_ref, waits=()):
+def piece_copies(plan, source, dest, sems, first):
+    copies = []
+    for n in range(plan.slots // plan.y_lanes):
+        rows = pl.ds(n * plan.y_lanes, plan.y_lanes)
+        copies.append(pltpu.make_async_copy(source.at[rows], dest.at[rows], sems.at[first + n]))
+    return copies
+
+
+def forward_plane(
+    plan, me_ref, pieces, y_table, x_table, rows_ref, freq_ref, waits=(), arrivals=None
+):
     special = me_ref[0] == 0
     sign = far_sign(plan, me_ref)
     rows = 2 * plan.steps * plan.row_block
@@ -247,6 +257,8 @@
     for cell in range(plan.cells):
         for group in range(plan.slabs // plan.y_lanes):
             first = cell * plan.slabs + group * plan.y_lanes
+            if arrivals:
+                arrivals[first // plan.y_lanes].wait()
             parts = [pieces[first + i, :rows] for i in range(plan.y_lanes)]
             parts = swap_groups(parts, plan.width)
             for place, value in enumerate(parts):
@@ -284,7 +296,7 @@
     return product(split(freq_ref[...]), (x_table[0][0], x_table[1][0]))
 
 
-def backward_plane(plan, me_ref, freqs, x_table, y_table, out, rows_ref):
+def backward_plane(plan, me_ref, freqs, x_table, y_table, out, rows_ref, departures=None):
     special = me_ref[0] == 0
     sign = far_sign(plan, me_ref)
     width = plan.x_chunk
@@ -330,6 +342,8 @@
             first = cell * plan.slabs + group * plan.y_lanes
             for i in range(plan.y_lanes):
                 out[first + i] = parts[i].reshape(2, plan.steps, plan.row_block, LANES)
+            if departures:
+                departures[first // plan.y_lanes].start()
 
 
 def first_plane_kernel(plan, me_ref, pieces, y_high, y_low, x_high, x_low, out, rows_ref, freq_ref):
@@ -340,13 +354,15 @@
     late, refs = (refs[:10], refs[10:])
     strips, refs = (refs[: plan.inner], refs[plan.inner :])
     blocks, refs = (refs[: plan.outer], refs[plan.outer :])
-    out, rest, rows_ref, freq_ref, sum_ref, rest_ref, weights = refs[:7]
-    held, sems = (refs[7:17], refs[17])
+    out, rest, rows_ref, freq_ref, sum_ref, rest_ref, weights, result = refs[:8]
+    held, sems, piece_sems = (refs[8:18], refs[18], refs[19])
     pieces, yf_high, yf_low, xf_high, xf_low, even, xb_high, xb_low, yb_high, yb_low = held
     slab = lax.rem(me_ref[0], plan.slabs)
     place = lax.rem(slab, plan.half)
     outer_id, inner_id = (place // plan.inner, lax.rem(place, plan.inner))
     copies = [pltpu.make_async_copy(late[n], held[n], sems.at[n]) for n in range(len(held))]
+    arrivals = piece_copies(plan, late[0], pieces, piece_sems, 0)
+    departures = piece_copies(plan, result, out, piece_sems, len(arrivals))
     count = plan.ky_local
     placed = []
     for i in range(plan.inner):
@@ -357,21 +373,20 @@
             for m, source in enumerate((strips[i].at[j], blocks[j].at[i])):
                 sem = sems.at[len(held) + len(placed)]
                 placed.append(pltpu.make_async_copy(source, weights.at[m, rows], sem))
-    for copy in copies[:6] + placed + copies[6:]:
+    for copy in arrivals + copies[1:6] + placed + copies[6:]:
         copy.start()
-    copies[0].wait()
+    special = me_ref[0] == 0
+    width = plan.x_chunk
+    middle = plan.ny // 2
+    x_table = (xf_high.at[pl.ds(0, 1)], xf_low.at[pl.ds(0, 1)])
+    odd = forward_plane(
+        plan, me_ref, pieces, (yf_high, yf_low), x_table, rows_ref, freq_ref, copies[1:5], arrivals
+    )
     cell_first = me_ref[0] - slab
     tile = pieces[cell_first + jnp.where(slab < plan.half, plan.half, 0), plan.piece_rows :]
     parts = plan.nx // LANES
     own_edge = jnp.concatenate([tile[n : n + 1] for n in range(parts)], axis=1)
     edge = jnp.concatenate([tile[n : n + 1] for n in range(parts, 2 * parts)], axis=1)
-    special = me_ref[0] == 0
-    width = plan.x_chunk
-    middle = plan.ny // 2
-    x_table = (xf_high.at[pl.ds(0, 1)], xf_low.at[pl.ds(0, 1)])
-    odd = forward_plane(
-        plan, me_ref, pieces, (yf_high, yf_low), x_table, rows_ref, freq_ref, copies[1:5]
-    )
     for copy in copies[5:6] + placed:
         copy.wait()
     row = lax.broadcasted_iota(jnp.int32, (middle, width), 0)
@@ -402,8 +417,10 @@
     last.start()
     for copy in copies[6:]:
         copy.wait()
-    backward_plane(plan, me_ref, sum_ref[...], (xb_high, xb_low), (yb_high, yb_low), out, rows_ref)
-    last.wait()
+    tables = ((xb_high, xb_low), (yb_high, yb_low))
+    backward_plane(plan, me_ref, sum_ref[...], *tables, result, rows_ref, departures)
+    for copy in departures + [last]:
+        copy.wait()
 
 
 def last_plane_kernel(plan, me_ref, freqs, x_high, x_low, y_high, y_low, out, rows_ref):
@@ -477,7 +494,7 @@
                 out[p, :, lanes] = jnp.where(counts[:, lanes] > p, far[p], 0.0) if last else far[p]
             return carry
 
-        lax.fori_loop(0, plan.steps * plan.step_blocks, body, 0)
+        lax.fori_loop(0, plan.steps * plan.step_blocks, body, 0, unroll=True)
 
 
 def gather(plan, chunk, counts, before, projection, high, low, pieces):
@@ -703,7 +720,6 @@
     plain, mirror = (moved[: plan.outer], moved[plan.outer :])
     odd_pieces = exchange(second)
     strips = second_weights(plan, plain, mirror)
-    in_vmem = pl.BlockSpec(memory_space=pltpu.VMEM)
     in_place = pl.BlockSpec(memory_space=pl.ANY)
     (even,) = plane_call(
         plan, first_plane_kernel, "even_planes", me, [], [even_pieces],
@@ -714,9 +730,12 @@
     late += [x_backward[0][:1], x_backward[1][:1], *y_backward]
     copies = [pltpu.VMEM(array.shape, array.dtype) for array in late]
     copies.append(pltpu.SemaphoreType.DMA((len(late) + 2 * plan.half + 1,)))
+    copies.append(pltpu.SemaphoreType.DMA((2 * plan.slots // plan.y_lanes,)))
     back, rest = plane_call(
-        plan, middle_plane_kernel, "middle_planes", me, [], [], [], late + strips, [in_vmem, in_place], [piece_shape(plan), freq_shape],
-        values(rows_shape, freq_shape, freq_shape, freq_shape, (2, plan.ny // 2, plan.nx)) + copies, 4,
+        plan, middle_plane_kernel, "middle_planes", me, [], [], [], late + strips,
+        [in_place, in_place], [piece_shape(plan), freq_shape],
+        values(rows_shape, freq_shape, freq_shape, freq_shape, (2, plan.ny // 2, plan.nx))
+        + values(piece_shape(plan)) + copies, 4,
     )
     even_back = exchange(back)
     (back,) = plane_call(

time: 152 us -> 154 us (1.013)
    pallas_call x3, Pallas kernels: 22.4 us -> 24 us  [plane_call(): pl.pallas_call(functools.partial(kernel, plan), grid=(1,) if tables else...]
where the time goes in v13:
time: 154 us; the launch traced here: 153 us
  Pallas kernels  65.6 us (43%)
  waiting for transfers between devices  43.1 us (28%)
  starting transfers between devices  33 us (21%)
  other arithmetic  6.06 us (4%)
  local copies, waits for them, and re-layouts  4.53 us (3%)
    pallas_call x3, Pallas kernels, plane_call(): pl.pallas_call(functools.partial(kernel, plan), grid=(1,) if tables else...  24 us
    pallas_call x4, Pallas kernels, projection_call(): pl.pallas_call(kernel, in_specs=[pl.BlockSpec(memory_space=pl.ANY)] * (le...  23.8 us
    all_to_all x4, starting transfers between devices, exchange(): return lax.all_to_all(pieces, axes, split_axis=0, concat_axis=0, tiled=True)  17.6 us
    all_to_all x4, waiting for transfers between devices, exchange(): return lax.all_to_all(pieces, axes, split_axis=0, concat_axis=0, tiled=True)  16.1 us
    pallas_call x1, Pallas kernels, near_field(): pl.pallas_call(functools.partial(near_kernel, plan), grid=(plan.cell_cols...  15.5 us
    ppermute x1, waiting for transfers between devices, extend_planes(): before = lax.ppermute(wide[:, -1:], 'slab', up)  11.7 us
    ppermute x2, waiting for transfers between devices, outer_shift(): return lax.ppermute(value, 'slab', pairs)  6.67 us
    ppermute x6, starting transfers between devices, inner_shift(): return lax.ppermute(value, 'slab', pairs)  4.69 us
  transfers between devices with their start and end apart: 16, of which 10 were waited for; matrix products, arithmetic and copies ran while one was open for 7% of the time, Pallas kernels for 28%

profile of v13, /device:TPU:0, one launch (start us, length us, event | category | flops | bytes accessed | tf_op | source)
XLA Modules:
  0.0 152.8 jit_solution(5827158609660124306)
XLA Ops:
  0.0 6.1 %project_depth.3 = f32[32,64,128]{2,1,0:T(8,128)} custom-call(f32[8,8,1024]{2,1,0:T(8,128)} %refs_0_.3, s32[8,1024]{1,0:T(8,128)} %counts_in.3, bf16[512,512]{1,0:T(8,128)(2,1)} %constant.63.clone.refs_2_, bf16[512,512]{1,0:T(8,128)(2,1)} %constant.64.clone.refs_3_, f32[8,2,2,16,8,1024]{5,4,3,2,1,0:T(8,128)} %bitcast.18), custom_call_target="tpu_custom_call" | custom-call | flops 4194304 | bytes 8388608 | tf_op jit(solution)/shard_map/project_depth/pallas_call | solution.py:208
  6.1 0.0 copy-start
  6.1 0.0 copy-start.2
  6.1 7.4 %all-to-all-start.1 = ((f32[32,64,128]{2,1,0:T(8,128)}), f32[32,64,128]{2,1,0:T(8,128)}, u32[]{:S(2)}, u32[]{:S(2)}) async-start(f32[32,64,128]{2,1,0:T(8,128)} %project_depth.3), calls=%async_computation.1 | async-start | bytes 2097152 | tf_op jit(solution)/shard_map/all_to_all | solution.py:698
  13.5 2.3 %pick_planes.1 = (f32[4,32,512]{2,1,0:T(8,128)}, f32[4,32,512]{2,1,0:T(8,128)}, f32[2,32,512]{2,1,0:T(8,128)}, f32[2,32,512]{2,1,0:T(8,128)}, f32[2,32,512]{2,1,0:T(8,128)}, /*index=5*/f32[2,32,512]{2,1,0:T(8,128)}) custom-call(s32[1]{0:T(128)} %bitcast.ids_ref.me_ref, f32[64,32,512]{2,1,0:T(8,128)} %bitcast.22), custom_call_target="tpu_custom_call" | custom-call | bytes 2097152 | tf_op jit(solution)/shard_map/pick_planes/pallas_call | solution.py:621
  15.9 1.8 %collective-permute-start.2 = (f32[4,32,512]{2,1,0:T(8,128)}, f32[4,32,512]{2,1,0:T(8,128)}, u32[]{:S(2)}, u32[]{:S(2)}) collective-permute-start(f32[4,32,512]{2,1,0:T(8,128)} %get-tuple-element.34), channel_id=1, source_target_pairs={{0,8},{2,10},{4,12},{6,14},{8,0},{10,2},{12,4},{14,6},{16,24},{18,... | collective-permute-start | bytes 786440 | tf_op jit(solution)/shard_map/ppermute | solution.py:642
  17.6 0.0 collective-permute-start.3
  17.6 1.5 collective-permute-start.4
  19.1 1.4 collective-permute-start.5
  20.6 1.3 slice.56
  21.9 0.1 rev.4
  22.1 0.0 copy-done
  22.1 0.0 copy-done.2
  22.1 0.7 fusion.2
  22.8 0.7 pad_maximum_fusion.5.refs_4_
  23.5 6.1 %project_depth.2 = f32[32,72,128]{2,1,0:T(8,128)} custom-call(f32[8,8,1024]{2,1,0:T(8,128)} %refs_0_.3, s32[8,1024]{1,0:T(8,128)} %counts_in.3, bf16[512,512]{1,0:T(8,128)(2,1)} %constant.63.clone.refs_2_, bf16[512,512]{1,0:T(8,128)(2,1)} %constant.64.clone.refs_3_, f32[32,8,128]{2,1,0:T(8,128)} %pad_maximum_fusion.5.refs_4_, f32[8,2,2,16,8,1024]{5,4,3,2,1,0:T(8,128)} %bitcast.19), custom_call_target="tpu_custom_call" | custom-call | flops 4194304 | bytes 8388608 | tf_op jit(solution)/shard_map/project_depth/pallas_call | solution.py:208
  29.7 0.0 copy-done.1
  29.7 0.0 copy-start.3
  29.7 0.1 fusion.4
  29.8 1.5 collective-permute-start
  31.3 2.6 %collective-permute-done = f32[8,8,16]{2,1,0:T(8,128)S(1)} collective-permute-done((f32[8,8,16]{2,1,0:T(8,128)S(1)}, f32[8,8,16]{2,1,0:T(8,128)S(1)}, u32[]{:S(2)}, u32[]{:S(2)}) %collective-permute-start) | collective-permute-done | bytes 4128 | tf_op jit(solution)/shard_map/ppermute | solution.py:578
  33.8 1.4 collective-permute-start.1
  35.2 2.8 %collective-permute-done.1 = f32[8,8,16]{2,1,0:T(8,128)S(1)} collective-permute-done((f32[8,8,16]{2,1,0:T(8,128)S(1)}, f32[8,8,16]{2,1,0:T(8,128)S(1)}, u32[]{:S(2)}, u32[]{:S(2)}) %collective-permute-start.1) | collective-permute-done | bytes 4128 | tf_op jit(solution)/shard_map/ppermute | solution.py:579
  38.0 0.0 collective-permute-done.3
  38.0 0.0 collective-permute-done.4
  38.0 0.0 collective-permute-done.5
  38.0 0.0 collective-permute-done.2
  38.0 2.7 %all-to-all-done.1.pieces = f32[32,64,128]{2,1,0:T(8,128)} async-done(((f32[32,64,128]{2,1,0:T(8,128)}), f32[32,64,128]{2,1,0:T(8,128)}, u32[]{:S(2)}, u32[]{:S(2)}) %all-to-all-start.1) | async-done | bytes 1048608 | tf_op jit(solution)/shard_map/all_to_all | solution.py:698
  40.7 3.4 %all-to-all-start = ((f32[32,72,128]{2,1,0:T(8,128)}), f32[32,72,128]{2,1,0:T(8,128)}, u32[]{:S(2)}, u32[]{:S(2)}) async-start(f32[32,72,128]{2,1,0:T(8,128)} %project_depth.2), calls=%async_computation | async-start | bytes 2359296 | tf_op jit(solution)/shard_map/all_to_all | solution.py:698
  44.1 0.9 fusion.5
  45.0 1.0 fusion.7
  46.0 0.7 pad_maximum_fusion.4
  46.7 1.6 %collective-permute-start.9 = (f32[4,32,512]{2,1,0:T(8,128)}, f32[4,32,512]{2,1,0:T(8,128)}, u32[]{:S(2)}, u32[]{:S(2)}) collective-permute-start(f32[4,32,512]{2,1,0:T(8,128)} %pad_maximum_fusion.4), channel_id=1, source_target_pairs={{0,8},{2,10},{4,12},{6,14},{8,0},{10,2},{12,4},{14,6},{16,24},{18,... | collective-permute-start | bytes 786440 | tf_op jit(solution)/shard_map/ppermute | solution.py:642
  48.3 1.0 constant_dynamic-slice_fusion
  49.3 1.0 collective-permute-start.8
  50.3 0.7 pad_maximum_fusion.8
  51.0 0.5 collective-permute-start.7
  51.5 0.7 pad_maximum_fusion.7
  52.2 0.2 collective-permute-start.6
  52.4 0.7 pad_maximum_fusion.3.refs_14_
  53.1 0.7 pad_maximum_fusion.6.refs_10_
  53.8 5.8 %even_planes.1.refs_5_ = f32[1024,512]{1,0:T(8,128)} custom-call(s32[1]{0:T(128)} %bitcast.ids_ref.me_ref, f32[32,64,128]{2,1,0:T(8,128)} %all-to-all-done.1.pieces, bf16[512,512]{1,0:T(8,128)(2,1)} %constant.65.clone.y_high.refs_1_, bf16[512,512]{1,0:T(8,128)(2,1)} %constant.66.clone.y_low.refs_2_, bf16[2,256,512]{2,1,0:T(8,128)(2,1)} %constant.67.clone.x_high, ...), custom_call_target="tpu_custom_call" | custom-call | flops 1610612736 | bytes 3145728 | tf_op jit(solution)/shard_map/even_planes/pallas_call | solution.py:443
  59.5 0.0 collective-permute-done.8.refs_13_
  59.5 2.4 %collective-permute-done.7.refs_12_ = f32[2,32,512]{2,1,0:T(8,128)} collective-permute-done((f32[2,32,512]{2,1,0:T(8,128)}, f32[2,32,512]{2,1,0:T(8,128)}, u32[]{:S(2)}, u32[]{:S(2)}) %collective-permute-start.7) | collective-permute-done | bytes 131104 | tf_op jit(solution)/shard_map/ppermute | solution.py:652
  61.9 0.9 collective-permute-done.6.refs_11_
  62.8 6.7 %collective-permute-done.9.refs_15_ = f32[4,32,512]{2,1,0:T(8,128)} collective-permute-done((f32[4,32,512]{2,1,0:T(8,128)}, f32[4,32,512]{2,1,0:T(8,128)}, u32[]{:S(2)}, u32[]{:S(2)}) %collective-permute-start.9) | collective-permute-done | bytes 262176 | tf_op jit(solution)/shard_map/ppermute | solution.py:642
  69.5 4.6 %all-to-all-done.refs_0_ = f32[32,72,128]{2,1,0:T(8,128)} async-done(((f32[32,72,128]{2,1,0:T(8,128)}), f32[32,72,128]{2,1,0:T(8,128)}, u32[]{:S(2)}, u32[]{:S(2)}) %all-to-all-start) | async-done | bytes 1179680 | tf_op jit(solution)/shard_map/all_to_all | solution.py:698
  74.1 11.6 %middle_planes.1 = (f32[32,2,4,8,128]{4,3,2,1,0:T(8,128)}, f32[1024,256]{1,0:T(8,128)}) custom-call(s32[1]{0:T(128)} %bitcast.ids_ref.me_ref, f32[32,72,128]{2,1,0:T(8,128)} %all-to-all-done.refs_0_, bf16[512,512]{1,0:T(8,128)(2,1)} %constant.65.clone.y_high.refs_1_, bf16[512,512]{1,0:T(8,128)(2,1)} %constant.66.clone.y_low.refs_2_, ...), custom_call_target="tpu_custom_call" | custom-call | flops 3221225472 | bytes 10616832 | tf_op jit(solution)/shard_map/middle_planes/pallas_call | solution.py:443
  85.7 3.4 %all-to-all-start.3 = ((f32[32,2,4,8,128]{4,3,2,1,0:T(8,128)}), f32[32,2,4,8,128]{4,3,2,1,0:T(8,128)}, u32[]{:S(2)}, u32[]{:S(2)}) async-start(f32[32,2,4,8,128]{4,3,2,1,0:T(8,128)} %get-tuple-element.53), calls=%async_computation.3 | async-start | bytes 2097152 | tf_op jit(solution)/shard_map/all_to_all | solution.py:698
  89.1 6.6 %odd_planes.1 = f32[32,2,4,8,128]{4,3,2,1,0:T(8,128)} custom-call(s32[1]{0:T(128)} %bitcast.ids_ref.me_ref, f32[1024,256]{1,0:T(8,128)} %get-tuple-element.47.freqs, bf16[2,256,512]{2,1,0:T(8,128)(2,1)} %constant.75.clone.x_high, bf16[2,256,512]{2,1,0:T(8,128)(2,1)} %constant.76.clone.x_low, bf16[512,512]{1,0:T(8,128)(2,1)} %constant.73.clone.refs_8_.y_high, ...), custom_call_target="tpu_custom_call" | custom-call | flops 1610612736 | bytes 3145728 | tf_op jit(solution)/shard_map/odd_planes/pallas_call | solution.py:443
  95.7 0.1 concatenate.34
  95.8 0.1 fusion.3
  95.9 0.1 collective-permute-start.10
  96.0 4.4 %collective-permute-start.11 = (f32[8,1,1280]{2,1,0:T(1,128)S(1)}, f32[8,1,1280]{2,1,0:T(1,128)S(1)}, u32[]{:S(2)}, u32[]{:S(2)}) collective-permute-start(f32[8,1,1280]{2,1,0:T(1,128)S(1)} %get-tuple-element.58), channel_id=1, source_target_pairs={{2,0},{4,2},{6,4},{8,6},{10,8},{12,10},{14,12},{16,14},{18,16},{20... | collective-permute-start | bytes 122888 | tf_op jit(solution)/shard_map/ppermute | solution.py:588
  100.4 11.7 %collective-permute-done.10 = f32[8,1,1280]{2,1,0:T(1,128)S(1)} collective-permute-done((f32[8,1,1280]{2,1,0:T(1,128)S(1)}, f32[8,1,1280]{2,1,0:T(1,128)S(1)}, u32[]{:S(2)}, u32[]{:S(2)}) %collective-permute-start.10) | collective-permute-done | bytes 40992 | tf_op jit(solution)/shard_map/ppermute | solution.py:587
  112.1 0.0 collective-permute-done.11
  112.1 0.1 fusion.1
  112.2 1.1 pad_maximum_fusion.extended
  113.3 3.0 %all-to-all-done.3.sent = f32[32,2,4,8,128]{4,3,2,1,0:T(8,128)} async-done(((f32[32,2,4,8,128]{4,3,2,1,0:T(8,128)}), f32[32,2,4,8,128]{4,3,2,1,0:T(8,128)}, u32[]{:S(2)}, u32[]{:S(2)}) %all-to-all-start.3) | async-done | bytes 1048608 | tf_op jit(solution)/shard_map/all_to_all | solution.py:698
  116.3 3.4 %all-to-all-start.2 = ((f32[32,2,4,8,128]{4,3,2,1,0:T(8,128)}), f32[32,2,4,8,128]{4,3,2,1,0:T(8,128)}, u32[]{:S(2)}, u32[]{:S(2)}) async-start(f32[32,2,4,8,128]{4,3,2,1,0:T(8,128)} %odd_planes.1), calls=%async_computation.2 | async-start | bytes 2097152 | tf_op jit(solution)/shard_map/all_to_all | solution.py:698
  119.6 15.5 %near_blocks.1.before_in = f32[8,8,1024]{2,1,0:T(8,128)} custom-call(f32[8,3,8,1280]{3,2,1,0:T(8,128)} %pad_maximum_fusion.extended, s32[6,8,1024]{2,1,0:T(8,128)} %codes.1, f32[6,8,8,8,1024]{4,3,2,1,0:T(8,128)} %blocks_ref.1), custom_call_target="tpu_custom_call" | custom-call | flops 6291456 | bytes 12582912 | tf_op jit(solution)/shard_map/near_blocks/pallas_call | solution.py:550
  135.1 5.8 %depth_gather.2.before_in = f32[8,8,1024]{2,1,0:T(8,128)} custom-call(f32[32,2,4,8,128]{4,3,2,1,0:T(8,128)} %all-to-all-done.3.sent, bf16[512,512]{1,0:T(8,128)(2,1)} %constant.77.clone.high_in, bf16[512,512]{1,0:T(8,128)(2,1)} %constant.78.clone.low_in, f32[8,8,1024]{2,1,0:T(8,128)} %near_blocks.1.before_in, s32[8,1024]{1,0:T(8,128)} %counts_in.3, ...), custom_call_target="tpu_custom_call" | custom-call | flops 4194304 | bytes 8388608 | tf_op jit(solution)/shard_map/depth_gather/pallas_call | solution.py:208
  141.0 5.8 %all-to-all-done.2.sent = f32[32,2,4,8,128]{4,3,2,1,0:T(8,128)} async-done(((f32[32,2,4,8,128]{4,3,2,1,0:T(8,128)}), f32[32,2,4,8,128]{4,3,2,1,0:T(8,128)}, u32[]{:S(2)}, u32[]{:S(2)}) %all-to-all-start.2) | async-done | bytes 1048608 | tf_op jit(solution)/shard_map/all_to_all | solution.py:698
  146.8 5.8 %depth_gather.3 = f32[8,8,1024]{2,1,0:T(8,128)} custom-call(f32[32,2,4,8,128]{4,3,2,1,0:T(8,128)} %all-to-all-done.2.sent, bf16[512,512]{1,0:T(8,128)(2,1)} %constant.77.clone.high_in, bf16[512,512]{1,0:T(8,128)(2,1)} %constant.78.clone.low_in, f32[8,8,1024]{2,1,0:T(8,128)} %depth_gather.2.before_in, s32[8,1024]{1,0:T(8,128)} %counts_in.3, ...), custom_call_target="tpu_custom_call" | custom-call | flops 4194304 | bytes 8388608 | tf_op jit(solution)/shard_map/depth_gather/pallas_call | solution.py:208
  (11 shorter events, 0.1 us)
Async XLA Ops:
  6.1 16.0 %copy-start = (f32[8,8,1024]{2,1,0:T(8,128)S(1)}, f32[8,8,1024]{2,1,0:T(8,128)}, u32[]{:S(2)}) copy-start(f32[8,8,1024]{2,1,0:T(8,128)} %refs_0_.3) | copy-start | bytes 786436
  6.1 16.0 %copy-start.2 = (s32[8,1024]{1,0:T(8,128)S(1)}, s32[8,1024]{1,0:T(8,128)}, u32[]{:S(2)}) copy-start(s32[8,1024]{1,0:T(8,128)} %counts_in.3) | copy-start | bytes 98308
  6.1 34.6 %all-to-all-start.1 = ((f32[32,64,128]{2,1,0:T(8,128)}), f32[32,64,128]{2,1,0:T(8,128)}, u32[]{:S(2)}, u32[]{:S(2)}) async-start(f32[32,64,128]{2,1,0:T(8,128)} %project_depth.3), calls=%async_computation.1 | async-start | bytes 2097152 | tf_op jit(solution)/shard_map/all_to_all | solution.py:698
  15.9 22.1 %collective-permute-start.2 = (f32[4,32,512]{2,1,0:T(8,128)}, f32[4,32,512]{2,1,0:T(8,128)}, u32[]{:S(2)}, u32[]{:S(2)}) collective-permute-start(f32[4,32,512]{2,1,0:T(8,128)} %get-tuple-element.34), channel_id=1, source_target_pairs={{0,8},{2,10},{4,12},{6,14},{8,0},{10,2},{12,4},{14,6},{16,24},{18,... | collective-permute-start | bytes 786440 | tf_op jit(solution)/shard_map/ppermute | solution.py:642
  17.6 20.3 %collective-permute-start.3 = (f32[2,32,512]{2,1,0:T(8,128)}, f32[2,32,512]{2,1,0:T(8,128)}, u32[]{:S(2)}, u32[]{:S(2)}) collective-permute-start(f32[2,32,512]{2,1,0:T(8,128)} %get-tuple-element.36), channel_id=1, source_target_pairs={{0,2},{2,4},{4,6},{6,0},{8,10},{10,12},{12,14},{14,8},{16,18},{18,... | collective-permute-start | bytes 393224 | tf_op jit(solution)/shard_map/ppermute | solution.py:652
  17.6 20.3 %collective-permute-start.4 = (f32[2,32,512]{2,1,0:T(8,128)}, f32[2,32,512]{2,1,0:T(8,128)}, u32[]{:S(2)}, u32[]{:S(2)}) collective-permute-start(f32[2,32,512]{2,1,0:T(8,128)} %get-tuple-element.37), channel_id=1, source_target_pairs={{0,4},{2,6},{4,0},{6,2},{8,12},{10,14},{12,8},{14,10},{16,20},{18,... | collective-permute-start | bytes 393224 | tf_op jit(solution)/shard_map/ppermute | solution.py:652
  19.1 18.8 %collective-permute-start.5 = (f32[2,32,512]{2,1,0:T(8,128)}, f32[2,32,512]{2,1,0:T(8,128)}, u32[]{:S(2)}, u32[]{:S(2)}) collective-permute-start(f32[2,32,512]{2,1,0:T(8,128)} %get-tuple-element.38), channel_id=1, source_target_pairs={{0,6},{2,0},{4,2},{6,4},{8,14},{10,8},{12,10},{14,12},{16,22},{18,... | collective-permute-start | bytes 393224 | tf_op jit(solution)/shard_map/ppermute | solution.py:652
  23.5 6.2 %copy-start.1 = (f32[8,8,1024]{2,1,0:T(8,128)S(1)}, f32[8,8,1024]{2,1,0:T(8,128)}, u32[]{:S(2)}) copy-start(f32[8,8,1024]{2,1,0:T(8,128)} %fusion.2) | copy-start | bytes 786436
  23.5 20.6 %copy-start.4 = (f32[2,32,512]{2,1,0:T(8,128)S(1)}, f32[2,32,512]{2,1,0:T(8,128)}, u32[]{:S(2)}) copy-start(f32[2,32,512]{2,1,0:T(8,128)} %get-tuple-element.43) | copy-start | bytes 393220
  29.7 18.6 %copy-start.3 = (f32[4,32,512]{2,1,0:T(8,128)S(1)}, f32[4,32,512]{2,1,0:T(8,128)}, u32[]{:S(2)}) copy-start(f32[4,32,512]{2,1,0:T(8,128)} %get-tuple-element.41) | copy-start | bytes 786436
  29.8 4.0 %collective-permute-start = (f32[8,8,16]{2,1,0:T(8,128)S(1)}, f32[8,8,16]{2,1,0:T(8,128)S(1)}, u32[]{:S(2)}, u32[]{:S(2)}) collective-permute-start(f32[8,8,16]{2,1,0:T(8,128)S(1)} %get-tuple-element.68), channel_id=1, source_target_pairs={{0,1},{1,0},{2,3},{3,2},{4,5},{5,4},{6,7},{7,6},{8,9},{9,8},{10,11... | collective-permute-start | bytes 12296 | tf_op jit(solution)/shard_map/ppermute | solution.py:578
  33.8 4.1 %collective-permute-start.1 = (f32[8,8,16]{2,1,0:T(8,128)S(1)}, f32[8,8,16]{2,1,0:T(8,128)S(1)}, u32[]{:S(2)}, u32[]{:S(2)}) collective-permute-start(f32[8,8,16]{2,1,0:T(8,128)S(1)} %get-tuple-element.67), channel_id=1, source_target_pairs={{1,0},{0,1},{3,2},{2,3},{5,4},{4,5},{7,6},{6,7},{9,8},{8,9},{11,10... | collective-permute-start | bytes 12296 | tf_op jit(solution)/shard_map/ppermute | solution.py:579
  40.7 33.4 %all-to-all-start = ((f32[32,72,128]{2,1,0:T(8,128)}), f32[32,72,128]{2,1,0:T(8,128)}, u32[]{:S(2)}, u32[]{:S(2)}) async-start(f32[32,72,128]{2,1,0:T(8,128)} %project_depth.2), calls=%async_computation | async-start | bytes 2359296 | tf_op jit(solution)/shard_map/all_to_all | solution.py:698
  46.7 22.8 %collective-permute-start.9 = (f32[4,32,512]{2,1,0:T(8,128)}, f32[4,32,512]{2,1,0:T(8,128)}, u32[]{:S(2)}, u32[]{:S(2)}) collective-permute-start(f32[4,32,512]{2,1,0:T(8,128)} %pad_maximum_fusion.4), channel_id=1, source_target_pairs={{0,8},{2,10},{4,12},{6,14},{8,0},{10,2},{12,4},{14,6},{16,24},{18,... | collective-permute-start | bytes 786440 | tf_op jit(solution)/shard_map/ppermute | solution.py:642
  49.3 10.2 %collective-permute-start.8 = (f32[2,32,512]{2,1,0:T(8,128)S(1)}, f32[2,32,512]{2,1,0:T(8,128)}, u32[]{:S(2)}, u32[]{:S(2)}) collective-permute-start(f32[2,32,512]{2,1,0:T(8,128)S(1)} %pad_maximum_fusion.9), channel_id=1, source_target_pairs={{0,6},{2,0},{4,2},{6,4},{8,14},{10,8},{12,10},{14,12},{16,22},{18,... | collective-permute-start | bytes 393224 | tf_op jit(solution)/shard_map/ppermute | solution.py:652
  51.0 10.9 %collective-permute-start.7 = (f32[2,32,512]{2,1,0:T(8,128)}, f32[2,32,512]{2,1,0:T(8,128)}, u32[]{:S(2)}, u32[]{:S(2)}) collective-permute-start(f32[2,32,512]{2,1,0:T(8,128)} %pad_maximum_fusion.8), channel_id=1, source_target_pairs={{0,4},{2,6},{4,0},{6,2},{8,12},{10,14},{12,8},{14,10},{16,20},{18,... | collective-permute-start | bytes 393224 | tf_op jit(solution)/shard_map/ppermute | solution.py:652
  52.2 10.6 %collective-permute-start.6 = (f32[2,32,512]{2,1,0:T(8,128)}, f32[2,32,512]{2,1,0:T(8,128)}, u32[]{:S(2)}, u32[]{:S(2)}) collective-permute-start(f32[2,32,512]{2,1,0:T(8,128)} %pad_maximum_fusion.7), channel_id=1, source_target_pairs={{0,2},{2,4},{4,6},{6,0},{8,10},{10,12},{12,14},{14,8},{16,18},{18,... | collective-permute-start | bytes 393224 | tf_op jit(solution)/shard_map/ppermute | solution.py:652
  85.7 30.6 %all-to-all-start.3 = ((f32[32,2,4,8,128]{4,3,2,1,0:T(8,128)}), f32[32,2,4,8,128]{4,3,2,1,0:T(8,128)}, u32[]{:S(2)}, u32[]{:S(2)}) async-start(f32[32,2,4,8,128]{4,3,2,1,0:T(8,128)} %get-tuple-element.53), calls=%async_computation.3 | async-start | bytes 2097152 | tf_op jit(solution)/shard_map/all_to_all | solution.py:698
  95.9 16.2 %collective-permute-start.10 = (f32[8,1,1280]{2,1,0:T(1,128)S(1)}, f32[8,1,1280]{2,1,0:T(1,128)S(1)}, u32[]{:S(2)}, u32[]{:S(2)}) collective-permute-start(f32[8,1,1280]{2,1,0:T(1,128)S(1)} %get-tuple-element.57), channel_id=1, source_target_pairs={{0,2},{2,4},{4,6},{6,8},{8,10},{10,12},{12,14},{14,16},{16,18},{18... | collective-permute-start | bytes 122888 | tf_op jit(solution)/shard_map/ppermute | solution.py:587
  96.0 16.1 %collective-permute-start.11 = (f32[8,1,1280]{2,1,0:T(1,128)S(1)}, f32[8,1,1280]{2,1,0:T(1,128)S(1)}, u32[]{:S(2)}, u32[]{:S(2)}) collective-permute-start(f32[8,1,1280]{2,1,0:T(1,128)S(1)} %get-tuple-element.58), channel_id=1, source_target_pairs={{2,0},{4,2},{6,4},{8,6},{10,8},{12,10},{14,12},{16,14},{18,16},{20... | collective-permute-start | bytes 122888 | tf_op jit(solution)/shard_map/ppermute | solution.py:588
  116.3 30.5 %all-to-all-start.2 = ((f32[32,2,4,8,128]{4,3,2,1,0:T(8,128)}), f32[32,2,4,8,128]{4,3,2,1,0:T(8,128)}, u32[]{:S(2)}, u32[]{:S(2)}) async-start(f32[32,2,4,8,128]{4,3,2,1,0:T(8,128)} %odd_planes.1), calls=%async_computation.2 | async-start | bytes 2097152 | tf_op jit(solution)/shard_map/all_to_all | solution.py:698

commit v14 on v12

--- a/solution.py
+++ b/solution.py
@@ -177,7 +177,7 @@
                 scratch[rows, tz * LANES : (tz + 1) * LANES] = total
             return carry
 
-        lax.fori_loop(0, plan.steps * plan.step_blocks, body, 0)
+        lax.fori_loop(0, plan.steps * plan.step_blocks, body, 0, unroll=True)
     for copy in loads[2:]:
         copy.wait()
     spectra = product(split(scratch[...]), (high[...], low[...])).T
@@ -357,9 +357,11 @@
             for m, source in enumerate((strips[i].at[j], blocks[j].at[i])):
                 sem = sems.at[len(held) + len(placed)]
                 placed.append(pltpu.make_async_copy(source, weights.at[m, rows], sem))
-    for copy in copies[:6] + placed + copies[6:]:
+    for copy in copies[:3]:
         copy.start()
     copies[0].wait()
+    for copy in copies[3:6] + placed + copies[6:]:
+        copy.start()
     cell_first = me_ref[0] - slab
     tile = pieces[cell_first + jnp.where(slab < plan.half, plan.half, 0), plan.piece_rows :]
     parts = plan.nx // LANES
@@ -477,7 +479,7 @@
                 out[p, :, lanes] = jnp.where(counts[:, lanes] > p, far[p], 0.0) if last else far[p]
             return carry
 
-        lax.fori_loop(0, plan.steps * plan.step_blocks, body, 0)
+        lax.fori_loop(0, plan.steps * plan.step_blocks, body, 0, unroll=True)
 
 
 def gather(plan, chunk, counts, before, projection, high, low, pieces):

time: 152 us -> 152 us (level)
  no operation moved by 1% of the time
where the time goes in v14:
time: 152 us; the launch traced here: 151 us
  Pallas kernels  64.3 us (42%)
  waiting for transfers between devices  43.1 us (28%)
  starting transfers between devices  33 us (22%)
  other arithmetic  6.06 us (4%)
  local copies, waits for them, and re-layouts  4.53 us (3%)
    pallas_call x4, Pallas kernels, projection_call(): pl.pallas_call(kernel, in_specs=[pl.BlockSpec(memory_space=pl.ANY)] * (le...  23.8 us
    pallas_call x3, Pallas kernels, plane_call(): pl.pallas_call(functools.partial(kernel, plan), grid=(1,) if tables else...  22.6 us
    all_to_all x4, starting transfers between devices, exchange(): return lax.all_to_all(pieces, axes, split_axis=0, concat_axis=0, tiled=True)  17.6 us
    all_to_all x4, waiting for transfers between devices, exchange(): return lax.all_to_all(pieces, axes, split_axis=0, concat_axis=0, tiled=True)  16.1 us
    pallas_call x1, Pallas kernels, near_field(): pl.pallas_call(functools.partial(near_kernel, plan), grid=(plan.cell_cols...  15.5 us
    ppermute x1, waiting for transfers between devices, extend_planes(): before = lax.ppermute(wide[:, -1:], 'slab', up)  11.7 us
    ppermute x2, waiting for transfers between devices, outer_shift(): return lax.ppermute(value, 'slab', pairs)  6.67 us
    ppermute x6, starting transfers between devices, inner_shift(): return lax.ppermute(value, 'slab', pairs)  4.69 us
  transfers between devices with their start and end apart: 16, of which 10 were waited for; matrix products, arithmetic and copies ran while one was open for 7% of the time, Pallas kernels for 28%

profile of v14, /device:TPU:0, one launch (start us, length us, event | category | flops | bytes accessed | tf_op | source)
XLA Modules:
  0.0 151.4 jit_solution(16363306521299392178)
XLA Ops:
  0.0 6.1 %project_depth.3 = f32[32,64,128]{2,1,0:T(8,128)} custom-call(f32[8,8,1024]{2,1,0:T(8,128)} %refs_0_.3, s32[8,1024]{1,0:T(8,128)} %counts_in.3, bf16[512,512]{1,0:T(8,128)(2,1)} %constant.63.clone.refs_2_, bf16[512,512]{1,0:T(8,128)(2,1)} %constant.64.clone.refs_3_, f32[8,2,2,16,8,1024]{5,4,3,2,1,0:T(8,128)} %bitcast.18), custom_call_target="tpu_custom_call" | custom-call | flops 4194304 | bytes 8388608 | tf_op jit(solution)/shard_map/project_depth/pallas_call | solution.py:208
  6.1 0.0 copy-start
  6.1 0.0 copy-start.2
  6.1 7.4 %all-to-all-start.1 = ((f32[32,64,128]{2,1,0:T(8,128)}), f32[32,64,128]{2,1,0:T(8,128)}, u32[]{:S(2)}, u32[]{:S(2)}) async-start(f32[32,64,128]{2,1,0:T(8,128)} %project_depth.3), calls=%async_computation.1 | async-start | bytes 2097152 | tf_op jit(solution)/shard_map/all_to_all | solution.py:683
  13.5 2.3 %pick_planes.1 = (f32[4,32,512]{2,1,0:T(8,128)}, f32[4,32,512]{2,1,0:T(8,128)}, f32[2,32,512]{2,1,0:T(8,128)}, f32[2,32,512]{2,1,0:T(8,128)}, f32[2,32,512]{2,1,0:T(8,128)}, /*index=5*/f32[2,32,512]{2,1,0:T(8,128)}) custom-call(s32[1]{0:T(128)} %bitcast.ids_ref.me_ref, f32[64,32,512]{2,1,0:T(8,128)} %bitcast.22), custom_call_target="tpu_custom_call" | custom-call | bytes 2097152 | tf_op jit(solution)/shard_map/pick_planes/pallas_call | solution.py:606
  15.9 1.8 %collective-permute-start.2 = (f32[4,32,512]{2,1,0:T(8,128)}, f32[4,32,512]{2,1,0:T(8,128)}, u32[]{:S(2)}, u32[]{:S(2)}) collective-permute-start(f32[4,32,512]{2,1,0:T(8,128)} %get-tuple-element.34), channel_id=1, source_target_pairs={{0,8},{2,10},{4,12},{6,14},{8,0},{10,2},{12,4},{14,6},{16,24},{18,... | collective-permute-start | bytes 786440 | tf_op jit(solution)/shard_map/ppermute | solution.py:627
  17.6 0.0 collective-permute-start.3
  17.6 1.5 collective-permute-start.4
  19.1 1.4 collective-permute-start.5
  20.6 1.3 slice.56
  21.9 0.1 rev.4
  22.1 0.0 copy-done
  22.1 0.0 copy-done.2
  22.1 0.7 fusion.2
  22.8 0.7 pad_maximum_fusion.5.refs_4_
  23.5 6.1 %project_depth.2 = f32[32,72,128]{2,1,0:T(8,128)} custom-call(f32[8,8,1024]{2,1,0:T(8,128)} %refs_0_.3, s32[8,1024]{1,0:T(8,128)} %counts_in.3, bf16[512,512]{1,0:T(8,128)(2,1)} %constant.63.clone.refs_2_, bf16[512,512]{1,0:T(8,128)(2,1)} %constant.64.clone.refs_3_, f32[32,8,128]{2,1,0:T(8,128)} %pad_maximum_fusion.5.refs_4_, f32[8,2,2,16,8,1024]{5,4,3,2,1,0:T(8,128)} %bitcast.19), custom_call_target="tpu_custom_call" | custom-call | flops 4194304 | bytes 8388608 | tf_op jit(solution)/shard_map/project_depth/pallas_call | solution.py:208
  29.7 0.0 copy-done.1
  29.7 0.0 copy-start.3
  29.7 0.1 fusion.4
  29.8 1.5 collective-permute-start
  31.3 2.6 %collective-permute-done = f32[8,8,16]{2,1,0:T(8,128)S(1)} collective-permute-done((f32[8,8,16]{2,1,0:T(8,128)S(1)}, f32[8,8,16]{2,1,0:T(8,128)S(1)}, u32[]{:S(2)}, u32[]{:S(2)}) %collective-permute-start) | collective-permute-done | bytes 4128 | tf_op jit(solution)/shard_map/ppermute | solution.py:563
  33.8 1.4 collective-permute-start.1
  35.2 2.8 %collective-permute-done.1 = f32[8,8,16]{2,1,0:T(8,128)S(1)} collective-permute-done((f32[8,8,16]{2,1,0:T(8,128)S(1)}, f32[8,8,16]{2,1,0:T(8,128)S(1)}, u32[]{:S(2)}, u32[]{:S(2)}) %collective-permute-start.1) | collective-permute-done | bytes 4128 | tf_op jit(solution)/shard_map/ppermute | solution.py:564
  38.0 0.0 collective-permute-done.3
  38.0 0.0 collective-permute-done.4
  38.0 0.0 collective-permute-done.5
  38.0 0.0 collective-permute-done.2
  38.0 2.7 %all-to-all-done.1.pieces = f32[32,64,128]{2,1,0:T(8,128)} async-done(((f32[32,64,128]{2,1,0:T(8,128)}), f32[32,64,128]{2,1,0:T(8,128)}, u32[]{:S(2)}, u32[]{:S(2)}) %all-to-all-start.1) | async-done | bytes 1048608 | tf_op jit(solution)/shard_map/all_to_all | solution.py:683
  40.7 3.4 %all-to-all-start = ((f32[32,72,128]{2,1,0:T(8,128)}), f32[32,72,128]{2,1,0:T(8,128)}, u32[]{:S(2)}, u32[]{:S(2)}) async-start(f32[32,72,128]{2,1,0:T(8,128)} %project_depth.2), calls=%async_computation | async-start | bytes 2359296 | tf_op jit(solution)/shard_map/all_to_all | solution.py:683
  44.1 0.9 fusion.5
  45.0 1.0 fusion.7
  46.0 0.7 pad_maximum_fusion.4
  46.7 1.6 %collective-permute-start.9 = (f32[4,32,512]{2,1,0:T(8,128)}, f32[4,32,512]{2,1,0:T(8,128)}, u32[]{:S(2)}, u32[]{:S(2)}) collective-permute-start(f32[4,32,512]{2,1,0:T(8,128)} %pad_maximum_fusion.4), channel_id=1, source_target_pairs={{0,8},{2,10},{4,12},{6,14},{8,0},{10,2},{12,4},{14,6},{16,24},{18,... | collective-permute-start | bytes 786440 | tf_op jit(solution)/shard_map/ppermute | solution.py:627
  48.3 1.0 constant_dynamic-slice_fusion
  49.3 1.0 collective-permute-start.8
  50.3 0.7 pad_maximum_fusion.8
  51.0 0.5 collective-permute-start.7
  51.5 0.7 pad_maximum_fusion.7
  52.2 0.2 collective-permute-start.6
  52.4 0.7 pad_maximum_fusion.3.refs_14_
  53.1 0.7 pad_maximum_fusion.6.refs_10_
  53.8 5.8 %even_planes.1.refs_5_ = f32[1024,512]{1,0:T(8,128)} custom-call(s32[1]{0:T(128)} %bitcast.ids_ref.me_ref, f32[32,64,128]{2,1,0:T(8,128)} %all-to-all-done.1.pieces, bf16[512,512]{1,0:T(8,128)(2,1)} %constant.65.clone.y_high.refs_1_, bf16[512,512]{1,0:T(8,128)(2,1)} %constant.66.clone.y_low.refs_2_, bf16[2,256,512]{2,1,0:T(8,128)(2,1)} %constant.67.clone.x_high, ...), custom_call_target="tpu_custom_call" | custom-call | flops 1610612736 | bytes 3145728 | tf_op jit(solution)/shard_map/even_planes/pallas_call | solution.py:428
  59.5 0.0 collective-permute-done.8.refs_13_
  59.5 2.4 %collective-permute-done.7.refs_12_ = f32[2,32,512]{2,1,0:T(8,128)} collective-permute-done((f32[2,32,512]{2,1,0:T(8,128)}, f32[2,32,512]{2,1,0:T(8,128)}, u32[]{:S(2)}, u32[]{:S(2)}) %collective-permute-start.7) | collective-permute-done | bytes 131104 | tf_op jit(solution)/shard_map/ppermute | solution.py:637
  61.9 0.9 collective-permute-done.6.refs_11_
  62.8 6.7 %collective-permute-done.9.refs_15_ = f32[4,32,512]{2,1,0:T(8,128)} collective-permute-done((f32[4,32,512]{2,1,0:T(8,128)}, f32[4,32,512]{2,1,0:T(8,128)}, u32[]{:S(2)}, u32[]{:S(2)}) %collective-permute-start.9) | collective-permute-done | bytes 262176 | tf_op jit(solution)/shard_map/ppermute | solution.py:627
  69.5 4.6 %all-to-all-done.refs_0_ = f32[32,72,128]{2,1,0:T(8,128)} async-done(((f32[32,72,128]{2,1,0:T(8,128)}), f32[32,72,128]{2,1,0:T(8,128)}, u32[]{:S(2)}, u32[]{:S(2)}) %all-to-all-start) | async-done | bytes 1179680 | tf_op jit(solution)/shard_map/all_to_all | solution.py:683
  74.1 10.2 %middle_planes.1 = (f32[32,2,4,8,128]{4,3,2,1,0:T(8,128)}, f32[1024,256]{1,0:T(8,128)}) custom-call(s32[1]{0:T(128)} %bitcast.ids_ref.me_ref, f32[32,72,128]{2,1,0:T(8,128)} %all-to-all-done.refs_0_, bf16[512,512]{1,0:T(8,128)(2,1)} %constant.65.clone.y_high.refs_1_, bf16[512,512]{1,0:T(8,128)(2,1)} %constant.66.clone.y_low.refs_2_, ...), custom_call_target="tpu_custom_call" | custom-call | flops 3221225472 | bytes 10616832 | tf_op jit(solution)/shard_map/middle_planes/pallas_call | solution.py:428
  84.3 3.4 %all-to-all-start.3 = ((f32[32,2,4,8,128]{4,3,2,1,0:T(8,128)}), f32[32,2,4,8,128]{4,3,2,1,0:T(8,128)}, u32[]{:S(2)}, u32[]{:S(2)}) async-start(f32[32,2,4,8,128]{4,3,2,1,0:T(8,128)} %get-tuple-element.53), calls=%async_computation.3 | async-start | bytes 2097152 | tf_op jit(solution)/shard_map/all_to_all | solution.py:683
  87.7 6.6 %odd_planes.1 = f32[32,2,4,8,128]{4,3,2,1,0:T(8,128)} custom-call(s32[1]{0:T(128)} %bitcast.ids_ref.me_ref, f32[1024,256]{1,0:T(8,128)} %get-tuple-element.47.freqs, bf16[2,256,512]{2,1,0:T(8,128)(2,1)} %constant.75.clone.x_high, bf16[2,256,512]{2,1,0:T(8,128)(2,1)} %constant.76.clone.x_low, bf16[512,512]{1,0:T(8,128)(2,1)} %constant.73.clone.refs_8_.y_high, ...), custom_call_target="tpu_custom_call" | custom-call | flops 1610612736 | bytes 3145728 | tf_op jit(solution)/shard_map/odd_planes/pallas_call | solution.py:428
  94.4 0.1 concatenate.34
  94.5 0.1 fusion.3
  94.5 0.1 collective-permute-start.10
  94.6 4.4 %collective-permute-start.11 = (f32[8,1,1280]{2,1,0:T(1,128)S(1)}, f32[8,1,1280]{2,1,0:T(1,128)S(1)}, u32[]{:S(2)}, u32[]{:S(2)}) collective-permute-start(f32[8,1,1280]{2,1,0:T(1,128)S(1)} %get-tuple-element.58), channel_id=1, source_target_pairs={{2,0},{4,2},{6,4},{8,6},{10,8},{12,10},{14,12},{16,14},{18,16},{20... | collective-permute-start | bytes 122888 | tf_op jit(solution)/shard_map/ppermute | solution.py:573
  99.0 11.7 %collective-permute-done.10 = f32[8,1,1280]{2,1,0:T(1,128)S(1)} collective-permute-done((f32[8,1,1280]{2,1,0:T(1,128)S(1)}, f32[8,1,1280]{2,1,0:T(1,128)S(1)}, u32[]{:S(2)}, u32[]{:S(2)}) %collective-permute-start.10) | collective-permute-done | bytes 40992 | tf_op jit(solution)/shard_map/ppermute | solution.py:572
  110.7 0.0 collective-permute-done.11
  110.7 0.1 fusion.1
  110.8 1.1 pad_maximum_fusion.extended
  111.9 3.0 %all-to-all-done.3.sent = f32[32,2,4,8,128]{4,3,2,1,0:T(8,128)} async-done(((f32[32,2,4,8,128]{4,3,2,1,0:T(8,128)}), f32[32,2,4,8,128]{4,3,2,1,0:T(8,128)}, u32[]{:S(2)}, u32[]{:S(2)}) %all-to-all-start.3) | async-done | bytes 1048608 | tf_op jit(solution)/shard_map/all_to_all | solution.py:683
  114.9 3.4 %all-to-all-start.2 = ((f32[32,2,4,8,128]{4,3,2,1,0:T(8,128)}), f32[32,2,4,8,128]{4,3,2,1,0:T(8,128)}, u32[]{:S(2)}, u32[]{:S(2)}) async-start(f32[32,2,4,8,128]{4,3,2,1,0:T(8,128)} %odd_planes.1), calls=%async_computation.2 | async-start | bytes 2097152 | tf_op jit(solution)/shard_map/all_to_all | solution.py:683
  118.3 15.5 %near_blocks.1.before_in = f32[8,8,1024]{2,1,0:T(8,128)} custom-call(f32[8,3,8,1280]{3,2,1,0:T(8,128)} %pad_maximum_fusion.extended, s32[6,8,1024]{2,1,0:T(8,128)} %codes.1, f32[6,8,8,8,1024]{4,3,2,1,0:T(8,128)} %blocks_ref.1), custom_call_target="tpu_custom_call" | custom-call | flops 6291456 | bytes 12582912 | tf_op jit(solution)/shard_map/near_blocks/pallas_call | solution.py:535
  133.8 5.8 %depth_gather.2.before_in = f32[8,8,1024]{2,1,0:T(8,128)} custom-call(f32[32,2,4,8,128]{4,3,2,1,0:T(8,128)} %all-to-all-done.3.sent, bf16[512,512]{1,0:T(8,128)(2,1)} %constant.77.clone.high_in, bf16[512,512]{1,0:T(8,128)(2,1)} %constant.78.clone.low_in, f32[8,8,1024]{2,1,0:T(8,128)} %near_blocks.1.before_in, s32[8,1024]{1,0:T(8,128)} %counts_in.3, ...), custom_call_target="tpu_custom_call" | custom-call | flops 4194304 | bytes 8388608 | tf_op jit(solution)/shard_map/depth_gather/pallas_call | solution.py:208
  139.6 5.8 %all-to-all-done.2.sent = f32[32,2,4,8,128]{4,3,2,1,0:T(8,128)} async-done(((f32[32,2,4,8,128]{4,3,2,1,0:T(8,128)}), f32[32,2,4,8,128]{4,3,2,1,0:T(8,128)}, u32[]{:S(2)}, u32[]{:S(2)}) %all-to-all-start.2) | async-done | bytes 1048608 | tf_op jit(solution)/shard_map/all_to_all | solution.py:683
  145.5 5.8 %depth_gather.3 = f32[8,8,1024]{2,1,0:T(8,128)} custom-call(f32[32,2,4,8,128]{4,3,2,1,0:T(8,128)} %all-to-all-done.2.sent, bf16[512,512]{1,0:T(8,128)(2,1)} %constant.77.clone.high_in, bf16[512,512]{1,0:T(8,128)(2,1)} %constant.78.clone.low_in, f32[8,8,1024]{2,1,0:T(8,128)} %depth_gather.2.before_in, s32[8,1024]{1,0:T(8,128)} %counts_in.3, ...), custom_call_target="tpu_custom_call" | custom-call | flops 4194304 | bytes 8388608 | tf_op jit(solution)/shard_map/depth_gather/pallas_call | solution.py:208
  (11 shorter events, 0.1 us)
Async XLA Ops:
  6.1 16.0 %copy-start = (f32[8,8,1024]{2,1,0:T(8,128)S(1)}, f32[8,8,1024]{2,1,0:T(8,128)}, u32[]{:S(2)}) copy-start(f32[8,8,1024]{2,1,0:T(8,128)} %refs_0_.3) | copy-start | bytes 786436
  6.1 16.0 %copy-start.2 = (s32[8,1024]{1,0:T(8,128)S(1)}, s32[8,1024]{1,0:T(8,128)}, u32[]{:S(2)}) copy-start(s32[8,1024]{1,0:T(8,128)} %counts_in.3) | copy-start | bytes 98308
  6.1 34.6 %all-to-all-start.1 = ((f32[32,64,128]{2,1,0:T(8,128)}), f32[32,64,128]{2,1,0:T(8,128)}, u32[]{:S(2)}, u32[]{:S(2)}) async-start(f32[32,64,128]{2,1,0:T(8,128)} %project_depth.3), calls=%async_computation.1 | async-start | bytes 2097152 | tf_op jit(solution)/shard_map/all_to_all | solution.py:683
  15.9 22.1 %collective-permute-start.2 = (f32[4,32,512]{2,1,0:T(8,128)}, f32[4,32,512]{2,1,0:T(8,128)}, u32[]{:S(2)}, u32[]{:S(2)}) collective-permute-start(f32[4,32,512]{2,1,0:T(8,128)} %get-tuple-element.34), channel_id=1, source_target_pairs={{0,8},{2,10},{4,12},{6,14},{8,0},{10,2},{12,4},{14,6},{16,24},{18,... | collective-permute-start | bytes 786440 | tf_op jit(solution)/shard_map/ppermute | solution.py:627
  17.6 20.3 %collective-permute-start.3 = (f32[2,32,512]{2,1,0:T(8,128)}, f32[2,32,512]{2,1,0:T(8,128)}, u32[]{:S(2)}, u32[]{:S(2)}) collective-permute-start(f32[2,32,512]{2,1,0:T(8,128)} %get-tuple-element.36), channel_id=1, source_target_pairs={{0,2},{2,4},{4,6},{6,0},{8,10},{10,12},{12,14},{14,8},{16,18},{18,... | collective-permute-start | bytes 393224 | tf_op jit(solution)/shard_map/ppermute | solution.py:637
  17.6 20.3 %collective-permute-start.4 = (f32[2,32,512]{2,1,0:T(8,128)}, f32[2,32,512]{2,1,0:T(8,128)}, u32[]{:S(2)}, u32[]{:S(2)}) collective-permute-start(f32[2,32,512]{2,1,0:T(8,128)} %get-tuple-element.37), channel_id=1, source_target_pairs={{0,4},{2,6},{4,0},{6,2},{8,12},{10,14},{12,8},{14,10},{16,20},{18,... | collective-permute-start | bytes 393224 | tf_op jit(solution)/shard_map/ppermute | solution.py:637
  19.1 18.8 %collective-permute-start.5 = (f32[2,32,512]{2,1,0:T(8,128)}, f32[2,32,512]{2,1,0:T(8,128)}, u32[]{:S(2)}, u32[]{:S(2)}) collective-permute-start(f32[2,32,512]{2,1,0:T(8,128)} %get-tuple-element.38), channel_id=1, source_target_pairs={{0,6},{2,0},{4,2},{6,4},{8,14},{10,8},{12,10},{14,12},{16,22},{18,... | collective-permute-start | bytes 393224 | tf_op jit(solution)/shard_map/ppermute | solution.py:637
  23.5 6.2 %copy-start.1 = (f32[8,8,1024]{2,1,0:T(8,128)S(1)}, f32[8,8,1024]{2,1,0:T(8,128)}, u32[]{:S(2)}) copy-start(f32[8,8,1024]{2,1,0:T(8,128)} %fusion.2) | copy-start | bytes 786436
  23.5 20.6 %copy-start.4 = (f32[2,32,512]{2,1,0:T(8,128)S(1)}, f32[2,32,512]{2,1,0:T(8,128)}, u32[]{:S(2)}) copy-start(f32[2,32,512]{2,1,0:T(8,128)} %get-tuple-element.43) | copy-start | bytes 393220
  29.7 18.6 %copy-start.3 = (f32[4,32,512]{2,1,0:T(8,128)S(1)}, f32[4,32,512]{2,1,0:T(8,128)}, u32[]{:S(2)}) copy-start(f32[4,32,512]{2,1,0:T(8,128)} %get-tuple-element.41) | copy-start | bytes 786436
  29.8 4.0 %collective-permute-start = (f32[8,8,16]{2,1,0:T(8,128)S(1)}, f32[8,8,16]{2,1,0:T(8,128)S(1)}, u32[]{:S(2)}, u32[]{:S(2)}) collective-permute-start(f32[8,8,16]{2,1,0:T(8,128)S(1)} %get-tuple-element.68), channel_id=1, source_target_pairs={{0,1},{1,0},{2,3},{3,2},{4,5},{5,4},{6,7},{7,6},{8,9},{9,8},{10,11... | collective-permute-start | bytes 12296 | tf_op jit(solution)/shard_map/ppermute | solution.py:563
  33.8 4.1 %collective-permute-start.1 = (f32[8,8,16]{2,1,0:T(8,128)S(1)}, f32[8,8,16]{2,1,0:T(8,128)S(1)}, u32[]{:S(2)}, u32[]{:S(2)}) collective-permute-start(f32[8,8,16]{2,1,0:T(8,128)S(1)} %get-tuple-element.67), channel_id=1, source_target_pairs={{1,0},{0,1},{3,2},{2,3},{5,4},{4,5},{7,6},{6,7},{9,8},{8,9},{11,10... | collective-permute-start | bytes 12296 | tf_op jit(solution)/shard_map/ppermute | solution.py:564
  40.7 33.4 %all-to-all-start = ((f32[32,72,128]{2,1,0:T(8,128)}), f32[32,72,128]{2,1,0:T(8,128)}, u32[]{:S(2)}, u32[]{:S(2)}) async-start(f32[32,72,128]{2,1,0:T(8,128)} %project_depth.2), calls=%async_computation | async-start | bytes 2359296 | tf_op jit(solution)/shard_map/all_to_all | solution.py:683
  46.7 22.8 %collective-permute-start.9 = (f32[4,32,512]{2,1,0:T(8,128)}, f32[4,32,512]{2,1,0:T(8,128)}, u32[]{:S(2)}, u32[]{:S(2)}) collective-permute-start(f32[4,32,512]{2,1,0:T(8,128)} %pad_maximum_fusion.4), channel_id=1, source_target_pairs={{0,8},{2,10},{4,12},{6,14},{8,0},{10,2},{12,4},{14,6},{16,24},{18,... | collective-permute-start | bytes 786440 | tf_op jit(solution)/shard_map/ppermute | solution.py:627
  49.3 10.2 %collective-permute-start.8 = (f32[2,32,512]{2,1,0:T(8,128)S(1)}, f32[2,32,512]{2,1,0:T(8,128)}, u32[]{:S(2)}, u32[]{:S(2)}) collective-permute-start(f32[2,32,512]{2,1,0:T(8,128)S(1)} %pad_maximum_fusion.9), channel_id=1, source_target_pairs={{0,6},{2,0},{4,2},{6,4},{8,14},{10,8},{12,10},{14,12},{16,22},{18,... | collective-permute-start | bytes 393224 | tf_op jit(solution)/shard_map/ppermute | solution.py:637
  51.0 10.9 %collective-permute-start.7 = (f32[2,32,512]{2,1,0:T(8,128)}, f32[2,32,512]{2,1,0:T(8,128)}, u32[]{:S(2)}, u32[]{:S(2)}) collective-permute-start(f32[2,32,512]{2,1,0:T(8,128)} %pad_maximum_fusion.8), channel_id=1, source_target_pairs={{0,4},{2,6},{4,0},{6,2},{8,12},{10,14},{12,8},{14,10},{16,20},{18,... | collective-permute-start | bytes 393224 | tf_op jit(solution)/shard_map/ppermute | solution.py:637
  52.2 10.6 %collective-permute-start.6 = (f32[2,32,512]{2,1,0:T(8,128)}, f32[2,32,512]{2,1,0:T(8,128)}, u32[]{:S(2)}, u32[]{:S(2)}) collective-permute-start(f32[2,32,512]{2,1,0:T(8,128)} %pad_maximum_fusion.7), channel_id=1, source_target_pairs={{0,2},{2,4},{4,6},{6,0},{8,10},{10,12},{12,14},{14,8},{16,18},{18,... | collective-permute-start | bytes 393224 | tf_op jit(solution)/shard_map/ppermute | solution.py:637
  84.3 30.6 %all-to-all-start.3 = ((f32[32,2,4,8,128]{4,3,2,1,0:T(8,128)}), f32[32,2,4,8,128]{4,3,2,1,0:T(8,128)}, u32[]{:S(2)}, u32[]{:S(2)}) async-start(f32[32,2,4,8,128]{4,3,2,1,0:T(8,128)} %get-tuple-element.53), calls=%async_computation.3 | async-start | bytes 2097152 | tf_op jit(solution)/shard_map/all_to_all | solution.py:683
  94.5 16.2 %collective-permute-start.10 = (f32[8,1,1280]{2,1,0:T(1,128)S(1)}, f32[8,1,1280]{2,1,0:T(1,128)S(1)}, u32[]{:S(2)}, u32[]{:S(2)}) collective-permute-start(f32[8,1,1280]{2,1,0:T(1,128)S(1)} %get-tuple-element.57), channel_id=1, source_target_pairs={{0,2},{2,4},{4,6},{6,8},{8,10},{10,12},{12,14},{14,16},{16,18},{18... | collective-permute-start | bytes 122888 | tf_op jit(solution)/shard_map/ppermute | solution.py:572
  94.6 16.1 %collective-permute-start.11 = (f32[8,1,1280]{2,1,0:T(1,128)S(1)}, f32[8,1,1280]{2,1,0:T(1,128)S(1)}, u32[]{:S(2)}, u32[]{:S(2)}) collective-permute-start(f32[8,1,1280]{2,1,0:T(1,128)S(1)} %get-tuple-element.58), channel_id=1, source_target_pairs={{2,0},{4,2},{6,4},{8,6},{10,8},{12,10},{14,12},{16,14},{18,16},{20... | collective-permute-start | bytes 122888 | tf_op jit(solution)/shard_map/ppermute | solution.py:573
  114.9 30.5 %all-to-all-start.2 = ((f32[32,2,4,8,128]{4,3,2,1,0:T(8,128)}), f32[32,2,4,8,128]{4,3,2,1,0:T(8,128)}, u32[]{:S(2)}, u32[]{:S(2)}) async-start(f32[32,2,4,8,128]{4,3,2,1,0:T(8,128)} %odd_planes.1), calls=%async_computation.2 | async-start | bytes 2097152 | tf_op jit(solution)/shard_map/all_to_all | solution.py:683

commit v15 on v14

--- a/solution.py
+++ b/solution.py
@@ -357,11 +357,9 @@
             for m, source in enumerate((strips[i].at[j], blocks[j].at[i])):
                 sem = sems.at[len(held) + len(placed)]
                 placed.append(pltpu.make_async_copy(source, weights.at[m, rows], sem))
-    for copy in copies[:3]:
+    for copy in copies[:6] + placed + copies[6:]:
         copy.start()
     copies[0].wait()
-    for copy in copies[3:6] + placed + copies[6:]:
-        copy.start()
     cell_first = me_ref[0] - slab
     tile = pieces[cell_first + jnp.where(slab < plan.half, plan.half, 0), plan.piece_rows :]
     parts = plan.nx // LANES
@@ -560,9 +558,11 @@
 
 def extend_rows(plan, masked):
     up, down = ring_pairs("cell")
-    left = lax.ppermute(masked[:, :, -NZC:], "cell", up)
-    right = lax.ppermute(masked[:, :, :NZC], "cell", down)
-    return (left, right)
+    first, last = (masked[:, :, :NZC], masked[:, :, -NZC:])
+    if plan.cells == 2:
+        both = lax.ppermute(jnp.concatenate([last, first], axis=2), "cell", up)
+        return (both[:, :, :NZC], both[:, :, NZC:])
+    return (lax.ppermute(last, "cell", up), lax.ppermute(first, "cell", down))
 
 
 def extend_planes(plan, masked, left, right):

time: 152 us -> 152 us (level)
  waiting for transfers between devices: 43.1 us -> 46.1 us
    ppermute x6, waiting for transfers between devices: 3.29 us -> 10.2 us  [inner_shift(): return lax.ppermute(value, 'slab', pairs)]
    ppermute x1, waiting for transfers between devices: 0.01 us -> 6.91 us  [extend_planes(): after = lax.ppermute(wide[:, :1], 'slab', down)]
    ppermute x1, waiting for transfers between devices: 11.7 us -> 5.01 us  [extend_planes(): before = lax.ppermute(wide[:, -1:], 'slab', up)]
    ppermute x2 -> x1, waiting for transfers between devices: 5.34 us -> 0.01 us  [extend_rows(): both = lax.ppermute(jnp.concatenate([last, first], axis=2), 'cell', up)]
  transfers between devices with their start and end apart: 16 -> 15, of which waited for: 10 -> 12; matrix products, arithmetic and copies ran while one was open for 7% -> 6% of each run, Pallas kernels for 28% -> 28%
where the time goes in v15:
time: 152 us
  Pallas kernels  64.3 us (42%)
  waiting for transfers between devices  46.1 us (30%)
  starting transfers between devices  31.6 us (21%)
  other arithmetic  4.7 us (3%)
  local copies, waits for them, and re-layouts  4.36 us (3%)
    pallas_call x4, Pallas kernels, projection_call(): pl.pallas_call(kernel, in_specs=[pl.BlockSpec(memory_space=pl.ANY)] * (le...  23.8 us
    pallas_call x3, Pallas kernels, plane_call(): pl.pallas_call(functools.partial(kernel, plan), grid=(1,) if tables else...  22.6 us
    all_to_all x4, starting transfers between devices, exchange(): return lax.all_to_all(pieces, axes, split_axis=0, concat_axis=0, tiled=True)  17.7 us
    all_to_all x4, waiting for transfers between devices, exchange(): return lax.all_to_all(pieces, axes, split_axis=0, concat_axis=0, tiled=True)  16.5 us
    pallas_call x1, Pallas kernels, near_field(): pl.pallas_call(functools.partial(near_kernel, plan), grid=(plan.cell_cols...  15.5 us
    ppermute x6, waiting for transfers between devices, inner_shift(): return lax.ppermute(value, 'slab', pairs)  10.2 us
    ppermute x2, waiting for transfers between devices, outer_shift(): return lax.ppermute(value, 'slab', pairs)  7.49 us
    ppermute x1, waiting for transfers between devices, extend_planes(): after = lax.ppermute(wide[:, :1], 'slab', down)  6.91 us
  transfers between devices with their start and end apart: 15, of which 12 were waited for; matrix products, arithmetic and copies ran while one was open for 6% of the time, Pallas kernels for 28%

profile of v15, /device:TPU:0, one launch (start us, length us, event | category | flops | bytes accessed | tf_op | source)
XLA Modules:
  0.0 151.5 jit_solution(7065718780558804605)
XLA Ops:
  0.0 6.1 %project_depth.3 = f32[32,64,128]{2,1,0:T(8,128)} custom-call(f32[8,8,1024]{2,1,0:T(8,128)} %refs_0_.3, s32[8,1024]{1,0:T(8,128)} %counts_in.3, bf16[512,512]{1,0:T(8,128)(2,1)} %constant.63.clone.refs_2_, bf16[512,512]{1,0:T(8,128)(2,1)} %constant.64.clone.refs_3_, f32[8,2,2,16,8,1024]{5,4,3,2,1,0:T(8,128)} %bitcast.18), custom_call_target="tpu_custom_call" | custom-call | flops 4194304 | bytes 8388608 | tf_op jit(solution)/shard_map/project_depth/pallas_call | solution.py:208
  6.1 7.4 %all-to-all-start.1 = ((f32[32,64,128]{2,1,0:T(8,128)}), f32[32,64,128]{2,1,0:T(8,128)}, u32[]{:S(2)}, u32[]{:S(2)}) async-start(f32[32,64,128]{2,1,0:T(8,128)} %project_depth.3), calls=%async_computation.1 | async-start | bytes 2097152 | tf_op jit(solution)/shard_map/all_to_all | solution.py:683
  13.5 2.3 %pick_planes.1 = (f32[4,32,512]{2,1,0:T(8,128)}, f32[4,32,512]{2,1,0:T(8,128)}, f32[2,32,512]{2,1,0:T(8,128)}, f32[2,32,512]{2,1,0:T(8,128)}, f32[2,32,512]{2,1,0:T(8,128)}, /*index=5*/f32[2,32,512]{2,1,0:T(8,128)}) custom-call(s32[1]{0:T(128)} %bitcast.ids_ref.me_ref, f32[64,32,512]{2,1,0:T(8,128)} %bitcast.22), custom_call_target="tpu_custom_call" | custom-call | bytes 2097152 | tf_op jit(solution)/shard_map/pick_planes/pallas_call | solution.py:606
  15.9 1.8 %collective-permute-start.1 = (f32[4,32,512]{2,1,0:T(8,128)}, f32[4,32,512]{2,1,0:T(8,128)}, u32[]{:S(2)}, u32[]{:S(2)}) collective-permute-start(f32[4,32,512]{2,1,0:T(8,128)} %get-tuple-element.34), channel_id=1, source_target_pairs={{0,8},{2,10},{4,12},{6,14},{8,0},{10,2},{12,4},{14,6},{16,24},{18,... | collective-permute-start | bytes 786440 | tf_op jit(solution)/shard_map/ppermute | solution.py:627
  17.6 1.3 slice.62
  18.9 0.1 rev.4
  19.1 0.7 pad_maximum_fusion.5.refs_4_
  19.8 0.0 copy-start
  19.8 6.1 %project_depth.2 = f32[32,72,128]{2,1,0:T(8,128)} custom-call(f32[8,8,1024]{2,1,0:T(8,128)} %refs_0_.3, s32[8,1024]{1,0:T(8,128)} %counts_in.3, bf16[512,512]{1,0:T(8,128)(2,1)} %constant.63.clone.refs_2_, bf16[512,512]{1,0:T(8,128)(2,1)} %constant.64.clone.refs_3_, f32[32,8,128]{2,1,0:T(8,128)} %pad_maximum_fusion.5.refs_4_, f32[8,2,2,16,8,1024]{5,4,3,2,1,0:T(8,128)} %bitcast.19), custom_call_target="tpu_custom_call" | custom-call | flops 4194304 | bytes 8388608 | tf_op jit(solution)/shard_map/project_depth/pallas_call | solution.py:208
  26.0 0.0 copy-done
  26.0 0.0 copy-done.3
  26.0 0.0 copy-start.4
  26.0 0.0 copy-start.1
  26.0 0.7 copy-done.1
  26.8 0.1 fusion.4
  26.8 0.1 pad_maximum_fusion.11
  26.9 1.5 collective-permute-start
  28.4 0.0 collective-permute-start.2
  28.4 1.5 collective-permute-start.3
  29.9 1.4 collective-permute-start.4
  31.3 0.0 collective-permute-done
  31.3 0.1 fusion.10
  31.4 3.2 %collective-permute-done.2 = f32[2,32,512]{2,1,0:T(8,128)S(1)} collective-permute-done((f32[2,32,512]{2,1,0:T(8,128)}, f32[2,32,512]{2,1,0:T(8,128)S(1)}, u32[]{:S(2)}, u32[]{:S(2)}) %collective-permute-start.2) | collective-permute-done | bytes 131104 | tf_op jit(solution)/shard_map/ppermute | solution.py:637
  34.6 1.1 collective-permute-done.3
  35.6 2.1 %collective-permute-done.4 = f32[2,32,512]{2,1,0:T(8,128)S(1)} collective-permute-done((f32[2,32,512]{2,1,0:T(8,128)}, f32[2,32,512]{2,1,0:T(8,128)S(1)}, u32[]{:S(2)}, u32[]{:S(2)}) %collective-permute-start.4) | collective-permute-done | bytes 131104 | tf_op jit(solution)/shard_map/ppermute | solution.py:637
  37.7 0.0 collective-permute-done.1
  37.7 3.0 %all-to-all-done.1.pieces = f32[32,64,128]{2,1,0:T(8,128)} async-done(((f32[32,64,128]{2,1,0:T(8,128)}), f32[32,64,128]{2,1,0:T(8,128)}, u32[]{:S(2)}, u32[]{:S(2)}) %all-to-all-start.1) | async-done | bytes 1048608 | tf_op jit(solution)/shard_map/all_to_all | solution.py:683
  40.7 3.4 %all-to-all-start = ((f32[32,72,128]{2,1,0:T(8,128)}), f32[32,72,128]{2,1,0:T(8,128)}, u32[]{:S(2)}, u32[]{:S(2)}) async-start(f32[32,72,128]{2,1,0:T(8,128)} %project_depth.2), calls=%async_computation | async-start | bytes 2359296 | tf_op jit(solution)/shard_map/all_to_all | solution.py:683
  44.1 0.9 fusion.5
  45.0 1.7 %collective-permute-start.8 = (f32[4,32,512]{2,1,0:T(8,128)S(1)}, f32[4,32,512]{2,1,0:T(8,128)}, u32[]{:S(2)}, u32[]{:S(2)}) collective-permute-start(f32[4,32,512]{2,1,0:T(8,128)S(1)} %pad_maximum_fusion.4), channel_id=1, source_target_pairs={{0,8},{2,10},{4,12},{6,14},{8,0},{10,2},{12,4},{14,6},{16,24},{18,... | collective-permute-start | bytes 786440 | tf_op jit(solution)/shard_map/ppermute | solution.py:627
  46.7 0.0 copy-done.4
  46.7 1.0 constant_dynamic-slice_fusion
  47.7 1.0 collective-permute-start.7
  48.7 0.7 pad_maximum_fusion.8
  49.4 0.5 collective-permute-start.6
  49.9 0.7 pad_maximum_fusion.7
  50.6 0.2 collective-permute-start.5
  50.8 0.7 pad_maximum_fusion.3.refs_14_
  51.5 0.7 pad_maximum_fusion.6.refs_10_
  52.2 5.8 %even_planes.1.refs_5_ = f32[1024,512]{1,0:T(8,128)} custom-call(s32[1]{0:T(128)} %bitcast.ids_ref.me_ref, f32[32,64,128]{2,1,0:T(8,128)} %all-to-all-done.1.pieces, bf16[512,512]{1,0:T(8,128)(2,1)} %constant.65.clone.y_high.refs_1_, bf16[512,512]{1,0:T(8,128)(2,1)} %constant.66.clone.y_low.refs_2_, bf16[2,256,512]{2,1,0:T(8,128)(2,1)} %constant.67.clone.x_high, ...), custom_call_target="tpu_custom_call" | custom-call | flops 1610612736 | bytes 3145728 | tf_op jit(solution)/shard_map/even_planes/pallas_call | solution.py:426
  57.9 0.0 collective-permute-done.7.refs_13_
  57.9 3.8 %collective-permute-done.6.refs_12_ = f32[2,32,512]{2,1,0:T(8,128)} collective-permute-done((f32[2,32,512]{2,1,0:T(8,128)}, f32[2,32,512]{2,1,0:T(8,128)}, u32[]{:S(2)}, u32[]{:S(2)}) %collective-permute-start.6) | collective-permute-done | bytes 131104 | tf_op jit(solution)/shard_map/ppermute | solution.py:637
  61.7 0.2 collective-permute-done.5.refs_11_
  61.9 7.5 %collective-permute-done.8.refs_15_ = f32[4,32,512]{2,1,0:T(8,128)} collective-permute-done((f32[4,32,512]{2,1,0:T(8,128)S(1)}, f32[4,32,512]{2,1,0:T(8,128)}, u32[]{:S(2)}, u32[]{:S(2)}) %collective-permute-start.8) | collective-permute-done | bytes 262176 | tf_op jit(solution)/shard_map/ppermute | solution.py:627
  69.4 4.7 %all-to-all-done.refs_0_ = f32[32,72,128]{2,1,0:T(8,128)} async-done(((f32[32,72,128]{2,1,0:T(8,128)}), f32[32,72,128]{2,1,0:T(8,128)}, u32[]{:S(2)}, u32[]{:S(2)}) %all-to-all-start) | async-done | bytes 1179680 | tf_op jit(solution)/shard_map/all_to_all | solution.py:683
  74.0 10.2 %middle_planes.1 = (f32[32,2,4,8,128]{4,3,2,1,0:T(8,128)}, f32[1024,256]{1,0:T(8,128)}) custom-call(s32[1]{0:T(128)} %bitcast.ids_ref.me_ref, f32[32,72,128]{2,1,0:T(8,128)} %all-to-all-done.refs_0_, bf16[512,512]{1,0:T(8,128)(2,1)} %constant.65.clone.y_high.refs_1_, bf16[512,512]{1,0:T(8,128)(2,1)} %constant.66.clone.y_low.refs_2_, ...), custom_call_target="tpu_custom_call" | custom-call | flops 3221225472 | bytes 10616832 | tf_op jit(solution)/shard_map/middle_planes/pallas_call | solution.py:426
  84.3 0.0 copy-start.2
  84.3 3.5 %all-to-all-start.3 = ((f32[32,2,4,8,128]{4,3,2,1,0:T(8,128)}), f32[32,2,4,8,128]{4,3,2,1,0:T(8,128)}, u32[]{:S(2)}, u32[]{:S(2)}) async-start(f32[32,2,4,8,128]{4,3,2,1,0:T(8,128)} %get-tuple-element.53), calls=%async_computation.3 | async-start | bytes 2097152 | tf_op jit(solution)/shard_map/all_to_all | solution.py:683
  87.8 6.6 %odd_planes.1 = f32[32,2,4,8,128]{4,3,2,1,0:T(8,128)} custom-call(s32[1]{0:T(128)} %bitcast.ids_ref.me_ref, f32[1024,256]{1,0:T(8,128)} %get-tuple-element.47.freqs, bf16[2,256,512]{2,1,0:T(8,128)(2,1)} %constant.75.clone.x_high, bf16[2,256,512]{2,1,0:T(8,128)(2,1)} %constant.76.clone.x_low, bf16[512,512]{1,0:T(8,128)(2,1)} %constant.73.clone.refs_8_.y_high, ...), custom_call_target="tpu_custom_call" | custom-call | flops 1610612736 | bytes 3145728 | tf_op jit(solution)/shard_map/odd_planes/pallas_call | solution.py:426
  94.5 0.0 copy-done.2
  94.5 0.1 concatenate.38
  94.6 0.1 fusion.3
  94.6 4.3 %collective-permute-start.10 = (f32[8,1,1280]{2,1,0:T(1,128)S(1)}, f32[8,1,1280]{2,1,0:T(1,128)S(1)}, u32[]{:S(2)}, u32[]{:S(2)}) collective-permute-start(f32[8,1,1280]{2,1,0:T(1,128)S(1)} %get-tuple-element.58), channel_id=1, source_target_pairs={{2,0},{4,2},{6,4},{8,6},{10,8},{12,10},{14,12},{16,14},{18,16},{20... | collective-permute-start | bytes 122888 | tf_op jit(solution)/shard_map/ppermute | solution.py:573
  98.9 0.0 collective-permute-start.9
  98.9 6.9 %collective-permute-done.10 = f32[8,1,1280]{2,1,0:T(1,128)S(1)} collective-permute-done((f32[8,1,1280]{2,1,0:T(1,128)S(1)}, f32[8,1,1280]{2,1,0:T(1,128)S(1)}, u32[]{:S(2)}, u32[]{:S(2)}) %collective-permute-start.10) | collective-permute-done | bytes 40992 | tf_op jit(solution)/shard_map/ppermute | solution.py:573
  105.8 5.0 %collective-permute-done.9 = f32[8,1,1280]{2,1,0:T(1,128)S(1)} collective-permute-done((f32[8,1,1280]{2,1,0:T(1,128)S(1)}, f32[8,1,1280]{2,1,0:T(1,128)S(1)}, u32[]{:S(2)}, u32[]{:S(2)}) %collective-permute-start.9) | collective-permute-done | bytes 40992 | tf_op jit(solution)/shard_map/ppermute | solution.py:572
  110.8 0.1 fusion.1
  110.9 1.1 pad_maximum_fusion.extended
  112.0 3.0 %all-to-all-done.3.sent = f32[32,2,4,8,128]{4,3,2,1,0:T(8,128)} async-done(((f32[32,2,4,8,128]{4,3,2,1,0:T(8,128)}), f32[32,2,4,8,128]{4,3,2,1,0:T(8,128)}, u32[]{:S(2)}, u32[]{:S(2)}) %all-to-all-start.3) | async-done | bytes 1048608 | tf_op jit(solution)/shard_map/all_to_all | solution.py:683
  115.0 3.4 %all-to-all-start.2 = ((f32[32,2,4,8,128]{4,3,2,1,0:T(8,128)}), f32[32,2,4,8,128]{4,3,2,1,0:T(8,128)}, u32[]{:S(2)}, u32[]{:S(2)}) async-start(f32[32,2,4,8,128]{4,3,2,1,0:T(8,128)} %odd_planes.1), calls=%async_computation.2 | async-start | bytes 2097152 | tf_op jit(solution)/shard_map/all_to_all | solution.py:683
  118.4 15.5 %near_blocks.1.before_in = f32[8,8,1024]{2,1,0:T(8,128)} custom-call(f32[8,3,8,1280]{3,2,1,0:T(8,128)} %pad_maximum_fusion.extended, s32[6,8,1024]{2,1,0:T(8,128)} %codes.1, f32[6,8,8,8,1024]{4,3,2,1,0:T(8,128)} %blocks_ref.1), custom_call_target="tpu_custom_call" | custom-call | flops 6291456 | bytes 12582912 | tf_op jit(solution)/shard_map/near_blocks/pallas_call | solution.py:533
  133.9 5.8 %depth_gather.2.before_in = f32[8,8,1024]{2,1,0:T(8,128)} custom-call(f32[32,2,4,8,128]{4,3,2,1,0:T(8,128)} %all-to-all-done.3.sent, bf16[512,512]{1,0:T(8,128)(2,1)} %constant.77.clone.high_in, bf16[512,512]{1,0:T(8,128)(2,1)} %constant.78.clone.low_in, f32[8,8,1024]{2,1,0:T(8,128)} %near_blocks.1.before_in, s32[8,1024]{1,0:T(8,128)} %counts_in.3, ...), custom_call_target="tpu_custom_call" | custom-call | flops 4194304 | bytes 8388608 | tf_op jit(solution)/shard_map/depth_gather/pallas_call | solution.py:208
  139.7 5.8 %all-to-all-done.2.sent = f32[32,2,4,8,128]{4,3,2,1,0:T(8,128)} async-done(((f32[32,2,4,8,128]{4,3,2,1,0:T(8,128)}), f32[32,2,4,8,128]{4,3,2,1,0:T(8,128)}, u32[]{:S(2)}, u32[]{:S(2)}) %all-to-all-start.2) | async-done | bytes 1048608 | tf_op jit(solution)/shard_map/all_to_all | solution.py:683
  145.6 5.8 %depth_gather.3 = f32[8,8,1024]{2,1,0:T(8,128)} custom-call(f32[32,2,4,8,128]{4,3,2,1,0:T(8,128)} %all-to-all-done.2.sent, bf16[512,512]{1,0:T(8,128)(2,1)} %constant.77.clone.high_in, bf16[512,512]{1,0:T(8,128)(2,1)} %constant.78.clone.low_in, f32[8,8,1024]{2,1,0:T(8,128)} %depth_gather.2.before_in, s32[8,1024]{1,0:T(8,128)} %counts_in.3, ...), custom_call_target="tpu_custom_call" | custom-call | flops 4194304 | bytes 8388608 | tf_op jit(solution)/shard_map/depth_gather/pallas_call | solution.py:208
  (11 shorter events, 0.1 us)
Async XLA Ops:
  6.1 34.6 %all-to-all-start.1 = ((f32[32,64,128]{2,1,0:T(8,128)}), f32[32,64,128]{2,1,0:T(8,128)}, u32[]{:S(2)}, u32[]{:S(2)}) async-start(f32[32,64,128]{2,1,0:T(8,128)} %project_depth.3), calls=%async_computation.1 | async-start | bytes 2097152 | tf_op jit(solution)/shard_map/all_to_all | solution.py:683
  15.9 21.8 %collective-permute-start.1 = (f32[4,32,512]{2,1,0:T(8,128)}, f32[4,32,512]{2,1,0:T(8,128)}, u32[]{:S(2)}, u32[]{:S(2)}) collective-permute-start(f32[4,32,512]{2,1,0:T(8,128)} %get-tuple-element.34), channel_id=1, source_target_pairs={{0,8},{2,10},{4,12},{6,14},{8,0},{10,2},{12,4},{14,6},{16,24},{18,... | collective-permute-start | bytes 786440 | tf_op jit(solution)/shard_map/ppermute | solution.py:627
  19.8 6.2 %copy-start = (f32[8,8,1024]{2,1,0:T(8,128)S(1)}, f32[8,8,1024]{2,1,0:T(8,128)}, u32[]{:S(2)}) copy-start(f32[8,8,1024]{2,1,0:T(8,128)} %refs_0_.3) | copy-start | bytes 786436
  19.8 6.2 %copy-start.3 = (s32[8,1024]{1,0:T(8,128)S(1)}, s32[8,1024]{1,0:T(8,128)}, u32[]{:S(2)}) copy-start(s32[8,1024]{1,0:T(8,128)} %counts_in.3) | copy-start | bytes 98308
  26.0 20.7 %copy-start.4 = (f32[4,32,512]{2,1,0:T(8,128)S(1)}, f32[4,32,512]{2,1,0:T(8,128)}, u32[]{:S(2)}) copy-start(f32[4,32,512]{2,1,0:T(8,128)} %get-tuple-element.41) | copy-start | bytes 786436
  26.0 0.7 copy-start.1
  26.9 4.4 %collective-permute-start = (f32[8,8,32]{2,1,0:T(8,128)S(1)}, f32[8,8,32]{2,1,0:T(8,128)S(1)}, u32[]{:S(2)}, u32[]{:S(2)}) collective-permute-start(f32[8,8,32]{2,1,0:T(8,128)S(1)} %pad_maximum_fusion.11), channel_id=1, source_target_pairs={{0,1},{1,0},{2,3},{3,2},{4,5},{5,4},{6,7},{7,6},{8,9},{9,8},{10,11... | collective-permute-start | bytes 24584 | tf_op jit(solution)/shard_map/ppermute | solution.py:563
  28.4 6.2 %collective-permute-start.2 = (f32[2,32,512]{2,1,0:T(8,128)}, f32[2,32,512]{2,1,0:T(8,128)S(1)}, u32[]{:S(2)}, u32[]{:S(2)}) collective-permute-start(f32[2,32,512]{2,1,0:T(8,128)} %get-tuple-element.36), channel_id=1, source_target_pairs={{0,2},{2,4},{4,6},{6,0},{8,10},{10,12},{12,14},{14,8},{16,18},{18,... | collective-permute-start | bytes 393224 | tf_op jit(solution)/shard_map/ppermute | solution.py:637
  28.4 7.2 %collective-permute-start.3 = (f32[2,32,512]{2,1,0:T(8,128)}, f32[2,32,512]{2,1,0:T(8,128)S(1)}, u32[]{:S(2)}, u32[]{:S(2)}) collective-permute-start(f32[2,32,512]{2,1,0:T(8,128)} %get-tuple-element.37), channel_id=1, source_target_pairs={{0,4},{2,6},{4,0},{6,2},{8,12},{10,14},{12,8},{14,10},{16,20},{18,... | collective-permute-start | bytes 393224 | tf_op jit(solution)/shard_map/ppermute | solution.py:637
  29.9 7.8 %collective-permute-start.4 = (f32[2,32,512]{2,1,0:T(8,128)}, f32[2,32,512]{2,1,0:T(8,128)S(1)}, u32[]{:S(2)}, u32[]{:S(2)}) collective-permute-start(f32[2,32,512]{2,1,0:T(8,128)} %get-tuple-element.38), channel_id=1, source_target_pairs={{0,6},{2,0},{4,2},{6,4},{8,14},{10,8},{12,10},{14,12},{16,22},{18,... | collective-permute-start | bytes 393224 | tf_op jit(solution)/shard_map/ppermute | solution.py:637
  40.7 33.4 %all-to-all-start = ((f32[32,72,128]{2,1,0:T(8,128)}), f32[32,72,128]{2,1,0:T(8,128)}, u32[]{:S(2)}, u32[]{:S(2)}) async-start(f32[32,72,128]{2,1,0:T(8,128)} %project_depth.2), calls=%async_computation | async-start | bytes 2359296 | tf_op jit(solution)/shard_map/all_to_all | solution.py:683
  45.0 24.3 %collective-permute-start.8 = (f32[4,32,512]{2,1,0:T(8,128)S(1)}, f32[4,32,512]{2,1,0:T(8,128)}, u32[]{:S(2)}, u32[]{:S(2)}) collective-permute-start(f32[4,32,512]{2,1,0:T(8,128)S(1)} %pad_maximum_fusion.4), channel_id=1, source_target_pairs={{0,8},{2,10},{4,12},{6,14},{8,0},{10,2},{12,4},{14,6},{16,24},{18,... | collective-permute-start | bytes 786440 | tf_op jit(solution)/shard_map/ppermute | solution.py:627
  47.7 10.2 %collective-permute-start.7 = (f32[2,32,512]{2,1,0:T(8,128)S(1)}, f32[2,32,512]{2,1,0:T(8,128)}, u32[]{:S(2)}, u32[]{:S(2)}) collective-permute-start(f32[2,32,512]{2,1,0:T(8,128)S(1)} %pad_maximum_fusion.9), channel_id=1, source_target_pairs={{0,6},{2,0},{4,2},{6,4},{8,14},{10,8},{12,10},{14,12},{16,22},{18,... | collective-permute-start | bytes 393224 | tf_op jit(solution)/shard_map/ppermute | solution.py:637
  49.4 12.3 %collective-permute-start.6 = (f32[2,32,512]{2,1,0:T(8,128)}, f32[2,32,512]{2,1,0:T(8,128)}, u32[]{:S(2)}, u32[]{:S(2)}) collective-permute-start(f32[2,32,512]{2,1,0:T(8,128)} %pad_maximum_fusion.8), channel_id=1, source_target_pairs={{0,4},{2,6},{4,0},{6,2},{8,12},{10,14},{12,8},{14,10},{16,20},{18,... | collective-permute-start | bytes 393224 | tf_op jit(solution)/shard_map/ppermute | solution.py:637
  50.6 11.3 %collective-permute-start.5 = (f32[2,32,512]{2,1,0:T(8,128)}, f32[2,32,512]{2,1,0:T(8,128)}, u32[]{:S(2)}, u32[]{:S(2)}) collective-permute-start(f32[2,32,512]{2,1,0:T(8,128)} %pad_maximum_fusion.7), channel_id=1, source_target_pairs={{0,2},{2,4},{4,6},{6,0},{8,10},{10,12},{12,14},{14,8},{16,18},{18,... | collective-permute-start | bytes 393224 | tf_op jit(solution)/shard_map/ppermute | solution.py:637
  84.3 10.2 %copy-start.2 = (f32[8,8,1024]{2,1,0:T(8,128)S(1)}, f32[8,8,1024]{2,1,0:T(8,128)}, u32[]{:S(2)}) copy-start(f32[8,8,1024]{2,1,0:T(8,128)} %copy-done.1) | copy-start | bytes 786436
  84.3 30.7 %all-to-all-start.3 = ((f32[32,2,4,8,128]{4,3,2,1,0:T(8,128)}), f32[32,2,4,8,128]{4,3,2,1,0:T(8,128)}, u32[]{:S(2)}, u32[]{:S(2)}) async-start(f32[32,2,4,8,128]{4,3,2,1,0:T(8,128)} %get-tuple-element.53), calls=%async_computation.3 | async-start | bytes 2097152 | tf_op jit(solution)/shard_map/all_to_all | solution.py:683
  94.6 11.2 %collective-permute-start.10 = (f32[8,1,1280]{2,1,0:T(1,128)S(1)}, f32[8,1,1280]{2,1,0:T(1,128)S(1)}, u32[]{:S(2)}, u32[]{:S(2)}) collective-permute-start(f32[8,1,1280]{2,1,0:T(1,128)S(1)} %get-tuple-element.58), channel_id=1, source_target_pairs={{2,0},{4,2},{6,4},{8,6},{10,8},{12,10},{14,12},{16,14},{18,16},{20... | collective-permute-start | bytes 122888 | tf_op jit(solution)/shard_map/ppermute | solution.py:573
  98.9 11.9 %collective-permute-start.9 = (f32[8,1,1280]{2,1,0:T(1,128)S(1)}, f32[8,1,1280]{2,1,0:T(1,128)S(1)}, u32[]{:S(2)}, u32[]{:S(2)}) collective-permute-start(f32[8,1,1280]{2,1,0:T(1,128)S(1)} %get-tuple-element.57), channel_id=1, source_target_pairs={{0,2},{2,4},{4,6},{6,8},{8,10},{10,12},{12,14},{14,16},{16,18},{18... | collective-permute-start | bytes 122888 | tf_op jit(solution)/shard_map/ppermute | solution.py:572
  115.0 30.5 %all-to-all-start.2 = ((f32[32,2,4,8,128]{4,3,2,1,0:T(8,128)}), f32[32,2,4,8,128]{4,3,2,1,0:T(8,128)}, u32[]{:S(2)}, u32[]{:S(2)}) async-start(f32[32,2,4,8,128]{4,3,2,1,0:T(8,128)} %odd_planes.1), calls=%async_computation.2 | async-start | bytes 2097152 | tf_op jit(solution)/shard_map/all_to_all | solution.py:683
